TPU v7x, 32 devices: a whole 2x2x4 slice. The times are simulated.
32 devices in a mesh: group: 2 (over y), node: 4 (over z), sample: 2 (over x), head: 2 (over core).
Axes of the slice: x: 2, y: 2, z: 4, core: 2. Of those that a mesh axis runs over, the one named last changes fastest.
Arguments:
- mesh_node_state: bfloat16 [4, 2048, 512], P(('group', 'sample'), 'node'), parts along dimension 0, may hold values from -6 to 6
- cotangent: bfloat16 [4, 2048, 512], P(('group', 'sample'), 'node', 'head'), parts along dimension 0, may hold values from -6 to 6
- query_weight: bfloat16 [512, 512], P('node', 'head'), may hold values from -8 to 8
- key_weight: bfloat16 [512, 512], P('node', 'head'), may hold values from -8 to 8
- value_weight: bfloat16 [512, 512], P('node', 'head'), may hold values from -0.25 to 0.25
- output_weight: bfloat16 [512, 512], P('head', 'node'), may hold values from -0.25 to 0.25
- adapter_down_weight: bfloat16 [3, 512, 16], replicated, may hold values from -0.25 to 0.25
- adapter_up_weight: bfloat16 [3, 16, 512], P(None, None, 'head'), may hold values from -1.5 to 1.5
- neighbour_key_blocks: int32 [16, 6], replicated, may hold values from 0 to 15, as said below
- block_node_order: int32 [2048], P('node'), may hold values from 0 to 2047, as said below
Outputs:
- mesh_out: bfloat16 [4, 2048, 512], P(('group', 'sample'), 'node', 'head'), parts along dimension 0
- lora_down_grad: float32 [6, 512, 16], P('group'), parts along dimension 0
- lora_up_grad: float32 [6, 16, 512], P('group', None, 'head'), parts along dimension 0
There are 2 independent parts, one for each index of `group`. A program takes and returns all parts, laid end to end along the dimension named above; an argument that names none is the same for every part. Nothing has to cross between parts.
Inputs may be any that keep to these rules, and one draw needn't show every extreme that they name: `neighbour_key_blocks`: row b starts with b itself; every entry lies within 4 of b; entries may repeat. `block_node_order`: A permutation that maps each aligned range of 512 positions onto the same range of nodes.
All inputs are finite; a program needn't handle non-finite values.
Results may differ from a plain program's by a relative error of at most 0.011.
Values may be sent and summed in bfloat16 or wider, within the bound.
No kernel may reach another device: no remote copies, remote signals or barrier semaphores. Data moves between devices by JAX's collectives and lax.ppermute only.
A program may use at most 64 MiB of HBM per device.

v0:
```python
import math

import jax
import jax.numpy as jnp
from jax import lax
from jax.sharding import PartitionSpec as P

LATENT_WIDTH = 512
H = 4
BLK = 128
HB = 4


adapter_scale = 0.5
masked_value = -1e30
pad_block = -1000000


def padded(value, sides, width):
    for axis, dim in sides:
        size, length = (lax.axis_size(axis), value.shape[dim])
        up = [(i, (i + 1) % size) for i in range(size - 1)]
        down = [(j, i) for i, j in up]
        last = lax.slice_in_dim(value, length - width, length, axis=dim)
        initial = lax.slice_in_dim(value, 0, width, axis=dim)
        before = lax.ppermute(last, axis, up)
        after = lax.ppermute(initial, axis, down)
        value = jnp.concatenate([before, value, after], axis=dim)
    return value


def shifted(value, axis, steps):
    count = lax.axis_size(axis)
    initial, last = (max(0, -steps), min(count, count - steps))
    return lax.ppermute(value, axis, [(source, source + steps) for source in range(initial, last)])


def norm_rows(values):
    widened = values.astype(jnp.float32)
    center = widened - jnp.mean(widened, axis=-1, keepdims=True)
    spread = jnp.mean(center * center, axis=-1, keepdims=True)
    return (center * lax.rsqrt(spread + 1e-05)).astype(jnp.bfloat16)


def block_allowed(table_rows, first_block):
    block_ids = first_block + jnp.arange(table_rows.shape[0], dtype=jnp.int32)
    targets = block_ids[:, None] + jnp.arange(2 * HB + 1, dtype=jnp.int32)[None, :] - HB
    return jnp.any(table_rows[:, :, None] == targets[:, None, :], axis=1)


def head_tiles(source, column):
    head_size = LATENT_WIDTH // H
    picked = source[:, :, column * head_size : (column + 1) * head_size]
    return picked.reshape(source.shape[0], source.shape[1] // BLK, BLK, head_size)


def join_heads(tile_list, samples, node_count):
    return jnp.concatenate([tiles.reshape(samples, node_count, -1) for tiles in tile_list], axis=2)


def window_stack(extended, block_count):
    span_list = []
    for offset in range(2 * HB + 1):
        span_list.append(extended[:, offset : offset + block_count])
    return jnp.stack(span_list, axis=2)


def score_tiles(query_tiles, key_window, allowed):
    scores = jnp.einsum(
        "sibd,siokd->sibok", query_tiles, key_window, preferred_element_type=jnp.float32
    )
    scores = scores * (1.0 / math.sqrt(LATENT_WIDTH // H))
    return jnp.where(allowed[None, :, None, :, None], scores, masked_value)


def head_forward(query_tiles, key_window, value_window, allowed):
    scores = score_tiles(query_tiles, key_window, allowed)
    row_max = jnp.max(scores, axis=(3, 4), keepdims=True)
    log_total = row_max + jnp.log(jnp.sum(jnp.exp(scores - row_max), axis=(3, 4), keepdims=True))
    prob_narrow = jnp.exp(scores - log_total).astype(jnp.bfloat16)
    attended = jnp.einsum(
        "sibok,siokd->sibd", prob_narrow, value_window, preferred_element_type=jnp.float32
    )
    return (attended.astype(jnp.bfloat16), log_total[:, :, :, 0, 0])


def query_backward(
    query_tiles, key_window, value_window, grad_tiles, log_total, row_delta, allowed
):
    scores = score_tiles(query_tiles, key_window, allowed)
    prob_wide = jnp.exp(scores - log_total[:, :, :, None, None])
    prob_grad = jnp.einsum(
        "sibd,siokd->sibok", grad_tiles, value_window, preferred_element_type=jnp.float32
    )
    score_grad = (
        prob_wide
        * (prob_grad - row_delta[:, :, :, None, None])
        * (1.0 / math.sqrt(LATENT_WIDTH // H))
    ).astype(jnp.bfloat16)
    query_grad = jnp.einsum(
        "sibok,siokd->sibd", score_grad, key_window, preferred_element_type=jnp.float32
    )
    return (query_grad.astype(jnp.bfloat16), score_grad, prob_wide.astype(jnp.bfloat16))


def fold_windows(tiles, block_count):
    extended = jnp.zeros((tiles.shape[0], block_count + 2 * HB) + tiles.shape[3:], jnp.float32)
    for offset in range(2 * HB + 1):
        extended = extended.at[:, offset : offset + block_count].add(tiles[:, :, offset])
    return extended


def shards(
    mesh_node_state,
    cotangent,
    query_weight,
    key_weight,
    value_weight,
    output_weight,
    adapter_down_weight,
    adapter_up_weight,
    neighbour_key_blocks,
    block_node_order,
):
    samples, node_count, model_width = mesh_node_state.shape
    columns = query_weight.shape[1]
    head_count = columns // (LATENT_WIDTH // H)
    block_count = node_count // BLK
    rim_rows = HB * BLK
    node_rank = lax.axis_index("node")
    local_order = block_node_order - node_rank * node_count
    ordered = mesh_node_state[:, local_order, :]
    normed = norm_rows(ordered)
    flattened_rows = normed.reshape(-1, model_width)
    reduced_rank_term = [
        jnp.dot(
            flattened_rows, adapter_down_weight[member_block], preferred_element_type=jnp.float32
        ).astype(jnp.bfloat16)
        for member_block in range(3)
    ]
    pieces = (
        lax.all_gather(query_weight, "node", axis=0, tiled=True),
        lax.all_gather(key_weight, "node", axis=0, tiled=True),
        lax.all_gather(value_weight, "node", axis=0, tiled=True),
    )
    inputs = flattened_rows
    principal_terms = tuple(
        (
            jnp.dot(inputs, weight_piece, preferred_element_type=jnp.float32)
            for weight_piece in pieces
        )
    )
    projected = []
    for member_block in range(3):
        summed_result = principal_terms[member_block] + adapter_scale * jnp.dot(
            reduced_rank_term[member_block],
            adapter_up_weight[member_block],
            preferred_element_type=jnp.float32,
        )
        projected.append(summed_result.astype(jnp.bfloat16).reshape(samples, node_count, columns))
    queries, key_rows, value_rows = projected
    key_value = jnp.concatenate([key_rows, value_rows], axis=2)
    key_value_ext = padded(key_value, (("node", 1),), rim_rows)
    key_ext = key_value_ext[:, :, :columns]
    value_ext = key_value_ext[:, :, columns:]
    padded_table = jnp.pad(neighbour_key_blocks, ((HB, HB), (0, 0)), constant_values=pad_block)
    first_block = node_rank * block_count
    allowed = block_allowed(
        lax.dynamic_slice_in_dim(padded_table, first_block + HB, block_count, 0), first_block
    )
    cot_full = lax.all_gather(cotangent, "head", axis=2, tiled=True)
    grad_rows = cot_full[:, local_order, :].reshape(-1, model_width)
    inputs = grad_rows
    att_grad = jnp.dot(
        inputs,
        lax.all_gather(output_weight, "node", axis=1, tiled=True).T,
        preferred_element_type=jnp.float32,
    )
    att_grad = att_grad.astype(jnp.bfloat16).reshape(samples, node_count, columns)
    attended_parts = []
    totals = []
    deltas = []
    for column in range(head_count):
        key_window = window_stack(head_tiles(key_ext, column), block_count)
        value_window = window_stack(head_tiles(value_ext, column), block_count)
        attended, log_total = head_forward(
            head_tiles(queries, column), key_window, value_window, allowed
        )
        grad_tiles = head_tiles(att_grad, column)
        deltas.append(
            jnp.sum(grad_tiles.astype(jnp.float32) * attended.astype(jnp.float32), axis=-1)
        )
        attended_parts.append(attended)
        totals.append(log_total)
    att_rows = join_heads(attended_parts, samples, node_count).reshape(-1, columns)
    share_width = model_width // lax.axis_size("head")
    partial_out = jnp.dot(
        att_rows,
        lax.all_gather(output_weight, "node", axis=1, tiled=True),
        preferred_element_type=jnp.float32,
    )
    own_cols = lax.psum_scatter(
        partial_out.reshape(samples, node_count, model_width),
        "head",
        scatter_dimension=2,
        tiled=True,
    )
    residual = lax.dynamic_slice_in_dim(
        ordered, lax.axis_index("head") * share_width, share_width, 2
    )
    ordered_out = (residual.astype(jnp.float32) + own_cols).astype(jnp.bfloat16)
    mesh_out = jnp.zeros_like(ordered_out).at[:, local_order, :].set(ordered_out)
    query_grads = []
    key_parts = []
    value_parts = []
    for column in range(head_count):
        query_tiles = head_tiles(queries, column)
        grad_tiles = head_tiles(att_grad, column)
        key_window = window_stack(head_tiles(key_ext, column), block_count)
        value_window = window_stack(head_tiles(value_ext, column), block_count)
        query_grad, score_grad, prob_narrow = query_backward(
            query_tiles,
            key_window,
            value_window,
            grad_tiles,
            totals[column],
            deltas[column],
            allowed,
        )
        query_grads.append(query_grad)
        key_parts.append(
            fold_windows(
                jnp.einsum(
                    "sibok,sibd->siokd", score_grad, query_tiles, preferred_element_type=jnp.float32
                ),
                block_count,
            )
        )
        value_parts.append(
            fold_windows(
                jnp.einsum(
                    "sibok,sibd->siokd", prob_narrow, grad_tiles, preferred_element_type=jnp.float32
                ),
                block_count,
            )
        )
    ext_rows = node_count + 2 * rim_rows
    grads_ext = jnp.concatenate(
        [tiles.reshape(samples, ext_rows, -1) for tiles in key_parts + value_parts], axis=2
    )
    from_right = shifted(grads_ext[:, :rim_rows].astype(jnp.bfloat16), "node", -1).astype(
        jnp.float32
    )
    from_left = shifted(grads_ext[:, ext_rows - rim_rows :].astype(jnp.bfloat16), "node", 1).astype(
        jnp.float32
    )
    own_grads = grads_ext[:, rim_rows : rim_rows + node_count]
    own_grads = own_grads.at[:, :rim_rows].add(from_left)
    own_grads = own_grads.at[:, node_count - rim_rows :].add(from_right)
    key_grad = own_grads[:, :, :columns].astype(jnp.bfloat16)
    value_grad = own_grads[:, :, columns:].astype(jnp.bfloat16)
    query_grad_all = join_heads(query_grads, samples, node_count)
    flattened_wide = flattened_rows.astype(jnp.float32)
    down_terms = []
    up_terms = []
    for member_block, gradient in enumerate((query_grad_all, key_grad, value_grad)):
        gradient_flattened = gradient.reshape(-1, columns)
        backward_term = jnp.dot(
            gradient_flattened,
            adapter_up_weight[member_block].T,
            preferred_element_type=jnp.float32,
        )
        down_terms.append(
            adapter_scale
            * jnp.dot(flattened_wide.T, backward_term, precision=lax.Precision.HIGHEST)
        )
        up_terms.append(
            adapter_scale
            * jnp.dot(
                reduced_rank_term[member_block].T,
                gradient_flattened,
                preferred_element_type=jnp.float32,
            )
        )
    down_total = lax.psum(jnp.stack(down_terms), ("node", "sample", "head"))
    up_total = lax.psum(jnp.stack(up_terms), ("node", "sample"))
    return (mesh_out, down_total, up_total)


def solution(mesh):
    in_specs = (
        P(("group", "sample"), "node", None),
        P(("group", "sample"), "node", "head"),
        P("node", "head"),
        P("node", "head"),
        P("node", "head"),
        P("head", "node"),
        P(),
        P(None, None, "head"),
        P(),
        P("node"),
    )
    out_specs = (
        P(("group", "sample"), "node", "head"),
        P("group", None, None),
        P("group", None, "head"),
    )
    return jax.shard_map(shards, mesh=mesh, in_specs=in_specs, out_specs=out_specs, check_vma=False)
```

profile of v0, /device:TPU:0, one launch (start us, length us, event | category | flops | bytes accessed | tf_op | source)
XLA Modules:
  0.0 237.0 jit_solution(951882596947815362)
XLA Ops:
  8.1 0.7 compare_select_fusion
  8.8 0.3 copy-done
  9.1 2.0 gather_fusion
  11.2 0.3 fusion.56
  12.0 0.3 copy-done.10
  12.8 15.6 %all_gather.17 = bf16[512,256]{1,0:T(8,128)(2,1)S(1)} all-gather(bf16[128,256]{1,0:T(8,128)(2,1)S(1)} %copy-done.6), channel_id=1, replica_groups=mesh['group'=2,'node'=4,'sample'=2,'head'=2] {'node'}, dimensions={0}, use_global_device_ids=true | all-gather | bytes 327680 | tf_op jit(solution)/shard_map/all_gather | solution.py:143
  28.4 14.6 %all_gather.18 = bf16[512,256]{1,0:T(8,128)(2,1)S(1)} all-gather(bf16[128,256]{1,0:T(8,128)(2,1)S(1)} %copy-done.7), channel_id=1, replica_groups=mesh['group'=2,'node'=4,'sample'=2,'head'=2] {'node'}, dimensions={0}, use_global_device_ids=true | all-gather | bytes 327680 | tf_op jit(solution)/shard_map/all_gather | solution.py:144
  43.0 0.3 fusion.211
  43.3 0.3 fusion.210
  43.8 0.3 fusion.34
  44.0 0.3 fusion.33
  44.3 0.8 pad_maximum_fusion.2
  45.1 1.3 collective-permute-start.1
  46.4 5.4 %collective-permute-start = (bf16[1,512,512]{2,1,0:T(8,128)(2,1)}, bf16[1,512,512]{2,1,0:T(8,128)(2,1)}, u32[]{:S(2)}, u32[]{:S(2)}) collective-permute-start(bf16[1,512,512]{2,1,0:T(8,128)(2,1)} %pad_maximum_fusion.2), channel_id=1, source_target_pairs={{0,4},{4,8},{8,12},{1,5},{5,9},{9,13},{2,6},{6,10},{10,14},{3,7},{... | collective-permute-start | bytes 1572872 | tf_op jit(solution)/shard_map/ppermute | solution.py:26
  52.1 16.2 %all_gather.19 = bf16[256,512]{1,0:T(8,128)(2,1)S(1)} all-gather(bf16[256,128]{1,0:T(8,128)(2,1)S(1)} %copy-done.8), channel_id=1, replica_groups=mesh['group'=2,'node'=4,'sample'=2,'head'=2] {'node'}, dimensions={1}, use_global_device_ids=true | all-gather | bytes 327680 | tf_op jit(solution)/shard_map/all_gather | solution.py:199
  68.3 13.8 %all_gather.16 = bf16[512,256]{1,0:T(8,128)(2,1)S(1)} all-gather(bf16[128,256]{1,0:T(8,128)(2,1)S(1)} %copy-done.9), channel_id=1, replica_groups=mesh['group'=2,'node'=4,'sample'=2,'head'=2] {'node'}, dimensions={0}, use_global_device_ids=true | all-gather | bytes 327680 | tf_op jit(solution)/shard_map/all_gather | solution.py:142
  82.1 0.3 fusion.209
  82.4 2.4 all_gather.20
  84.8 2.0 gather_fusion.1
  86.8 0.3 fusion.32
  87.1 0.3 fusion.35
  87.6 1.3 pad_maximum_fusion.1
  88.9 0.3 fusion.204
  89.7 0.5 fusion.207
  90.2 0.3 exponential_reduce_fusion
  90.5 0.5 convolution_bitcast_fusion
  91.0 0.8 multiply_reduce_fusion
  91.8 0.7 multiply_convert_fusion
  92.5 0.5 fusion.39
  93.0 0.5 convolution_bitcast_fusion.2
  93.9 0.5 fusion.208
  94.4 0.3 exponential_reduce_fusion.1
  94.8 0.5 convolution_bitcast_fusion.1
  95.3 0.8 multiply_reduce_fusion.1
  96.0 0.7 multiply_convert_fusion.1
  96.7 0.5 fusion.45
  97.3 1.9 convolution_bitcast_fusion.3
  100.5 1.0 scatter-add.150
  101.4 1.7 fusion.104
  103.1 1.7 fusion.102
  104.8 1.7 fusion.100
  106.5 1.7 fusion.98
  108.2 1.7 fusion.96
  109.9 1.7 fusion.94
  111.5 1.7 fusion.92
  113.2 1.7 fusion.90
  114.9 1.3 convolution_bitcast_fusion.4
  116.2 0.3 all-reduce.7.cloned.1.call-start
  116.5 1.1 slice_bitcast_fusion.37
  117.7 1.0 fusion.136
  119.2 1.3 fusion.202
  120.6 2.3 collective-permute-start.2
  122.9 1.3 collective-permute-start.3
  124.6 0.4 fusion.50
  124.9 1.3 pad_maximum_fusion
  126.3 8.1 %collective-permute-done.2 = bf16[1,512,512]{2,1,0:T(8,128)(2,1)S(1)} collective-permute-done((bf16[1,512,512]{2,1,0:T(8,128)(2,1)S(1)}, bf16[1,512,512]{2,1,0:T(8,128)(2,1)S(1)}, u32[]{:S(2)}, u32[]{:S(2)}) %collective-permute-start.2) | collective-permute-done | bytes 524320 | tf_op jit(solution)/shard_map/ppermute | solution.py:35
  134.3 4.1 %collective-permute-done.3 = bf16[1,512,512]{2,1,0:T(8,128)(2,1)S(1)} collective-permute-done((bf16[1,512,512]{2,1,0:T(8,128)(2,1)S(1)}, bf16[1,512,512]{2,1,0:T(8,128)(2,1)S(1)}, u32[]{:S(2)}, u32[]{:S(2)}) %collective-permute-start.3) | collective-permute-done | bytes 524320 | tf_op jit(solution)/shard_map/ppermute | solution.py:35
  138.9 0.4 fusion.49
  139.5 0.4 fusion.48
  139.9 0.7 pad_maximum_fusion.3
  140.9 36.3 %psum.15 = f32[3,16,256]{2,1,0:T(8,128)} all-reduce(f32[3,16,256]{2,1,0:T(8,128)S(1)} %pad_maximum_fusion.4), channel_id=1, replica_groups=mesh['group'=2,'node'=4,'sample'=2,'head'=2] {'node','sample'}, use_global_device_ids=true, to_apply=%region_12.13 | all-reduce | flops 12288 | bytes 98304 | tf_op jit(solution)/shard_map/psum | solution.py:286
  177.1 3.5 %scatter_custom_fusion = bf16[512,256]{1,0:T(8,128)(2,1)} fusion(s32[512]{0:T(512)S(1)} %compare_select_fusion, f32[1,512,256]{2,1,0:T(8,128)} %reduce-scatter.2.cloned.1.call-done, bf16[512,512]{1,0:T(8,128)(2,1)S(1)} %copy-done.2, s32[]{:T(128)} %constant.879.clone.1, s32[]{:T(128)S(6)} %select_n.23, bf16[]{:T(256)} %constant.875.clone.1), kind=kCustom, calls=%fused_computation.89 | custom fusion | flops 393216 | bytes 1048586 | tf_op jit(solution)/shard_map/scatter | solution.py:212
  180.6 47.4 %all-reduce.7.cloned.1.call-done = f32[3,512,16]{1,2,0:T(8,128)} async-done(((f32[3,512,16]{1,2,0:T(8,128)}), f32[3,512,16]{1,2,0:T(8,128)}) %all-reduce.7.cloned.1.call-update) | async-done | bytes 98320 | tf_op jit(solution)/shard_map/psum | solution.py:285
  228.0 1.5 copy.277
  (119 shorter events, 5.6 us)
Async XLA Ops:
  8.0 1.1 copy-start
  8.0 169.1 %reduce-scatter.2.cloned.1.call-start = ((), (), s32[]{:S(2)}) async-start(), calls=%async_computation.1 | async-start | bytes 1572864 | tf_op jit(solution)/shard_map/reduce_scatter | solution.py:202
  11.0 0.9 copy-start.1
  11.5 0.8 copy-start.10
  11.7 1.1 copy-start.6
  11.8 16.7 %copy-start.7 = (bf16[128,256]{1,0:T(8,128)(2,1)S(1)}, bf16[128,256]{1,0:T(8,128)(2,1)}, u32[]{:S(2)}) copy-start(bf16[128,256]{1,0:T(8,128)(2,1)} %param.94) | copy-start | bytes 196612
  43.0 0.7 copy-start.5
  44.0 8.1 %copy-start.8 = (bf16[256,128]{1,0:T(8,128)(2,1)S(1)}, bf16[256,128]{1,0:T(8,128)(2,1)}, u32[]{:S(2)}) copy-start(bf16[256,128]{1,0:T(8,128)(2,1)} %param.95) | copy-start | bytes 196612
  44.0 24.3 %copy-start.9 = (bf16[128,256]{1,0:T(8,128)(2,1)S(1)}, bf16[128,256]{1,0:T(8,128)(2,1)}, u32[]{:S(2)}) copy-start(bf16[128,256]{1,0:T(8,128)(2,1)} %param.92) | copy-start | bytes 196612
  45.1 42.5 %collective-permute-start.1 = (bf16[1,512,512]{2,1,0:T(8,128)(2,1)}, bf16[1,512,512]{2,1,0:T(8,128)(2,1)}, u32[]{:S(2)}, u32[]{:S(2)}) collective-permute-start(bf16[1,512,512]{2,1,0:T(8,128)(2,1)} %pad_maximum_fusion.2), channel_id=1, source_target_pairs={{4,0},{8,4},{12,8},{5,1},{9,5},{13,9},{6,2},{10,6},{14,10},{7,3},{... | collective-permute-start | bytes 1572872 | tf_op jit(solution)/shard_map/ppermute | solution.py:27
  46.4 41.2 %collective-permute-start = (bf16[1,512,512]{2,1,0:T(8,128)(2,1)}, bf16[1,512,512]{2,1,0:T(8,128)(2,1)}, u32[]{:S(2)}, u32[]{:S(2)}) collective-permute-start(bf16[1,512,512]{2,1,0:T(8,128)(2,1)} %pad_maximum_fusion.2), channel_id=1, source_target_pairs={{0,4},{4,8},{8,12},{1,5},{5,9},{9,13},{2,6},{6,10},{10,14},{3,7},{... | collective-permute-start | bytes 1572872 | tf_op jit(solution)/shard_map/ppermute | solution.py:26
  52.0 30.4 %copy-start.4 = (bf16[1,512,256]{2,1,0:T(8,128)(2,1)S(1)}, bf16[1,512,256]{2,1,0:T(8,128)(2,1)}, u32[]{:S(2)}) copy-start(bf16[1,512,256]{2,1,0:T(8,128)(2,1)} %param.91) | copy-start | bytes 786436
  84.8 2.0 copy-start.11
  116.2 111.7 %all-reduce.7.cloned.1.call-start = ((), (), s32[]{:S(2)}) async-start(), calls=%async_computation.2 | async-start | bytes 196608 | tf_op jit(solution)/shard_map/psum | solution.py:285
  116.5 2.2 copy-start.3
  120.6 13.7 %collective-permute-start.2 = (bf16[1,512,512]{2,1,0:T(8,128)(2,1)S(1)}, bf16[1,512,512]{2,1,0:T(8,128)(2,1)S(1)}, u32[]{:S(2)}, u32[]{:S(2)}) collective-permute-start(bf16[1,512,512]{2,1,0:T(8,128)(2,1)S(1)} %get-tuple-element.475), channel_id=1, source_target_pairs={{0,4},{4,8},{8,12},{1,5},{5,9},{9,13},{2,6},{6,10},{10,14},{3,7},{... | collective-permute-start | bytes 1572872 | tf_op jit(solution)/shard_map/ppermute | solution.py:35
  122.9 15.6 %collective-permute-start.3 = (bf16[1,512,512]{2,1,0:T(8,128)(2,1)S(1)}, bf16[1,512,512]{2,1,0:T(8,128)(2,1)S(1)}, u32[]{:S(2)}, u32[]{:S(2)}) collective-permute-start(bf16[1,512,512]{2,1,0:T(8,128)(2,1)S(1)} %get-tuple-element.476), channel_id=1, source_target_pairs={{4,0},{8,4},{12,8},{5,1},{9,5},{13,9},{6,2},{10,6},{14,10},{7,3},{... | collective-permute-start | bytes 1572872 | tf_op jit(solution)/shard_map/ppermute | solution.py:35
  139.3 37.8 %copy-start.2 = (bf16[512,512]{1,0:T(8,128)(2,1)S(1)}, bf16[512,512]{1,0:T(8,128)(2,1)}, u32[]{:S(2)}) copy-start(bf16[512,512]{1,0:T(8,128)(2,1)} %copy-done.1) | copy-start | bytes 1572868
Sparse Core Ops, SparseCore 0:
  116.3 8.3 reduce-scatter.1
Sparse Core Ops, SparseCore 1:
  140.9 87.0 all-reduce.6
where the time goes:
time: 238 us; the launch traced here: 237 us
  blocking collectives  98.8 us (42%)
  waiting for transfers between devices  59.6 us (25%)
  other arithmetic  27.7 us (12%)
  between operations  16.3 us (7%)
  matrix products  14.4 us (6%)
  starting transfers between devices  10.5 us (4%)
  local copies, waits for them, and re-layouts  9.68 us (4%)
    psum x1, waiting for transfers between devices, shards(): down_total = lax.psum(jnp.stack(down_terms), ('node', 'sample', 'head'))  47.4 us
    psum x1, blocking collectives, shards(): up_total = lax.psum(jnp.stack(up_terms), ('node', 'sample'))  36.3 us
    all_gather x1, blocking collectives, shards(): lax.all_gather(output_weight, 'node', axis=1, tiled=True)  16.2 us
    scatter-add x32, other arithmetic, fold_windows(): extended.at[:, offset:offset + block_count].add(tiles[:, :, offset])  16 us
    all_gather x1, blocking collectives, shards(): lax.all_gather(key_weight, 'node', axis=0, tiled=True)  15.6 us
    all_gather x1, blocking collectives, shards(): lax.all_gather(value_weight, 'node', axis=0, tiled=True)  14.6 us
    all_gather x1, blocking collectives, shards(): lax.all_gather(query_weight, 'node', axis=0, tiled=True)  13.8 us
    ppermute x2, waiting for transfers between devices, shifted(): lax.ppermute(value, axis, [(source, source + steps) for source in range(i...  12.2 us
  transfers between devices with their start and end apart: 6, of which 3 were waited for; matrix products, arithmetic and copies ran while one was open for 6% of the time, Pallas kernels for 0%

commit v1 on v0

v1 whole, which is shorter than its diff:
```python
import functools
import math

import jax
import jax.numpy as jnp
from jax import lax
from jax.experimental import pallas as pl
from jax.experimental.pallas import tpu as pltpu
from jax.sharding import PartitionSpec as P

DH = 128
BLK = 128
HB = 4
RANK = 16
LOW = 128

adapter_scale = 0.5
masked_value = -1e30
F32 = jnp.float32
BF16 = jnp.bfloat16


def nn(a, b):
    return lax.dot_general(a, b, (((1,), (0,)), ((), ())), preferred_element_type=F32)


def nt(a, b):
    return lax.dot_general(a, b, (((1,), (1,)), ((), ())), preferred_element_type=F32)


def tn(a, b):
    return lax.dot_general(a, b, (((0,), (0,)), ((), ())), preferred_element_type=F32)


def scatter_matrix(order_ref, rows):
    local = order_ref[...] - lax.axis_index("node") * rows
    nodes = lax.broadcasted_iota(jnp.int32, (rows, rows), 0)
    return jnp.where(nodes == local, 1.0, 0.0).astype(BF16)


def prep_kernel(order_ref, x_ref, cot_ref, normed_ref, half_ref, cot_out_ref):
    rows = x_ref.shape[0]
    place = scatter_matrix(order_ref, rows)
    ordered = tn(place, x_ref[...])
    center = ordered - jnp.mean(ordered, axis=-1, keepdims=True)
    spread = jnp.mean(center * center, axis=-1, keepdims=True)
    normed_ref[...] = (center * lax.rsqrt(spread + 1e-05)).astype(BF16)
    cot_out_ref[...] = tn(place, cot_ref[...]).astype(BF16)
    start = pl.multiple_of(lax.axis_index("head") * (rows // 2), rows // 2)
    half_ref[...] = normed_ref[pl.ds(start, rows // 2), :]


def main_kernel(
    piece_rows,
    table_ref,
    order_ref,
    x_ref,
    normed_ref,
    a_own_ref,
    a_sib_ref,
    b_own_ref,
    b_sib_ref,
    cot_own_ref,
    cot_sib_ref,
    down_ref,
    up_ref,
    *rest,
):
    pieces, outs, scratch = rest[:-14], rest[-14:-11], rest[-11:]
    base_ref, other_ref, lora_ref = outs
    w_ref, kv_ref, low_ref, q_ref, do_ref, dq_ref, att_ref, tk_ref, tv_ref, bk_ref, bv_ref = scratch
    rows, width = normed_ref.shape
    cols = w_ref.shape[1]
    heads = cols // DH
    blocks = rows // BLK
    half = rows // 2
    node, head = lax.axis_index("node"), lax.axis_index("head")
    first = node * blocks
    inverse_root = 1.0 / math.sqrt(DH)

    for piece, (matrix, row) in zip(pieces, piece_rows(node)):
        start = pl.multiple_of(matrix * width + row, piece.shape[0])
        w_ref[pl.ds(start, piece.shape[0]), :] = piece[...]
    wq = w_ref[0:width, :]
    wk = w_ref[width : 2 * width, :]
    wv = w_ref[2 * width : 3 * width, :]

    def out_rows(which):
        start = pl.multiple_of(3 * width + which * (width // 2), width // 2)
        return w_ref[pl.ds(start, width // 2), :]

    mine, theirs = head * half, (1 - head) * half
    segments = [
        (normed_ref, 0),
        (a_own_ref, rows + mine),
        (a_sib_ref, rows + theirs),
        (b_own_ref, 2 * rows + mine),
        (b_sib_ref, 2 * rows + theirs),
    ]
    segments = [(r, s if isinstance(s, int) else pl.multiple_of(s, half)) for r, s in segments]
    for member, start in segments:
        value = member[...]
        low = nn(value, down_ref[...]).astype(BF16)
        span = pl.ds(start, value.shape[0])
        low_ref[span, :] = low
        kv_ref[span, :cols] = (nn(value, wk) + nn(low, up_ref[:, cols : 2 * cols])).astype(BF16)
        kv_ref[span, cols:] = (nn(value, wv) + nn(low, up_ref[:, 2 * cols :])).astype(BF16)
    low_own = low_ref[0:rows, :]
    q_ref[...] = (nn(normed_ref[...], wq) + nn(low_own, up_ref[:, :cols])).astype(BF16)
    do_ref[...] = (
        nn(cot_own_ref[...], out_rows(head)) + nn(cot_sib_ref[...], out_rows(1 - head))
    ).astype(BF16)
    bk_ref[...] = jnp.zeros_like(bk_ref)
    bv_ref[...] = jnp.zeros_like(bv_ref)

    odd = lax.rem(node, 2)
    left, right = 2 - odd, 1 + odd
    for i in range(blocks):
        named = [table_ref[first + i, e] for e in range(table_ref.shape[1])]
        starts, valid = [], []
        for e, c in enumerate(named):
            rel = c - first
            block = jnp.where(
                rel < 0,
                left * blocks + rel + blocks,
                jnp.where(rel >= blocks, (right - 1) * blocks + rel, rel),
            )
            starts.append(pl.multiple_of(block * BLK, BLK))
            fresh = c >= 0
            for before in named[:e]:
                fresh = jnp.logical_and(fresh, c != before)
            valid.append(fresh)
        own = slice(i * BLK, (i + 1) * BLK)
        low_sel = jnp.concatenate([low_ref[pl.ds(s, BLK), :] for s in starts], axis=0)
        for g in range(heads):
            lanes = slice(g * DH, (g + 1) * DH)
            vlanes = slice(cols + g * DH, cols + (g + 1) * DH)
            keys = jnp.concatenate([kv_ref[pl.ds(s, BLK), lanes] for s in starts], axis=0)
            values = jnp.concatenate([kv_ref[pl.ds(s, BLK), vlanes] for s in starts], axis=0)
            query, grad = q_ref[own, lanes], do_ref[own, lanes]
            scores = nt(query, keys) * inverse_root
            scores = jnp.concatenate(
                [
                    jnp.where(ok, scores[:, e * BLK : (e + 1) * BLK], masked_value)
                    for e, ok in enumerate(valid)
                ],
                axis=1,
            )
            row_max = jnp.max(scores, axis=-1, keepdims=True)
            weights = jnp.exp(scores - row_max)
            prob = weights * (1.0 / jnp.sum(weights, axis=-1, keepdims=True))
            prob_b = prob.astype(BF16)
            mixed = nn(prob_b, jnp.concatenate([values, low_sel], axis=1))
            attended = mixed[:, :DH].astype(BF16)
            att_ref[own, lanes] = attended
            tv_ref[own, g * LOW : (g + 1) * LOW] = mixed[:, DH:].astype(BF16)
            delta = jnp.sum(grad.astype(F32) * attended.astype(F32), axis=-1, keepdims=True)
            score_grad = (prob * (nt(grad, values) - delta) * inverse_root).astype(BF16)
            mixed = nn(score_grad, jnp.concatenate([keys, low_sel], axis=1))
            dq_ref[own, lanes] = mixed[:, :DH].astype(BF16)
            tk_ref[own, g * LOW : (g + 1) * LOW] = mixed[:, DH:].astype(BF16)
            up_k = up_ref[RANK : 2 * RANK, cols + g * DH : cols + (g + 1) * DH]
            up_v = up_ref[2 * RANK : 3 * RANK, 2 * cols + g * DH : 2 * cols + (g + 1) * DH]
            back_k = nn(nt(up_k, query).astype(BF16), score_grad)
            back_v = nn(nt(up_v, grad).astype(BF16), prob_b)
            for e, s in enumerate(starts):
                bk_ref[:, pl.ds(s, BLK)] += back_k[:, e * BLK : (e + 1) * BLK]
                bv_ref[:, pl.ds(s, BLK)] += back_v[:, e * BLK : (e + 1) * BLK]

    back_q = nt(up_ref[0:RANK, 0:cols], dq_ref[...])
    lhs = jnp.concatenate([back_q, bk_ref[:, 0:rows], bv_ref[:, 0:rows]], axis=0).astype(BF16)
    down = nn(lhs, normed_ref[...])
    halo = jnp.zeros((2 * RANK, width), F32)
    for member, start in segments[1:]:
        span = pl.ds(start, half)
        lhs = jnp.concatenate([bk_ref[:, span], bv_ref[:, span]], axis=0).astype(BF16)
        halo += nn(lhs, member[...])
    lora_ref[:, :width] = (
        down + jnp.concatenate([jnp.zeros((RANK, width), F32), halo], axis=0)
    ).astype(lora_ref.dtype)
    for g in range(heads):
        lanes = slice(g * DH, (g + 1) * DH)
        tlanes = slice(g * LOW, (g + 1) * LOW)
        grads = jnp.concatenate(
            [
                tn(low_own, dq_ref[:, lanes])[0:RANK],
                tn(tk_ref[:, tlanes], q_ref[:, lanes])[RANK : 2 * RANK],
                tn(tv_ref[:, tlanes], do_ref[:, lanes])[2 * RANK : 3 * RANK],
            ],
            axis=0,
        )
        lora_ref[:, width + g * DH : width + (g + 1) * DH] = (adapter_scale * grads).astype(
            lora_ref.dtype
        )

    place = scatter_matrix(order_ref, rows)
    attended = att_ref[...]
    own_cols = pl.ds(pl.multiple_of(head * cols, cols), cols)
    own_part = nn(place, nt(attended, out_rows(head)).astype(BF16))
    base_ref[...] = x_ref[:, own_cols].astype(F32) + own_part
    other_ref[...] = nn(place, nt(attended, out_rows(1 - head)).astype(BF16)).astype(BF16)


VMEM = pl.BlockSpec(memory_space=pltpu.VMEM)
SMEM = pl.BlockSpec(memory_space=pltpu.SMEM)


def swap(value, axis, step):
    size = lax.axis_size(axis)
    return lax.ppermute(value, axis, [(i, i ^ step) for i in range(size)])


def chain_pairs(size):
    pairs = {0: 0, size - 1: size - 1}
    for i in range(1, size - 1, 2):
        pairs[i], pairs[i + 1] = i + 1, i
    return sorted(pairs.items())


def gather_weights(matrices):
    count = lax.axis_size("node")
    depth = matrices[0].shape[0]
    if count > 4:
        whole = [lax.all_gather(m, "node", axis=0, tiled=True) for m in matrices]
        return whole, lambda node: [(m, 0) for m in range(4)]
    packed = jnp.concatenate(matrices, axis=1)
    pieces = [packed] + [swap(packed, "node", k) for k in range(1, count)]
    cols = matrices[0].shape[1]
    cut = [p[:, m * cols : (m + 1) * cols] for p in pieces for m in range(4)]
    return cut, lambda node: [
        (m, jnp.bitwise_xor(node, k) * depth) for k in range(count) for m in range(4)
    ]


def shards(
    mesh_node_state,
    cotangent,
    query_weight,
    key_weight,
    value_weight,
    output_weight,
    adapter_down_weight,
    adapter_up_weight,
    neighbour_key_blocks,
    block_node_order,
):
    _, rows, width = mesh_node_state.shape
    cols = query_weight.shape[1]
    state = mesh_node_state[0]
    order = block_node_order.reshape(1, rows)

    pieces, piece_rows = gather_weights(
        [query_weight, key_weight, value_weight, output_weight.T]
    )
    down = jnp.concatenate(list(adapter_down_weight), axis=1)
    down = jnp.pad(down, ((0, 0), (0, LOW - 3 * RANK)))
    up = jnp.concatenate(
        [
            jnp.pad(adapter_scale * adapter_up_weight[j], ((j * RANK, LOW - (j + 1) * RANK), (0, 0)))
            for j in range(3)
        ],
        axis=1,
    )
    normed, half, cot_own = pl.pallas_call(
        prep_kernel,
        out_shape=(
            jax.ShapeDtypeStruct((rows, width), BF16),
            jax.ShapeDtypeStruct((rows // 2, width), BF16),
            jax.ShapeDtypeStruct((rows, cols), BF16),
        ),
        in_specs=[VMEM] * 3,
        out_specs=(VMEM,) * 3,
        compiler_params=pltpu.CompilerParams(vmem_limit_bytes=24 * 2**20),
    )(order, state, cotangent[0])
    cot_sib = swap(cot_own, "head", 1)
    a_own = swap(half, "node", 1)
    b_own = lax.ppermute(half, "node", chain_pairs(lax.axis_size("node")))
    a_sib = swap(a_own, "head", 1)
    b_sib = swap(b_own, "head", 1)

    base, other, lora = pl.pallas_call(
        functools.partial(main_kernel, piece_rows),
        out_shape=(
            jax.ShapeDtypeStruct((rows, cols), F32),
            jax.ShapeDtypeStruct((rows, cols), BF16),
            jax.ShapeDtypeStruct((3 * RANK, width + cols), BF16),
        ),
        in_specs=[SMEM] + [VMEM] * (11 + len(pieces)),
        out_specs=(VMEM,) * 3,
        scratch_shapes=[
            pltpu.VMEM((4 * width, cols), BF16),
            pltpu.VMEM((3 * rows, 2 * cols), BF16),
            pltpu.VMEM((3 * rows, LOW), BF16),
            pltpu.VMEM((rows, cols), BF16),
            pltpu.VMEM((rows, cols), BF16),
            pltpu.VMEM((rows, cols), BF16),
            pltpu.VMEM((rows, cols), BF16),
            pltpu.VMEM((rows, cols // DH * LOW), BF16),
            pltpu.VMEM((rows, cols // DH * LOW), BF16),
            pltpu.VMEM((RANK, 3 * rows), F32),
            pltpu.VMEM((RANK, 3 * rows), F32),
        ],
        compiler_params=pltpu.CompilerParams(vmem_limit_bytes=40 * 2**20),
    )(
        neighbour_key_blocks,
        order,
        state,
        normed,
        a_own,
        a_sib,
        b_own,
        b_sib,
        cot_own,
        cot_sib,
        down,
        up,
        *pieces,
    )
    mesh_out = (base + swap(other, "head", 1).astype(F32)).astype(BF16)[None]

    total = lora.astype(F32)
    for axis in ("sample", "node"):
        step = 1
        while step < lax.axis_size(axis):
            sent = total.astype(BF16)
            total = sent.astype(F32) + swap(sent, axis, step).astype(F32)
            step *= 2
    sent = total[:, :width].astype(BF16)
    down_total = sent.astype(F32) + swap(sent, "head", 1).astype(F32)
    down_total = down_total.reshape(3, RANK, width).transpose(0, 2, 1)
    up_total = total[:, width:].reshape(3, RANK, cols)
    return (mesh_out, down_total, up_total)


def solution(mesh):
    in_specs = (
        P(("group", "sample"), "node", None),
        P(("group", "sample"), "node", "head"),
        P("node", "head"),
        P("node", "head"),
        P("node", "head"),
        P("head", "node"),
        P(),
        P(None, None, "head"),
        P(),
        P("node"),
    )
    out_specs = (
        P(("group", "sample"), "node", "head"),
        P("group", None, None),
        P("group", None, "head"),
    )
    return jax.shard_map(shards, mesh=mesh, in_specs=in_specs, out_specs=out_specs, check_vma=False)
```

time: 238 us -> 65.2 us (0.27)
  blocking collectives: 98.8 us -> 0 us
  waiting for transfers between devices: 59.6 us -> 22.1 us
  other arithmetic: 27.7 us -> 2.37 us
  between operations: 16.3 us -> 0.87 us
  matrix products: 14.4 us -> 0 us
  Pallas kernels: 0 us -> 12.6 us
  starting transfers between devices: 10.5 us -> 21.7 us
  local copies, waits for them, and re-layouts: 9.68 us -> 5.19 us
    all_gather x5 -> x0, blocking collectives: 62.6 us -> none  [the longest x1 16.2 us: shards(): lax.all_gather(output_weight, 'node', axis=1, tiled=True)]
    psum x1 -> x0, waiting for transfers between devices: 47.4 us -> none  [shards(): down_total = lax.psum(jnp.stack(down_terms), ('node', 'sample', 'head'))]
    psum x1 -> x0, blocking collectives: 36.3 us -> none  [shards(): up_total = lax.psum(jnp.stack(up_terms), ('node', 'sample'))]
    scatter-add x32 -> x0, other arithmetic: 16 us -> none  [fold_windows(): extended.at[:, offset:offset + block_count].add(tiles[:, :, offset])]
    dot_general x32 -> x0, matrix products: 14.4 us -> none  [the longest x2 2.32 us: shards(): jnp.einsum('sibok,sibd->siokd', score_grad, query_tiles, preferred_elemen...]
    pallas_call x0 -> x2, Pallas kernels: none -> 12.6 us  [the longest x1 11.8 us: shards(): pl.pallas_call(functools.partial(main_kernel, piece_rows), out_shape=(jax...]
    ppermute x4 -> x13, starting transfers between devices: 10.2 us -> 21.7 us  [the longest x12 21 us: swap(): return lax.ppermute(value, axis, [(i, i ^ step) for i in range(size)])]
    ppermute x4 -> x13, waiting for transfers between devices: 12.2 us -> 22.1 us  [the longest x12 22.1 us: swap(): return lax.ppermute(value, axis, [(i, i ^ step) for i in range(size)])]
  transfers between devices with their start and end apart: 6 -> 13, of which waited for: 3 -> 7; matrix products, arithmetic and copies ran while one was open for 6% -> 4% of each run, Pallas kernels for 0% -> 1%
where the time goes in v1:
time: 65.2 us; the launch traced here: 64.8 us
  waiting for transfers between devices  22.1 us (34%)
  starting transfers between devices  21.7 us (33%)
  Pallas kernels  12.6 us (19%)
  local copies, waits for them, and re-layouts  5.19 us (8%)
  other arithmetic  2.37 us (4%)
  between operations  0.87 us (1%)
    ppermute x12, waiting for transfers between devices, swap(): return lax.ppermute(value, axis, [(i, i ^ step) for i in range(size)])  22.1 us
    ppermute x12, starting transfers between devices, swap(): return lax.ppermute(value, axis, [(i, i ^ step) for i in range(size)])  21 us
    pallas_call x1, Pallas kernels, shards(): pl.pallas_call(functools.partial(main_kernel, piece_rows), out_shape=(jax...  11.8 us
    unnamed x20, local copies, waits for them, and re-layouts  3.41 us
  transfers between devices with their start and end apart: 13, of which 7 were waited for; matrix products, arithmetic and copies ran while one was open for 4% of the time, Pallas kernels for 1%

profile of v1, /device:TPU:0, one launch (start us, length us, event | category | flops | bytes accessed | tf_op | source)
XLA Modules:
  0.0 64.8 jit_solution(13573600559624958962)
XLA Ops:
  0.6 0.0 copy-start.2
  0.6 0.0 copy-start.1
  0.7 0.0 copy-start
  0.7 1.0 %copy.19 = bf16[256,128]{0,1:T(8,128)(2,1)S(1)} copy(bf16[256,128]{1,0:T(8,128)(2,1)} %param.15) | data formatting | bytes 131072 | tf_op args[5]
  1.7 0.0 copy-done.2
  1.7 0.0 copy-done.1
  1.7 0.9 %pad_maximum_fusion = bf16[128,1024]{1,0:T(8,128)(2,1)S(1)} fusion(bf16[128,256]{1,0:T(8,128)(2,1)S(1)} %bitcast.24, bf16[128,256]{1,0:T(8,128)(2,1)} %rest_2_.1, bf16[128,256]{1,0:T(8,128)(2,1)S(1)} %copy-done.2, bf16[128,256]{1,0:T(8,128)(2,1)S(1)} %copy-done.1), kind=kLoop, calls=%fused_computation.10 | loop fusion | flops 1048576 | bytes 524288 | tf_op jit(solution)/shard_map/concatenate | solution.py:226
  2.6 5.1 %collective-permute-start.7 = (bf16[128,1024]{1,0:T(8,128)(2,1)S(1)}, bf16[128,1024]{1,0:T(8,128)(2,1)}, u32[]{:S(2)}, u32[]{:S(2)}) collective-permute-start(bf16[128,1024]{1,0:T(8,128)(2,1)S(1)} %pad_maximum_fusion), channel_id=1, source_target_pairs={{0,12},{4,8},{8,4},{12,0},{1,13},{5,9},{9,5},{13,1},{2,14},{6,10},... | collective-permute-start | bytes 786440 | tf_op jit(solution)/shard_map/ppermute | solution.py:210
  7.7 0.0 collective-permute-start.6
  7.7 0.6 collective-permute-start.5
  8.3 0.0 copy-start.5
  8.3 0.0 copy-done
  8.3 0.7 %copy-done.5 = s32[512]{0:T(512)S(1)} copy-done((s32[512]{0:T(512)S(1)}, s32[512]{0:T(512)}, u32[]{:S(2)}) %copy-start.5) | copy-done | bytes 2072
  9.0 0.0 copy-start.4
  9.0 0.9 %copy-done.4 = bf16[1,512,256]{2,1,0:T(8,128)(2,1)S(1)} copy-done((bf16[1,512,256]{2,1,0:T(8,128)(2,1)S(1)}, bf16[1,512,256]{2,1,0:T(8,128)(2,1)}, u32[]{:S(2)}) %copy-start.4) | copy-done | bytes 262168
  9.9 0.0 copy-start.6
  9.9 0.8 %shard_map.121 = (bf16[512,512]{1,0:T(8,128)(2,1)S(1)}, bf16[256,512]{1,0:T(8,128)(2,1)S(1)}, bf16[512,256]{1,0:T(8,128)(2,1)S(1)}) custom-call(s32[1,512]{1,0:T(1,128)S(1)} %bitcast.27, bf16[512,512]{1,0:T(8,128)(2,1)S(1)} %bitcast.22, bf16[512,256]{1,0:T(8,128)(2,1)S(1)} %bitcast.26), custom_call_target="tpu_custom_call" | custom-call | tf_op jit(solution)/shard_map/pallas_call | solution.py:264
  10.8 0.0 copy-start.7
  10.8 0.7 %collective-permute-start.2 = (bf16[256,512]{1,0:T(8,128)(2,1)S(1)}, bf16[256,512]{1,0:T(8,128)(2,1)S(1)}, u32[]{:S(2)}, u32[]{:S(2)}) collective-permute-start(bf16[256,512]{1,0:T(8,128)(2,1)S(1)} %get-tuple-element.10), channel_id=1, source_target_pairs={{0,0},{4,8},{8,4},{12,12},{1,1},{5,9},{9,5},{13,13},{2,2},{6,10},{... | collective-permute-start | bytes 786440 | tf_op jit(solution)/shard_map/ppermute | solution.py:277
  11.5 4.1 %collective-permute-start = (bf16[256,512]{1,0:T(8,128)(2,1)S(1)}, bf16[256,512]{1,0:T(8,128)(2,1)S(1)}, u32[]{:S(2)}, u32[]{:S(2)}) collective-permute-start(bf16[256,512]{1,0:T(8,128)(2,1)S(1)} %get-tuple-element.10), channel_id=1, source_target_pairs={{0,4},{4,0},{8,12},{12,8},{1,5},{5,1},{9,13},{13,9},{2,6},{6,2},{1... | collective-permute-start | bytes 786440 | tf_op jit(solution)/shard_map/ppermute | solution.py:210
  15.6 0.0 copy-done.6
  15.6 0.0 copy-done.7
  15.7 0.0 copy-start.8
  15.7 0.7 %copy-done.8 = s32[16,6]{0,1:T(8,128)S(1)} copy-done((s32[16,6]{0,1:T(8,128)S(1)}, s32[16,6]{0,1:T(8,128)}, u32[]{:S(2)}) %copy-start.8) | copy-done | bytes 408
  16.3 0.1 copy.20.table_ref
  16.4 0.1 copy.18
  16.6 0.0 collective-permute-done.7
  16.6 0.1 collective-permute-start.4
  16.7 1.0 %fusion.7 = (bf16[128,256]{1,0:T(8,128)(2,1)S(1)}, bf16[128,256]{1,0:T(8,128)(2,1)S(1)}, bf16[128,256]{1,0:T(8,128)(2,1)S(1)}, bf16[128,256]{1,0:T(8,128)(2,1)S(1)}) fusion(bf16[128,1024]{1,0:T(8,128)(2,1)} %collective-permute-done.7), kind=kLoop, calls=%fused_computation.25 | loop fusion | bytes 524288 | tf_op jit(solution)/shard_map/slice | solution.py:229
  17.6 0.0 collective-permute-done.2.b_own_ref
  17.7 0.6 collective-permute-start.3
  18.2 12.7 %collective-permute-done.a_own_ref = bf16[256,512]{1,0:T(8,128)(2,1)S(1)} collective-permute-done((bf16[256,512]{1,0:T(8,128)(2,1)S(1)}, bf16[256,512]{1,0:T(8,128)(2,1)S(1)}, u32[]{:S(2)}, u32[]{:S(2)}) %collective-permute-start) | collective-permute-done | bytes 262176 | tf_op jit(solution)/shard_map/ppermute | solution.py:210
  30.9 0.0 collective-permute-start.1
  30.9 0.1 collective-permute-done.6
  31.0 0.0 collective-permute-done.5
  31.0 0.0 copy-start.3
  31.1 0.0 collective-permute-done.4.cot_sib_ref
  31.1 0.0 collective-permute-done.3.b_sib_ref
  31.1 1.3 %collective-permute-done.1.a_sib_ref = bf16[256,512]{1,0:T(8,128)(2,1)S(1)} collective-permute-done((bf16[256,512]{1,0:T(8,128)(2,1)S(1)}, bf16[256,512]{1,0:T(8,128)(2,1)S(1)}, u32[]{:S(2)}, u32[]{:S(2)}) %collective-permute-start.1) | collective-permute-done | bytes 262176 | tf_op jit(solution)/shard_map/ppermute | solution.py:210
  32.4 0.0 copy-done.3
  32.4 11.8 %shard_map.122 = (f32[512,256]{1,0:T(8,128)S(1)}, bf16[512,256]{1,0:T(8,128)(2,1)S(1)}, bf16[48,768]{1,0:T(8,128)(2,1)S(1)}) custom-call(s32[16,6]{1,0:T(8,128)S(1)} %copy.20.table_ref, s32[1,512]{1,0:T(1,128)S(1)} %bitcast.28, bf16[512,512]{1,0:T(8,128)(2,1)S(1)} %bitcast.23, bf16[512,512]{1,0:T(8,128)(2,1)S(1)} %get-tuple-element.9.normed_ref, ...), custom_call_target="tpu_custom_call" | custom-call | tf_op jit(solution)/shard_map/pallas_call | solution.py:281
  44.2 1.6 %collective-permute-start.9 = (bf16[48,768]{1,0:T(8,128)(2,1)S(1)}, bf16[48,768]{1,0:T(8,128)(2,1)S(1)}, u32[]{:S(2)}, u32[]{:S(2)}) collective-permute-start(bf16[48,768]{1,0:T(8,128)(2,1)S(1)} %get-tuple-element.14), channel_id=1, source_target_pairs={{0,2},{2,0},{1,3},{3,1},{4,6},{6,4},{5,7},{7,5},{8,10},{10,8},{9,1... | collective-permute-start | bytes 221192 | tf_op jit(solution)/shard_map/ppermute | solution.py:210
  45.8 2.8 %collective-permute-done.9 = bf16[48,768]{1,0:T(8,128)(2,1)S(1)} collective-permute-done((bf16[48,768]{1,0:T(8,128)(2,1)S(1)}, bf16[48,768]{1,0:T(8,128)(2,1)S(1)}, u32[]{:S(2)}, u32[]{:S(2)}) %collective-permute-start.9) | collective-permute-done | bytes 73760 | tf_op jit(solution)/shard_map/ppermute | solution.py:210
  48.7 5.8 %collective-permute-start.10 = (bf16[48,768]{1,0:T(8,128)(2,1)S(1)}, bf16[48,768]{1,0:T(8,128)(2,1)S(1)}, u32[]{:S(2)}, u32[]{:S(2)}) collective-permute-start(bf16[48,768]{1,0:T(8,128)(2,1)S(1)} %add_convert_fusion.2), channel_id=1, source_target_pairs={{0,4},{4,0},{8,12},{12,8},{1,5},{5,1},{9,13},{13,9},{2,6},{6,2},{1... | collective-permute-start | bytes 221192 | tf_op jit(solution)/shard_map/ppermute | solution.py:210
  54.5 2.3 %collective-permute-done.10 = bf16[48,768]{1,0:T(8,128)(2,1)S(1)} collective-permute-done((bf16[48,768]{1,0:T(8,128)(2,1)S(1)}, bf16[48,768]{1,0:T(8,128)(2,1)S(1)}, u32[]{:S(2)}, u32[]{:S(2)}) %collective-permute-start.10) | collective-permute-done | bytes 73760 | tf_op jit(solution)/shard_map/ppermute | solution.py:210
  56.8 3.1 %collective-permute-start.11 = (bf16[48,768]{1,0:T(8,128)(2,1)S(1)}, bf16[48,768]{1,0:T(8,128)(2,1)S(1)}, u32[]{:S(2)}, u32[]{:S(2)}) collective-permute-start(bf16[48,768]{1,0:T(8,128)(2,1)S(1)} %add_convert_fusion.1), channel_id=1, source_target_pairs={{0,8},{4,12},{8,0},{12,4},{1,9},{5,13},{9,1},{13,5},{2,10},{6,14},... | collective-permute-start | bytes 221192 | tf_op jit(solution)/shard_map/ppermute | solution.py:210
  59.9 0.0 collective-permute-start.8
  59.9 2.3 %collective-permute-done.11 = bf16[48,768]{1,0:T(8,128)(2,1)S(1)} collective-permute-done((bf16[48,768]{1,0:T(8,128)(2,1)S(1)}, bf16[48,768]{1,0:T(8,128)(2,1)S(1)}, u32[]{:S(2)}, u32[]{:S(2)}) %collective-permute-start.11) | collective-permute-done | bytes 73760 | tf_op jit(solution)/shard_map/ppermute | solution.py:210
  62.3 0.6 slice.82
  62.9 0.0 collective-permute-start.12
  62.9 0.0 collective-permute-done.8
  62.9 0.8 %fusion.4 = bf16[1,512,256]{2,1,0:T(8,128)(2,1)} fusion(f32[512,256]{1,0:T(8,128)S(1)} %get-tuple-element.12, bf16[512,256]{1,0:T(8,128)(2,1)S(1)} %collective-permute-done.8), kind=kLoop, calls=%fused_computation.9 | loop fusion | flops 393216 | bytes 1048576 | tf_op jit(solution)/shard_map/broadcast_in_dim | solution.py:319
  63.7 0.4 collective-permute-done.12
  64.1 0.7 %convert_add_fusion.1 = f32[48,512]{1,0:T(8,128)} fusion(bf16[48,512]{1,0:T(8,128)(2,1)S(1)} %collective-permute-done.12, f32[48,768]{1,0:T(8,128)S(1)} %convert_add_fusion), kind=kLoop, calls=%fused_computation.17 | loop fusion | flops 73728 | bytes 196608 | tf_op jit(solution)/shard_map/add | solution.py:329
  (11 shorter events, 0.2 us)
Async XLA Ops:
  0.6 1.0 %copy-start.2 = (bf16[128,256]{1,0:T(8,128)(2,1)S(1)}, bf16[128,256]{1,0:T(8,128)(2,1)}, u32[]{:S(2)}) copy-start(bf16[128,256]{1,0:T(8,128)(2,1)} %rest_1_.1) | copy-start | bytes 196612
  0.6 1.0 %copy-start.1 = (bf16[128,256]{1,0:T(8,128)(2,1)S(1)}, bf16[128,256]{1,0:T(8,128)(2,1)}, u32[]{:S(2)}) copy-start(bf16[128,256]{1,0:T(8,128)(2,1)} %rest_0_.1) | copy-start | bytes 196612
  0.7 7.7 %copy-start = (bf16[1,512,512]{2,1,0:T(8,128)(2,1)S(1)}, bf16[1,512,512]{2,1,0:T(8,128)(2,1)}, u32[]{:S(2)}) copy-start(bf16[1,512,512]{2,1,0:T(8,128)(2,1)} %param.10) | copy-start | bytes 1572868
  2.6 14.0 %collective-permute-start.7 = (bf16[128,1024]{1,0:T(8,128)(2,1)S(1)}, bf16[128,1024]{1,0:T(8,128)(2,1)}, u32[]{:S(2)}, u32[]{:S(2)}) collective-permute-start(bf16[128,1024]{1,0:T(8,128)(2,1)S(1)} %pad_maximum_fusion), channel_id=1, source_target_pairs={{0,12},{4,8},{8,4},{12,0},{1,13},{5,9},{9,5},{13,1},{2,14},{6,10},... | collective-permute-start | bytes 786440 | tf_op jit(solution)/shard_map/ppermute | solution.py:210
  7.7 23.3 %collective-permute-start.6 = (bf16[128,1024]{1,0:T(8,128)(2,1)S(1)}, bf16[128,1024]{1,0:T(8,128)(2,1)S(1)}, u32[]{:S(2)}, u32[]{:S(2)}) collective-permute-start(bf16[128,1024]{1,0:T(8,128)(2,1)S(1)} %pad_maximum_fusion), channel_id=1, source_target_pairs={{0,8},{4,12},{8,0},{12,4},{1,9},{5,13},{9,1},{13,5},{2,10},{6,14},... | collective-permute-start | bytes 786440 | tf_op jit(solution)/shard_map/ppermute | solution.py:210
  7.7 23.3 %collective-permute-start.5 = (bf16[128,1024]{1,0:T(8,128)(2,1)S(1)}, bf16[128,1024]{1,0:T(8,128)(2,1)S(1)}, u32[]{:S(2)}, u32[]{:S(2)}) collective-permute-start(bf16[128,1024]{1,0:T(8,128)(2,1)S(1)} %pad_maximum_fusion), channel_id=1, source_target_pairs={{0,4},{4,0},{8,12},{12,8},{1,5},{5,1},{9,13},{13,9},{2,6},{6,2},{1... | collective-permute-start | bytes 786440 | tf_op jit(solution)/shard_map/ppermute | solution.py:210
  8.3 0.7 %copy-start.5 = (s32[512]{0:T(512)S(1)}, s32[512]{0:T(512)}, u32[]{:S(2)}) copy-start(s32[512]{0:T(512)} %param.19) | copy-start | bytes 6148
  9.0 0.9 %copy-start.4 = (bf16[1,512,256]{2,1,0:T(8,128)(2,1)S(1)}, bf16[1,512,256]{2,1,0:T(8,128)(2,1)}, u32[]{:S(2)}) copy-start(bf16[1,512,256]{2,1,0:T(8,128)(2,1)} %param.11) | copy-start | bytes 786436
  9.9 5.7 %copy-start.6 = (bf16[3,512,16]{1,2,0:T(8,128)(2,1)S(1)}, bf16[3,512,16]{1,2,0:T(8,128)(2,1)}, u32[]{:S(2)}) copy-start(bf16[3,512,16]{1,2,0:T(8,128)(2,1)} %param.16) | copy-start | bytes 147460
  10.8 4.9 %copy-start.7 = (bf16[3,16,256]{2,1,0:T(8,128)(2,1)S(1)}, bf16[3,16,256]{2,1,0:T(8,128)(2,1)}, u32[]{:S(2)}) copy-start(bf16[3,16,256]{2,1,0:T(8,128)(2,1)} %param.17) | copy-start | bytes 73732
  10.8 6.9 %collective-permute-start.2 = (bf16[256,512]{1,0:T(8,128)(2,1)S(1)}, bf16[256,512]{1,0:T(8,128)(2,1)S(1)}, u32[]{:S(2)}, u32[]{:S(2)}) collective-permute-start(bf16[256,512]{1,0:T(8,128)(2,1)S(1)} %get-tuple-element.10), channel_id=1, source_target_pairs={{0,0},{4,8},{8,4},{12,12},{1,1},{5,9},{9,5},{13,13},{2,2},{6,10},{... | collective-permute-start | bytes 786440 | tf_op jit(solution)/shard_map/ppermute | solution.py:277
  11.5 19.4 %collective-permute-start = (bf16[256,512]{1,0:T(8,128)(2,1)S(1)}, bf16[256,512]{1,0:T(8,128)(2,1)S(1)}, u32[]{:S(2)}, u32[]{:S(2)}) collective-permute-start(bf16[256,512]{1,0:T(8,128)(2,1)S(1)} %get-tuple-element.10), channel_id=1, source_target_pairs={{0,4},{4,0},{8,12},{12,8},{1,5},{5,1},{9,13},{13,9},{2,6},{6,2},{1... | collective-permute-start | bytes 786440 | tf_op jit(solution)/shard_map/ppermute | solution.py:210
  15.7 0.7 %copy-start.8 = (s32[16,6]{0,1:T(8,128)S(1)}, s32[16,6]{0,1:T(8,128)}, u32[]{:S(2)}) copy-start(s32[16,6]{0,1:T(8,128)} %param.18) | copy-start | bytes 1156
  16.6 14.5 %collective-permute-start.4 = (bf16[512,256]{1,0:T(8,128)(2,1)S(1)}, bf16[512,256]{1,0:T(8,128)(2,1)S(1)}, u32[]{:S(2)}, u32[]{:S(2)}) collective-permute-start(bf16[512,256]{1,0:T(8,128)(2,1)S(1)} %get-tuple-element.11.cot_own_ref), channel_id=1, source_target_pairs={{0,1},{1,0},{2,3},{3,2},{4,5},{5,4},{6,7},{7,6},{8,9},{9,8},{10,11... | collective-permute-start | bytes 786440 | tf_op jit(solution)/shard_map/ppermute | solution.py:210
  17.7 13.4 %collective-permute-start.3 = (bf16[256,512]{1,0:T(8,128)(2,1)S(1)}, bf16[256,512]{1,0:T(8,128)(2,1)S(1)}, u32[]{:S(2)}, u32[]{:S(2)}) collective-permute-start(bf16[256,512]{1,0:T(8,128)(2,1)S(1)} %collective-permute-done.2.b_own_ref), channel_id=1, source_target_pairs={{0,1},{1,0},{2,3},{3,2},{4,5},{5,4},{6,7},{7,6},{8,9},{9,8},{10,11... | collective-permute-start | bytes 786440 | tf_op jit(solution)/shard_map/ppermute | solution.py:210
  30.9 1.5 %collective-permute-start.1 = (bf16[256,512]{1,0:T(8,128)(2,1)S(1)}, bf16[256,512]{1,0:T(8,128)(2,1)S(1)}, u32[]{:S(2)}, u32[]{:S(2)}) collective-permute-start(bf16[256,512]{1,0:T(8,128)(2,1)S(1)} %collective-permute-done.a_own_ref), channel_id=1, source_target_pairs={{0,1},{1,0},{2,3},{3,2},{4,5},{5,4},{6,7},{7,6},{8,9},{9,8},{10,11... | collective-permute-start | bytes 786440 | tf_op jit(solution)/shard_map/ppermute | solution.py:210
  31.0 1.4 %copy-start.3 = (bf16[128,256]{1,0:T(8,128)(2,1)S(1)}, bf16[128,256]{1,0:T(8,128)(2,1)}, u32[]{:S(2)}) copy-start(bf16[128,256]{1,0:T(8,128)(2,1)} %rest_2_.1) | copy-start | bytes 196612
  44.2 4.4 %collective-permute-start.9 = (bf16[48,768]{1,0:T(8,128)(2,1)S(1)}, bf16[48,768]{1,0:T(8,128)(2,1)S(1)}, u32[]{:S(2)}, u32[]{:S(2)}) collective-permute-start(bf16[48,768]{1,0:T(8,128)(2,1)S(1)} %get-tuple-element.14), channel_id=1, source_target_pairs={{0,2},{2,0},{1,3},{3,1},{4,6},{6,4},{5,7},{7,5},{8,10},{10,8},{9,1... | collective-permute-start | bytes 221192 | tf_op jit(solution)/shard_map/ppermute | solution.py:210
  48.7 8.1 %collective-permute-start.10 = (bf16[48,768]{1,0:T(8,128)(2,1)S(1)}, bf16[48,768]{1,0:T(8,128)(2,1)S(1)}, u32[]{:S(2)}, u32[]{:S(2)}) collective-permute-start(bf16[48,768]{1,0:T(8,128)(2,1)S(1)} %add_convert_fusion.2), channel_id=1, source_target_pairs={{0,4},{4,0},{8,12},{12,8},{1,5},{5,1},{9,13},{13,9},{2,6},{6,2},{1... | collective-permute-start | bytes 221192 | tf_op jit(solution)/shard_map/ppermute | solution.py:210
  56.8 5.4 %collective-permute-start.11 = (bf16[48,768]{1,0:T(8,128)(2,1)S(1)}, bf16[48,768]{1,0:T(8,128)(2,1)S(1)}, u32[]{:S(2)}, u32[]{:S(2)}) collective-permute-start(bf16[48,768]{1,0:T(8,128)(2,1)S(1)} %add_convert_fusion.1), channel_id=1, source_target_pairs={{0,8},{4,12},{8,0},{12,4},{1,9},{5,13},{9,1},{13,5},{2,10},{6,14},... | collective-permute-start | bytes 221192 | tf_op jit(solution)/shard_map/ppermute | solution.py:210
  59.9 3.0 %collective-permute-start.8 = (bf16[512,256]{1,0:T(8,128)(2,1)S(1)}, bf16[512,256]{1,0:T(8,128)(2,1)S(1)}, u32[]{:S(2)}, u32[]{:S(2)}) collective-permute-start(bf16[512,256]{1,0:T(8,128)(2,1)S(1)} %get-tuple-element.13), channel_id=1, source_target_pairs={{0,1},{1,0},{2,3},{3,2},{4,5},{5,4},{6,7},{7,6},{8,9},{9,8},{10,11... | collective-permute-start | bytes 786440 | tf_op jit(solution)/shard_map/ppermute | solution.py:210
  62.9 1.2 %collective-permute-start.12 = (bf16[48,512]{1,0:T(8,128)(2,1)S(1)}, bf16[48,512]{1,0:T(8,128)(2,1)S(1)}, u32[]{:S(2)}, u32[]{:S(2)}) collective-permute-start(bf16[48,512]{1,0:T(8,128)(2,1)S(1)} %slice.87), channel_id=1, source_target_pairs={{0,1},{1,0},{2,3},{3,2},{4,5},{5,4},{6,7},{7,6},{8,9},{9,8},{10,11... | collective-permute-start | bytes 147464 | tf_op jit(solution)/shard_map/ppermute | solution.py:210

commit v2 on v1

v2 whole, which is shorter than its diff:
```python
import functools
import math

import jax
import jax.numpy as jnp
from jax import lax
from jax.experimental import pallas as pl
from jax.experimental.pallas import tpu as pltpu
from jax.sharding import PartitionSpec as P

DH = 128
BLK = 128
RANK = 16
LOW = 128

adapter_scale = 0.5
masked_value = -1e30
F32 = jnp.float32
BF16 = jnp.bfloat16


def nn(a, b):
    return lax.dot_general(a, b, (((1,), (0,)), ((), ())), preferred_element_type=F32)


def nt(a, b):
    return lax.dot_general(a, b, (((1,), (1,)), ((), ())), preferred_element_type=F32)


def tn(a, b):
    return lax.dot_general(a, b, (((0,), (0,)), ((), ())), preferred_element_type=F32)


def scatter_matrix(order_ref, rows):
    local = order_ref[...] - lax.axis_index("node") * rows
    nodes = lax.broadcasted_iota(jnp.int32, (rows, rows), 0)
    return jnp.where(nodes == local, 1.0, 0.0).astype(BF16)


def head_at(split, which):
    if not split:
        return which
    return jnp.bitwise_xor(lax.rem(lax.axis_index("sample"), 2), which)


def lanes_at(index):
    if isinstance(index, int):
        return pl.ds(index * DH, DH)
    return pl.ds(pl.multiple_of(index * DH, DH), DH)


def pack_kernel(split, wq_ref, wk_ref, wv_ref, wo_ref, *outs):
    for which, out in enumerate(outs):
        lanes = lanes_at(head_at(split, which))
        for j, member in enumerate((wq_ref, wk_ref, wv_ref)):
            out[:, j * DH : (j + 1) * DH] = member[:, lanes]
        out[:, 3 * DH :] = wo_ref[lanes, :].T


def prep_kernel(order_ref, x_ref, cot_ref, normed_ref, half_ref, cot_out_ref):
    rows = x_ref.shape[0]
    place = scatter_matrix(order_ref, rows)
    ordered = tn(place, x_ref[...])
    center = ordered - jnp.mean(ordered, axis=-1, keepdims=True)
    spread = jnp.mean(center * center, axis=-1, keepdims=True)
    normed_ref[...] = (center * lax.rsqrt(spread + 1e-05)).astype(BF16)
    cot_out_ref[...] = tn(place, cot_ref[...]).astype(BF16)
    start = pl.multiple_of(lax.axis_index("head") * (rows // 2), rows // 2)
    half_ref[...] = normed_ref[pl.ds(start, rows // 2), :]


def head_kernel(split, which, piece_rows, *refs):
    (
        table_ref,
        normed_ref,
        a_own_ref,
        a_sib_ref,
        b_own_ref,
        b_sib_ref,
        cot_own_ref,
        cot_sib_ref,
        down_ref,
        up_ref,
    ) = refs[:10]
    rest = refs[10:]
    scratch = rest[-12:]
    if which == 0:
        pieces, (att_ref, wo_ref, down_out, up_out) = rest[:-16], rest[-16:-12]
    else:
        pieces, (down_in, up_in, att_ref, wo_ref, lora_ref) = rest[:-17], rest[-17:-12]
    w_ref, u_ref, kv_ref, low_ref, q_ref, do_ref, dq_ref, tk_ref, tv_ref, bk_ref, bv_ref, sum_ref = (
        scratch
    )
    rows, width = normed_ref.shape
    blocks = rows // BLK
    half = rows // 2
    node, core = lax.axis_index("node"), lax.axis_index("head")
    head = head_at(split, which)
    first = node * blocks
    inverse_root = 1.0 / math.sqrt(DH)

    for piece, row in zip(pieces, piece_rows(node)):
        if isinstance(row, int):
            w_ref[pl.ds(row, piece.shape[0]), :] = piece[...]
        else:
            w_ref[pl.ds(pl.multiple_of(row, piece.shape[0]), piece.shape[0]), :] = piece[...]
    wo_ref[...] = w_ref[:, 3 * DH :]
    u_ref[...] = jnp.zeros_like(u_ref)
    for j in range(3):
        u_ref[j * RANK : (j + 1) * RANK, j * DH : (j + 1) * DH] = (
            adapter_scale * up_ref[j * RANK : (j + 1) * RANK, lanes_at(head)]
        )

    mine, theirs = core * half, (1 - core) * half
    segments = [
        (normed_ref, 0),
        (a_own_ref, pl.multiple_of(rows + mine, half)),
        (a_sib_ref, pl.multiple_of(rows + theirs, half)),
        (b_own_ref, pl.multiple_of(2 * rows + mine, half)),
        (b_sib_ref, pl.multiple_of(2 * rows + theirs, half)),
    ]
    low_ref[...] = jnp.zeros_like(low_ref)
    for j, (member, start) in enumerate(segments):
        value = member[...]
        span = pl.ds(start, value.shape[0])
        low_ref[span, : 3 * RANK] = nt(value, down_ref[...]).astype(BF16)
        low = low_ref[span, :]
        skip = DH if j else 0
        projected = (nn(value, w_ref[:, skip : 3 * DH]) + nn(low, u_ref[:, skip:])).astype(BF16)
        if j == 0:
            q_ref[...] = projected[:, :DH]
        kv_ref[span, :] = projected[:, DH - skip :]
    low_own = low_ref[0:rows, :]

    def out_rows(side):
        return w_ref[pl.ds(pl.multiple_of(side * (width // 2), width // 2), width // 2), 3 * DH :]

    do_ref[...] = (
        nn(cot_own_ref[...], out_rows(core)) + nn(cot_sib_ref[...], out_rows(1 - core))
    ).astype(BF16)
    bk_ref[...] = jnp.zeros_like(bk_ref)
    bv_ref[...] = jnp.zeros_like(bv_ref)

    odd = lax.rem(node, 2)
    left, right = 2 - odd, 1 + odd
    for i in range(blocks):
        named = [table_ref[first + i, e] for e in range(table_ref.shape[1])]
        starts, valid = [], []
        for e, c in enumerate(named):
            rel = c - first
            block = jnp.where(
                rel < 0,
                left * blocks + rel + blocks,
                jnp.where(rel >= blocks, (right - 1) * blocks + rel, rel),
            )
            starts.append(pl.multiple_of(block * BLK, BLK))
            fresh = c >= 0
            for before in named[:e]:
                fresh = jnp.logical_and(fresh, c != before)
            valid.append(fresh)
        own = slice(i * BLK, (i + 1) * BLK)
        low_sel = jnp.concatenate([low_ref[pl.ds(s, BLK), :] for s in starts], axis=0)
        keys = jnp.concatenate([kv_ref[pl.ds(s, BLK), :DH] for s in starts], axis=0)
        values = jnp.concatenate([kv_ref[pl.ds(s, BLK), DH:] for s in starts], axis=0)
        query, grad = q_ref[own, :], do_ref[own, :]
        scores = nt(query, keys) * inverse_root
        scores = jnp.concatenate(
            [
                jnp.where(ok, scores[:, e * BLK : (e + 1) * BLK], masked_value)
                for e, ok in enumerate(valid)
            ],
            axis=1,
        )
        row_max = jnp.max(scores, axis=-1, keepdims=True)
        weights = jnp.exp(scores - row_max)
        prob = weights * (1.0 / jnp.sum(weights, axis=-1, keepdims=True))
        prob_b = prob.astype(BF16)
        mixed = nn(prob_b, jnp.concatenate([values, low_sel], axis=1))
        attended = mixed[:, :DH].astype(BF16)
        att_ref[own, :] = attended
        tv_ref[own, :] = mixed[:, DH:].astype(BF16)
        delta = jnp.sum(grad.astype(F32) * attended.astype(F32), axis=-1, keepdims=True)
        score_grad = (prob * (nt(grad, values) - delta) * inverse_root).astype(BF16)
        mixed = nn(score_grad, jnp.concatenate([keys, low_sel], axis=1))
        dq_ref[own, :] = mixed[:, :DH].astype(BF16)
        tk_ref[own, :] = mixed[:, DH:].astype(BF16)
        up_k = u_ref[RANK : 2 * RANK, DH : 2 * DH]
        up_v = u_ref[2 * RANK : 3 * RANK, 2 * DH :]
        back_k = nn(nt(up_k, query).astype(BF16), score_grad)
        back_v = nn(nt(up_v, grad).astype(BF16), prob_b)
        for e, s in enumerate(starts):
            bk_ref[:, pl.ds(s, BLK)] += back_k[:, e * BLK : (e + 1) * BLK]
            bv_ref[:, pl.ds(s, BLK)] += back_v[:, e * BLK : (e + 1) * BLK]

    back_q = nt(u_ref[0:RANK, 0:DH], dq_ref[...])
    lhs = jnp.concatenate([back_q, bk_ref[:, 0:rows], bv_ref[:, 0:rows]], axis=0).astype(BF16)
    sum_ref[...] = nn(lhs, normed_ref[...])
    for member, start in segments[1:]:
        span = pl.ds(start, half)
        lhs = jnp.concatenate([bk_ref[:, span], bv_ref[:, span]], axis=0).astype(BF16)
        sum_ref[RANK:, :] += nn(lhs, member[...])
    up_grad = adapter_scale * jnp.concatenate(
        [
            tn(low_own, dq_ref[...])[0:RANK],
            tn(tk_ref[...], q_ref[...])[RANK : 2 * RANK],
            tn(tv_ref[...], do_ref[...])[2 * RANK : 3 * RANK],
        ],
        axis=0,
    )
    if which == 0:
        down_out[...] = sum_ref[...]
        up_out[...] = up_grad
        return
    lora_ref[:, :width] = (sum_ref[...] + down_in[...]).astype(BF16)
    up_at = [pl.multiple_of(width + g * DH, DH) for g in (head, 1 - head)]
    lora_ref[:, pl.ds(up_at[0], DH)] = up_grad.astype(BF16)
    lora_ref[:, pl.ds(up_at[1], DH)] = up_in[...].astype(BF16)


def out_kernel(order_ref, x_ref, att1_ref, att2_ref, wo1_ref, wo2_ref, base_ref, other_ref):
    rows, width = x_ref.shape
    cols = width // 2
    core = lax.axis_index("head")
    place = scatter_matrix(order_ref, rows)

    def part(side):
        span = pl.ds(pl.multiple_of(side * cols, cols), cols)
        terms = nt(att1_ref[...], wo1_ref[span, :]) + nt(att2_ref[...], wo2_ref[span, :])
        return nn(place, terms.astype(BF16))

    other_ref[...] = part(1 - core).astype(BF16)
    own = pl.ds(pl.multiple_of(core * cols, cols), cols)
    base_ref[...] = x_ref[:, own].astype(F32) + part(core)


VMEM = pl.BlockSpec(memory_space=pltpu.VMEM)
SMEM = pl.BlockSpec(memory_space=pltpu.SMEM)


def shape(dims, dtype=BF16):
    return jax.ShapeDtypeStruct(dims, dtype)


def call(kernel, outs, ins, scratch=(), smem=0, flops=0, limit=32):
    return pl.pallas_call(
        kernel,
        out_shape=outs,
        in_specs=[SMEM] * smem + [VMEM] * (len(ins) - smem),
        out_specs=(VMEM,) * len(outs),
        scratch_shapes=list(scratch),
        cost_estimate=pl.CostEstimate(flops=flops, bytes_accessed=1 << 20, transcendentals=0),
        compiler_params=pltpu.CompilerParams(vmem_limit_bytes=limit * 2**20),
    )(*ins)


def swap(value, axis, step=1):
    size = lax.axis_size(axis)
    return lax.ppermute(value, axis, [(i, i ^ step) for i in range(size)])


def chain_pairs(size):
    pairs = {0: 0, size - 1: size - 1}
    for i in range(1, size - 1, 2):
        pairs[i], pairs[i + 1] = i + 1, i
    return sorted(pairs.items())


def gather_weights(first, second):
    count, depth = lax.axis_size("node"), first.shape[0]
    if not split_weights():
        whole = [lax.all_gather(m, "node", axis=0, tiled=True) for m in (first, second)]
        return [[whole[0]], [whole[1]]], [lambda node: [0]] * 2
    near = swap(first, "node", 1)
    far_pairs = [(g * 4 + n, g * 4 + (n ^ (2 + g))) for g in range(2) for n in range(4)]
    far = lax.ppermute(first, ("group", "node"), far_pairs)
    other_far = swap(far, "group")

    def places(node, steps):
        return [jnp.bitwise_xor(node, k) * depth for k in steps]

    def piece_rows(node):
        group = lax.axis_index("group")
        return places(node, (0, 1, 2 + group, 3 - group))

    own = [first, near, far, other_far]
    return [own, [second] + [swap(p, "sample") for p in own[1:]]], [piece_rows] * 2


def split_weights():
    return lax.axis_size("node") == 4 and lax.axis_size("group") == 2 and lax.axis_size("sample") == 2


def shards(
    mesh_node_state,
    cotangent,
    query_weight,
    key_weight,
    value_weight,
    output_weight,
    adapter_down_weight,
    adapter_up_weight,
    neighbour_key_blocks,
    block_node_order,
):
    _, rows, width = mesh_node_state.shape
    cols = query_weight.shape[1]
    depth = query_weight.shape[0]
    state = mesh_node_state[0]
    order = block_node_order.reshape(1, rows)
    split = split_weights()

    packed = call(
        functools.partial(pack_kernel, split),
        (shape((depth, 4 * DH)),) * 2,
        (query_weight, key_weight, value_weight, output_weight),
        limit=8,
    )
    pieces, piece_rows = gather_weights(*packed)
    down = adapter_down_weight.transpose(0, 2, 1).reshape(3 * RANK, width)
    up = adapter_up_weight.reshape(3 * RANK, cols)
    normed, half, cot_own = call(
        prep_kernel,
        (shape((rows, width)), shape((rows // 2, width)), shape((rows, cols))),
        (order, state, cotangent[0]),
        flops=2 * rows * rows * (width + cols),
        limit=16,
    )
    cot_sib = swap(cot_own, "head")
    a_own = swap(half, "node", 1)
    b_own = lax.ppermute(half, "node", chain_pairs(lax.axis_size("node")))
    a_sib = swap(a_own, "head")
    b_sib = swap(b_own, "head")

    shared = (
        neighbour_key_blocks,
        normed,
        a_own,
        a_sib,
        b_own,
        b_sib,
        cot_own,
        cot_sib,
        down,
        up,
    )
    scratch = [
        pltpu.VMEM((width, 4 * DH), BF16),
        pltpu.VMEM((LOW, 3 * DH), BF16),
        pltpu.VMEM((3 * rows, 2 * DH), BF16),
        pltpu.VMEM((3 * rows, LOW), BF16),
        pltpu.VMEM((rows, DH), BF16),
        pltpu.VMEM((rows, DH), BF16),
        pltpu.VMEM((rows, DH), BF16),
        pltpu.VMEM((rows, LOW), BF16),
        pltpu.VMEM((rows, LOW), BF16),
        pltpu.VMEM((RANK, 3 * rows), F32),
        pltpu.VMEM((RANK, 3 * rows), F32),
        pltpu.VMEM((3 * RANK, width), F32),
    ]
    att1, wo1, down1, up1 = call(
        functools.partial(head_kernel, split, 0, piece_rows[0]),
        (shape((rows, DH)), shape((width, DH)), shape((3 * RANK, width), F32), shape((3 * RANK, DH), F32)),
        shared + tuple(pieces[0]),
        scratch,
        smem=1,
        flops=4 * 10**9,
    )
    att2, wo2, lora = call(
        functools.partial(head_kernel, split, 1, piece_rows[1]),
        (shape((rows, DH)), shape((width, DH)), shape((3 * RANK, width + cols))),
        shared + tuple(pieces[1]) + (down1, up1),
        scratch,
        smem=1,
        flops=4 * 10**9,
    )
    base, other = call(
        out_kernel,
        (shape((rows, cols), F32), shape((rows, cols))),
        (order, state, att1, att2, wo1, wo2),
        flops=10**9,
    )
    mesh_out = (base + swap(other, "head").astype(F32)).astype(BF16)[None]

    total = lora.astype(F32)
    for axis in ("sample", "node"):
        step = 1
        while step < lax.axis_size(axis):
            sent = total.astype(BF16)
            total = sent.astype(F32) + swap(sent, axis, step).astype(F32)
            step *= 2
    sent = total[:, :width].astype(BF16)
    down_total = sent.astype(F32) + swap(sent, "head").astype(F32)
    down_total = down_total.reshape(3, RANK, width).transpose(0, 2, 1)
    up_total = total[:, width:].reshape(3, RANK, cols)
    return (mesh_out, down_total, up_total)


def solution(mesh):
    in_specs = (
        P(("group", "sample"), "node", None),
        P(("group", "sample"), "node", "head"),
        P("node", "head"),
        P("node", "head"),
        P("node", "head"),
        P("head", "node"),
        P(),
        P(None, None, "head"),
        P(),
        P("node"),
    )
    out_specs = (
        P(("group", "sample"), "node", "head"),
        P("group", None, None),
        P("group", None, "head"),
    )
    return jax.shard_map(shards, mesh=mesh, in_specs=in_specs, out_specs=out_specs, check_vma=False)
```

time: 65.2 us -> 62.4 us (0.957)
  waiting for transfers between devices: 22.1 us -> 13.8 us
  starting transfers between devices: 21.7 us -> 26.9 us
  Pallas kernels: 12.6 us -> 15.8 us
  local copies, waits for them, and re-layouts: 5.19 us -> 3.42 us
  other arithmetic: 2.37 us -> 1.47 us
    ppermute x12 -> x14, waiting for transfers between devices: 22.1 us -> 12.7 us  [swap(): return lax.ppermute(value, axis, [(i, i ^ step) for i in range(size)])]
    ppermute x0 -> x1, starting transfers between devices: none -> 3.9 us  [gather_weights(): far = lax.ppermute(first, ('group', 'node'), far_pairs)]
    pallas_call x2 -> x5, Pallas kernels: 12.6 us -> 15.8 us  [call(): pl.pallas_call(kernel, out_shape=outs, in_specs=[SMEM] * smem + [VMEM] *...]
    ppermute x12 -> x14, starting transfers between devices: 21 us -> 22.3 us  [swap(): return lax.ppermute(value, axis, [(i, i ^ step) for i in range(size)])]
    ppermute x0 -> x1, waiting for transfers between devices: none -> 1.1 us  [gather_weights(): far = lax.ppermute(first, ('group', 'node'), far_pairs)]
    slice x3 -> x0, local copies, waits for them, and re-layouts: 1 us -> none  [gather_weights(): cut = [p[:, m * cols:(m + 1) * cols] for p in pieces for m in range(4)]]
    concatenate x3 -> x0, other arithmetic: 0.88 us -> none  [the longest x1 0.86 us: gather_weights(): packed = jnp.concatenate(matrices, axis=1)]
    unnamed x20 -> x23, local copies, waits for them, and re-layouts: 3.41 us -> 2.79 us
  transfers between devices with their start and end apart: 13 -> 16, of which waited for: 7 -> 8; matrix products, arithmetic and copies ran while one was open for 4% -> 2% of each run, Pallas kernels for 1% -> 13%
where the time goes in v2:
time: 62.4 us; the launch traced here: 62.2 us
  starting transfers between devices  26.9 us (43%)
  Pallas kernels  15.8 us (25%)
  waiting for transfers between devices  13.8 us (22%)
  local copies, waits for them, and re-layouts  3.42 us (5%)
  other arithmetic  1.47 us (2%)
  between operations  0.83 us (1%)
    ppermute x14, starting transfers between devices, swap(): return lax.ppermute(value, axis, [(i, i ^ step) for i in range(size)])  22.3 us
    pallas_call x5, Pallas kernels, call(): pl.pallas_call(kernel, out_shape=outs, in_specs=[SMEM] * smem + [VMEM] *...  15.8 us
    ppermute x14, waiting for transfers between devices, swap(): return lax.ppermute(value, axis, [(i, i ^ step) for i in range(size)])  12.7 us
    ppermute x1, starting transfers between devices, gather_weights(): far = lax.ppermute(first, ('group', 'node'), far_pairs)  3.9 us
    unnamed x23, local copies, waits for them, and re-layouts  2.79 us
  transfers between devices with their start and end apart: 16, of which 8 were waited for; matrix products, arithmetic and copies ran while one was open for 2% of the time, Pallas kernels for 13%

profile of v2, /device:TPU:0, one launch (start us, length us, event | category | flops | bytes accessed | tf_op | source)
XLA Modules:
  0.0 62.2 jit_solution(13466389882132360744)
XLA Ops:
  0.6 0.0 copy-start.9
  0.6 0.7 %copy-done.9 = s32[512]{0:T(512)S(1)} copy-done((s32[512]{0:T(512)S(1)}, s32[512]{0:T(512)}, u32[]{:S(2)}) %copy-start.9) | copy-done | bytes 2072
  1.3 0.0 copy-start.4
  1.3 1.0 %copy-done.4 = bf16[1,512,512]{2,1,0:T(8,128)(2,1)S(1)} copy-done((bf16[1,512,512]{2,1,0:T(8,128)(2,1)S(1)}, bf16[1,512,512]{2,1,0:T(8,128)(2,1)}, u32[]{:S(2)}) %copy-start.4) | copy-done | bytes 524312
  2.4 0.0 copy-start.6
  2.4 0.9 %copy-done.6 = bf16[1,512,256]{2,1,0:T(8,128)(2,1)S(1)} copy-done((bf16[1,512,256]{2,1,0:T(8,128)(2,1)S(1)}, bf16[1,512,256]{2,1,0:T(8,128)(2,1)}, u32[]{:S(2)}) %copy-start.6) | copy-done | bytes 262168
  3.3 0.0 copy-start
  3.3 0.0 copy-start.1
  3.3 0.0 copy-start.2
  3.3 0.0 copy-start.3
  3.3 0.8 %shard_map.121 = (bf16[512,512]{1,0:T(8,128)(2,1)S(1)}, bf16[256,512]{1,0:T(8,128)(2,1)S(1)}, bf16[512,256]{1,0:T(8,128)(2,1)S(1)}) custom-call(s32[1,512]{1,0:T(1,128)S(1)} %bitcast.20, bf16[512,512]{1,0:T(8,128)(2,1)S(1)} %bitcast.13, bf16[512,256]{1,0:T(8,128)(2,1)S(1)} %bitcast.15), custom_call_target="tpu_custom_call" | custom-call | flops 402653184 | bytes 1048576 | tf_op jit(solution)/shard_map/pallas_call | solution.py:245
  4.1 3.1 %collective-permute-start = (bf16[256,512]{1,0:T(8,128)(2,1)S(1)}, bf16[256,512]{1,0:T(8,128)(2,1)S(1)}, u32[]{:S(2)}, u32[]{:S(2)}) collective-permute-start(bf16[256,512]{1,0:T(8,128)(2,1)S(1)} %get-tuple-element.18), channel_id=1, source_target_pairs={{0,4},{4,0},{8,12},{12,8},{1,5},{5,1},{9,13},{13,9},{2,6},{6,2},{1... | collective-permute-start | bytes 786440 | tf_op jit(solution)/shard_map/ppermute | solution.py:258
  7.2 0.7 %collective-permute-start.2 = (bf16[256,512]{1,0:T(8,128)(2,1)S(1)}, bf16[256,512]{1,0:T(8,128)(2,1)S(1)}, u32[]{:S(2)}, u32[]{:S(2)}) collective-permute-start(bf16[256,512]{1,0:T(8,128)(2,1)S(1)} %get-tuple-element.18), channel_id=1, source_target_pairs={{0,0},{4,8},{8,4},{12,12},{1,1},{5,9},{9,5},{13,13},{2,2},{6,10},{... | collective-permute-start | bytes 786440 | tf_op jit(solution)/shard_map/ppermute | solution.py:330
  7.9 0.0 copy-start.7
  7.9 0.0 copy-start.8
  7.9 0.1 collective-permute-start.4
  8.0 0.0 copy-done
  8.0 0.0 copy-done.1
  8.0 0.0 copy-done.2
  8.0 0.0 copy-done.3
  8.0 0.0 copy-start.10
  8.1 0.1 shard_map.122
  8.2 3.9 %collective-permute-start.6 = (bf16[128,512]{1,0:T(8,128)(2,1)S(1)}, bf16[128,512]{1,0:T(8,128)(2,1)S(1)}, u32[]{:S(2)}, u32[]{:S(2)}) collective-permute-start(bf16[128,512]{1,0:T(8,128)(2,1)S(1)} %get-tuple-element.20.refs_10_), channel_id=1, source_target_pairs={{0,8},{4,12},{8,0},{12,4},{16,28},{20,24},{24,20},{28,16},{1,9},{5... | collective-permute-start | bytes 393224 | tf_op jit(solution)/shard_map/ppermute | solution.py:275
  12.1 1.5 %collective-permute-done.refs_2_ = bf16[256,512]{1,0:T(8,128)(2,1)S(1)} collective-permute-done((bf16[256,512]{1,0:T(8,128)(2,1)S(1)}, bf16[256,512]{1,0:T(8,128)(2,1)S(1)}, u32[]{:S(2)}, u32[]{:S(2)}) %collective-permute-start) | collective-permute-done | bytes 262176 | tf_op jit(solution)/shard_map/ppermute | solution.py:258
  13.5 0.0 collective-permute-start.1
  13.5 0.0 collective-permute-done.2.refs_4_
  13.6 0.5 collective-permute-start.3
  14.1 8.2 %collective-permute-start.5 = (bf16[128,512]{1,0:T(8,128)(2,1)S(1)}, bf16[128,512]{1,0:T(8,128)(2,1)S(1)}, u32[]{:S(2)}, u32[]{:S(2)}) collective-permute-start(bf16[128,512]{1,0:T(8,128)(2,1)S(1)} %get-tuple-element.20.refs_10_), channel_id=1, source_target_pairs={{0,4},{4,0},{8,12},{12,8},{1,5},{5,1},{9,13},{13,9},{2,6},{6,2},{1... | collective-permute-start | bytes 393224 | tf_op jit(solution)/shard_map/ppermute | solution.py:258
  22.3 1.1 %collective-permute-done.6.refs_12_ = bf16[128,512]{1,0:T(8,128)(2,1)S(1)} collective-permute-done((bf16[128,512]{1,0:T(8,128)(2,1)S(1)}, bf16[128,512]{1,0:T(8,128)(2,1)S(1)}, u32[]{:S(2)}, u32[]{:S(2)}) %collective-permute-start.6) | collective-permute-done | bytes 131104 | tf_op jit(solution)/shard_map/ppermute | solution.py:275
  23.4 0.4 collective-permute-start.7
  23.8 0.0 copy-done.10
  23.8 0.1 copy.13.refs_0_
  23.9 2.6 %collective-permute-done.5.refs_11_ = bf16[128,512]{1,0:T(8,128)(2,1)S(1)} collective-permute-done((bf16[128,512]{1,0:T(8,128)(2,1)S(1)}, bf16[128,512]{1,0:T(8,128)(2,1)S(1)}, u32[]{:S(2)}, u32[]{:S(2)}) %collective-permute-start.5) | collective-permute-done | bytes 131104 | tf_op jit(solution)/shard_map/ppermute | solution.py:258
  26.4 1.5 %collective-permute-start.9 = (bf16[128,512]{1,0:T(8,128)(2,1)S(1)}, bf16[128,512]{1,0:T(8,128)(2,1)S(1)}, u32[]{:S(2)}, u32[]{:S(2)}) collective-permute-start(bf16[128,512]{1,0:T(8,128)(2,1)S(1)} %collective-permute-done.6.refs_12_), channel_id=1, source_target_pairs={{0,2},{2,0},{1,3},{3,1},{4,6},{6,4},{5,7},{7,5},{8,10},{10,8},{9,1... | collective-permute-start | bytes 393224 | tf_op jit(solution)/shard_map/ppermute | solution.py:258
  27.9 0.0 collective-permute-done.4.refs_7_
  27.9 0.5 collective-permute-start.8
  28.5 0.0 collective-permute-done.7.refs_13_
  28.5 1.5 %collective-permute-start.10 = (bf16[128,512]{1,0:T(8,128)(2,1)S(1)}, bf16[128,512]{1,0:T(8,128)(2,1)S(1)}, u32[]{:S(2)}, u32[]{:S(2)}) collective-permute-start(bf16[128,512]{1,0:T(8,128)(2,1)S(1)} %collective-permute-done.7.refs_13_), channel_id=1, source_target_pairs={{0,2},{2,0},{1,3},{3,1},{4,6},{6,4},{5,7},{7,5},{8,10},{10,8},{9,1... | collective-permute-start | bytes 393224 | tf_op jit(solution)/shard_map/ppermute | solution.py:258
  29.9 0.0 collective-permute-done.1.refs_3_
  29.9 0.0 collective-permute-done.3.refs_5_
  30.0 0.0 copy-done.7
  30.0 0.0 copy-done.8
  30.0 6.9 %shard_map.123 = (bf16[512,128]{1,0:T(8,128)(2,1)S(1)}, bf16[512,128]{1,0:T(8,128)(2,1)S(1)}, f32[48,512]{1,0:T(8,128)S(1)}, f32[48,128]{1,0:T(8,128)S(1)}) custom-call(s32[16,6]{1,0:T(8,128)S(1)} %copy.13.refs_0_, bf16[512,512]{1,0:T(8,128)(2,1)S(1)} %get-tuple-element.17.refs_1_, bf16[256,512]{1,0:T(8,128)(2,1)S(1)} %collective-permute-done.refs_2_, ...), custom_call_target="tpu_custom_call" | custom-call | flops 4000000000 | bytes 1048576 | tf_op jit(solution)/shard_map/pallas_call | solution.py:245
  36.9 0.0 collective-permute-done.9.refs_12_
  36.9 0.0 collective-permute-done.8.refs_11_
  36.9 0.4 collective-permute-done.10.refs_13_
  37.4 0.0 copy-start.5
  37.4 6.9 %shard_map.124 = (bf16[512,128]{1,0:T(8,128)(2,1)S(1)}, bf16[512,128]{1,0:T(8,128)(2,1)S(1)}, bf16[48,768]{1,0:T(8,128)(2,1)S(1)}) custom-call(s32[16,6]{1,0:T(8,128)S(1)} %copy.13.refs_0_, bf16[512,512]{1,0:T(8,128)(2,1)S(1)} %get-tuple-element.17.refs_1_, bf16[256,512]{1,0:T(8,128)(2,1)S(1)} %collective-permute-done.refs_2_, ...), custom_call_target="tpu_custom_call" | custom-call | flops 4000000000 | bytes 1048576 | tf_op jit(solution)/shard_map/pallas_call | solution.py:245
  44.3 1.6 %collective-permute-start.12 = (bf16[48,768]{1,0:T(8,128)(2,1)S(1)}, bf16[48,768]{1,0:T(8,128)(2,1)S(1)}, u32[]{:S(2)}, u32[]{:S(2)}) collective-permute-start(bf16[48,768]{1,0:T(8,128)(2,1)S(1)} %get-tuple-element.30), channel_id=1, source_target_pairs={{0,2},{2,0},{1,3},{3,1},{4,6},{6,4},{5,7},{7,5},{8,10},{10,8},{9,1... | collective-permute-start | bytes 221192 | tf_op jit(solution)/shard_map/ppermute | solution.py:258
  45.9 2.9 %collective-permute-done.12 = bf16[48,768]{1,0:T(8,128)(2,1)S(1)} collective-permute-done((bf16[48,768]{1,0:T(8,128)(2,1)S(1)}, bf16[48,768]{1,0:T(8,128)(2,1)S(1)}, u32[]{:S(2)}, u32[]{:S(2)}) %collective-permute-start.12) | collective-permute-done | bytes 73760 | tf_op jit(solution)/shard_map/ppermute | solution.py:258
  48.7 1.6 %collective-permute-start.13 = (bf16[48,768]{1,0:T(8,128)(2,1)S(1)}, bf16[48,768]{1,0:T(8,128)(2,1)S(1)}, u32[]{:S(2)}, u32[]{:S(2)}) collective-permute-start(bf16[48,768]{1,0:T(8,128)(2,1)S(1)} %add_convert_fusion.2), channel_id=1, source_target_pairs={{0,4},{4,0},{8,12},{12,8},{1,5},{5,1},{9,13},{13,9},{2,6},{6,2},{1... | collective-permute-start | bytes 221192 | tf_op jit(solution)/shard_map/ppermute | solution.py:258
  50.3 2.8 %collective-permute-done.13 = bf16[48,768]{1,0:T(8,128)(2,1)S(1)} collective-permute-done((bf16[48,768]{1,0:T(8,128)(2,1)S(1)}, bf16[48,768]{1,0:T(8,128)(2,1)S(1)}, u32[]{:S(2)}, u32[]{:S(2)}) %collective-permute-start.13) | collective-permute-done | bytes 73760 | tf_op jit(solution)/shard_map/ppermute | solution.py:258
  53.2 3.3 %collective-permute-start.14 = (bf16[48,768]{1,0:T(8,128)(2,1)S(1)}, bf16[48,768]{1,0:T(8,128)(2,1)S(1)}, u32[]{:S(2)}, u32[]{:S(2)}) collective-permute-start(bf16[48,768]{1,0:T(8,128)(2,1)S(1)} %add_convert_fusion.1), channel_id=1, source_target_pairs={{0,8},{4,12},{8,0},{12,4},{1,9},{5,13},{9,1},{13,5},{2,10},{6,14},... | collective-permute-start | bytes 221192 | tf_op jit(solution)/shard_map/ppermute | solution.py:258
  56.5 0.0 copy-done.5
  56.5 1.0 %shard_map.125 = (f32[512,256]{1,0:T(8,128)S(1)}, bf16[512,256]{1,0:T(8,128)(2,1)S(1)}) custom-call(s32[1,512]{1,0:T(1,128)S(1)} %bitcast.21, bf16[512,512]{1,0:T(8,128)(2,1)S(1)} %bitcast.14, bf16[512,128]{1,0:T(8,128)(2,1)S(1)} %get-tuple-element.21.att1_ref, bf16[512,128]{1,0:T(8,128)(2,1)S(1)} %get-tuple-element.25.att2_ref, ...), custom_call_target="tpu_custom_call" | custom-call | flops 1000000000 | bytes 1048576 | tf_op jit(solution)/shard_map/pallas_call | solution.py:245
  57.5 0.1 collective-permute-start.11
  57.6 2.0 %collective-permute-done.14 = bf16[48,768]{1,0:T(8,128)(2,1)S(1)} collective-permute-done((bf16[48,768]{1,0:T(8,128)(2,1)S(1)}, bf16[48,768]{1,0:T(8,128)(2,1)S(1)}, u32[]{:S(2)}, u32[]{:S(2)}) %collective-permute-start.14) | collective-permute-done | bytes 73760 | tf_op jit(solution)/shard_map/ppermute | solution.py:258
  59.6 0.6 %slice.10 = f32[48,256]{1,0:T(8,128)} slice(f32[48,768]{1,0:T(8,128)S(1)} %convert_add_fusion), slice={[0:48], [512:768]} | slice | bytes 98304 | tf_op jit(solution)/shard_map/slice | solution.py:394
  60.3 0.0 collective-permute-start.15
  60.3 0.0 collective-permute-done.11
  60.3 0.8 %fusion = bf16[1,512,256]{2,1,0:T(8,128)(2,1)} fusion(f32[512,256]{1,0:T(8,128)S(1)} %get-tuple-element.28, bf16[512,256]{1,0:T(8,128)(2,1)S(1)} %collective-permute-done.11), kind=kLoop, calls=%fused_computation.1 | loop fusion | flops 393216 | bytes 1048576 | tf_op jit(solution)/shard_map/broadcast_in_dim | solution.py:382
  61.0 0.5 collective-permute-done.15
  61.5 0.7 %convert_add_fusion.1 = f32[48,512]{1,0:T(8,128)} fusion(bf16[48,512]{1,0:T(8,128)(2,1)S(1)} %collective-permute-done.15, f32[48,768]{1,0:T(8,128)S(1)} %convert_add_fusion), kind=kLoop, calls=%fused_computation.6 | loop fusion | flops 73728 | bytes 196608 | tf_op jit(solution)/shard_map/add | solution.py:392
  (4 shorter events, 0.1 us)
Async XLA Ops:
  0.6 0.7 %copy-start.9 = (s32[512]{0:T(512)S(1)}, s32[512]{0:T(512)}, u32[]{:S(2)}) copy-start(s32[512]{0:T(512)} %param.19) | copy-start | bytes 6148
  1.3 1.0 %copy-start.4 = (bf16[1,512,512]{2,1,0:T(8,128)(2,1)S(1)}, bf16[1,512,512]{2,1,0:T(8,128)(2,1)}, u32[]{:S(2)}) copy-start(bf16[1,512,512]{2,1,0:T(8,128)(2,1)} %param.10) | copy-start | bytes 1572868
  2.4 0.9 %copy-start.6 = (bf16[1,512,256]{2,1,0:T(8,128)(2,1)S(1)}, bf16[1,512,256]{2,1,0:T(8,128)(2,1)}, u32[]{:S(2)}) copy-start(bf16[1,512,256]{2,1,0:T(8,128)(2,1)} %param.11) | copy-start | bytes 786436
  3.3 4.7 %copy-start = (bf16[128,256]{1,0:T(8,128)(2,1)S(1)}, bf16[128,256]{1,0:T(8,128)(2,1)}, u32[]{:S(2)}) copy-start(bf16[128,256]{1,0:T(8,128)(2,1)} %wq_ref.1) | copy-start | bytes 196612
  3.3 4.7 %copy-start.1 = (bf16[128,256]{1,0:T(8,128)(2,1)S(1)}, bf16[128,256]{1,0:T(8,128)(2,1)}, u32[]{:S(2)}) copy-start(bf16[128,256]{1,0:T(8,128)(2,1)} %wk_ref.1) | copy-start | bytes 196612
  3.3 4.7 %copy-start.2 = (bf16[128,256]{1,0:T(8,128)(2,1)S(1)}, bf16[128,256]{1,0:T(8,128)(2,1)}, u32[]{:S(2)}) copy-start(bf16[128,256]{1,0:T(8,128)(2,1)} %wv_ref.1) | copy-start | bytes 196612
  3.3 4.7 %copy-start.3 = (bf16[256,128]{1,0:T(8,128)(2,1)S(1)}, bf16[256,128]{1,0:T(8,128)(2,1)}, u32[]{:S(2)}) copy-start(bf16[256,128]{1,0:T(8,128)(2,1)} %wo_ref.1) | copy-start | bytes 196612
  4.1 9.4 %collective-permute-start = (bf16[256,512]{1,0:T(8,128)(2,1)S(1)}, bf16[256,512]{1,0:T(8,128)(2,1)S(1)}, u32[]{:S(2)}, u32[]{:S(2)}) collective-permute-start(bf16[256,512]{1,0:T(8,128)(2,1)S(1)} %get-tuple-element.18), channel_id=1, source_target_pairs={{0,4},{4,0},{8,12},{12,8},{1,5},{5,1},{9,13},{13,9},{2,6},{6,2},{1... | collective-permute-start | bytes 786440 | tf_op jit(solution)/shard_map/ppermute | solution.py:258
  7.2 6.3 %collective-permute-start.2 = (bf16[256,512]{1,0:T(8,128)(2,1)S(1)}, bf16[256,512]{1,0:T(8,128)(2,1)S(1)}, u32[]{:S(2)}, u32[]{:S(2)}) collective-permute-start(bf16[256,512]{1,0:T(8,128)(2,1)S(1)} %get-tuple-element.18), channel_id=1, source_target_pairs={{0,0},{4,8},{8,4},{12,12},{1,1},{5,9},{9,5},{13,13},{2,2},{6,10},{... | collective-permute-start | bytes 786440 | tf_op jit(solution)/shard_map/ppermute | solution.py:330
  7.9 22.1 %copy-start.7 = (bf16[3,512,16]{1,2,0:T(8,128)(2,1)S(1)}, bf16[3,512,16]{1,2,0:T(8,128)(2,1)}, u32[]{:S(2)}) copy-start(bf16[3,512,16]{1,2,0:T(8,128)(2,1)} %param.16) | copy-start | bytes 147460
  7.9 22.1 %copy-start.8 = (bf16[3,16,256]{2,1,0:T(8,128)(2,1)S(1)}, bf16[3,16,256]{2,1,0:T(8,128)(2,1)}, u32[]{:S(2)}) copy-start(bf16[3,16,256]{2,1,0:T(8,128)(2,1)} %param.17) | copy-start | bytes 73732
  7.9 20.0 %collective-permute-start.4 = (bf16[512,256]{1,0:T(8,128)(2,1)S(1)}, bf16[512,256]{1,0:T(8,128)(2,1)S(1)}, u32[]{:S(2)}, u32[]{:S(2)}) collective-permute-start(bf16[512,256]{1,0:T(8,128)(2,1)S(1)} %get-tuple-element.19.refs_6_), channel_id=1, source_target_pairs={{0,1},{1,0},{2,3},{3,2},{4,5},{5,4},{6,7},{7,6},{8,9},{9,8},{10,11... | collective-permute-start | bytes 786440 | tf_op jit(solution)/shard_map/ppermute | solution.py:258
  8.0 15.7 %copy-start.10 = (s32[16,6]{0,1:T(8,128)S(1)}, s32[16,6]{0,1:T(8,128)}, u32[]{:S(2)}) copy-start(s32[16,6]{0,1:T(8,128)} %param.18) | copy-start | bytes 1156
  8.2 15.2 %collective-permute-start.6 = (bf16[128,512]{1,0:T(8,128)(2,1)S(1)}, bf16[128,512]{1,0:T(8,128)(2,1)S(1)}, u32[]{:S(2)}, u32[]{:S(2)}) collective-permute-start(bf16[128,512]{1,0:T(8,128)(2,1)S(1)} %get-tuple-element.20.refs_10_), channel_id=1, source_target_pairs={{0,8},{4,12},{8,0},{12,4},{16,28},{20,24},{24,20},{28,16},{1,9},{5... | collective-permute-start | bytes 393224 | tf_op jit(solution)/shard_map/ppermute | solution.py:275
  13.5 16.4 %collective-permute-start.1 = (bf16[256,512]{1,0:T(8,128)(2,1)S(1)}, bf16[256,512]{1,0:T(8,128)(2,1)S(1)}, u32[]{:S(2)}, u32[]{:S(2)}) collective-permute-start(bf16[256,512]{1,0:T(8,128)(2,1)S(1)} %collective-permute-done.refs_2_), channel_id=1, source_target_pairs={{0,1},{1,0},{2,3},{3,2},{4,5},{5,4},{6,7},{7,6},{8,9},{9,8},{10,11... | collective-permute-start | bytes 786440 | tf_op jit(solution)/shard_map/ppermute | solution.py:258
  13.6 16.4 %collective-permute-start.3 = (bf16[256,512]{1,0:T(8,128)(2,1)S(1)}, bf16[256,512]{1,0:T(8,128)(2,1)S(1)}, u32[]{:S(2)}, u32[]{:S(2)}) collective-permute-start(bf16[256,512]{1,0:T(8,128)(2,1)S(1)} %collective-permute-done.2.refs_4_), channel_id=1, source_target_pairs={{0,1},{1,0},{2,3},{3,2},{4,5},{5,4},{6,7},{7,6},{8,9},{9,8},{10,11... | collective-permute-start | bytes 786440 | tf_op jit(solution)/shard_map/ppermute | solution.py:258
  14.1 12.4 %collective-permute-start.5 = (bf16[128,512]{1,0:T(8,128)(2,1)S(1)}, bf16[128,512]{1,0:T(8,128)(2,1)S(1)}, u32[]{:S(2)}, u32[]{:S(2)}) collective-permute-start(bf16[128,512]{1,0:T(8,128)(2,1)S(1)} %get-tuple-element.20.refs_10_), channel_id=1, source_target_pairs={{0,4},{4,0},{8,12},{12,8},{1,5},{5,1},{9,13},{13,9},{2,6},{6,2},{1... | collective-permute-start | bytes 393224 | tf_op jit(solution)/shard_map/ppermute | solution.py:258
  23.4 5.1 %collective-permute-start.7 = (bf16[128,512]{1,0:T(8,128)(2,1)S(1)}, bf16[128,512]{1,0:T(8,128)(2,1)S(1)}, u32[]{:S(2)}, u32[]{:S(2)}) collective-permute-start(bf16[128,512]{1,0:T(8,128)(2,1)S(1)} %collective-permute-done.6.refs_12_), channel_id=1, source_target_pairs={{0,16},{16,0},{1,17},{17,1},{2,18},{18,2},{3,19},{19,3},{4,20},{20... | collective-permute-start | bytes 393224 | tf_op jit(solution)/shard_map/ppermute | solution.py:258
  26.4 10.5 %collective-permute-start.9 = (bf16[128,512]{1,0:T(8,128)(2,1)S(1)}, bf16[128,512]{1,0:T(8,128)(2,1)S(1)}, u32[]{:S(2)}, u32[]{:S(2)}) collective-permute-start(bf16[128,512]{1,0:T(8,128)(2,1)S(1)} %collective-permute-done.6.refs_12_), channel_id=1, source_target_pairs={{0,2},{2,0},{1,3},{3,1},{4,6},{6,4},{5,7},{7,5},{8,10},{10,8},{9,1... | collective-permute-start | bytes 393224 | tf_op jit(solution)/shard_map/ppermute | solution.py:258
  27.9 9.0 %collective-permute-start.8 = (bf16[128,512]{1,0:T(8,128)(2,1)S(1)}, bf16[128,512]{1,0:T(8,128)(2,1)S(1)}, u32[]{:S(2)}, u32[]{:S(2)}) collective-permute-start(bf16[128,512]{1,0:T(8,128)(2,1)S(1)} %collective-permute-done.5.refs_11_), channel_id=1, source_target_pairs={{0,2},{2,0},{1,3},{3,1},{4,6},{6,4},{5,7},{7,5},{8,10},{10,8},{9,1... | collective-permute-start | bytes 393224 | tf_op jit(solution)/shard_map/ppermute | solution.py:258
  28.5 8.9 %collective-permute-start.10 = (bf16[128,512]{1,0:T(8,128)(2,1)S(1)}, bf16[128,512]{1,0:T(8,128)(2,1)S(1)}, u32[]{:S(2)}, u32[]{:S(2)}) collective-permute-start(bf16[128,512]{1,0:T(8,128)(2,1)S(1)} %collective-permute-done.7.refs_13_), channel_id=1, source_target_pairs={{0,2},{2,0},{1,3},{3,1},{4,6},{6,4},{5,7},{7,5},{8,10},{10,8},{9,1... | collective-permute-start | bytes 393224 | tf_op jit(solution)/shard_map/ppermute | solution.py:258
  37.4 19.1 %copy-start.5 = (bf16[1,512,512]{2,1,0:T(8,128)(2,1)S(1)}, bf16[1,512,512]{2,1,0:T(8,128)(2,1)}, u32[]{:S(2)}) copy-start(bf16[1,512,512]{2,1,0:T(8,128)(2,1)} %param.10) | copy-start | bytes 1572868
  44.3 4.4 %collective-permute-start.12 = (bf16[48,768]{1,0:T(8,128)(2,1)S(1)}, bf16[48,768]{1,0:T(8,128)(2,1)S(1)}, u32[]{:S(2)}, u32[]{:S(2)}) collective-permute-start(bf16[48,768]{1,0:T(8,128)(2,1)S(1)} %get-tuple-element.30), channel_id=1, source_target_pairs={{0,2},{2,0},{1,3},{3,1},{4,6},{6,4},{5,7},{7,5},{8,10},{10,8},{9,1... | collective-permute-start | bytes 221192 | tf_op jit(solution)/shard_map/ppermute | solution.py:258
  48.7 4.4 %collective-permute-start.13 = (bf16[48,768]{1,0:T(8,128)(2,1)S(1)}, bf16[48,768]{1,0:T(8,128)(2,1)S(1)}, u32[]{:S(2)}, u32[]{:S(2)}) collective-permute-start(bf16[48,768]{1,0:T(8,128)(2,1)S(1)} %add_convert_fusion.2), channel_id=1, source_target_pairs={{0,4},{4,0},{8,12},{12,8},{1,5},{5,1},{9,13},{13,9},{2,6},{6,2},{1... | collective-permute-start | bytes 221192 | tf_op jit(solution)/shard_map/ppermute | solution.py:258
  53.2 6.4 %collective-permute-start.14 = (bf16[48,768]{1,0:T(8,128)(2,1)S(1)}, bf16[48,768]{1,0:T(8,128)(2,1)S(1)}, u32[]{:S(2)}, u32[]{:S(2)}) collective-permute-start(bf16[48,768]{1,0:T(8,128)(2,1)S(1)} %add_convert_fusion.1), channel_id=1, source_target_pairs={{0,8},{4,12},{8,0},{12,4},{1,9},{5,13},{9,1},{13,5},{2,10},{6,14},... | collective-permute-start | bytes 221192 | tf_op jit(solution)/shard_map/ppermute | solution.py:258
  57.5 2.8 %collective-permute-start.11 = (bf16[512,256]{1,0:T(8,128)(2,1)S(1)}, bf16[512,256]{1,0:T(8,128)(2,1)S(1)}, u32[]{:S(2)}, u32[]{:S(2)}) collective-permute-start(bf16[512,256]{1,0:T(8,128)(2,1)S(1)} %get-tuple-element.29), channel_id=1, source_target_pairs={{0,1},{1,0},{2,3},{3,2},{4,5},{5,4},{6,7},{7,6},{8,9},{9,8},{10,11... | collective-permute-start | bytes 786440 | tf_op jit(solution)/shard_map/ppermute | solution.py:258
  60.3 1.2 %collective-permute-start.15 = (bf16[48,512]{1,0:T(8,128)(2,1)S(1)}, bf16[48,512]{1,0:T(8,128)(2,1)S(1)}, u32[]{:S(2)}, u32[]{:S(2)}) collective-permute-start(bf16[48,512]{1,0:T(8,128)(2,1)S(1)} %slice.12), channel_id=1, source_target_pairs={{0,1},{1,0},{2,3},{3,2},{4,5},{5,4},{6,7},{7,6},{8,9},{9,8},{10,11... | collective-permute-start | bytes 147464 | tf_op jit(solution)/shard_map/ppermute | solution.py:258

commit v3 on v2

--- a/solution.py
+++ b/solution.py
@@ -49,7 +49,18 @@
     return pl.ds(pl.multiple_of(index * DH, DH), DH)
 
 
-def pack_kernel(split, wq_ref, wk_ref, wv_ref, wo_ref, *outs):
+def load_all(sources, buffers, sems):
+    copies = [pltpu.make_async_copy(a, b, sems.at[i]) for i, (a, b) in enumerate(zip(sources, buffers))]
+    for copy in copies:
+        copy.start()
+    return copies
+
+
+def pack_kernel(split, *refs):
+    sources, outs, buffers, sems = refs[:4], refs[4:6], refs[6:10], refs[10]
+    for copy in load_all(sources, buffers, sems):
+        copy.wait()
+    wq_ref, wk_ref, wv_ref, wo_ref = buffers
     for which, out in enumerate(outs):
         lanes = lanes_at(head_at(split, which))
         for j, member in enumerate((wq_ref, wk_ref, wv_ref)):
@@ -57,13 +68,19 @@
         out[:, 3 * DH :] = wo_ref[lanes, :].T
 
 
-def prep_kernel(order_ref, x_ref, cot_ref, normed_ref, half_ref, cot_out_ref):
+def prep_kernel(
+    order_hbm, x_hbm, cot_hbm, normed_ref, half_ref, cot_out_ref, order_ref, x_ref, cot_ref, sems
+):
     rows = x_ref.shape[0]
+    copies = load_all((order_hbm, x_hbm, cot_hbm), (order_ref, x_ref, cot_ref), sems)
+    copies[0].wait()
     place = scatter_matrix(order_ref, rows)
+    copies[1].wait()
     ordered = tn(place, x_ref[...])
     center = ordered - jnp.mean(ordered, axis=-1, keepdims=True)
     spread = jnp.mean(center * center, axis=-1, keepdims=True)
     normed_ref[...] = (center * lax.rsqrt(spread + 1e-05)).astype(BF16)
+    copies[2].wait()
     cot_out_ref[...] = tn(place, cot_ref[...]).astype(BF16)
     start = pl.multiple_of(lax.axis_index("head") * (rows // 2), rows // 2)
     half_ref[...] = normed_ref[pl.ds(start, rows // 2), :]
@@ -87,7 +104,7 @@
     if which == 0:
         pieces, (att_ref, wo_ref, down_out, up_out) = rest[:-16], rest[-16:-12]
     else:
-        pieces, (down_in, up_in, att_ref, wo_ref, lora_ref) = rest[:-17], rest[-17:-12]
+        pieces, (down_in, up_in, att_ref, wo_ref, down_out, up_out) = rest[:-18], rest[-18:-12]
     w_ref, u_ref, kv_ref, low_ref, q_ref, do_ref, dq_ref, tk_ref, tv_ref, bk_ref, bv_ref, sum_ref = (
         scratch
     )
@@ -211,10 +228,15 @@
         down_out[...] = sum_ref[...]
         up_out[...] = up_grad
         return
-    lora_ref[:, :width] = (sum_ref[...] + down_in[...]).astype(BF16)
-    up_at = [pl.multiple_of(width + g * DH, DH) for g in (head, 1 - head)]
-    lora_ref[:, pl.ds(up_at[0], DH)] = up_grad.astype(BF16)
-    lora_ref[:, pl.ds(up_at[1], DH)] = up_in[...].astype(BF16)
+    down_out[...] = (sum_ref[...] + down_in[...]).astype(BF16)
+    up_out[:, lanes_at(head)] = up_grad.astype(BF16)
+    up_out[:, lanes_at(1 - head)] = up_in[...].astype(BF16)
+
+
+def merge_kernel(down_ref, sibling_ref, up_ref, out_ref):
+    width = down_ref.shape[1]
+    out_ref[:, :width] = (down_ref[...].astype(F32) + sibling_ref[...].astype(F32)).astype(BF16)
+    out_ref[:, width:] = up_ref[...]
 
 
 def out_kernel(order_ref, x_ref, att1_ref, att2_ref, wo1_ref, wo2_ref, base_ref, other_ref):
@@ -233,6 +255,7 @@
     base_ref[...] = x_ref[:, own].astype(F32) + part(core)
 
 
+HBM = pl.BlockSpec(memory_space=pltpu.HBM)
 VMEM = pl.BlockSpec(memory_space=pltpu.VMEM)
 SMEM = pl.BlockSpec(memory_space=pltpu.SMEM)
 
@@ -241,11 +264,11 @@
     return jax.ShapeDtypeStruct(dims, dtype)
 
 
-def call(kernel, outs, ins, scratch=(), smem=0, flops=0, limit=32):
+def call(kernel, outs, ins, scratch=(), smem=0, hbm=0, flops=0, limit=32):
     return pl.pallas_call(
         kernel,
         out_shape=outs,
-        in_specs=[SMEM] * smem + [VMEM] * (len(ins) - smem),
+        in_specs=[SMEM] * smem + [HBM] * hbm + [VMEM] * (len(ins) - smem - hbm),
         out_specs=(VMEM,) * len(outs),
         scratch_shapes=list(scratch),
         cost_estimate=pl.CostEstimate(flops=flops, bytes_accessed=1 << 20, transcendentals=0),
@@ -313,19 +336,31 @@
         functools.partial(pack_kernel, split),
         (shape((depth, 4 * DH)),) * 2,
         (query_weight, key_weight, value_weight, output_weight),
+        [pltpu.VMEM((depth, cols), BF16)] * 3
+        + [pltpu.VMEM((cols, depth), BF16), pltpu.SemaphoreType.DMA((4,))],
+        hbm=4,
         limit=8,
     )
     pieces, piece_rows = gather_weights(*packed)
     down = adapter_down_weight.transpose(0, 2, 1).reshape(3 * RANK, width)
     up = adapter_up_weight.reshape(3 * RANK, cols)
+    order, _ = lax.optimization_barrier((order, packed[0]))
     normed, half, cot_own = call(
         prep_kernel,
         (shape((rows, width)), shape((rows // 2, width)), shape((rows, cols))),
         (order, state, cotangent[0]),
+        [
+            pltpu.VMEM((1, rows), jnp.int32),
+            pltpu.VMEM((rows, width), BF16),
+            pltpu.VMEM((rows, cols), BF16),
+            pltpu.SemaphoreType.DMA((3,)),
+        ],
+        hbm=3,
         flops=2 * rows * rows * (width + cols),
         limit=16,
     )
     cot_sib = swap(cot_own, "head")
+    half, _ = lax.optimization_barrier((half, pieces[0][min(1, len(pieces[0]) - 1)]))
     a_own = swap(half, "node", 1)
     b_own = lax.ppermute(half, "node", chain_pairs(lax.axis_size("node")))
     a_sib = swap(a_own, "head")
@@ -365,20 +400,22 @@
         smem=1,
         flops=4 * 10**9,
     )
-    att2, wo2, lora = call(
+    att2, wo2, down2, up2 = call(
         functools.partial(head_kernel, split, 1, piece_rows[1]),
-        (shape((rows, DH)), shape((width, DH)), shape((3 * RANK, width + cols))),
+        (shape((rows, DH)), shape((width, DH)), shape((3 * RANK, width)), shape((3 * RANK, cols))),
         shared + tuple(pieces[1]) + (down1, up1),
         scratch,
         smem=1,
         flops=4 * 10**9,
     )
+    down_sib = swap(down2, "head")
     base, other = call(
         out_kernel,
         (shape((rows, cols), F32), shape((rows, cols))),
         (order, state, att1, att2, wo1, wo2),
         flops=10**9,
     )
+    lora = call(merge_kernel, (shape((3 * RANK, width + cols)),), (down2, down_sib, up2))[0]
     mesh_out = (base + swap(other, "head").astype(F32)).astype(BF16)[None]
 
     total = lora.astype(F32)
@@ -388,9 +425,7 @@
             sent = total.astype(BF16)
             total = sent.astype(F32) + swap(sent, axis, step).astype(F32)
             step *= 2
-    sent = total[:, :width].astype(BF16)
-    down_total = sent.astype(F32) + swap(sent, "head").astype(F32)
-    down_total = down_total.reshape(3, RANK, width).transpose(0, 2, 1)
+    down_total = total[:, :width].reshape(3, RANK, width).transpose(0, 2, 1)
     up_total = total[:, width:].reshape(3, RANK, cols)
     return (mesh_out, down_total, up_total)
 

time: 62.4 us -> 66.1 us (1.059)
  waiting for transfers between devices: 13.8 us -> 25.1 us
  starting transfers between devices: 26.9 us -> 15.8 us
  local copies, waits for them, and re-layouts: 3.42 us -> 6.44 us
  Pallas kernels: 15.8 us -> 16.8 us
    ppermute x14, starting transfers between devices: 22.3 us -> 11.2 us  [swap(): return lax.ppermute(value, axis, [(i, i ^ step) for i in range(size)])]
    ppermute x1, waiting for transfers between devices: 1.1 us -> 8.91 us  [gather_weights(): far = lax.ppermute(first, ('group', 'node'), far_pairs)]
    ppermute x14, waiting for transfers between devices: 12.7 us -> 16.2 us  [swap(): return lax.ppermute(value, axis, [(i, i ^ step) for i in range(size)])]
    unnamed x23, local copies, waits for them, and re-layouts: 2.79 us -> 5.17 us
    pallas_call x5 -> x6, Pallas kernels: 15.8 us -> 16.8 us  [call(): pl.pallas_call(kernel, out_shape=outs, in_specs=[SMEM] * smem + [HBM] * h...]
  transfers between devices with their start and end apart: 16 -> 16, of which waited for: 8 -> 8; matrix products, arithmetic and copies ran while one was open for 2% -> 1% of each run, Pallas kernels for 13% -> 14%
where the time goes in v3:
time: 66.1 us; the launch traced here: 65.8 us
  waiting for transfers between devices  25.1 us (38%)
  Pallas kernels  16.8 us (25%)
  starting transfers between devices  15.8 us (24%)
  local copies, waits for them, and re-layouts  6.44 us (10%)
  other arithmetic  0.83 us (1%)
  between operations  0.79 us (1%)
    pallas_call x6, Pallas kernels, call(): pl.pallas_call(kernel, out_shape=outs, in_specs=[SMEM] * smem + [HBM] * h...  16.8 us
    ppermute x14, waiting for transfers between devices, swap(): return lax.ppermute(value, axis, [(i, i ^ step) for i in range(size)])  16.2 us
    ppermute x14, starting transfers between devices, swap(): return lax.ppermute(value, axis, [(i, i ^ step) for i in range(size)])  11.2 us
    ppermute x1, waiting for transfers between devices, gather_weights(): far = lax.ppermute(first, ('group', 'node'), far_pairs)  8.91 us
    unnamed x23, local copies, waits for them, and re-layouts  5.17 us
    ppermute x1, starting transfers between devices, gather_weights(): far = lax.ppermute(first, ('group', 'node'), far_pairs)  3.9 us
  transfers between devices with their start and end apart: 16, of which 8 were waited for; matrix products, arithmetic and copies ran while one was open for 1% of the time, Pallas kernels for 14%

profile of v3, /device:TPU:0, one launch (start us, length us, event | category | flops | bytes accessed | tf_op | source)
XLA Modules:
  0.0 65.8 jit_solution(17814686670258362071)
XLA Ops:
  0.6 0.0 copy-start
  0.6 0.8 %copy-done = bf16[128,256]{1,0:T(8,128)(2,1)S(1)} copy-done((bf16[128,256]{1,0:T(8,128)(2,1)S(1)}, bf16[128,256]{1,0:T(8,128)(2,1)}, u32[]{:S(2)}) %copy-start) | copy-done | bytes 65560
  1.5 0.0 copy-start.1
  1.5 0.8 %copy-done.1 = bf16[128,256]{1,0:T(8,128)(2,1)S(1)} copy-done((bf16[128,256]{1,0:T(8,128)(2,1)S(1)}, bf16[128,256]{1,0:T(8,128)(2,1)}, u32[]{:S(2)}) %copy-start.1) | copy-done | bytes 65560
  2.3 0.0 copy-start.2
  2.3 0.8 %copy-done.2 = bf16[128,256]{1,0:T(8,128)(2,1)S(1)} copy-done((bf16[128,256]{1,0:T(8,128)(2,1)S(1)}, bf16[128,256]{1,0:T(8,128)(2,1)}, u32[]{:S(2)}) %copy-start.2) | copy-done | bytes 65560
  3.2 0.0 copy-start.3
  3.2 0.8 %copy-done.3 = bf16[256,128]{1,0:T(8,128)(2,1)S(1)} copy-done((bf16[256,128]{1,0:T(8,128)(2,1)S(1)}, bf16[256,128]{1,0:T(8,128)(2,1)}, u32[]{:S(2)}) %copy-start.3) | copy-done | bytes 65560
  4.0 0.0 copy-start.6
  4.0 0.5 shard_map.121
  4.5 3.1 %collective-permute-start = (bf16[128,512]{1,0:T(8,128)(2,1)S(1)}, bf16[128,512]{1,0:T(8,128)(2,1)S(1)}, u32[]{:S(2)}, u32[]{:S(2)}) collective-permute-start(bf16[128,512]{1,0:T(8,128)(2,1)S(1)} %get-tuple-element.20.refs_10_), channel_id=1, source_target_pairs={{0,4},{4,0},{8,12},{12,8},{1,5},{5,1},{9,13},{13,9},{2,6},{6,2},{1... | collective-permute-start | bytes 393224 | tf_op jit(solution)/shard_map/ppermute | solution.py:281
  7.6 0.0 copy-start.9
  7.6 0.0 copy-done.6
  7.6 0.7 %copy-done.9 = s32[512]{0:T(512)S(1)} copy-done((s32[512]{0:T(512)S(1)}, s32[512]{0:T(512)}, u32[]{:S(2)}) %copy-start.9) | copy-done | bytes 2072
  8.2 0.0 copy-start.4
  8.2 1.0 %copy-done.4 = bf16[1,512,512]{2,1,0:T(8,128)(2,1)S(1)} copy-done((bf16[1,512,512]{2,1,0:T(8,128)(2,1)S(1)}, bf16[1,512,512]{2,1,0:T(8,128)(2,1)}, u32[]{:S(2)}) %copy-start.4) | copy-done | bytes 524312
  9.3 0.0 copy-start.10
  9.3 0.0 copy-start.7
  9.3 0.0 copy-start.8
  9.3 1.5 %shard_map.122 = (bf16[512,512]{1,0:T(8,128)(2,1)S(1)}, bf16[256,512]{1,0:T(8,128)(2,1)S(1)}, bf16[512,256]{1,0:T(8,128)(2,1)S(1)}) custom-call(s32[1,512]{1,0:T(1,128)S(1)} %bitcast.20, bf16[512,512]{1,0:T(8,128)(2,1)S(1)} %bitcast.13, bf16[512,256]{1,0:T(8,128)(2,1)S(1)} %bitcast.15), custom_call_target="tpu_custom_call" | custom-call | flops 402653184 | bytes 1048576 | tf_op jit(solution)/shard_map/pallas_call | solution.py:268
  10.8 0.3 collective-permute-done.refs_11_
  11.1 1.7 %collective-permute-start.1 = (bf16[256,512]{1,0:T(8,128)(2,1)S(1)}, bf16[256,512]{1,0:T(8,128)(2,1)S(1)}, u32[]{:S(2)}, u32[]{:S(2)}) collective-permute-start(bf16[256,512]{1,0:T(8,128)(2,1)S(1)} %get-tuple-element.24), channel_id=1, source_target_pairs={{0,4},{4,0},{8,12},{12,8},{1,5},{5,1},{9,13},{13,9},{2,6},{6,2},{1... | collective-permute-start | bytes 786440 | tf_op jit(solution)/shard_map/ppermute | solution.py:281
  12.8 0.7 %collective-permute-start.3 = (bf16[256,512]{1,0:T(8,128)(2,1)S(1)}, bf16[256,512]{1,0:T(8,128)(2,1)S(1)}, u32[]{:S(2)}, u32[]{:S(2)}) collective-permute-start(bf16[256,512]{1,0:T(8,128)(2,1)S(1)} %get-tuple-element.24), channel_id=1, source_target_pairs={{0,0},{4,8},{8,4},{12,12},{1,1},{5,9},{9,5},{13,13},{2,2},{6,10},{... | collective-permute-start | bytes 786440 | tf_op jit(solution)/shard_map/ppermute | solution.py:365
  13.5 0.1 collective-permute-start.5
  13.5 3.9 %collective-permute-start.6 = (bf16[128,512]{1,0:T(8,128)(2,1)S(1)}, bf16[128,512]{1,0:T(8,128)(2,1)S(1)}, u32[]{:S(2)}, u32[]{:S(2)}) collective-permute-start(bf16[128,512]{1,0:T(8,128)(2,1)S(1)} %get-tuple-element.20.refs_10_), channel_id=1, source_target_pairs={{0,8},{4,12},{8,0},{12,4},{16,28},{20,24},{24,20},{28,16},{1,9},{5... | collective-permute-start | bytes 393224 | tf_op jit(solution)/shard_map/ppermute | solution.py:298
  17.4 1.2 %collective-permute-done.1.refs_2_ = bf16[256,512]{1,0:T(8,128)(2,1)S(1)} collective-permute-done((bf16[256,512]{1,0:T(8,128)(2,1)S(1)}, bf16[256,512]{1,0:T(8,128)(2,1)S(1)}, u32[]{:S(2)}, u32[]{:S(2)}) %collective-permute-start.1) | collective-permute-done | bytes 262176 | tf_op jit(solution)/shard_map/ppermute | solution.py:281
  18.6 0.0 collective-permute-start.2
  18.6 0.0 collective-permute-done.3.refs_4_
  18.6 0.5 collective-permute-start.4
  19.1 8.9 %collective-permute-done.6.refs_12_ = bf16[128,512]{1,0:T(8,128)(2,1)S(1)} collective-permute-done((bf16[128,512]{1,0:T(8,128)(2,1)S(1)}, bf16[128,512]{1,0:T(8,128)(2,1)S(1)}, u32[]{:S(2)}, u32[]{:S(2)}) %collective-permute-start.6) | collective-permute-done | bytes 131104 | tf_op jit(solution)/shard_map/ppermute | solution.py:298
  28.0 0.0 collective-permute-start.7
  28.0 0.0 copy-done.10
  28.0 0.1 copy.13.refs_0_
  28.1 1.5 %collective-permute-start.8 = (bf16[128,512]{1,0:T(8,128)(2,1)S(1)}, bf16[128,512]{1,0:T(8,128)(2,1)S(1)}, u32[]{:S(2)}, u32[]{:S(2)}) collective-permute-start(bf16[128,512]{1,0:T(8,128)(2,1)S(1)} %collective-permute-done.refs_11_), channel_id=1, source_target_pairs={{0,2},{2,0},{1,3},{3,1},{4,6},{6,4},{5,7},{7,5},{8,10},{10,8},{9,1... | collective-permute-start | bytes 393224 | tf_op jit(solution)/shard_map/ppermute | solution.py:281
  29.6 0.0 collective-permute-done.5.refs_7_
  29.6 0.5 collective-permute-start.9
  30.2 2.8 %collective-permute-done.7.refs_13_ = bf16[128,512]{1,0:T(8,128)(2,1)S(1)} collective-permute-done((bf16[128,512]{1,0:T(8,128)(2,1)S(1)}, bf16[128,512]{1,0:T(8,128)(2,1)S(1)}, u32[]{:S(2)}, u32[]{:S(2)}) %collective-permute-start.7) | collective-permute-done | bytes 131104 | tf_op jit(solution)/shard_map/ppermute | solution.py:281
  33.0 1.5 %collective-permute-start.10 = (bf16[128,512]{1,0:T(8,128)(2,1)S(1)}, bf16[128,512]{1,0:T(8,128)(2,1)S(1)}, u32[]{:S(2)}, u32[]{:S(2)}) collective-permute-start(bf16[128,512]{1,0:T(8,128)(2,1)S(1)} %collective-permute-done.7.refs_13_), channel_id=1, source_target_pairs={{0,2},{2,0},{1,3},{3,1},{4,6},{6,4},{5,7},{7,5},{8,10},{10,8},{9,1... | collective-permute-start | bytes 393224 | tf_op jit(solution)/shard_map/ppermute | solution.py:281
  34.5 0.0 collective-permute-done.2.refs_3_
  34.5 0.0 collective-permute-done.4.refs_5_
  34.5 0.0 copy-done.7
  34.5 0.0 copy-done.8
  34.5 6.9 %shard_map.123 = (bf16[512,128]{1,0:T(8,128)(2,1)S(1)}, bf16[512,128]{1,0:T(8,128)(2,1)S(1)}, f32[48,512]{1,0:T(8,128)S(1)}, f32[48,128]{1,0:T(8,128)S(1)}) custom-call(s32[16,6]{1,0:T(8,128)S(1)} %copy.13.refs_0_, bf16[512,512]{1,0:T(8,128)(2,1)S(1)} %get-tuple-element.22.refs_1_, bf16[256,512]{1,0:T(8,128)(2,1)S(1)} %collective-permute-done.1.refs_2_, ...), custom_call_target="tpu_custom_call" | custom-call | flops 4000000000 | bytes 1048576 | tf_op jit(solution)/shard_map/pallas_call | solution.py:268
  41.5 0.0 collective-permute-done.8.refs_11_
  41.5 0.0 collective-permute-done.9.refs_12_
  41.5 0.0 collective-permute-done.10.refs_13_
  41.5 0.0 copy-start.5
  41.5 6.9 %shard_map.124 = (bf16[512,128]{1,0:T(8,128)(2,1)S(1)}, bf16[512,128]{1,0:T(8,128)(2,1)S(1)}, bf16[48,512]{1,0:T(8,128)(2,1)S(1)}, bf16[48,256]{1,0:T(8,128)(2,1)S(1)}) custom-call(s32[16,6]{1,0:T(8,128)S(1)} %copy.13.refs_0_, bf16[512,512]{1,0:T(8,128)(2,1)S(1)} %get-tuple-element.22.refs_1_, bf16[256,512]{1,0:T(8,128)(2,1)S(1)} %collective-permute-done.1.refs_2_, ...), custom_call_target="tpu_custom_call" | custom-call | flops 4000000000 | bytes 1048576 | tf_op jit(solution)/shard_map/pallas_call | solution.py:268
  48.4 0.1 collective-permute-start.12
  48.5 1.2 %collective-permute-done.12.sibling_ref = bf16[48,512]{1,0:T(8,128)(2,1)S(1)} collective-permute-done((bf16[48,512]{1,0:T(8,128)(2,1)S(1)}, bf16[48,512]{1,0:T(8,128)(2,1)S(1)}, u32[]{:S(2)}, u32[]{:S(2)}) %collective-permute-start.12) | collective-permute-done | bytes 49184 | tf_op jit(solution)/shard_map/ppermute | solution.py:281
  49.8 0.6 collective-permute-start.13
  50.4 3.8 %collective-permute-done.13 = bf16[48,768]{1,0:T(8,128)(2,1)S(1)} collective-permute-done((bf16[48,768]{1,0:T(8,128)(2,1)S(1)}, bf16[48,768]{1,0:T(8,128)(2,1)S(1)}, u32[]{:S(2)}, u32[]{:S(2)}) %collective-permute-start.13) | collective-permute-done | bytes 73760 | tf_op jit(solution)/shard_map/ppermute | solution.py:281
  54.2 0.2 collective-permute-start.14
  54.4 0.0 copy-done.5
  54.4 1.0 %shard_map.125 = (f32[512,256]{1,0:T(8,128)S(1)}, bf16[512,256]{1,0:T(8,128)(2,1)S(1)}) custom-call(s32[1,512]{1,0:T(1,128)S(1)} %bitcast.21, bf16[512,512]{1,0:T(8,128)(2,1)S(1)} %bitcast.14, bf16[512,128]{1,0:T(8,128)(2,1)S(1)} %get-tuple-element.26.att1_ref, bf16[512,128]{1,0:T(8,128)(2,1)S(1)} %get-tuple-element.30.att2_ref, ...), custom_call_target="tpu_custom_call" | custom-call | flops 1000000000 | bytes 1048576 | tf_op jit(solution)/shard_map/pallas_call | solution.py:268
  55.4 0.1 collective-permute-start.11
  55.5 3.1 %collective-permute-done.14 = bf16[48,768]{1,0:T(8,128)(2,1)S(1)} collective-permute-done((bf16[48,768]{1,0:T(8,128)(2,1)S(1)}, bf16[48,768]{1,0:T(8,128)(2,1)S(1)}, u32[]{:S(2)}, u32[]{:S(2)}) %collective-permute-start.14) | collective-permute-done | bytes 73760 | tf_op jit(solution)/shard_map/ppermute | solution.py:281
  58.6 1.3 %collective-permute-start.15 = (bf16[48,768]{1,0:T(8,128)(2,1)S(1)}, bf16[48,768]{1,0:T(8,128)(2,1)S(1)}, u32[]{:S(2)}, u32[]{:S(2)}) collective-permute-start(bf16[48,768]{1,0:T(8,128)(2,1)S(1)} %add_convert_fusion.1), channel_id=1, source_target_pairs={{0,8},{4,12},{8,0},{12,4},{1,9},{5,13},{9,1},{13,5},{2,10},{6,14},... | collective-permute-start | bytes 221192 | tf_op jit(solution)/shard_map/ppermute | solution.py:281
  60.0 0.0 collective-permute-done.11
  60.0 0.8 %fusion = bf16[1,512,256]{2,1,0:T(8,128)(2,1)} fusion(f32[512,256]{1,0:T(8,128)S(1)} %get-tuple-element.33, bf16[512,256]{1,0:T(8,128)(2,1)S(1)} %collective-permute-done.11), kind=kLoop, calls=%fused_computation.1 | loop fusion | flops 393216 | bytes 1048576 | tf_op jit(solution)/shard_map/broadcast_in_dim | solution.py:419
  60.8 3.7 %collective-permute-done.15 = bf16[48,768]{1,0:T(8,128)(2,1)S(1)} collective-permute-done((bf16[48,768]{1,0:T(8,128)(2,1)S(1)}, bf16[48,768]{1,0:T(8,128)(2,1)S(1)}, u32[]{:S(2)}, u32[]{:S(2)}) %collective-permute-start.15) | collective-permute-done | bytes 73760 | tf_op jit(solution)/shard_map/ppermute | solution.py:281
  64.5 0.6 slice.8
  65.1 0.6 slice.9
  (4 shorter events, 0.1 us)
Async XLA Ops:
  0.6 0.8 %copy-start = (bf16[128,256]{1,0:T(8,128)(2,1)S(1)}, bf16[128,256]{1,0:T(8,128)(2,1)}, u32[]{:S(2)}) copy-start(bf16[128,256]{1,0:T(8,128)(2,1)} %refs_0_.3) | copy-start | bytes 196612
  1.5 0.8 %copy-start.1 = (bf16[128,256]{1,0:T(8,128)(2,1)S(1)}, bf16[128,256]{1,0:T(8,128)(2,1)}, u32[]{:S(2)}) copy-start(bf16[128,256]{1,0:T(8,128)(2,1)} %refs_1_.1) | copy-start | bytes 196612
  2.3 0.8 %copy-start.2 = (bf16[128,256]{1,0:T(8,128)(2,1)S(1)}, bf16[128,256]{1,0:T(8,128)(2,1)}, u32[]{:S(2)}) copy-start(bf16[128,256]{1,0:T(8,128)(2,1)} %refs_2_.1) | copy-start | bytes 196612
  3.2 0.8 %copy-start.3 = (bf16[256,128]{1,0:T(8,128)(2,1)S(1)}, bf16[256,128]{1,0:T(8,128)(2,1)}, u32[]{:S(2)}) copy-start(bf16[256,128]{1,0:T(8,128)(2,1)} %refs_3_.1) | copy-start | bytes 196612
  4.0 3.6 %copy-start.6 = (bf16[1,512,256]{2,1,0:T(8,128)(2,1)S(1)}, bf16[1,512,256]{2,1,0:T(8,128)(2,1)}, u32[]{:S(2)}) copy-start(bf16[1,512,256]{2,1,0:T(8,128)(2,1)} %param.11) | copy-start | bytes 786436
  4.5 6.6 %collective-permute-start = (bf16[128,512]{1,0:T(8,128)(2,1)S(1)}, bf16[128,512]{1,0:T(8,128)(2,1)S(1)}, u32[]{:S(2)}, u32[]{:S(2)}) collective-permute-start(bf16[128,512]{1,0:T(8,128)(2,1)S(1)} %get-tuple-element.20.refs_10_), channel_id=1, source_target_pairs={{0,4},{4,0},{8,12},{12,8},{1,5},{5,1},{9,13},{13,9},{2,6},{6,2},{1... | collective-permute-start | bytes 393224 | tf_op jit(solution)/shard_map/ppermute | solution.py:281
  7.6 0.7 %copy-start.9 = (s32[512]{0:T(512)S(1)}, s32[512]{0:T(512)}, u32[]{:S(2)}) copy-start(s32[512]{0:T(512)} %param.19) | copy-start | bytes 6148
  8.2 1.0 %copy-start.4 = (bf16[1,512,512]{2,1,0:T(8,128)(2,1)S(1)}, bf16[1,512,512]{2,1,0:T(8,128)(2,1)}, u32[]{:S(2)}) copy-start(bf16[1,512,512]{2,1,0:T(8,128)(2,1)} %param.10) | copy-start | bytes 1572868
  9.3 18.8 %copy-start.10 = (s32[16,6]{0,1:T(8,128)S(1)}, s32[16,6]{0,1:T(8,128)}, u32[]{:S(2)}) copy-start(s32[16,6]{0,1:T(8,128)} %param.18) | copy-start | bytes 1156
  9.3 25.2 %copy-start.7 = (bf16[3,512,16]{1,2,0:T(8,128)(2,1)S(1)}, bf16[3,512,16]{1,2,0:T(8,128)(2,1)}, u32[]{:S(2)}) copy-start(bf16[3,512,16]{1,2,0:T(8,128)(2,1)} %param.16) | copy-start | bytes 147460
  9.3 25.2 %copy-start.8 = (bf16[3,16,256]{2,1,0:T(8,128)(2,1)S(1)}, bf16[3,16,256]{2,1,0:T(8,128)(2,1)}, u32[]{:S(2)}) copy-start(bf16[3,16,256]{2,1,0:T(8,128)(2,1)} %param.17) | copy-start | bytes 73732
  11.1 7.6 %collective-permute-start.1 = (bf16[256,512]{1,0:T(8,128)(2,1)S(1)}, bf16[256,512]{1,0:T(8,128)(2,1)S(1)}, u32[]{:S(2)}, u32[]{:S(2)}) collective-permute-start(bf16[256,512]{1,0:T(8,128)(2,1)S(1)} %get-tuple-element.24), channel_id=1, source_target_pairs={{0,4},{4,0},{8,12},{12,8},{1,5},{5,1},{9,13},{13,9},{2,6},{6,2},{1... | collective-permute-start | bytes 786440 | tf_op jit(solution)/shard_map/ppermute | solution.py:281
  12.8 5.8 %collective-permute-start.3 = (bf16[256,512]{1,0:T(8,128)(2,1)S(1)}, bf16[256,512]{1,0:T(8,128)(2,1)S(1)}, u32[]{:S(2)}, u32[]{:S(2)}) collective-permute-start(bf16[256,512]{1,0:T(8,128)(2,1)S(1)} %get-tuple-element.24), channel_id=1, source_target_pairs={{0,0},{4,8},{8,4},{12,12},{1,1},{5,9},{9,5},{13,13},{2,2},{6,10},{... | collective-permute-start | bytes 786440 | tf_op jit(solution)/shard_map/ppermute | solution.py:365
  13.5 16.2 %collective-permute-start.5 = (bf16[512,256]{1,0:T(8,128)(2,1)S(1)}, bf16[512,256]{1,0:T(8,128)(2,1)S(1)}, u32[]{:S(2)}, u32[]{:S(2)}) collective-permute-start(bf16[512,256]{1,0:T(8,128)(2,1)S(1)} %get-tuple-element.25.refs_6_), channel_id=1, source_target_pairs={{0,1},{1,0},{2,3},{3,2},{4,5},{5,4},{6,7},{7,6},{8,9},{9,8},{10,11... | collective-permute-start | bytes 786440 | tf_op jit(solution)/shard_map/ppermute | solution.py:281
  13.5 14.5 %collective-permute-start.6 = (bf16[128,512]{1,0:T(8,128)(2,1)S(1)}, bf16[128,512]{1,0:T(8,128)(2,1)S(1)}, u32[]{:S(2)}, u32[]{:S(2)}) collective-permute-start(bf16[128,512]{1,0:T(8,128)(2,1)S(1)} %get-tuple-element.20.refs_10_), channel_id=1, source_target_pairs={{0,8},{4,12},{8,0},{12,4},{16,28},{20,24},{24,20},{28,16},{1,9},{5... | collective-permute-start | bytes 393224 | tf_op jit(solution)/shard_map/ppermute | solution.py:298
  18.6 15.9 %collective-permute-start.2 = (bf16[256,512]{1,0:T(8,128)(2,1)S(1)}, bf16[256,512]{1,0:T(8,128)(2,1)S(1)}, u32[]{:S(2)}, u32[]{:S(2)}) collective-permute-start(bf16[256,512]{1,0:T(8,128)(2,1)S(1)} %collective-permute-done.1.refs_2_), channel_id=1, source_target_pairs={{0,1},{1,0},{2,3},{3,2},{4,5},{5,4},{6,7},{7,6},{8,9},{9,8},{10,11... | collective-permute-start | bytes 786440 | tf_op jit(solution)/shard_map/ppermute | solution.py:281
  18.6 15.9 %collective-permute-start.4 = (bf16[256,512]{1,0:T(8,128)(2,1)S(1)}, bf16[256,512]{1,0:T(8,128)(2,1)S(1)}, u32[]{:S(2)}, u32[]{:S(2)}) collective-permute-start(bf16[256,512]{1,0:T(8,128)(2,1)S(1)} %collective-permute-done.3.refs_4_), channel_id=1, source_target_pairs={{0,1},{1,0},{2,3},{3,2},{4,5},{5,4},{6,7},{7,6},{8,9},{9,8},{10,11... | collective-permute-start | bytes 786440 | tf_op jit(solution)/shard_map/ppermute | solution.py:281
  28.0 5.0 %collective-permute-start.7 = (bf16[128,512]{1,0:T(8,128)(2,1)S(1)}, bf16[128,512]{1,0:T(8,128)(2,1)S(1)}, u32[]{:S(2)}, u32[]{:S(2)}) collective-permute-start(bf16[128,512]{1,0:T(8,128)(2,1)S(1)} %collective-permute-done.6.refs_12_), channel_id=1, source_target_pairs={{0,16},{16,0},{1,17},{17,1},{2,18},{18,2},{3,19},{19,3},{4,20},{20... | collective-permute-start | bytes 393224 | tf_op jit(solution)/shard_map/ppermute | solution.py:281
  28.1 13.3 %collective-permute-start.8 = (bf16[128,512]{1,0:T(8,128)(2,1)S(1)}, bf16[128,512]{1,0:T(8,128)(2,1)S(1)}, u32[]{:S(2)}, u32[]{:S(2)}) collective-permute-start(bf16[128,512]{1,0:T(8,128)(2,1)S(1)} %collective-permute-done.refs_11_), channel_id=1, source_target_pairs={{0,2},{2,0},{1,3},{3,1},{4,6},{6,4},{5,7},{7,5},{8,10},{10,8},{9,1... | collective-permute-start | bytes 393224 | tf_op jit(solution)/shard_map/ppermute | solution.py:281
  29.6 11.8 %collective-permute-start.9 = (bf16[128,512]{1,0:T(8,128)(2,1)S(1)}, bf16[128,512]{1,0:T(8,128)(2,1)S(1)}, u32[]{:S(2)}, u32[]{:S(2)}) collective-permute-start(bf16[128,512]{1,0:T(8,128)(2,1)S(1)} %collective-permute-done.6.refs_12_), channel_id=1, source_target_pairs={{0,2},{2,0},{1,3},{3,1},{4,6},{6,4},{5,7},{7,5},{8,10},{10,8},{9,1... | collective-permute-start | bytes 393224 | tf_op jit(solution)/shard_map/ppermute | solution.py:281
  33.0 8.5 %collective-permute-start.10 = (bf16[128,512]{1,0:T(8,128)(2,1)S(1)}, bf16[128,512]{1,0:T(8,128)(2,1)S(1)}, u32[]{:S(2)}, u32[]{:S(2)}) collective-permute-start(bf16[128,512]{1,0:T(8,128)(2,1)S(1)} %collective-permute-done.7.refs_13_), channel_id=1, source_target_pairs={{0,2},{2,0},{1,3},{3,1},{4,6},{6,4},{5,7},{7,5},{8,10},{10,8},{9,1... | collective-permute-start | bytes 393224 | tf_op jit(solution)/shard_map/ppermute | solution.py:281
  41.5 12.9 %copy-start.5 = (bf16[1,512,512]{2,1,0:T(8,128)(2,1)S(1)}, bf16[1,512,512]{2,1,0:T(8,128)(2,1)}, u32[]{:S(2)}) copy-start(bf16[1,512,512]{2,1,0:T(8,128)(2,1)} %param.10) | copy-start | bytes 1572868
  48.4 1.3 %collective-permute-start.12 = (bf16[48,512]{1,0:T(8,128)(2,1)S(1)}, bf16[48,512]{1,0:T(8,128)(2,1)S(1)}, u32[]{:S(2)}, u32[]{:S(2)}) collective-permute-start(bf16[48,512]{1,0:T(8,128)(2,1)S(1)} %get-tuple-element.35.down_ref), channel_id=1, source_target_pairs={{0,1},{1,0},{2,3},{3,2},{4,5},{5,4},{6,7},{7,6},{8,9},{9,8},{10,11... | collective-permute-start | bytes 147464 | tf_op jit(solution)/shard_map/ppermute | solution.py:281
  49.8 4.4 %collective-permute-start.13 = (bf16[48,768]{1,0:T(8,128)(2,1)S(1)}, bf16[48,768]{1,0:T(8,128)(2,1)S(1)}, u32[]{:S(2)}, u32[]{:S(2)}) collective-permute-start(bf16[48,768]{1,0:T(8,128)(2,1)S(1)} %shard_map.126), channel_id=1, source_target_pairs={{0,2},{2,0},{1,3},{3,1},{4,6},{6,4},{5,7},{7,5},{8,10},{10,8},{9,1... | collective-permute-start | bytes 221192 | tf_op jit(solution)/shard_map/ppermute | solution.py:281
  54.2 4.4 %collective-permute-start.14 = (bf16[48,768]{1,0:T(8,128)(2,1)S(1)}, bf16[48,768]{1,0:T(8,128)(2,1)S(1)}, u32[]{:S(2)}, u32[]{:S(2)}) collective-permute-start(bf16[48,768]{1,0:T(8,128)(2,1)S(1)} %add_convert_fusion.2), channel_id=1, source_target_pairs={{0,4},{4,0},{8,12},{12,8},{1,5},{5,1},{9,13},{13,9},{2,6},{6,2},{1... | collective-permute-start | bytes 221192 | tf_op jit(solution)/shard_map/ppermute | solution.py:281
  55.4 4.6 %collective-permute-start.11 = (bf16[512,256]{1,0:T(8,128)(2,1)S(1)}, bf16[512,256]{1,0:T(8,128)(2,1)S(1)}, u32[]{:S(2)}, u32[]{:S(2)}) collective-permute-start(bf16[512,256]{1,0:T(8,128)(2,1)S(1)} %get-tuple-element.34), channel_id=1, source_target_pairs={{0,1},{1,0},{2,3},{3,2},{4,5},{5,4},{6,7},{7,6},{8,9},{9,8},{10,11... | collective-permute-start | bytes 786440 | tf_op jit(solution)/shard_map/ppermute | solution.py:281
  58.6 5.8 %collective-permute-start.15 = (bf16[48,768]{1,0:T(8,128)(2,1)S(1)}, bf16[48,768]{1,0:T(8,128)(2,1)S(1)}, u32[]{:S(2)}, u32[]{:S(2)}) collective-permute-start(bf16[48,768]{1,0:T(8,128)(2,1)S(1)} %add_convert_fusion.1), channel_id=1, source_target_pairs={{0,8},{4,12},{8,0},{12,4},{1,9},{5,13},{9,1},{13,5},{2,10},{6,14},... | collective-permute-start | bytes 221192 | tf_op jit(solution)/shard_map/ppermute | solution.py:281

commit v4 on v3

--- a/solution.py
+++ b/solution.py
@@ -56,23 +56,12 @@
     return copies
 
 
-def pack_kernel(split, *refs):
-    sources, outs, buffers, sems = refs[:4], refs[4:6], refs[6:10], refs[10]
-    for copy in load_all(sources, buffers, sems):
-        copy.wait()
-    wq_ref, wk_ref, wv_ref, wo_ref = buffers
-    for which, out in enumerate(outs):
-        lanes = lanes_at(head_at(split, which))
-        for j, member in enumerate((wq_ref, wk_ref, wv_ref)):
-            out[:, j * DH : (j + 1) * DH] = member[:, lanes]
-        out[:, 3 * DH :] = wo_ref[lanes, :].T
-
-
-def prep_kernel(
-    order_hbm, x_hbm, cot_hbm, normed_ref, half_ref, cot_out_ref, order_ref, x_ref, cot_ref, sems
-):
+def prep_kernel(split, *refs):
+    sources, outs, buffers, sems = refs[:7], refs[7:-8], refs[-8:-1], refs[-1]
+    copies = load_all(sources, buffers, sems)
+    order_ref, x_ref, wq_ref, wk_ref, wv_ref, wo_ref, cot_ref = buffers
+    normed_ref, half_ref, near_ref, cot_out_ref = outs[:4]
     rows = x_ref.shape[0]
-    copies = load_all((order_hbm, x_hbm, cot_hbm), (order_ref, x_ref, cot_ref), sems)
     copies[0].wait()
     place = scatter_matrix(order_ref, rows)
     copies[1].wait()
@@ -80,10 +69,20 @@
     center = ordered - jnp.mean(ordered, axis=-1, keepdims=True)
     spread = jnp.mean(center * center, axis=-1, keepdims=True)
     normed_ref[...] = (center * lax.rsqrt(spread + 1e-05)).astype(BF16)
-    copies[2].wait()
+    for copy in copies[2:]:
+        copy.wait()
+    for which, out in enumerate(outs[4:]):
+        lanes = lanes_at(head_at(split, which))
+        for j, member in enumerate((wq_ref, wk_ref, wv_ref)):
+            out[:, j * DH : (j + 1) * DH] = member[:, lanes]
+        out[:, 3 * DH :] = wo_ref[lanes, :].T
     cot_out_ref[...] = tn(place, cot_ref[...]).astype(BF16)
     start = pl.multiple_of(lax.axis_index("head") * (rows // 2), rows // 2)
     half_ref[...] = normed_ref[pl.ds(start, rows // 2), :]
+    skip = near_ref.shape[0] - rows // 2
+    if skip:
+        near_ref[:skip, :] = outs[4][...]
+    near_ref[skip:, :] = half_ref[...]
 
 
 def head_kernel(split, which, piece_rows, *refs):
@@ -120,7 +119,8 @@
         if isinstance(row, int):
             w_ref[pl.ds(row, piece.shape[0]), :] = piece[...]
         else:
-            w_ref[pl.ds(pl.multiple_of(row, piece.shape[0]), piece.shape[0]), :] = piece[...]
+            depth = rest[0].shape[0]
+            w_ref[pl.ds(pl.multiple_of(row, depth), depth), :] = piece[:depth, :]
     wo_ref[...] = w_ref[:, 3 * DH :]
     u_ref[...] = jnp.zeros_like(u_ref)
     for j in range(3):
@@ -131,7 +131,7 @@
     mine, theirs = core * half, (1 - core) * half
     segments = [
         (normed_ref, 0),
-        (a_own_ref, pl.multiple_of(rows + mine, half)),
+        (a_own_ref.at[pl.ds(a_own_ref.shape[0] - half, half), :], pl.multiple_of(rows + mine, half)),
         (a_sib_ref, pl.multiple_of(rows + theirs, half)),
         (b_own_ref, pl.multiple_of(2 * rows + mine, half)),
         (b_sib_ref, pl.multiple_of(2 * rows + theirs, half)),
@@ -239,6 +239,13 @@
     out_ref[:, width:] = up_ref[...]
 
 
+def final_kernel(own_ref, recv_ref, down_ref, up_ref):
+    width = down_ref.shape[1]
+    total = own_ref[...].astype(F32) + recv_ref[...].astype(F32)
+    down_ref[...] = total[:, :width]
+    up_ref[...] = total[:, width:]
+
+
 def out_kernel(order_ref, x_ref, att1_ref, att2_ref, wo1_ref, wo2_ref, base_ref, other_ref):
     rows, width = x_ref.shape
     cols = width // 2
@@ -264,7 +271,7 @@
     return jax.ShapeDtypeStruct(dims, dtype)
 
 
-def call(kernel, outs, ins, scratch=(), smem=0, hbm=0, flops=0, limit=32):
+def call(kernel, outs, ins, scratch=(), smem=0, hbm=0, flops=0, limit=None):
     return pl.pallas_call(
         kernel,
         out_shape=outs,
@@ -272,7 +279,7 @@
         out_specs=(VMEM,) * len(outs),
         scratch_shapes=list(scratch),
         cost_estimate=pl.CostEstimate(flops=flops, bytes_accessed=1 << 20, transcendentals=0),
-        compiler_params=pltpu.CompilerParams(vmem_limit_bytes=limit * 2**20),
+        compiler_params=pltpu.CompilerParams(vmem_limit_bytes=limit and limit * 2**20),
     )(*ins)
 
 
@@ -288,25 +295,27 @@
     return sorted(pairs.items())
 
 
-def gather_weights(first, second):
+def gather_weights(first, second, near):
     count, depth = lax.axis_size("node"), first.shape[0]
     if not split_weights():
         whole = [lax.all_gather(m, "node", axis=0, tiled=True) for m in (first, second)]
-        return [[whole[0]], [whole[1]]], [lambda node: [0]] * 2
-    near = swap(first, "node", 1)
+        return [[whole[0]], [whole[1]]], lambda node: [0]
     far_pairs = [(g * 4 + n, g * 4 + (n ^ (2 + g))) for g in range(2) for n in range(4)]
     far = lax.ppermute(first, ("group", "node"), far_pairs)
     other_far = swap(far, "group")
-
-    def places(node, steps):
-        return [jnp.bitwise_xor(node, k) * depth for k in steps]
+    diagonal = [(i, 3 - i) for i in range(4)]
+    theirs = [
+        second,
+        swap(near[:depth], "sample"),
+        swap(far, "sample"),
+        lax.ppermute(far, ("group", "sample"), diagonal),
+    ]
 
     def piece_rows(node):
         group = lax.axis_index("group")
-        return places(node, (0, 1, 2 + group, 3 - group))
-
-    own = [first, near, far, other_far]
-    return [own, [second] + [swap(p, "sample") for p in own[1:]]], [piece_rows] * 2
+        return [jnp.bitwise_xor(node, k) * depth for k in (0, 1, 2 + group, 3 - group)]
+
+    return [[first, near, far, other_far], theirs], piece_rows
 
 
 def split_weights():
@@ -332,39 +341,40 @@
     order = block_node_order.reshape(1, rows)
     split = split_weights()
 
-    packed = call(
-        functools.partial(pack_kernel, split),
-        (shape((depth, 4 * DH)),) * 2,
-        (query_weight, key_weight, value_weight, output_weight),
-        [pltpu.VMEM((depth, cols), BF16)] * 3
-        + [pltpu.VMEM((cols, depth), BF16), pltpu.SemaphoreType.DMA((4,))],
-        hbm=4,
-        limit=8,
-    )
-    pieces, piece_rows = gather_weights(*packed)
     down = adapter_down_weight.transpose(0, 2, 1).reshape(3 * RANK, width)
     up = adapter_up_weight.reshape(3 * RANK, cols)
-    order, _ = lax.optimization_barrier((order, packed[0]))
-    normed, half, cot_own = call(
-        prep_kernel,
-        (shape((rows, width)), shape((rows // 2, width)), shape((rows, cols))),
-        (order, state, cotangent[0]),
+    skip = depth if split else 0
+    normed, half, near, cot_own, *packed = call(
+        functools.partial(prep_kernel, split),
+        (
+            shape((rows, width)),
+            shape((rows // 2, width)),
+            shape((skip + rows // 2, width)),
+            shape((rows, cols)),
+            shape((depth, 4 * DH)),
+            shape((depth, 4 * DH)),
+        ),
+        (order, state, query_weight, key_weight, value_weight, output_weight, cotangent[0]),
         [
             pltpu.VMEM((1, rows), jnp.int32),
             pltpu.VMEM((rows, width), BF16),
+            pltpu.VMEM((depth, cols), BF16),
+            pltpu.VMEM((depth, cols), BF16),
+            pltpu.VMEM((depth, cols), BF16),
+            pltpu.VMEM((cols, depth), BF16),
             pltpu.VMEM((rows, cols), BF16),
-            pltpu.SemaphoreType.DMA((3,)),
+            pltpu.SemaphoreType.DMA((7,)),
         ],
-        hbm=3,
+        hbm=7,
         flops=2 * rows * rows * (width + cols),
-        limit=16,
-    )
+    )
+    a_own = swap(near, "node", 1)
+    b_own = lax.ppermute(half, "node", chain_pairs(lax.axis_size("node")))
+    pieces, piece_rows = gather_weights(*packed, a_own)
     cot_sib = swap(cot_own, "head")
-    half, _ = lax.optimization_barrier((half, pieces[0][min(1, len(pieces[0]) - 1)]))
-    a_own = swap(half, "node", 1)
-    b_own = lax.ppermute(half, "node", chain_pairs(lax.axis_size("node")))
-    a_sib = swap(a_own, "head")
-    b_sib = swap(b_own, "head")
+    a_half, b_half, _ = lax.optimization_barrier((a_own[skip:], b_own, pieces[0][-1]))
+    a_sib = swap(a_half, "head")
+    b_sib = swap(b_half, "head")
 
     shared = (
         neighbour_key_blocks,
@@ -393,19 +403,21 @@
         pltpu.VMEM((3 * RANK, width), F32),
     ]
     att1, wo1, down1, up1 = call(
-        functools.partial(head_kernel, split, 0, piece_rows[0]),
+        functools.partial(head_kernel, split, 0, piece_rows),
         (shape((rows, DH)), shape((width, DH)), shape((3 * RANK, width), F32), shape((3 * RANK, DH), F32)),
         shared + tuple(pieces[0]),
         scratch,
         smem=1,
+        limit=32,
         flops=4 * 10**9,
     )
     att2, wo2, down2, up2 = call(
-        functools.partial(head_kernel, split, 1, piece_rows[1]),
+        functools.partial(head_kernel, split, 1, piece_rows),
         (shape((rows, DH)), shape((width, DH)), shape((3 * RANK, width)), shape((3 * RANK, cols))),
         shared + tuple(pieces[1]) + (down1, up1),
         scratch,
         smem=1,
+        limit=32,
         flops=4 * 10**9,
     )
     down_sib = swap(down2, "head")
@@ -418,15 +430,17 @@
     lora = call(merge_kernel, (shape((3 * RANK, width + cols)),), (down2, down_sib, up2))[0]
     mesh_out = (base + swap(other, "head").astype(F32)).astype(BF16)[None]
 
-    total = lora.astype(F32)
-    for axis in ("sample", "node"):
-        step = 1
-        while step < lax.axis_size(axis):
-            sent = total.astype(BF16)
-            total = sent.astype(F32) + swap(sent, axis, step).astype(F32)
-            step *= 2
-    down_total = total[:, :width].reshape(3, RANK, width).transpose(0, 2, 1)
-    up_total = total[:, width:].reshape(3, RANK, cols)
+    hops = [("sample", 1 << i) for i in range(lax.axis_size("sample").bit_length() - 1)]
+    hops += [("node", 1 << i) for i in range(lax.axis_size("node").bit_length() - 1)]
+    for axis, step in hops[:-1]:
+        lora = (lora.astype(F32) + swap(lora, axis, step).astype(F32)).astype(BF16)
+    down_total, up_total = call(
+        final_kernel,
+        (shape((3 * RANK, width), F32), shape((3 * RANK, cols), F32)),
+        (lora, swap(lora, *hops[-1])),
+    )
+    down_total = down_total.reshape(3, RANK, width).transpose(0, 2, 1)
+    up_total = up_total.reshape(3, RANK, cols)
     return (mesh_out, down_total, up_total)
 
 

time: 66.1 us -> 69.7 us (1.054)
  Pallas kernels: 16.8 us -> 23.2 us
  waiting for transfers between devices: 25.1 us -> 20.9 us
  local copies, waits for them, and re-layouts: 6.44 us -> 3.02 us
  starting transfers between devices: 15.8 us -> 18.5 us
  other arithmetic: 0.83 us -> 2.73 us
    pallas_call x6, Pallas kernels: 16.8 us -> 23.2 us  [call(): pl.pallas_call(kernel, out_shape=outs, in_specs=[SMEM] * smem + [HBM] * h...]
    ppermute x14 -> x12, waiting for transfers between devices: 16.2 us -> 13.5 us  [swap(): return lax.ppermute(value, axis, [(i, i ^ step) for i in range(size)])]
    unnamed x23 -> x33, local copies, waits for them, and re-layouts: 5.17 us -> 2.99 us
    ppermute x0 -> x1, starting transfers between devices: none -> 2 us  [gather_weights(): lax.ppermute(far, ('group', 'sample'), diagonal)]
    ppermute x1, waiting for transfers between devices: 8.91 us -> 7.35 us  [gather_weights(): far = lax.ppermute(first, ('group', 'node'), far_pairs)]
    ppermute x1, starting transfers between devices: 3.9 us -> 2.59 us  [gather_weights(): far = lax.ppermute(first, ('group', 'node'), far_pairs)]
    slice x2, local copies, waits for them, and re-layouts: 1.27 us -> 0.03 us  [the longest x1 0.02 us: shards(): a_own[skip:]]
    ppermute x14 -> x12, starting transfers between devices: 11.2 us -> 12.4 us  [swap(): return lax.ppermute(value, axis, [(i, i ^ step) for i in range(size)])]
  transfers between devices with their start and end apart: 16 -> 15, of which waited for: 8 -> 6; matrix products, arithmetic and copies ran while one was open for 1% -> 3% of each run, Pallas kernels for 14% -> 14%
where the time goes in v4:
time: 69.7 us; the launch traced here: 69.2 us
  Pallas kernels  23.2 us (33%)
  waiting for transfers between devices  20.9 us (30%)
  starting transfers between devices  18.5 us (27%)
  local copies, waits for them, and re-layouts  3.02 us (4%)
  other arithmetic  2.73 us (4%)
  between operations  0.88 us (1%)
    pallas_call x6, Pallas kernels, call(): pl.pallas_call(kernel, out_shape=outs, in_specs=[SMEM] * smem + [HBM] * h...  23.2 us
    ppermute x12, waiting for transfers between devices, swap(): return lax.ppermute(value, axis, [(i, i ^ step) for i in range(size)])  13.5 us
    ppermute x12, starting transfers between devices, swap(): return lax.ppermute(value, axis, [(i, i ^ step) for i in range(size)])  12.4 us
    ppermute x1, waiting for transfers between devices, gather_weights(): far = lax.ppermute(first, ('group', 'node'), far_pairs)  7.35 us
    unnamed x33, local copies, waits for them, and re-layouts  2.99 us
    ppermute x1, starting transfers between devices, gather_weights(): far = lax.ppermute(first, ('group', 'node'), far_pairs)  2.59 us
    ppermute x1, starting transfers between devices, gather_weights(): lax.ppermute(far, ('group', 'sample'), diagonal)  2 us
    broadcast_in_dim x1, other arithmetic, shards(): mesh_out = (base + swap(other, 'head').astype(F32)).astype(BF16)[None]  1.8 us
  transfers between devices with their start and end apart: 15, of which 6 were waited for; matrix products, arithmetic and copies ran while one was open for 3% of the time, Pallas kernels for 14%

profile of v4, /device:TPU:0, one launch (start us, length us, event | category | flops | bytes accessed | tf_op | source)
XLA Modules:
  0.0 69.2 jit_solution(1991340348049097007)
XLA Ops:
  0.6 3.3 %shard_map.121 = (bf16[512,512]{1,0:T(8,128)(2,1)}, bf16[256,512]{1,0:T(8,128)(2,1)}, bf16[384,512]{1,0:T(8,128)(2,1)}, bf16[512,256]{1,0:T(8,128)(2,1)}, bf16[1...) custom-call(s32[1,512]{1,0:T(1,128)} %bitcast.22, bf16[512,512]{1,0:T(8,128)(2,1)} %bitcast.17, bf16[128,256]{1,0:T(8,128)(2,1)} %refs_2_.1, ...), custom_call_target="tpu_custom_call" | custom-call | flops 402653184 | bytes 1048576 | tf_op jit(solution)/shard_map/pallas_call | solution.py:275
  3.9 3.1 %collective-permute-start = (bf16[384,512]{1,0:T(8,128)(2,1)}, bf16[384,512]{1,0:T(8,128)(2,1)S(1)}, u32[]{:S(2)}, u32[]{:S(2)}) collective-permute-start(bf16[384,512]{1,0:T(8,128)(2,1)} %get-tuple-element.24), channel_id=1, source_target_pairs={{0,4},{4,0},{8,12},{12,8},{1,5},{5,1},{9,13},{13,9},{2,6},{6,2},{1... | collective-permute-start | bytes 1179656 | tf_op jit(solution)/shard_map/ppermute | solution.py:288
  7.0 2.6 %collective-permute-start.2 = (bf16[128,512]{1,0:T(8,128)(2,1)}, bf16[128,512]{1,0:T(8,128)(2,1)S(1)}, u32[]{:S(2)}, u32[]{:S(2)}) collective-permute-start(bf16[128,512]{1,0:T(8,128)(2,1)} %get-tuple-element.26.refs_10_), channel_id=1, source_target_pairs={{0,8},{4,12},{8,0},{12,4},{16,28},{20,24},{24,20},{28,16},{1,9},{5... | collective-permute-start | bytes 393224 | tf_op jit(solution)/shard_map/ppermute | solution.py:304
  9.6 1.6 %collective-permute-start.1 = (bf16[256,512]{1,0:T(8,128)(2,1)}, bf16[256,512]{1,0:T(8,128)(2,1)S(1)}, u32[]{:S(2)}, u32[]{:S(2)}) collective-permute-start(bf16[256,512]{1,0:T(8,128)(2,1)} %get-tuple-element.25), channel_id=1, source_target_pairs={{0,0},{4,8},{8,4},{12,12},{1,1},{5,9},{9,5},{13,13},{2,2},{6,10},{... | collective-permute-start | bytes 786440 | tf_op jit(solution)/shard_map/ppermute | solution.py:372
  11.2 7.4 %collective-permute-done.2.refs_12_ = bf16[128,512]{1,0:T(8,128)(2,1)S(1)} collective-permute-done((bf16[128,512]{1,0:T(8,128)(2,1)}, bf16[128,512]{1,0:T(8,128)(2,1)S(1)}, u32[]{:S(2)}, u32[]{:S(2)}) %collective-permute-start.2) | collective-permute-done | bytes 131104 | tf_op jit(solution)/shard_map/ppermute | solution.py:304
  18.6 4.4 %collective-permute-start.3 = (bf16[128,512]{1,0:T(8,128)(2,1)S(1)}, bf16[128,512]{1,0:T(8,128)(2,1)S(1)}, u32[]{:S(2)}, u32[]{:S(2)}) collective-permute-start(bf16[128,512]{1,0:T(8,128)(2,1)S(1)} %collective-permute-done.2.refs_12_), channel_id=1, source_target_pairs={{0,16},{16,0},{1,17},{17,1},{2,18},{18,2},{3,19},{19,3},{4,20},{20... | collective-permute-start | bytes 393224 | tf_op jit(solution)/shard_map/ppermute | solution.py:288
  23.0 0.0 collective-permute-start.6
  23.0 0.0 collective-permute-done.refs_2_.refs_11_
  23.0 0.0 copy-start.3
  23.0 0.0 copy-start.4
  23.0 0.0 copy-start.5
  23.0 0.0 copy-start.2
  23.1 2.9 %collective-permute-done.3.refs_13_ = bf16[128,512]{1,0:T(8,128)(2,1)S(1)} collective-permute-done((bf16[128,512]{1,0:T(8,128)(2,1)S(1)}, bf16[128,512]{1,0:T(8,128)(2,1)S(1)}, u32[]{:S(2)}, u32[]{:S(2)}) %collective-permute-start.3) | collective-permute-done | bytes 131104 | tf_op jit(solution)/shard_map/ppermute | solution.py:288
  25.9 0.0 collective-permute-done.1.refs_4_
  25.9 0.0 collective-permute-start.4
  25.9 0.5 collective-permute-start.5
  26.4 0.0 copy-done.15
  26.4 0.1 copy.13.refs_0_
  26.5 1.5 %collective-permute-start.8 = (bf16[128,512]{1,0:T(8,128)(2,1)S(1)}, bf16[128,512]{1,0:T(8,128)(2,1)S(1)}, u32[]{:S(2)}, u32[]{:S(2)}) collective-permute-start(bf16[128,512]{1,0:T(8,128)(2,1)S(1)} %collective-permute-done.2.refs_12_), channel_id=1, source_target_pairs={{0,2},{2,0},{1,3},{3,1},{4,6},{6,4},{5,7},{7,5},{8,10},{10,8},{9,1... | collective-permute-start | bytes 393224 | tf_op jit(solution)/shard_map/ppermute | solution.py:288
  28.0 2.0 %collective-permute-start.9 = (bf16[128,512]{1,0:T(8,128)(2,1)S(1)}, bf16[128,512]{1,0:T(8,128)(2,1)S(1)}, u32[]{:S(2)}, u32[]{:S(2)}) collective-permute-start(bf16[128,512]{1,0:T(8,128)(2,1)S(1)} %collective-permute-done.2.refs_12_), channel_id=1, source_target_pairs={{0,18},{2,16},{16,2},{18,0},{1,19},{3,17},{17,3},{19,1},{4,22},{6,... | collective-permute-start | bytes 393224 | tf_op jit(solution)/shard_map/ppermute | solution.py:311
  30.0 0.0 collective-permute-done.6.refs_7_
  30.0 1.6 %collective-permute-start.7 = (bf16[128,512]{1,0:T(8,128)(2,1)S(1)}, bf16[128,512]{1,0:T(8,128)(2,1)S(1)}, u32[]{:S(2)}, u32[]{:S(2)}) collective-permute-start(bf16[128,512]{1,0:T(8,128)(2,1)S(1)} %slice.9), channel_id=1, source_target_pairs={{0,2},{2,0},{1,3},{3,1},{4,6},{6,4},{5,7},{7,5},{8,10},{10,8},{9,1... | collective-permute-start | bytes 393224 | tf_op jit(solution)/shard_map/ppermute | solution.py:288
  31.6 0.0 collective-permute-done.4.refs_3_
  31.6 0.0 collective-permute-done.5.refs_5_
  31.6 0.0 copy-done.3
  31.6 0.0 copy-done.4
  31.6 0.0 copy-done.5
  31.6 0.0 copy-done.2
  31.6 0.0 copy-start.6
  31.6 1.0 %copy-done.6 = bf16[512,512]{1,0:T(8,128)(2,1)S(1)} copy-done((bf16[512,512]{1,0:T(8,128)(2,1)S(1)}, bf16[512,512]{1,0:T(8,128)(2,1)}, u32[]{:S(2)}) %copy-start.6) | copy-done | bytes 524312
  32.7 6.9 %shard_map.122 = (bf16[512,128]{1,0:T(8,128)(2,1)S(1)}, bf16[512,128]{1,0:T(8,128)(2,1)S(1)}, f32[48,512]{1,0:T(8,128)S(1)}, f32[48,128]{1,0:T(8,128)S(1)}) custom-call(s32[16,6]{1,0:T(8,128)S(1)} %copy.13.refs_0_, bf16[512,512]{1,0:T(8,128)(2,1)S(1)} %copy-done.6, bf16[384,512]{1,0:T(8,128)(2,1)S(1)} %collective-permute-done.refs_2_.refs_11_, ...), custom_call_target="tpu_custom_call" | custom-call | flops 4000000000 | bytes 1048576 | tf_op jit(solution)/shard_map/pallas_call | solution.py:275
  39.6 0.0 copy-start.8
  39.6 0.0 copy-start.9
  39.6 0.0 collective-permute-done.8.refs_12_
  39.6 0.0 collective-permute-done.9.refs_13_
  39.6 0.0 collective-permute-done.7.refs_11_
  39.6 0.0 copy-done.7
  39.6 6.9 %shard_map.123 = (bf16[512,128]{1,0:T(8,128)(2,1)S(1)}, bf16[512,128]{1,0:T(8,128)(2,1)S(1)}, bf16[48,512]{1,0:T(8,128)(2,1)S(1)}, bf16[48,256]{1,0:T(8,128)(2,1)S(1)}) custom-call(s32[16,6]{1,0:T(8,128)S(1)} %copy.13.refs_0_, bf16[512,512]{1,0:T(8,128)(2,1)S(1)} %copy-done.6, bf16[384,512]{1,0:T(8,128)(2,1)S(1)} %collective-permute-done.refs_2_.refs_11_, ...), custom_call_target="tpu_custom_call" | custom-call | flops 4000000000 | bytes 1048576 | tf_op jit(solution)/shard_map/pallas_call | solution.py:275
  46.6 0.0 copy-done.8
  46.6 0.0 copy-done.9
  46.6 0.0 copy-start.1
  46.6 0.6 copy-done.1
  47.2 0.0 collective-permute-start.11
  47.2 1.2 %collective-permute-done.11.sibling_ref = bf16[48,512]{1,0:T(8,128)(2,1)S(1)} collective-permute-done((bf16[48,512]{1,0:T(8,128)(2,1)S(1)}, bf16[48,512]{1,0:T(8,128)(2,1)S(1)}, u32[]{:S(2)}, u32[]{:S(2)}) %collective-permute-start.11) | collective-permute-done | bytes 49184 | tf_op jit(solution)/shard_map/ppermute | solution.py:288
  48.4 0.0 copy-done
  48.4 0.6 copy-done.14
  49.1 1.5 %shard_map.125 = bf16[48,768]{1,0:T(8,128)(2,1)} custom-call(bf16[48,512]{1,0:T(8,128)(2,1)} %copy-done, bf16[48,512]{1,0:T(8,128)(2,1)} %copy-done.14, bf16[48,256]{1,0:T(8,128)(2,1)} %copy-done.1), custom_call_target="tpu_custom_call" | custom-call | bytes 1048576 | tf_op jit(solution)/shard_map/pallas_call | solution.py:275
  50.5 0.5 collective-permute-start.12
  51.1 4.0 %collective-permute-done.12 = bf16[48,768]{1,0:T(8,128)(2,1)S(1)} collective-permute-done((bf16[48,768]{1,0:T(8,128)(2,1)}, bf16[48,768]{1,0:T(8,128)(2,1)S(1)}, u32[]{:S(2)}, u32[]{:S(2)}) %collective-permute-start.12) | collective-permute-done | bytes 73760 | tf_op jit(solution)/shard_map/ppermute | solution.py:288
  55.1 0.9 %add_convert_fusion.2 = bf16[48,768]{1,0:T(8,128)(2,1)S(1)} fusion(bf16[48,768]{1,0:T(8,128)(2,1)S(1)} %collective-permute-done.12, bf16[48,768]{1,0:T(8,128)(2,1)} %shard_map.125), kind=kLoop, calls=%fused_computation.3 | loop fusion | flops 147456 | bytes 221184 | tf_op jit(solution)/shard_map/convert_element_type | solution.py:436
  56.0 0.0 copy-done.10
  56.0 0.0 copy-done.11
  56.0 0.1 collective-permute-start.13
  56.1 3.0 %shard_map.124 = (f32[512,256]{1,0:T(8,128)}, bf16[512,256]{1,0:T(8,128)(2,1)}) custom-call(s32[1,512]{1,0:T(1,128)} %bitcast.23, bf16[512,512]{1,0:T(8,128)(2,1)} %bitcast.18, bf16[512,128]{1,0:T(8,128)(2,1)} %copy-done.8, bf16[512,128]{1,0:T(8,128)(2,1)} %copy-done.10, bf16[512,128]{1,0:T(8,128)(2,1)} %copy-done.9, bf16[512,128]{1,0:T(8,128)(2,1)} %copy-done.11), custom_call_target="tpu_custom_call" | custom-call | flops 1000000000 | bytes 1048576 | tf_op jit(solution)/shard_map/pallas_call | solution.py:275
  59.1 0.0 collective-permute-start.10
  59.1 1.3 %collective-permute-done.13 = bf16[48,768]{1,0:T(8,128)(2,1)S(1)} collective-permute-done((bf16[48,768]{1,0:T(8,128)(2,1)S(1)}, bf16[48,768]{1,0:T(8,128)(2,1)S(1)}, u32[]{:S(2)}, u32[]{:S(2)}) %collective-permute-start.13) | collective-permute-done | bytes 73760 | tf_op jit(solution)/shard_map/ppermute | solution.py:288
  60.5 0.0 copy-start.12
  60.5 0.7 %collective-permute-start.14 = (bf16[48,768]{1,0:T(8,128)(2,1)S(1)}, bf16[48,768]{1,0:T(8,128)(2,1)S(1)}, u32[]{:S(2)}, u32[]{:S(2)}) collective-permute-start(bf16[48,768]{1,0:T(8,128)(2,1)S(1)} %add_convert_fusion.1.own_ref), channel_id=1, source_target_pairs={{0,8},{4,12},{8,0},{12,4},{1,9},{5,13},{9,1},{13,5},{2,10},{6,14},... | collective-permute-start | bytes 221192 | tf_op jit(solution)/shard_map/ppermute | solution.py:288
  61.2 0.0 collective-permute-done.10
  61.2 1.8 %fusion = bf16[1,512,256]{2,1,0:T(8,128)(2,1)} fusion(f32[512,256]{1,0:T(8,128)} %get-tuple-element.37, bf16[512,256]{1,0:T(8,128)(2,1)S(1)} %collective-permute-done.10), kind=kLoop, calls=%fused_computation.1 | loop fusion | flops 393216 | bytes 1048576 | tf_op jit(solution)/shard_map/broadcast_in_dim | solution.py:431
  63.0 0.0 copy-done.12
  63.0 4.0 %collective-permute-done.14.recv_ref = bf16[48,768]{1,0:T(8,128)(2,1)S(1)} collective-permute-done((bf16[48,768]{1,0:T(8,128)(2,1)S(1)}, bf16[48,768]{1,0:T(8,128)(2,1)S(1)}, u32[]{:S(2)}, u32[]{:S(2)}) %collective-permute-start.14) | collective-permute-done | bytes 73760 | tf_op jit(solution)/shard_map/ppermute | solution.py:288
  67.0 0.6 copy-done.13
  67.6 1.6 %shard_map.126 = (f32[48,512]{1,0:T(8,128)}, f32[48,256]{1,0:T(8,128)}) custom-call(bf16[48,768]{1,0:T(8,128)(2,1)} %copy-done.12, bf16[48,768]{1,0:T(8,128)(2,1)} %copy-done.13), custom_call_target="tpu_custom_call" | custom-call | bytes 1048576 | tf_op jit(solution)/shard_map/pallas_call | solution.py:275
  (10 shorter events, 0.1 us)
Async XLA Ops:
  3.9 19.1 %collective-permute-start = (bf16[384,512]{1,0:T(8,128)(2,1)}, bf16[384,512]{1,0:T(8,128)(2,1)S(1)}, u32[]{:S(2)}, u32[]{:S(2)}) collective-permute-start(bf16[384,512]{1,0:T(8,128)(2,1)} %get-tuple-element.24), channel_id=1, source_target_pairs={{0,4},{4,0},{8,12},{12,8},{1,5},{5,1},{9,13},{13,9},{2,6},{6,2},{1... | collective-permute-start | bytes 1179656 | tf_op jit(solution)/shard_map/ppermute | solution.py:288
  7.0 11.5 %collective-permute-start.2 = (bf16[128,512]{1,0:T(8,128)(2,1)}, bf16[128,512]{1,0:T(8,128)(2,1)S(1)}, u32[]{:S(2)}, u32[]{:S(2)}) collective-permute-start(bf16[128,512]{1,0:T(8,128)(2,1)} %get-tuple-element.26.refs_10_), channel_id=1, source_target_pairs={{0,8},{4,12},{8,0},{12,4},{16,28},{20,24},{24,20},{28,16},{1,9},{5... | collective-permute-start | bytes 393224 | tf_op jit(solution)/shard_map/ppermute | solution.py:304
  9.6 16.3 %collective-permute-start.1 = (bf16[256,512]{1,0:T(8,128)(2,1)}, bf16[256,512]{1,0:T(8,128)(2,1)S(1)}, u32[]{:S(2)}, u32[]{:S(2)}) collective-permute-start(bf16[256,512]{1,0:T(8,128)(2,1)} %get-tuple-element.25), channel_id=1, source_target_pairs={{0,0},{4,8},{8,4},{12,12},{1,1},{5,9},{9,5},{13,13},{2,2},{6,10},{... | collective-permute-start | bytes 786440 | tf_op jit(solution)/shard_map/ppermute | solution.py:372
  18.6 7.4 %collective-permute-start.3 = (bf16[128,512]{1,0:T(8,128)(2,1)S(1)}, bf16[128,512]{1,0:T(8,128)(2,1)S(1)}, u32[]{:S(2)}, u32[]{:S(2)}) collective-permute-start(bf16[128,512]{1,0:T(8,128)(2,1)S(1)} %collective-permute-done.2.refs_12_), channel_id=1, source_target_pairs={{0,16},{16,0},{1,17},{17,1},{2,18},{18,2},{3,19},{19,3},{4,20},{20... | collective-permute-start | bytes 393224 | tf_op jit(solution)/shard_map/ppermute | solution.py:288
  23.0 3.5 %copy-start.15 = (s32[16,6]{0,1:T(8,128)S(1)}, s32[16,6]{0,1:T(8,128)}, u32[]{:S(2)}) copy-start(s32[16,6]{0,1:T(8,128)} %param.18) | copy-start | bytes 1156
  23.0 7.0 %collective-permute-start.6 = (bf16[512,256]{1,0:T(8,128)(2,1)}, bf16[512,256]{1,0:T(8,128)(2,1)S(1)}, u32[]{:S(2)}, u32[]{:S(2)}) collective-permute-start(bf16[512,256]{1,0:T(8,128)(2,1)} %get-tuple-element.29.refs_6_), channel_id=1, source_target_pairs={{0,1},{1,0},{2,3},{3,2},{4,5},{5,4},{6,7},{7,6},{8,9},{9,8},{10,11... | collective-permute-start | bytes 786440 | tf_op jit(solution)/shard_map/ppermute | solution.py:288
  23.0 8.6 %copy-start.3 = (bf16[128,512]{1,0:T(8,128)(2,1)S(1)}, bf16[128,512]{1,0:T(8,128)(2,1)}, u32[]{:S(2)}) copy-start(bf16[128,512]{1,0:T(8,128)(2,1)} %get-tuple-element.26.refs_10_) | copy-start | bytes 393220
  23.0 8.6 %copy-start.4 = (bf16[3,512,16]{1,2,0:T(8,128)(2,1)S(1)}, bf16[3,512,16]{1,2,0:T(8,128)(2,1)}, u32[]{:S(2)}) copy-start(bf16[3,512,16]{1,2,0:T(8,128)(2,1)} %param.16) | copy-start | bytes 147460
  23.0 8.6 %copy-start.5 = (bf16[3,16,256]{2,1,0:T(8,128)(2,1)S(1)}, bf16[3,16,256]{2,1,0:T(8,128)(2,1)}, u32[]{:S(2)}) copy-start(bf16[3,16,256]{2,1,0:T(8,128)(2,1)} %param.17) | copy-start | bytes 73732
  23.0 8.6 %copy-start.2 = (bf16[512,256]{1,0:T(8,128)(2,1)S(1)}, bf16[512,256]{1,0:T(8,128)(2,1)}, u32[]{:S(2)}) copy-start(bf16[512,256]{1,0:T(8,128)(2,1)} %get-tuple-element.29.refs_6_) | copy-start | bytes 786436
  25.9 5.7 %collective-permute-start.4 = (bf16[256,512]{1,0:T(8,128)(2,1)S(1)}, bf16[256,512]{1,0:T(8,128)(2,1)S(1)}, u32[]{:S(2)}, u32[]{:S(2)}) collective-permute-start(bf16[256,512]{1,0:T(8,128)(2,1)S(1)} %slice.8), channel_id=1, source_target_pairs={{0,1},{1,0},{2,3},{3,2},{4,5},{5,4},{6,7},{7,6},{8,9},{9,8},{10,11... | collective-permute-start | bytes 786440 | tf_op jit(solution)/shard_map/ppermute | solution.py:288
  25.9 5.7 %collective-permute-start.5 = (bf16[256,512]{1,0:T(8,128)(2,1)S(1)}, bf16[256,512]{1,0:T(8,128)(2,1)S(1)}, u32[]{:S(2)}, u32[]{:S(2)}) collective-permute-start(bf16[256,512]{1,0:T(8,128)(2,1)S(1)} %collective-permute-done.1.refs_4_), channel_id=1, source_target_pairs={{0,1},{1,0},{2,3},{3,2},{4,5},{5,4},{6,7},{7,6},{8,9},{9,8},{10,11... | collective-permute-start | bytes 786440 | tf_op jit(solution)/shard_map/ppermute | solution.py:288
  26.5 13.1 %collective-permute-start.8 = (bf16[128,512]{1,0:T(8,128)(2,1)S(1)}, bf16[128,512]{1,0:T(8,128)(2,1)S(1)}, u32[]{:S(2)}, u32[]{:S(2)}) collective-permute-start(bf16[128,512]{1,0:T(8,128)(2,1)S(1)} %collective-permute-done.2.refs_12_), channel_id=1, source_target_pairs={{0,2},{2,0},{1,3},{3,1},{4,6},{6,4},{5,7},{7,5},{8,10},{10,8},{9,1... | collective-permute-start | bytes 393224 | tf_op jit(solution)/shard_map/ppermute | solution.py:288
  28.0 11.6 %collective-permute-start.9 = (bf16[128,512]{1,0:T(8,128)(2,1)S(1)}, bf16[128,512]{1,0:T(8,128)(2,1)S(1)}, u32[]{:S(2)}, u32[]{:S(2)}) collective-permute-start(bf16[128,512]{1,0:T(8,128)(2,1)S(1)} %collective-permute-done.2.refs_12_), channel_id=1, source_target_pairs={{0,18},{2,16},{16,2},{18,0},{1,19},{3,17},{17,3},{19,1},{4,22},{6,... | collective-permute-start | bytes 393224 | tf_op jit(solution)/shard_map/ppermute | solution.py:311
  30.0 9.6 %collective-permute-start.7 = (bf16[128,512]{1,0:T(8,128)(2,1)S(1)}, bf16[128,512]{1,0:T(8,128)(2,1)S(1)}, u32[]{:S(2)}, u32[]{:S(2)}) collective-permute-start(bf16[128,512]{1,0:T(8,128)(2,1)S(1)} %slice.9), channel_id=1, source_target_pairs={{0,2},{2,0},{1,3},{3,1},{4,6},{6,4},{5,7},{7,5},{8,10},{10,8},{9,1... | collective-permute-start | bytes 393224 | tf_op jit(solution)/shard_map/ppermute | solution.py:288
  31.6 1.0 %copy-start.6 = (bf16[512,512]{1,0:T(8,128)(2,1)S(1)}, bf16[512,512]{1,0:T(8,128)(2,1)}, u32[]{:S(2)}) copy-start(bf16[512,512]{1,0:T(8,128)(2,1)} %get-tuple-element.23.refs_1_) | copy-start | bytes 1572868
  32.7 7.0 %copy-start.7 = (bf16[128,512]{1,0:T(8,128)(2,1)S(1)}, bf16[128,512]{1,0:T(8,128)(2,1)}, u32[]{:S(2)}) copy-start(bf16[128,512]{1,0:T(8,128)(2,1)} %get-tuple-element.31.refs_10_) | copy-start | bytes 393220
  39.6 7.0 %copy-start.8 = (bf16[512,128]{1,0:T(8,128)(2,1)}, bf16[512,128]{1,0:T(8,128)(2,1)S(1)}, u32[]{:S(2)}) copy-start(bf16[512,128]{1,0:T(8,128)(2,1)S(1)} %get-tuple-element.30.att1_ref) | copy-start | bytes 393220
  39.6 7.0 %copy-start.9 = (bf16[512,128]{1,0:T(8,128)(2,1)}, bf16[512,128]{1,0:T(8,128)(2,1)S(1)}, u32[]{:S(2)}) copy-start(bf16[512,128]{1,0:T(8,128)(2,1)S(1)} %get-tuple-element.35.wo1_ref) | copy-start | bytes 393220
  46.6 0.6 copy-start.1
  47.2 1.2 %copy-start = (bf16[48,512]{1,0:T(8,128)(2,1)}, bf16[48,512]{1,0:T(8,128)(2,1)S(1)}, u32[]{:S(2)}) copy-start(bf16[48,512]{1,0:T(8,128)(2,1)S(1)} %get-tuple-element.39.down_ref) | copy-start | bytes 147460
  47.2 8.8 %copy-start.10 = (bf16[512,128]{1,0:T(8,128)(2,1)}, bf16[512,128]{1,0:T(8,128)(2,1)S(1)}, u32[]{:S(2)}) copy-start(bf16[512,128]{1,0:T(8,128)(2,1)S(1)} %get-tuple-element.34.att2_ref) | copy-start | bytes 393220
  47.2 8.8 %copy-start.11 = (bf16[512,128]{1,0:T(8,128)(2,1)}, bf16[512,128]{1,0:T(8,128)(2,1)S(1)}, u32[]{:S(2)}) copy-start(bf16[512,128]{1,0:T(8,128)(2,1)S(1)} %get-tuple-element.36.wo2_ref) | copy-start | bytes 393220
  47.2 1.2 %collective-permute-start.11 = (bf16[48,512]{1,0:T(8,128)(2,1)S(1)}, bf16[48,512]{1,0:T(8,128)(2,1)S(1)}, u32[]{:S(2)}, u32[]{:S(2)}) collective-permute-start(bf16[48,512]{1,0:T(8,128)(2,1)S(1)} %get-tuple-element.39.down_ref), channel_id=1, source_target_pairs={{0,1},{1,0},{2,3},{3,2},{4,5},{5,4},{6,7},{7,6},{8,9},{9,8},{10,11... | collective-permute-start | bytes 147464 | tf_op jit(solution)/shard_map/ppermute | solution.py:288
  48.4 0.6 copy-start.14
  50.5 4.6 %collective-permute-start.12 = (bf16[48,768]{1,0:T(8,128)(2,1)}, bf16[48,768]{1,0:T(8,128)(2,1)S(1)}, u32[]{:S(2)}, u32[]{:S(2)}) collective-permute-start(bf16[48,768]{1,0:T(8,128)(2,1)} %shard_map.125), channel_id=1, source_target_pairs={{0,2},{2,0},{1,3},{3,1},{4,6},{6,4},{5,7},{7,5},{8,10},{10,8},{9,1... | collective-permute-start | bytes 221192 | tf_op jit(solution)/shard_map/ppermute | solution.py:288
  56.0 4.4 %collective-permute-start.13 = (bf16[48,768]{1,0:T(8,128)(2,1)S(1)}, bf16[48,768]{1,0:T(8,128)(2,1)S(1)}, u32[]{:S(2)}, u32[]{:S(2)}) collective-permute-start(bf16[48,768]{1,0:T(8,128)(2,1)S(1)} %add_convert_fusion.2), channel_id=1, source_target_pairs={{0,4},{4,0},{8,12},{12,8},{1,5},{5,1},{9,13},{13,9},{2,6},{6,2},{1... | collective-permute-start | bytes 221192 | tf_op jit(solution)/shard_map/ppermute | solution.py:288
  59.1 2.1 %collective-permute-start.10 = (bf16[512,256]{1,0:T(8,128)(2,1)}, bf16[512,256]{1,0:T(8,128)(2,1)S(1)}, u32[]{:S(2)}, u32[]{:S(2)}) collective-permute-start(bf16[512,256]{1,0:T(8,128)(2,1)} %get-tuple-element.38), channel_id=1, source_target_pairs={{0,1},{1,0},{2,3},{3,2},{4,5},{5,4},{6,7},{7,6},{8,9},{9,8},{10,11... | collective-permute-start | bytes 786440 | tf_op jit(solution)/shard_map/ppermute | solution.py:288
  60.5 2.5 %copy-start.12 = (bf16[48,768]{1,0:T(8,128)(2,1)}, bf16[48,768]{1,0:T(8,128)(2,1)S(1)}, u32[]{:S(2)}) copy-start(bf16[48,768]{1,0:T(8,128)(2,1)S(1)} %add_convert_fusion.1.own_ref) | copy-start | bytes 221188
  60.5 6.5 %collective-permute-start.14 = (bf16[48,768]{1,0:T(8,128)(2,1)S(1)}, bf16[48,768]{1,0:T(8,128)(2,1)S(1)}, u32[]{:S(2)}, u32[]{:S(2)}) collective-permute-start(bf16[48,768]{1,0:T(8,128)(2,1)S(1)} %add_convert_fusion.1.own_ref), channel_id=1, source_target_pairs={{0,8},{4,12},{8,0},{12,4},{1,9},{5,13},{9,1},{13,5},{2,10},{6,14},... | collective-permute-start | bytes 221192 | tf_op jit(solution)/shard_map/ppermute | solution.py:288
  67.0 0.6 copy-start.13

commit v5 on v4

--- a/solution.py
+++ b/solution.py
@@ -57,10 +57,10 @@
 
 
 def prep_kernel(split, *refs):
-    sources, outs, buffers, sems = refs[:7], refs[7:-8], refs[-8:-1], refs[-1]
-    copies = load_all(sources, buffers, sems)
-    order_ref, x_ref, wq_ref, wk_ref, wv_ref, wo_ref, cot_ref = buffers
-    normed_ref, half_ref, near_ref, cot_out_ref = outs[:4]
+    sources, outs, buffers, sems = refs[:9], refs[9:-7], refs[-7:-1], refs[-1]
+    order_ref, down_ref, up_ref, x_own_ref, normed_ref, half_ref, near_ref, cot_out_ref = outs[:8]
+    copies = load_all(sources, (order_ref,) + tuple(buffers) + (down_ref, up_ref), sems)
+    x_ref, wq_ref, wk_ref, wv_ref, wo_ref, cot_ref = buffers
     rows = x_ref.shape[0]
     copies[0].wait()
     place = scatter_matrix(order_ref, rows)
@@ -71,17 +71,19 @@
     normed_ref[...] = (center * lax.rsqrt(spread + 1e-05)).astype(BF16)
     for copy in copies[2:]:
         copy.wait()
-    for which, out in enumerate(outs[4:]):
+    for which, out in enumerate(outs[8:]):
         lanes = lanes_at(head_at(split, which))
         for j, member in enumerate((wq_ref, wk_ref, wv_ref)):
             out[:, j * DH : (j + 1) * DH] = member[:, lanes]
         out[:, 3 * DH :] = wo_ref[lanes, :].T
     cot_out_ref[...] = tn(place, cot_ref[...]).astype(BF16)
+    cols = x_own_ref.shape[1]
+    x_own_ref[...] = x_ref[:, pl.ds(pl.multiple_of(lax.axis_index("head") * cols, cols), cols)]
     start = pl.multiple_of(lax.axis_index("head") * (rows // 2), rows // 2)
     half_ref[...] = normed_ref[pl.ds(start, rows // 2), :]
     skip = near_ref.shape[0] - rows // 2
     if skip:
-        near_ref[:skip, :] = outs[4][...]
+        near_ref[:skip, :] = outs[8][...]
     near_ref[skip:, :] = half_ref[...]
 
 
@@ -247,8 +249,7 @@
 
 
 def out_kernel(order_ref, x_ref, att1_ref, att2_ref, wo1_ref, wo2_ref, base_ref, other_ref):
-    rows, width = x_ref.shape
-    cols = width // 2
+    rows, cols = x_ref.shape
     core = lax.axis_index("head")
     place = scatter_matrix(order_ref, rows)
 
@@ -258,8 +259,7 @@
         return nn(place, terms.astype(BF16))
 
     other_ref[...] = part(1 - core).astype(BF16)
-    own = pl.ds(pl.multiple_of(core * cols, cols), cols)
-    base_ref[...] = x_ref[:, own].astype(F32) + part(core)
+    base_ref[...] = x_ref[...].astype(F32) + part(core)
 
 
 HBM = pl.BlockSpec(memory_space=pltpu.HBM)
@@ -341,12 +341,14 @@
     order = block_node_order.reshape(1, rows)
     split = split_weights()
 
-    down = adapter_down_weight.transpose(0, 2, 1).reshape(3 * RANK, width)
-    up = adapter_up_weight.reshape(3 * RANK, cols)
     skip = depth if split else 0
-    normed, half, near, cot_own, *packed = call(
+    order, down, up, x_own, normed, half, near, cot_own, *packed = call(
         functools.partial(prep_kernel, split),
         (
+            shape((1, rows), jnp.int32),
+            shape((3 * RANK, width)),
+            shape((3 * RANK, cols)),
+            shape((rows, cols)),
             shape((rows, width)),
             shape((rows // 2, width)),
             shape((skip + rows // 2, width)),
@@ -354,18 +356,27 @@
             shape((depth, 4 * DH)),
             shape((depth, 4 * DH)),
         ),
-        (order, state, query_weight, key_weight, value_weight, output_weight, cotangent[0]),
+        (
+            order,
+            state,
+            query_weight,
+            key_weight,
+            value_weight,
+            output_weight,
+            cotangent[0],
+            adapter_down_weight.transpose(0, 2, 1).reshape(3 * RANK, width),
+            adapter_up_weight.reshape(3 * RANK, cols),
+        ),
         [
-            pltpu.VMEM((1, rows), jnp.int32),
             pltpu.VMEM((rows, width), BF16),
             pltpu.VMEM((depth, cols), BF16),
             pltpu.VMEM((depth, cols), BF16),
             pltpu.VMEM((depth, cols), BF16),
             pltpu.VMEM((cols, depth), BF16),
             pltpu.VMEM((rows, cols), BF16),
-            pltpu.SemaphoreType.DMA((7,)),
+            pltpu.SemaphoreType.DMA((9,)),
         ],
-        hbm=7,
+        hbm=9,
         flops=2 * rows * rows * (width + cols),
     )
     a_own = swap(near, "node", 1)
@@ -409,7 +420,6 @@
         scratch,
         smem=1,
         limit=32,
-        flops=4 * 10**9,
     )
     att2, wo2, down2, up2 = call(
         functools.partial(head_kernel, split, 1, piece_rows),
@@ -424,10 +434,11 @@
     base, other = call(
         out_kernel,
         (shape((rows, cols), F32), shape((rows, cols))),
-        (order, state, att1, att2, wo1, wo2),
+        (order, x_own, att1, att2, wo1, wo2),
         flops=10**9,
-    )
-    lora = call(merge_kernel, (shape((3 * RANK, width + cols)),), (down2, down_sib, up2))[0]
+        limit=16,
+    )
+    lora = call(merge_kernel, (shape((3 * RANK, width + cols)),), (down2, down_sib, up2), limit=16)[0]
     mesh_out = (base + swap(other, "head").astype(F32)).astype(BF16)[None]
 
     hops = [("sample", 1 << i) for i in range(lax.axis_size("sample").bit_length() - 1)]
@@ -438,6 +449,7 @@
         final_kernel,
         (shape((3 * RANK, width), F32), shape((3 * RANK, cols), F32)),
         (lora, swap(lora, *hops[-1])),
+        limit=16,
     )
     down_total = down_total.reshape(3, RANK, width).transpose(0, 2, 1)
     up_total = up_total.reshape(3, RANK, cols)

time: 69.7 us -> 64.2 us (0.921)
  Pallas kernels: 23.2 us -> 19.1 us
  other arithmetic: 2.73 us -> 0.8 us
  waiting for transfers between devices: 20.9 us -> 22.6 us
    pallas_call x6, Pallas kernels: 23.2 us -> 19.1 us  [call(): pl.pallas_call(kernel, out_shape=outs, in_specs=[SMEM] * smem + [HBM] * h...]
    ppermute x12, waiting for transfers between devices: 13.5 us -> 15.2 us  [swap(): return lax.ppermute(value, axis, [(i, i ^ step) for i in range(size)])]
    broadcast_in_dim x1, other arithmetic: 1.8 us -> 0.76 us  [shards(): mesh_out = (base + swap(other, 'head').astype(F32)).astype(BF16)[None]]
    convert_element_type x2, other arithmetic: 0.93 us -> 0.04 us  [shards(): lora = (lora.astype(F32) + swap(lora, axis, step).astype(F32)).astype(BF16)]
    unnamed x33 -> x19, local copies, waits for them, and re-layouts: 2.99 us -> 2.45 us
  transfers between devices with their start and end apart: 15 -> 15, of which waited for: 6 -> 6; matrix products, arithmetic and copies ran while one was open for 3% -> 1% of each run, Pallas kernels for 14% -> 12%
where the time goes in v5:
time: 64.2 us; the launch traced here: 63.9 us
  waiting for transfers between devices  22.6 us (35%)
  Pallas kernels  19.1 us (30%)
  starting transfers between devices  18.1 us (28%)
  local copies, waits for them, and re-layouts  2.48 us (4%)
  between operations  0.87 us (1%)
  other arithmetic  0.8 us (1%)
    pallas_call x6, Pallas kernels, call(): pl.pallas_call(kernel, out_shape=outs, in_specs=[SMEM] * smem + [HBM] * h...  19.1 us
    ppermute x12, waiting for transfers between devices, swap(): return lax.ppermute(value, axis, [(i, i ^ step) for i in range(size)])  15.2 us
    ppermute x12, starting transfers between devices, swap(): return lax.ppermute(value, axis, [(i, i ^ step) for i in range(size)])  11.9 us
    ppermute x1, waiting for transfers between devices, gather_weights(): far = lax.ppermute(first, ('group', 'node'), far_pairs)  7.36 us
    ppermute x1, starting transfers between devices, gather_weights(): far = lax.ppermute(first, ('group', 'node'), far_pairs)  2.59 us
    unnamed x19, local copies, waits for them, and re-layouts  2.45 us
    ppermute x1, starting transfers between devices, gather_weights(): lax.ppermute(far, ('group', 'sample'), diagonal)  1.99 us
    ppermute x1, starting transfers between devices, shards(): b_own = lax.ppermute(half, 'node', chain_pairs(lax.axis_size('node')))  1.6 us
  transfers between devices with their start and end apart: 15, of which 6 were waited for; matrix products, arithmetic and copies ran while one was open for 1% of the time, Pallas kernels for 12%

profile of v5, /device:TPU:0, one launch (start us, length us, event | category | flops | bytes accessed | tf_op | source)
XLA Modules:
  0.0 63.9 jit_solution(13416126498189682023)
XLA Ops:
  0.6 0.0 copy-start.8
  0.6 3.6 %shard_map.121 = (s32[1,512]{1,0:T(1,128)}, bf16[48,512]{1,0:T(8,128)(2,1)}, bf16[48,256]{1,0:T(8,128)(2,1)}, bf16[512,256]{1,0:T(8,128)(2,1)}, bf16[512,512]{1,...) custom-call(s32[1,512]{1,0:T(1,128)} %bitcast.19, ...), custom_call_target="tpu_custom_call" | custom-call | flops 402653184 | bytes 1048576 | tf_op jit(solution)/shard_map/pallas_call | solution.py:275
  4.2 0.0 copy-start
  4.2 3.1 %collective-permute-start = (bf16[384,512]{1,0:T(8,128)(2,1)}, bf16[384,512]{1,0:T(8,128)(2,1)S(1)}, u32[]{:S(2)}, u32[]{:S(2)}) collective-permute-start(bf16[384,512]{1,0:T(8,128)(2,1)} %get-tuple-element.30), channel_id=1, source_target_pairs={{0,4},{4,0},{8,12},{12,8},{1,5},{5,1},{9,13},{13,9},{2,6},{6,2},{1... | collective-permute-start | bytes 1179656 | tf_op jit(solution)/shard_map/ppermute | solution.py:288
  7.3 2.6 %collective-permute-start.2 = (bf16[128,512]{1,0:T(8,128)(2,1)}, bf16[128,512]{1,0:T(8,128)(2,1)S(1)}, u32[]{:S(2)}, u32[]{:S(2)}) collective-permute-start(bf16[128,512]{1,0:T(8,128)(2,1)} %get-tuple-element.32.refs_10_), channel_id=1, source_target_pairs={{0,8},{4,12},{8,0},{12,4},{16,28},{20,24},{24,20},{28,16},{1,9},{5... | collective-permute-start | bytes 393224 | tf_op jit(solution)/shard_map/ppermute | solution.py:304
  9.9 1.6 %collective-permute-start.1 = (bf16[256,512]{1,0:T(8,128)(2,1)}, bf16[256,512]{1,0:T(8,128)(2,1)S(1)}, u32[]{:S(2)}, u32[]{:S(2)}) collective-permute-start(bf16[256,512]{1,0:T(8,128)(2,1)} %get-tuple-element.31), channel_id=1, source_target_pairs={{0,0},{4,8},{8,4},{12,12},{1,1},{5,9},{9,5},{13,13},{2,2},{6,10},{... | collective-permute-start | bytes 786440 | tf_op jit(solution)/shard_map/ppermute | solution.py:383
  11.5 7.4 %collective-permute-done.2.refs_12_ = bf16[128,512]{1,0:T(8,128)(2,1)S(1)} collective-permute-done((bf16[128,512]{1,0:T(8,128)(2,1)}, bf16[128,512]{1,0:T(8,128)(2,1)S(1)}, u32[]{:S(2)}, u32[]{:S(2)}) %collective-permute-start.2) | collective-permute-done | bytes 131104 | tf_op jit(solution)/shard_map/ppermute | solution.py:304
  18.9 4.4 %collective-permute-start.3 = (bf16[128,512]{1,0:T(8,128)(2,1)S(1)}, bf16[128,512]{1,0:T(8,128)(2,1)S(1)}, u32[]{:S(2)}, u32[]{:S(2)}) collective-permute-start(bf16[128,512]{1,0:T(8,128)(2,1)S(1)} %collective-permute-done.2.refs_12_), channel_id=1, source_target_pairs={{0,16},{16,0},{1,17},{17,1},{2,18},{18,2},{3,19},{19,3},{4,20},{20... | collective-permute-start | bytes 393224 | tf_op jit(solution)/shard_map/ppermute | solution.py:288
  23.3 0.0 collective-permute-start.6
  23.3 0.0 collective-permute-done.refs_2_.refs_11_
  23.3 0.0 copy-start.4
  23.3 0.0 copy-start.1
  23.3 0.0 collective-permute-done.1.refs_4_
  23.3 2.9 %collective-permute-done.3.refs_13_ = bf16[128,512]{1,0:T(8,128)(2,1)S(1)} collective-permute-done((bf16[128,512]{1,0:T(8,128)(2,1)S(1)}, bf16[128,512]{1,0:T(8,128)(2,1)S(1)}, u32[]{:S(2)}, u32[]{:S(2)}) %collective-permute-start.3) | collective-permute-done | bytes 131104 | tf_op jit(solution)/shard_map/ppermute | solution.py:288
  26.2 0.0 collective-permute-start.4
  26.2 0.5 collective-permute-start.5
  26.7 1.5 %collective-permute-start.8 = (bf16[128,512]{1,0:T(8,128)(2,1)S(1)}, bf16[128,512]{1,0:T(8,128)(2,1)S(1)}, u32[]{:S(2)}, u32[]{:S(2)}) collective-permute-start(bf16[128,512]{1,0:T(8,128)(2,1)S(1)} %collective-permute-done.2.refs_12_), channel_id=1, source_target_pairs={{0,2},{2,0},{1,3},{3,1},{4,6},{6,4},{5,7},{7,5},{8,10},{10,8},{9,1... | collective-permute-start | bytes 393224 | tf_op jit(solution)/shard_map/ppermute | solution.py:288
  28.2 2.0 %collective-permute-start.9 = (bf16[128,512]{1,0:T(8,128)(2,1)S(1)}, bf16[128,512]{1,0:T(8,128)(2,1)S(1)}, u32[]{:S(2)}, u32[]{:S(2)}) collective-permute-start(bf16[128,512]{1,0:T(8,128)(2,1)S(1)} %collective-permute-done.2.refs_12_), channel_id=1, source_target_pairs={{0,18},{2,16},{16,2},{18,0},{1,19},{3,17},{17,3},{19,1},{4,22},{6,... | collective-permute-start | bytes 393224 | tf_op jit(solution)/shard_map/ppermute | solution.py:311
  30.2 0.0 collective-permute-done.6.refs_7_
  30.2 1.6 %collective-permute-start.7 = (bf16[128,512]{1,0:T(8,128)(2,1)S(1)}, bf16[128,512]{1,0:T(8,128)(2,1)S(1)}, u32[]{:S(2)}, u32[]{:S(2)}) collective-permute-start(bf16[128,512]{1,0:T(8,128)(2,1)S(1)} %slice.9), channel_id=1, source_target_pairs={{0,2},{2,0},{1,3},{3,1},{4,6},{6,4},{5,7},{7,5},{8,10},{10,8},{9,1... | collective-permute-start | bytes 393224 | tf_op jit(solution)/shard_map/ppermute | solution.py:288
  31.8 0.0 copy-done.8
  31.8 0.1 copy.13.refs_0_
  31.9 0.0 collective-permute-done.4.refs_3_
  31.9 0.0 collective-permute-done.5.refs_5_
  31.9 0.0 copy-done
  31.9 0.0 copy-done.4
  31.9 0.0 copy-done.1
  31.9 0.0 copy-start.2
  31.9 0.9 %copy-done.2 = bf16[128,512]{1,0:T(8,128)(2,1)S(1)} copy-done((bf16[128,512]{1,0:T(8,128)(2,1)S(1)}, bf16[128,512]{1,0:T(8,128)(2,1)}, u32[]{:S(2)}) %copy-start.2) | copy-done | bytes 131096
  32.8 0.0 copy-start.3
  32.8 0.8 %copy-done.3 = bf16[48,512]{1,0:T(8,128)(2,1)S(1)} copy-done((bf16[48,512]{1,0:T(8,128)(2,1)S(1)}, bf16[48,512]{1,0:T(8,128)(2,1)}, u32[]{:S(2)}) %copy-start.3) | copy-done | bytes 49176
  33.6 0.0 copy-start.6
  33.6 6.9 %shard_map.122 = (bf16[512,128]{1,0:T(8,128)(2,1)S(1)}, bf16[512,128]{1,0:T(8,128)(2,1)S(1)}, f32[48,512]{1,0:T(8,128)S(1)}, f32[48,128]{1,0:T(8,128)S(1)}) custom-call(s32[16,6]{1,0:T(8,128)S(1)} %copy.13.refs_0_, bf16[512,512]{1,0:T(8,128)(2,1)S(1)} %copy-done, bf16[384,512]{1,0:T(8,128)(2,1)S(1)} %collective-permute-done.refs_2_.refs_11_, ...), custom_call_target="tpu_custom_call" | custom-call | bytes 1048576 | tf_op jit(solution)/shard_map/pallas_call | solution.py:275
  40.5 0.0 collective-permute-done.8.refs_12_
  40.6 0.0 collective-permute-done.9.refs_13_
  40.6 0.0 collective-permute-done.7.refs_11_
  40.6 0.0 copy-done.6
  40.6 6.9 %shard_map.123 = (bf16[512,128]{1,0:T(8,128)(2,1)S(1)}, bf16[512,128]{1,0:T(8,128)(2,1)S(1)}, bf16[48,512]{1,0:T(8,128)(2,1)S(1)}, bf16[48,256]{1,0:T(8,128)(2,1)S(1)}) custom-call(s32[16,6]{1,0:T(8,128)S(1)} %copy.13.refs_0_, bf16[512,512]{1,0:T(8,128)(2,1)S(1)} %copy-done, bf16[384,512]{1,0:T(8,128)(2,1)S(1)} %collective-permute-done.refs_2_.refs_11_, ...), custom_call_target="tpu_custom_call" | custom-call | flops 4000000000 | bytes 1048576 | tf_op jit(solution)/shard_map/pallas_call | solution.py:275
  47.5 0.0 copy-start.5
  47.5 0.1 collective-permute-start.11
  47.6 1.2 %collective-permute-done.11.sibling_ref = bf16[48,512]{1,0:T(8,128)(2,1)S(1)} collective-permute-done((bf16[48,512]{1,0:T(8,128)(2,1)S(1)}, bf16[48,512]{1,0:T(8,128)(2,1)S(1)}, u32[]{:S(2)}, u32[]{:S(2)}) %collective-permute-start.11) | collective-permute-done | bytes 49184 | tf_op jit(solution)/shard_map/ppermute | solution.py:288
  48.8 0.6 collective-permute-start.12
  49.4 3.8 %collective-permute-done.12 = bf16[48,768]{1,0:T(8,128)(2,1)S(1)} collective-permute-done((bf16[48,768]{1,0:T(8,128)(2,1)S(1)}, bf16[48,768]{1,0:T(8,128)(2,1)S(1)}, u32[]{:S(2)}, u32[]{:S(2)}) %collective-permute-start.12) | collective-permute-done | bytes 73760 | tf_op jit(solution)/shard_map/ppermute | solution.py:288
  53.3 0.1 collective-permute-start.13
  53.4 0.0 copy-start.7
  53.4 0.0 copy-done.5
  53.4 0.6 %copy-done.7 = s32[1,512]{1,0:T(1,128)S(1)} copy-done((s32[1,512]{1,0:T(1,128)S(1)}, s32[1,512]{1,0:T(1,128)}, u32[]{:S(2)}) %copy-start.7) | copy-done | bytes 2072
  54.0 1.0 %shard_map.124 = (f32[512,256]{1,0:T(8,128)S(1)}, bf16[512,256]{1,0:T(8,128)(2,1)S(1)}) custom-call(s32[1,512]{1,0:T(1,128)S(1)} %copy-done.7, bf16[512,256]{1,0:T(8,128)(2,1)S(1)} %copy-done.5, bf16[512,128]{1,0:T(8,128)(2,1)S(1)} %get-tuple-element.38.att1_ref, bf16[512,128]{1,0:T(8,128)(2,1)S(1)} %get-tuple-element.42.att2_ref, ...), custom_call_target="tpu_custom_call" | custom-call | flops 1000000000 | bytes 1048576 | tf_op jit(solution)/shard_map/pallas_call | solution.py:275
  55.0 0.1 collective-permute-start.10
  55.1 2.6 %collective-permute-done.13 = bf16[48,768]{1,0:T(8,128)(2,1)S(1)} collective-permute-done((bf16[48,768]{1,0:T(8,128)(2,1)S(1)}, bf16[48,768]{1,0:T(8,128)(2,1)S(1)}, u32[]{:S(2)}, u32[]{:S(2)}) %collective-permute-start.13) | collective-permute-done | bytes 73760 | tf_op jit(solution)/shard_map/ppermute | solution.py:288
  57.7 0.1 collective-permute-start.14
  57.8 0.0 collective-permute-done.10
  57.8 0.8 %fusion = bf16[1,512,256]{2,1,0:T(8,128)(2,1)} fusion(f32[512,256]{1,0:T(8,128)S(1)} %get-tuple-element.45, bf16[512,256]{1,0:T(8,128)(2,1)S(1)} %collective-permute-done.10), kind=kLoop, calls=%fused_computation.1 | loop fusion | flops 393216 | bytes 1048576 | tf_op jit(solution)/shard_map/broadcast_in_dim | solution.py:442
  58.6 4.7 %collective-permute-done.14.recv_ref = bf16[48,768]{1,0:T(8,128)(2,1)S(1)} collective-permute-done((bf16[48,768]{1,0:T(8,128)(2,1)S(1)}, bf16[48,768]{1,0:T(8,128)(2,1)S(1)}, u32[]{:S(2)}, u32[]{:S(2)}) %collective-permute-start.14) | collective-permute-done | bytes 73760 | tf_op jit(solution)/shard_map/ppermute | solution.py:288
  63.3 0.7 %shard_map.126 = (f32[48,512]{1,0:T(8,128)}, f32[48,256]{1,0:T(8,128)}) custom-call(bf16[48,768]{1,0:T(8,128)(2,1)S(1)} %add_convert_fusion.1.own_ref, bf16[48,768]{1,0:T(8,128)(2,1)S(1)} %collective-permute-done.14.recv_ref), custom_call_target="tpu_custom_call" | custom-call | bytes 1048576 | tf_op jit(solution)/shard_map/pallas_call | solution.py:275
  (5 shorter events, 0.1 us)
Async XLA Ops:
  0.6 31.2 %copy-start.8 = (s32[16,6]{0,1:T(8,128)S(1)}, s32[16,6]{0,1:T(8,128)}, u32[]{:S(2)}) copy-start(s32[16,6]{0,1:T(8,128)} %param.18) | copy-start | bytes 1156
  4.2 27.7 %copy-start = (bf16[512,512]{1,0:T(8,128)(2,1)S(1)}, bf16[512,512]{1,0:T(8,128)(2,1)}, u32[]{:S(2)}) copy-start(bf16[512,512]{1,0:T(8,128)(2,1)} %get-tuple-element.29.refs_1_) | copy-start | bytes 1572868
  4.2 19.0 %collective-permute-start = (bf16[384,512]{1,0:T(8,128)(2,1)}, bf16[384,512]{1,0:T(8,128)(2,1)S(1)}, u32[]{:S(2)}, u32[]{:S(2)}) collective-permute-start(bf16[384,512]{1,0:T(8,128)(2,1)} %get-tuple-element.30), channel_id=1, source_target_pairs={{0,4},{4,0},{8,12},{12,8},{1,5},{5,1},{9,13},{13,9},{2,6},{6,2},{1... | collective-permute-start | bytes 1179656 | tf_op jit(solution)/shard_map/ppermute | solution.py:288
  7.3 11.5 %collective-permute-start.2 = (bf16[128,512]{1,0:T(8,128)(2,1)}, bf16[128,512]{1,0:T(8,128)(2,1)S(1)}, u32[]{:S(2)}, u32[]{:S(2)}) collective-permute-start(bf16[128,512]{1,0:T(8,128)(2,1)} %get-tuple-element.32.refs_10_), channel_id=1, source_target_pairs={{0,8},{4,12},{8,0},{12,4},{16,28},{20,24},{24,20},{28,16},{1,9},{5... | collective-permute-start | bytes 393224 | tf_op jit(solution)/shard_map/ppermute | solution.py:304
  9.9 13.4 %collective-permute-start.1 = (bf16[256,512]{1,0:T(8,128)(2,1)}, bf16[256,512]{1,0:T(8,128)(2,1)S(1)}, u32[]{:S(2)}, u32[]{:S(2)}) collective-permute-start(bf16[256,512]{1,0:T(8,128)(2,1)} %get-tuple-element.31), channel_id=1, source_target_pairs={{0,0},{4,8},{8,4},{12,12},{1,1},{5,9},{9,5},{13,13},{2,2},{6,10},{... | collective-permute-start | bytes 786440 | tf_op jit(solution)/shard_map/ppermute | solution.py:383
  18.9 7.3 %collective-permute-start.3 = (bf16[128,512]{1,0:T(8,128)(2,1)S(1)}, bf16[128,512]{1,0:T(8,128)(2,1)S(1)}, u32[]{:S(2)}, u32[]{:S(2)}) collective-permute-start(bf16[128,512]{1,0:T(8,128)(2,1)S(1)} %collective-permute-done.2.refs_12_), channel_id=1, source_target_pairs={{0,16},{16,0},{1,17},{17,1},{2,18},{18,2},{3,19},{19,3},{4,20},{20... | collective-permute-start | bytes 393224 | tf_op jit(solution)/shard_map/ppermute | solution.py:288
  23.3 7.0 %collective-permute-start.6 = (bf16[512,256]{1,0:T(8,128)(2,1)}, bf16[512,256]{1,0:T(8,128)(2,1)S(1)}, u32[]{:S(2)}, u32[]{:S(2)}) collective-permute-start(bf16[512,256]{1,0:T(8,128)(2,1)} %get-tuple-element.35.refs_6_), channel_id=1, source_target_pairs={{0,1},{1,0},{2,3},{3,2},{4,5},{5,4},{6,7},{7,6},{8,9},{9,8},{10,11... | collective-permute-start | bytes 786440 | tf_op jit(solution)/shard_map/ppermute | solution.py:288
  23.3 8.6 %copy-start.4 = (bf16[48,256]{1,0:T(8,128)(2,1)S(1)}, bf16[48,256]{1,0:T(8,128)(2,1)}, u32[]{:S(2)}) copy-start(bf16[48,256]{1,0:T(8,128)(2,1)} %get-tuple-element.37.refs_9_) | copy-start | bytes 73732
  23.3 8.6 %copy-start.1 = (bf16[512,256]{1,0:T(8,128)(2,1)S(1)}, bf16[512,256]{1,0:T(8,128)(2,1)}, u32[]{:S(2)}) copy-start(bf16[512,256]{1,0:T(8,128)(2,1)} %get-tuple-element.35.refs_6_) | copy-start | bytes 786436
  26.2 5.7 %collective-permute-start.4 = (bf16[256,512]{1,0:T(8,128)(2,1)S(1)}, bf16[256,512]{1,0:T(8,128)(2,1)S(1)}, u32[]{:S(2)}, u32[]{:S(2)}) collective-permute-start(bf16[256,512]{1,0:T(8,128)(2,1)S(1)} %slice.8), channel_id=1, source_target_pairs={{0,1},{1,0},{2,3},{3,2},{4,5},{5,4},{6,7},{7,6},{8,9},{9,8},{10,11... | collective-permute-start | bytes 786440 | tf_op jit(solution)/shard_map/ppermute | solution.py:288
  26.2 5.7 %collective-permute-start.5 = (bf16[256,512]{1,0:T(8,128)(2,1)S(1)}, bf16[256,512]{1,0:T(8,128)(2,1)S(1)}, u32[]{:S(2)}, u32[]{:S(2)}) collective-permute-start(bf16[256,512]{1,0:T(8,128)(2,1)S(1)} %collective-permute-done.1.refs_4_), channel_id=1, source_target_pairs={{0,1},{1,0},{2,3},{3,2},{4,5},{5,4},{6,7},{7,6},{8,9},{9,8},{10,11... | collective-permute-start | bytes 786440 | tf_op jit(solution)/shard_map/ppermute | solution.py:288
  26.7 13.8 %collective-permute-start.8 = (bf16[128,512]{1,0:T(8,128)(2,1)S(1)}, bf16[128,512]{1,0:T(8,128)(2,1)S(1)}, u32[]{:S(2)}, u32[]{:S(2)}) collective-permute-start(bf16[128,512]{1,0:T(8,128)(2,1)S(1)} %collective-permute-done.2.refs_12_), channel_id=1, source_target_pairs={{0,2},{2,0},{1,3},{3,1},{4,6},{6,4},{5,7},{7,5},{8,10},{10,8},{9,1... | collective-permute-start | bytes 393224 | tf_op jit(solution)/shard_map/ppermute | solution.py:288
  28.2 12.3 %collective-permute-start.9 = (bf16[128,512]{1,0:T(8,128)(2,1)S(1)}, bf16[128,512]{1,0:T(8,128)(2,1)S(1)}, u32[]{:S(2)}, u32[]{:S(2)}) collective-permute-start(bf16[128,512]{1,0:T(8,128)(2,1)S(1)} %collective-permute-done.2.refs_12_), channel_id=1, source_target_pairs={{0,18},{2,16},{16,2},{18,0},{1,19},{3,17},{17,3},{19,1},{4,22},{6,... | collective-permute-start | bytes 393224 | tf_op jit(solution)/shard_map/ppermute | solution.py:311
  30.2 10.3 %collective-permute-start.7 = (bf16[128,512]{1,0:T(8,128)(2,1)S(1)}, bf16[128,512]{1,0:T(8,128)(2,1)S(1)}, u32[]{:S(2)}, u32[]{:S(2)}) collective-permute-start(bf16[128,512]{1,0:T(8,128)(2,1)S(1)} %slice.9), channel_id=1, source_target_pairs={{0,2},{2,0},{1,3},{3,1},{4,6},{6,4},{5,7},{7,5},{8,10},{10,8},{9,1... | collective-permute-start | bytes 393224 | tf_op jit(solution)/shard_map/ppermute | solution.py:288
  31.9 0.9 %copy-start.2 = (bf16[128,512]{1,0:T(8,128)(2,1)S(1)}, bf16[128,512]{1,0:T(8,128)(2,1)}, u32[]{:S(2)}) copy-start(bf16[128,512]{1,0:T(8,128)(2,1)} %get-tuple-element.32.refs_10_) | copy-start | bytes 393220
  32.8 0.8 %copy-start.3 = (bf16[48,512]{1,0:T(8,128)(2,1)S(1)}, bf16[48,512]{1,0:T(8,128)(2,1)}, u32[]{:S(2)}) copy-start(bf16[48,512]{1,0:T(8,128)(2,1)} %get-tuple-element.36.refs_8_) | copy-start | bytes 147460
  33.6 6.9 %copy-start.6 = (bf16[128,512]{1,0:T(8,128)(2,1)S(1)}, bf16[128,512]{1,0:T(8,128)(2,1)}, u32[]{:S(2)}) copy-start(bf16[128,512]{1,0:T(8,128)(2,1)} %get-tuple-element.39.refs_10_) | copy-start | bytes 393220
  47.5 5.9 %copy-start.5 = (bf16[512,256]{1,0:T(8,128)(2,1)S(1)}, bf16[512,256]{1,0:T(8,128)(2,1)}, u32[]{:S(2)}) copy-start(bf16[512,256]{1,0:T(8,128)(2,1)} %get-tuple-element.28.x_ref) | copy-start | bytes 786436
  47.5 1.3 %collective-permute-start.11 = (bf16[48,512]{1,0:T(8,128)(2,1)S(1)}, bf16[48,512]{1,0:T(8,128)(2,1)S(1)}, u32[]{:S(2)}, u32[]{:S(2)}) collective-permute-start(bf16[48,512]{1,0:T(8,128)(2,1)S(1)} %get-tuple-element.47.down_ref), channel_id=1, source_target_pairs={{0,1},{1,0},{2,3},{3,2},{4,5},{5,4},{6,7},{7,6},{8,9},{9,8},{10,11... | collective-permute-start | bytes 147464 | tf_op jit(solution)/shard_map/ppermute | solution.py:288
  48.8 4.4 %collective-permute-start.12 = (bf16[48,768]{1,0:T(8,128)(2,1)S(1)}, bf16[48,768]{1,0:T(8,128)(2,1)S(1)}, u32[]{:S(2)}, u32[]{:S(2)}) collective-permute-start(bf16[48,768]{1,0:T(8,128)(2,1)S(1)} %shard_map.125), channel_id=1, source_target_pairs={{0,2},{2,0},{1,3},{3,1},{4,6},{6,4},{5,7},{7,5},{8,10},{10,8},{9,1... | collective-permute-start | bytes 221192 | tf_op jit(solution)/shard_map/ppermute | solution.py:288
  53.3 4.4 %collective-permute-start.13 = (bf16[48,768]{1,0:T(8,128)(2,1)S(1)}, bf16[48,768]{1,0:T(8,128)(2,1)S(1)}, u32[]{:S(2)}, u32[]{:S(2)}) collective-permute-start(bf16[48,768]{1,0:T(8,128)(2,1)S(1)} %add_convert_fusion.2), channel_id=1, source_target_pairs={{0,4},{4,0},{8,12},{12,8},{1,5},{5,1},{9,13},{13,9},{2,6},{6,2},{1... | collective-permute-start | bytes 221192 | tf_op jit(solution)/shard_map/ppermute | solution.py:288
  53.4 0.7 %copy-start.7 = (s32[1,512]{1,0:T(1,128)S(1)}, s32[1,512]{1,0:T(1,128)}, u32[]{:S(2)}) copy-start(s32[1,512]{1,0:T(1,128)} %get-tuple-element.27.order_ref) | copy-start | bytes 6148
  55.0 2.8 %collective-permute-start.10 = (bf16[512,256]{1,0:T(8,128)(2,1)S(1)}, bf16[512,256]{1,0:T(8,128)(2,1)S(1)}, u32[]{:S(2)}, u32[]{:S(2)}) collective-permute-start(bf16[512,256]{1,0:T(8,128)(2,1)S(1)} %get-tuple-element.46), channel_id=1, source_target_pairs={{0,1},{1,0},{2,3},{3,2},{4,5},{5,4},{6,7},{7,6},{8,9},{9,8},{10,11... | collective-permute-start | bytes 786440 | tf_op jit(solution)/shard_map/ppermute | solution.py:288
  57.7 5.5 %collective-permute-start.14 = (bf16[48,768]{1,0:T(8,128)(2,1)S(1)}, bf16[48,768]{1,0:T(8,128)(2,1)S(1)}, u32[]{:S(2)}, u32[]{:S(2)}) collective-permute-start(bf16[48,768]{1,0:T(8,128)(2,1)S(1)} %add_convert_fusion.1.own_ref), channel_id=1, source_target_pairs={{0,8},{4,12},{8,0},{12,4},{1,9},{5,13},{9,1},{13,5},{2,10},{6,14},... | collective-permute-start | bytes 221192 | tf_op jit(solution)/shard_map/ppermute | solution.py:288

commit v6 on v5

--- a/solution.py
+++ b/solution.py
@@ -56,11 +56,22 @@
     return copies
 
 
-def prep_kernel(split, *refs):
-    sources, outs, buffers, sems = refs[:9], refs[9:-7], refs[-7:-1], refs[-1]
-    order_ref, down_ref, up_ref, x_own_ref, normed_ref, half_ref, near_ref, cot_out_ref = outs[:8]
-    copies = load_all(sources, (order_ref,) + tuple(buffers) + (down_ref, up_ref), sems)
-    x_ref, wq_ref, wk_ref, wv_ref, wo_ref, cot_ref = buffers
+def pack_kernel(split, *refs):
+    sources, outs, buffers, sems = refs[:4], refs[4:6], refs[6:-1], refs[-1]
+    for copy in load_all(sources, buffers, sems):
+        copy.wait()
+    for which, out in enumerate(outs):
+        lanes = lanes_at(head_at(split, which))
+        for j, member in enumerate(buffers[:3]):
+            out[:, j * DH : (j + 1) * DH] = member[:, lanes]
+        out[:, 3 * DH :] = buffers[3][lanes, :].T
+
+
+def prep_kernel(*refs):
+    sources, outs, buffers, sems = refs[:5], refs[5:-3], refs[-3:-1], refs[-1]
+    order_ref, down_ref, up_ref, x_own_ref, normed_ref, half_ref, cot_out_ref = outs
+    x_ref, cot_ref = buffers
+    copies = load_all(sources, (order_ref, x_ref, cot_ref, down_ref, up_ref), sems)
     rows = x_ref.shape[0]
     copies[0].wait()
     place = scatter_matrix(order_ref, rows)
@@ -69,87 +80,64 @@
     center = ordered - jnp.mean(ordered, axis=-1, keepdims=True)
     spread = jnp.mean(center * center, axis=-1, keepdims=True)
     normed_ref[...] = (center * lax.rsqrt(spread + 1e-05)).astype(BF16)
+    start = pl.multiple_of(lax.axis_index("head") * (rows // 2), rows // 2)
+    half_ref[...] = normed_ref[pl.ds(start, rows // 2), :]
     for copy in copies[2:]:
         copy.wait()
-    for which, out in enumerate(outs[8:]):
-        lanes = lanes_at(head_at(split, which))
-        for j, member in enumerate((wq_ref, wk_ref, wv_ref)):
-            out[:, j * DH : (j + 1) * DH] = member[:, lanes]
-        out[:, 3 * DH :] = wo_ref[lanes, :].T
     cot_out_ref[...] = tn(place, cot_ref[...]).astype(BF16)
     cols = x_own_ref.shape[1]
     x_own_ref[...] = x_ref[:, pl.ds(pl.multiple_of(lax.axis_index("head") * cols, cols), cols)]
-    start = pl.multiple_of(lax.axis_index("head") * (rows // 2), rows // 2)
-    half_ref[...] = normed_ref[pl.ds(start, rows // 2), :]
-    skip = near_ref.shape[0] - rows // 2
-    if skip:
-        near_ref[:skip, :] = outs[8][...]
-    near_ref[skip:, :] = half_ref[...]
 
 
 def head_kernel(split, which, piece_rows, *refs):
-    (
-        table_ref,
-        normed_ref,
-        a_own_ref,
-        a_sib_ref,
-        b_own_ref,
-        b_sib_ref,
-        cot_own_ref,
-        cot_sib_ref,
-        down_ref,
-        up_ref,
-    ) = refs[:10]
-    rest = refs[10:]
-    scratch = rest[-12:]
+    table_ref, normed_ref, a_own_ref, a_sib_ref, b_own_ref, b_sib_ref = refs[:6]
+    cot_own_ref, cot_sib_ref, down_ref, up_ref = refs[6:10]
+    rest, scratch = refs[10:-8], refs[-8:]
     if which == 0:
-        pieces, (att_ref, wo_ref, down_out, up_out) = rest[:-16], rest[-16:-12]
+        pieces, (att_ref, wo_ref, low_ref, acc_ref, up_out) = rest[:-5], rest[-5:]
     else:
-        pieces, (down_in, up_in, att_ref, wo_ref, down_out, up_out) = rest[:-18], rest[-18:-12]
-    w_ref, u_ref, kv_ref, low_ref, q_ref, do_ref, dq_ref, tk_ref, tv_ref, bk_ref, bv_ref, sum_ref = (
-        scratch
-    )
+        low_ref, acc_in, up_in = rest[:3]
+        pieces, (att_ref, wo_ref, down_out, up_out) = rest[3:-4], rest[-4:]
+    w_ref, kv_ref, q_ref, do_ref, dq_ref, t_ref, back_ref = scratch[:7]
+    if which:
+        acc_ref = scratch[7]
     rows, width = normed_ref.shape
-    blocks = rows // BLK
-    half = rows // 2
+    blocks, half = rows // BLK, rows // 2
     node, core = lax.axis_index("node"), lax.axis_index("head")
     head = head_at(split, which)
     first = node * blocks
     inverse_root = 1.0 / math.sqrt(DH)
 
     for piece, row in zip(pieces, piece_rows(node)):
-        if isinstance(row, int):
-            w_ref[pl.ds(row, piece.shape[0]), :] = piece[...]
-        else:
-            depth = rest[0].shape[0]
-            w_ref[pl.ds(pl.multiple_of(row, depth), depth), :] = piece[:depth, :]
-    wo_ref[...] = w_ref[:, 3 * DH :]
-    u_ref[...] = jnp.zeros_like(u_ref)
+        start = row if isinstance(row, int) else pl.multiple_of(row, pieces[0].shape[0])
+        w_ref[pl.ds(start, piece.shape[0]), :] = piece[...]
+    wo_ref[...] = w_ref[:width, 3 * DH :]
+    w_ref[width:, :] = jnp.zeros((LOW, 4 * DH), BF16)
     for j in range(3):
-        u_ref[j * RANK : (j + 1) * RANK, j * DH : (j + 1) * DH] = (
-            adapter_scale * up_ref[j * RANK : (j + 1) * RANK, lanes_at(head)]
+        span = slice(j * RANK, (j + 1) * RANK)
+        w_ref[width + j * RANK : width + (j + 1) * RANK, j * DH : (j + 1) * DH] = (
+            adapter_scale * up_ref[span, lanes_at(head)]
         )
 
-    mine, theirs = core * half, (1 - core) * half
     segments = [
         (normed_ref, 0),
-        (a_own_ref.at[pl.ds(a_own_ref.shape[0] - half, half), :], pl.multiple_of(rows + mine, half)),
-        (a_sib_ref, pl.multiple_of(rows + theirs, half)),
-        (b_own_ref, pl.multiple_of(2 * rows + mine, half)),
-        (b_sib_ref, pl.multiple_of(2 * rows + theirs, half)),
+        (a_own_ref, pl.multiple_of(rows + core * half, half)),
+        (a_sib_ref, pl.multiple_of(rows + (1 - core) * half, half)),
+        (b_own_ref, pl.multiple_of(2 * rows + core * half, half)),
+        (b_sib_ref, pl.multiple_of(2 * rows + (1 - core) * half, half)),
     ]
-    low_ref[...] = jnp.zeros_like(low_ref)
+    if which == 0:
+        for member, start in segments:
+            low = nt(member[...], down_ref[...]).astype(BF16)
+            blank = jnp.zeros((low.shape[0], LOW - 3 * RANK), BF16)
+            low_ref[pl.ds(start, low.shape[0]), :] = jnp.concatenate([low, blank], axis=1)
     for j, (member, start) in enumerate(segments):
-        value = member[...]
-        span = pl.ds(start, value.shape[0])
-        low_ref[span, : 3 * RANK] = nt(value, down_ref[...]).astype(BF16)
-        low = low_ref[span, :]
-        skip = DH if j else 0
-        projected = (nn(value, w_ref[:, skip : 3 * DH]) + nn(low, u_ref[:, skip:])).astype(BF16)
+        span = pl.ds(start, member.shape[0])
+        value = jnp.concatenate([member[...], low_ref[span, :]], axis=1)
+        projected = nn(value, w_ref[:, (DH if j else 0) : 3 * DH]).astype(BF16)
         if j == 0:
             q_ref[...] = projected[:, :DH]
-        kv_ref[span, :] = projected[:, DH - skip :]
-    low_own = low_ref[0:rows, :]
+        kv_ref[span, :] = projected[:, -2 * DH :]
 
     def out_rows(side):
         return w_ref[pl.ds(pl.multiple_of(side * (width // 2), width // 2), width // 2), 3 * DH :]
@@ -157,11 +145,15 @@
     do_ref[...] = (
         nn(cot_own_ref[...], out_rows(core)) + nn(cot_sib_ref[...], out_rows(1 - core))
     ).astype(BF16)
-    bk_ref[...] = jnp.zeros_like(bk_ref)
-    bv_ref[...] = jnp.zeros_like(bv_ref)
+    up_q = w_ref[width : width + RANK, :DH]
+    up_k = w_ref[width + RANK : width + 2 * RANK, DH : 2 * DH]
+    up_v = w_ref[width + 2 * RANK : width + 3 * RANK, 2 * DH : 3 * DH]
+    query_up = nt(up_k, q_ref[...]).astype(BF16)
+    grad_up = nt(up_v, do_ref[...]).astype(BF16)
 
     odd = lax.rem(node, 2)
     left, right = 2 - odd, 1 + odd
+    all_starts = []
     for i in range(blocks):
         named = [table_ref[first + i, e] for e in range(table_ref.shape[1])]
         starts, valid = [], []
@@ -177,6 +169,7 @@
             for before in named[:e]:
                 fresh = jnp.logical_and(fresh, c != before)
             valid.append(fresh)
+        all_starts.append(starts)
         own = slice(i * BLK, (i + 1) * BLK)
         low_sel = jnp.concatenate([low_ref[pl.ds(s, BLK), :] for s in starts], axis=0)
         keys = jnp.concatenate([kv_ref[pl.ds(s, BLK), :DH] for s in starts], axis=0)
@@ -197,40 +190,37 @@
         mixed = nn(prob_b, jnp.concatenate([values, low_sel], axis=1))
         attended = mixed[:, :DH].astype(BF16)
         att_ref[own, :] = attended
-        tv_ref[own, :] = mixed[:, DH:].astype(BF16)
+        t_ref[own, LOW:] = mixed[:, DH:].astype(BF16)
         delta = jnp.sum(grad.astype(F32) * attended.astype(F32), axis=-1, keepdims=True)
         score_grad = (prob * (nt(grad, values) - delta) * inverse_root).astype(BF16)
         mixed = nn(score_grad, jnp.concatenate([keys, low_sel], axis=1))
         dq_ref[own, :] = mixed[:, :DH].astype(BF16)
-        tk_ref[own, :] = mixed[:, DH:].astype(BF16)
-        up_k = u_ref[RANK : 2 * RANK, DH : 2 * DH]
-        up_v = u_ref[2 * RANK : 3 * RANK, 2 * DH :]
-        back_k = nn(nt(up_k, query).astype(BF16), score_grad)
-        back_v = nn(nt(up_v, grad).astype(BF16), prob_b)
+        t_ref[own, :LOW] = mixed[:, DH:].astype(BF16)
+        back_ref[i, :RANK, :] = nn(query_up[:, own], score_grad)
+        back_ref[i, RANK:, :] = nn(grad_up[:, own], prob_b)
+
+    acc_ref[...] = acc_in[...] if which else jnp.zeros_like(acc_ref)
+    acc_ref[:RANK, :rows] += nt(up_q, dq_ref[...])
+    for i, starts in enumerate(all_starts):
         for e, s in enumerate(starts):
-            bk_ref[:, pl.ds(s, BLK)] += back_k[:, e * BLK : (e + 1) * BLK]
-            bv_ref[:, pl.ds(s, BLK)] += back_v[:, e * BLK : (e + 1) * BLK]
-
-    back_q = nt(u_ref[0:RANK, 0:DH], dq_ref[...])
-    lhs = jnp.concatenate([back_q, bk_ref[:, 0:rows], bv_ref[:, 0:rows]], axis=0).astype(BF16)
-    sum_ref[...] = nn(lhs, normed_ref[...])
-    for member, start in segments[1:]:
-        span = pl.ds(start, half)
-        lhs = jnp.concatenate([bk_ref[:, span], bv_ref[:, span]], axis=0).astype(BF16)
-        sum_ref[RANK:, :] += nn(lhs, member[...])
+            acc_ref[RANK:, pl.ds(s, BLK)] += back_ref[i, :, e * BLK : (e + 1) * BLK]
     up_grad = adapter_scale * jnp.concatenate(
         [
-            tn(low_own, dq_ref[...])[0:RANK],
-            tn(tk_ref[...], q_ref[...])[RANK : 2 * RANK],
-            tn(tv_ref[...], do_ref[...])[2 * RANK : 3 * RANK],
+            tn(low_ref[:rows, :], dq_ref[...])[0:RANK],
+            tn(t_ref[:, :LOW], q_ref[...])[RANK : 2 * RANK],
+            tn(t_ref[:, LOW:], do_ref[...])[2 * RANK : 3 * RANK],
         ],
         axis=0,
     )
     if which == 0:
-        down_out[...] = sum_ref[...]
         up_out[...] = up_grad
         return
-    down_out[...] = (sum_ref[...] + down_in[...]).astype(BF16)
+    total = nn(acc_ref[:, :rows].astype(BF16), normed_ref[...])
+    halo = jnp.zeros((2 * RANK, width), F32)
+    for member, start in segments[1:]:
+        halo += nn(acc_ref[RANK:, pl.ds(start, half)].astype(BF16), member[...])
+    down_out[:RANK, :] = total[:RANK].astype(BF16)
+    down_out[RANK:, :] = (total[RANK:] + halo).astype(BF16)
     up_out[:, lanes_at(head)] = up_grad.astype(BF16)
     up_out[:, lanes_at(1 - head)] = up_in[...].astype(BF16)
 
@@ -272,6 +262,9 @@
 
 
 def call(kernel, outs, ins, scratch=(), smem=0, hbm=0, flops=0, limit=None):
+    if hbm:
+        ins = tuple(pltpu.with_memory_space_constraint(x, pltpu.HBM) for x in ins)
+        outs = tuple(pltpu.VMEM(x.shape, x.dtype) for x in outs)
     return pl.pallas_call(
         kernel,
         out_shape=outs,
@@ -295,18 +288,19 @@
     return sorted(pairs.items())
 
 
-def gather_weights(first, second, near):
+def gather_weights(first, second, half):
     count, depth = lax.axis_size("node"), first.shape[0]
     if not split_weights():
         whole = [lax.all_gather(m, "node", axis=0, tiled=True) for m in (first, second)]
-        return [[whole[0]], [whole[1]]], lambda node: [0]
+        return [whole[:1], whole[1:]], lambda node: [0], whole
     far_pairs = [(g * 4 + n, g * 4 + (n ^ (2 + g))) for g in range(2) for n in range(4)]
     far = lax.ppermute(first, ("group", "node"), far_pairs)
-    other_far = swap(far, "group")
+    near = swap(first, "node")
+    far, near, _ = lax.optimization_barrier((far, near, half))
     diagonal = [(i, 3 - i) for i in range(4)]
     theirs = [
         second,
-        swap(near[:depth], "sample"),
+        swap(near, "sample"),
         swap(far, "sample"),
         lax.ppermute(far, ("group", "sample"), diagonal),
     ]
@@ -315,7 +309,8 @@
         group = lax.axis_index("group")
         return [jnp.bitwise_xor(node, k) * depth for k in (0, 1, 2 + group, 3 - group)]
 
-    return [[first, near, far, other_far], theirs], piece_rows
+    ours = [first, near, far, swap(far, "group")]
+    return [ours, theirs], piece_rows, (theirs[3], ours[3])
 
 
 def split_weights():
@@ -341,9 +336,18 @@
     order = block_node_order.reshape(1, rows)
     split = split_weights()
 
-    skip = depth if split else 0
-    order, down, up, x_own, normed, half, near, cot_own, *packed = call(
-        functools.partial(prep_kernel, split),
+    packed = call(
+        functools.partial(pack_kernel, split),
+        (shape((depth, 4 * DH)),) * 2,
+        (query_weight, key_weight, value_weight, output_weight),
+        [pltpu.VMEM((depth, cols), BF16)] * 3
+        + [pltpu.VMEM((cols, depth), BF16), pltpu.SemaphoreType.DMA((4,))],
+        hbm=4,
+        limit=16,
+    )
+    order, _ = lax.optimization_barrier((order, packed[0]))
+    order, down, up, x_own, normed, half, cot_own = call(
+        prep_kernel,
         (
             shape((1, rows), jnp.int32),
             shape((3 * RANK, width)),
@@ -351,39 +355,29 @@
             shape((rows, cols)),
             shape((rows, width)),
             shape((rows // 2, width)),
-            shape((skip + rows // 2, width)),
             shape((rows, cols)),
-            shape((depth, 4 * DH)),
-            shape((depth, 4 * DH)),
         ),
         (
             order,
             state,
-            query_weight,
-            key_weight,
-            value_weight,
-            output_weight,
             cotangent[0],
             adapter_down_weight.transpose(0, 2, 1).reshape(3 * RANK, width),
             adapter_up_weight.reshape(3 * RANK, cols),
         ),
         [
             pltpu.VMEM((rows, width), BF16),
-            pltpu.VMEM((depth, cols), BF16),
-            pltpu.VMEM((depth, cols), BF16),
-            pltpu.VMEM((depth, cols), BF16),
-            pltpu.VMEM((cols, depth), BF16),
             pltpu.VMEM((rows, cols), BF16),
-            pltpu.SemaphoreType.DMA((9,)),
+            pltpu.SemaphoreType.DMA((5,)),
         ],
-        hbm=9,
+        hbm=5,
         flops=2 * rows * rows * (width + cols),
-    )
-    a_own = swap(near, "node", 1)
+        limit=16,
+    )
+    pieces, piece_rows, late = gather_weights(*packed, half)
+    a_own = swap(half, "node", 1)
     b_own = lax.ppermute(half, "node", chain_pairs(lax.axis_size("node")))
-    pieces, piece_rows = gather_weights(*packed, a_own)
     cot_sib = swap(cot_own, "head")
-    a_half, b_half, _ = lax.optimization_barrier((a_own[skip:], b_own, pieces[0][-1]))
+    a_half, b_half, _ = lax.optimization_barrier((a_own, b_own, late))
     a_sib = swap(a_half, "head")
     b_sib = swap(b_half, "head")
 
@@ -399,23 +393,26 @@
         down,
         up,
     )
+    entries = neighbour_key_blocks.shape[1]
     scratch = [
-        pltpu.VMEM((width, 4 * DH), BF16),
-        pltpu.VMEM((LOW, 3 * DH), BF16),
+        pltpu.VMEM((width + LOW, 4 * DH), BF16),
         pltpu.VMEM((3 * rows, 2 * DH), BF16),
-        pltpu.VMEM((3 * rows, LOW), BF16),
         pltpu.VMEM((rows, DH), BF16),
         pltpu.VMEM((rows, DH), BF16),
         pltpu.VMEM((rows, DH), BF16),
-        pltpu.VMEM((rows, LOW), BF16),
-        pltpu.VMEM((rows, LOW), BF16),
-        pltpu.VMEM((RANK, 3 * rows), F32),
-        pltpu.VMEM((RANK, 3 * rows), F32),
-        pltpu.VMEM((3 * RANK, width), F32),
+        pltpu.VMEM((rows, 2 * LOW), BF16),
+        pltpu.VMEM((rows // BLK, 2 * RANK, entries * BLK), F32),
+        pltpu.VMEM((3 * RANK, 3 * rows), F32),
     ]
-    att1, wo1, down1, up1 = call(
+    att1, wo1, low, acc, up1 = call(
         functools.partial(head_kernel, split, 0, piece_rows),
-        (shape((rows, DH)), shape((width, DH)), shape((3 * RANK, width), F32), shape((3 * RANK, DH), F32)),
+        (
+            shape((rows, DH)),
+            shape((width, DH)),
+            shape((3 * rows, LOW)),
+            shape((3 * RANK, 3 * rows), F32),
+            shape((3 * RANK, DH), F32),
+        ),
         shared + tuple(pieces[0]),
         scratch,
         smem=1,
@@ -424,7 +421,7 @@
     att2, wo2, down2, up2 = call(
         functools.partial(head_kernel, split, 1, piece_rows),
         (shape((rows, DH)), shape((width, DH)), shape((3 * RANK, width)), shape((3 * RANK, cols))),
-        shared + tuple(pieces[1]) + (down1, up1),
+        shared + (low, acc, up1) + tuple(pieces[1]),
         scratch,
         smem=1,
         limit=32,

time: 64.2 us -> 52.7 us (0.82)
  waiting for transfers between devices: 22.6 us -> 17 us
  local copies, waits for them, and re-layouts: 2.48 us -> 0.09 us
  Pallas kernels: 19.1 us -> 16.8 us
  starting transfers between devices: 18.1 us -> 17.1 us
    ppermute x1, waiting for transfers between devices: 7.36 us -> 1.27 us  [gather_weights(): far = lax.ppermute(first, ('group', 'node'), far_pairs)]
    ppermute x12 -> x13, starting transfers between devices: 11.9 us -> 8.68 us  [swap(): return lax.ppermute(value, axis, [(i, i ^ step) for i in range(size)])]
    unnamed x19 -> x3, local copies, waits for them, and re-layouts: 2.45 us -> 0.09 us
    pallas_call x6 -> x7, Pallas kernels: 19.1 us -> 16.8 us  [call(): pl.pallas_call(kernel, out_shape=outs, in_specs=[SMEM] * smem + [HBM] * h...]
    ppermute x1, starting transfers between devices: 1.99 us -> 3.63 us  [gather_weights(): lax.ppermute(far, ('group', 'sample'), diagonal)]
    ppermute x1, starting transfers between devices: 2.59 us -> 4.1 us  [gather_weights(): far = lax.ppermute(first, ('group', 'node'), far_pairs)]
    ppermute x1, waiting for transfers between devices: 0.01 us -> 1.21 us  [gather_weights(): lax.ppermute(far, ('group', 'sample'), diagonal)]
    ppermute x1, starting transfers between devices: 1.6 us -> 0.67 us  [shards(): b_own = lax.ppermute(half, 'node', chain_pairs(lax.axis_size('node')))]
  transfers between devices with their start and end apart: 15 -> 16, of which waited for: 6 -> 10; matrix products, arithmetic and copies ran while one was open for 1% -> 2% of each run, Pallas kernels for 12% -> 17%
where the time goes in v6:
time: 52.7 us; the launch traced here: 52.5 us
  starting transfers between devices  17.1 us (32%)
  waiting for transfers between devices  17 us (32%)
  Pallas kernels  16.8 us (32%)
  other arithmetic  0.8 us (2%)
  between operations  0.72 us (1%)
    pallas_call x7, Pallas kernels, call(): pl.pallas_call(kernel, out_shape=outs, in_specs=[SMEM] * smem + [HBM] * h...  16.8 us
    ppermute x13, waiting for transfers between devices, swap(): return lax.ppermute(value, axis, [(i, i ^ step) for i in range(size)])  14.6 us
    ppermute x13, starting transfers between devices, swap(): return lax.ppermute(value, axis, [(i, i ^ step) for i in range(size)])  8.68 us
    ppermute x1, starting transfers between devices, gather_weights(): far = lax.ppermute(first, ('group', 'node'), far_pairs)  4.1 us
    ppermute x1, starting transfers between devices, gather_weights(): lax.ppermute(far, ('group', 'sample'), diagonal)  3.63 us
    ppermute x1, waiting for transfers between devices, gather_weights(): far = lax.ppermute(first, ('group', 'node'), far_pairs)  1.27 us
    ppermute x1, waiting for transfers between devices, gather_weights(): lax.ppermute(far, ('group', 'sample'), diagonal)  1.21 us
  transfers between devices with their start and end apart: 16, of which 10 were waited for; matrix products, arithmetic and copies ran while one was open for 2% of the time, Pallas kernels for 17%

profile of v6, /device:TPU:0, one launch (start us, length us, event | category | flops | bytes accessed | tf_op | source)
XLA Modules:
  0.0 52.5 jit_solution(1255825799856616851)
XLA Ops:
  0.6 1.1 %shard_map.121 = (bf16[128,512]{1,0:T(8,128)(2,1)S(1)}, bf16[128,512]{1,0:T(8,128)(2,1)S(1)}) custom-call(bf16[128,256]{1,0:T(8,128)(2,1)} %refs_0_.3, bf16[128,256]{1,0:T(8,128)(2,1)} %refs_1_.1, bf16[128,256]{1,0:T(8,128)(2,1)} %refs_2_.1, bf16[256,128]{1,0:T(8,128)(2,1)} %refs_3_.1), custom_call_target="tpu_custom_call" | custom-call | bytes 1048576 | tf_op jit(solution)/shard_map/pallas_call | solution.py:268
  1.7 4.1 %collective-permute-start.2 = (bf16[128,512]{1,0:T(8,128)(2,1)S(1)}, bf16[128,512]{1,0:T(8,128)(2,1)S(1)}, u32[]{:S(2)}, u32[]{:S(2)}) collective-permute-start(bf16[128,512]{1,0:T(8,128)(2,1)S(1)} %get-tuple-element.30.refs_10_), channel_id=1, source_target_pairs={{0,8},{4,12},{8,0},{12,4},{16,28},{20,24},{24,20},{28,16},{1,9},{5... | collective-permute-start | bytes 393224 | tf_op jit(solution)/shard_map/ppermute | solution.py:297
  5.8 1.6 %collective-permute-start.3 = (bf16[128,512]{1,0:T(8,128)(2,1)S(1)}, bf16[128,512]{1,0:T(8,128)(2,1)S(1)}, u32[]{:S(2)}, u32[]{:S(2)}) collective-permute-start(bf16[128,512]{1,0:T(8,128)(2,1)S(1)} %get-tuple-element.30.refs_10_), channel_id=1, source_target_pairs={{0,4},{4,0},{8,12},{12,8},{1,5},{5,1},{9,13},{13,9},{2,6},{6,2},{1... | collective-permute-start | bytes 393224 | tf_op jit(solution)/shard_map/ppermute | solution.py:281
  7.4 0.0 copy-start
  7.4 2.4 %shard_map.122 = (s32[1,512]{1,0:T(1,128)S(1)}, bf16[48,512]{1,0:T(8,128)(2,1)S(1)}, bf16[48,256]{1,0:T(8,128)(2,1)S(1)}, bf16[512,256]{1,0:T(8,128)(2,1)S(1)}, ...) custom-call(s32[1,512]{1,0:T(1,128)} %bitcast.19, ...), custom_call_target="tpu_custom_call" | custom-call | flops 402653184 | bytes 1048576 | tf_op jit(solution)/shard_map/pallas_call | solution.py:268
  9.8 0.5 collective-permute-start
  10.3 0.7 %collective-permute-start.1 = (bf16[256,512]{1,0:T(8,128)(2,1)S(1)}, bf16[256,512]{1,0:T(8,128)(2,1)S(1)}, u32[]{:S(2)}, u32[]{:S(2)}) collective-permute-start(bf16[256,512]{1,0:T(8,128)(2,1)S(1)} %get-tuple-element.35), channel_id=1, source_target_pairs={{0,0},{4,8},{8,4},{12,12},{1,1},{5,9},{9,5},{13,13},{2,2},{6,10},{... | collective-permute-start | bytes 786440 | tf_op jit(solution)/shard_map/ppermute | solution.py:378
  11.0 1.3 %collective-permute-done.2.refs_12_ = bf16[128,512]{1,0:T(8,128)(2,1)S(1)} collective-permute-done((bf16[128,512]{1,0:T(8,128)(2,1)S(1)}, bf16[128,512]{1,0:T(8,128)(2,1)S(1)}, u32[]{:S(2)}, u32[]{:S(2)}) %collective-permute-start.2) | collective-permute-done | bytes 131104 | tf_op jit(solution)/shard_map/ppermute | solution.py:297
  12.2 0.3 collective-permute-done.3.refs_11_
  12.6 3.6 %collective-permute-start.4 = (bf16[128,512]{1,0:T(8,128)(2,1)S(1)}, bf16[128,512]{1,0:T(8,128)(2,1)S(1)}, u32[]{:S(2)}, u32[]{:S(2)}) collective-permute-start(bf16[128,512]{1,0:T(8,128)(2,1)S(1)} %collective-permute-done.2.refs_12_), channel_id=1, source_target_pairs={{0,18},{2,16},{16,2},{18,0},{1,19},{3,17},{17,3},{19,1},{4,22},{6,... | collective-permute-start | bytes 393224 | tf_op jit(solution)/shard_map/ppermute | solution.py:305
  16.2 0.0 collective-permute-start.5
  16.2 0.0 collective-permute-start.8
  16.2 1.8 %collective-permute-done.refs_2_ = bf16[256,512]{1,0:T(8,128)(2,1)S(1)} collective-permute-done((bf16[256,512]{1,0:T(8,128)(2,1)S(1)}, bf16[256,512]{1,0:T(8,128)(2,1)S(1)}, u32[]{:S(2)}, u32[]{:S(2)}) %collective-permute-start) | collective-permute-done | bytes 262176 | tf_op jit(solution)/shard_map/ppermute | solution.py:281
  18.0 0.0 collective-permute-done.1.refs_4_
  18.0 1.2 %collective-permute-done.4.refs_16_ = bf16[128,512]{1,0:T(8,128)(2,1)S(1)} collective-permute-done((bf16[128,512]{1,0:T(8,128)(2,1)S(1)}, bf16[128,512]{1,0:T(8,128)(2,1)S(1)}, u32[]{:S(2)}, u32[]{:S(2)}) %collective-permute-start.4) | collective-permute-done | bytes 131104 | tf_op jit(solution)/shard_map/ppermute | solution.py:305
  19.3 2.5 %collective-permute-done.5.refs_13_ = bf16[128,512]{1,0:T(8,128)(2,1)S(1)} collective-permute-done((bf16[128,512]{1,0:T(8,128)(2,1)S(1)}, bf16[128,512]{1,0:T(8,128)(2,1)S(1)}, u32[]{:S(2)}, u32[]{:S(2)}) %collective-permute-start.5) | collective-permute-done | bytes 131104 | tf_op jit(solution)/shard_map/ppermute | solution.py:281
  21.8 0.0 collective-permute-start.6
  21.8 0.5 collective-permute-start.7
  22.3 0.5 %collective-permute-start.9 = (bf16[128,512]{1,0:T(8,128)(2,1)S(1)}, bf16[128,512]{1,0:T(8,128)(2,1)S(1)}, u32[]{:S(2)}, u32[]{:S(2)}) collective-permute-start(bf16[128,512]{1,0:T(8,128)(2,1)S(1)} %collective-permute-done.3.refs_11_), channel_id=1, source_target_pairs={{0,2},{2,0},{1,3},{3,1},{4,6},{6,4},{5,7},{7,5},{8,10},{10,8},{9,1... | collective-permute-start | bytes 393224 | tf_op jit(solution)/shard_map/ppermute | solution.py:281
  22.8 1.5 %collective-permute-start.10 = (bf16[128,512]{1,0:T(8,128)(2,1)S(1)}, bf16[128,512]{1,0:T(8,128)(2,1)S(1)}, u32[]{:S(2)}, u32[]{:S(2)}) collective-permute-start(bf16[128,512]{1,0:T(8,128)(2,1)S(1)} %collective-permute-done.2.refs_12_), channel_id=1, source_target_pairs={{0,2},{2,0},{1,3},{3,1},{4,6},{6,4},{5,7},{7,5},{8,10},{10,8},{9,1... | collective-permute-start | bytes 393224 | tf_op jit(solution)/shard_map/ppermute | solution.py:281
  24.3 0.0 copy-done
  24.3 0.1 copy.13.refs_0_
  24.4 0.0 collective-permute-done.8.refs_7_
  24.4 0.0 collective-permute-done.6.refs_3_
  24.4 0.0 collective-permute-done.7.refs_5_
  24.4 5.8 %shard_map.123 = (bf16[512,128]{1,0:T(8,128)(2,1)S(1)}, bf16[512,128]{1,0:T(8,128)(2,1)S(1)}, bf16[1536,128]{1,0:T(8,128)(2,1)S(1)}, f32[48,1536]{1,0:T(8,128)S(1)}, f32[48,128]{1,0:T(8,128)S(1)}) custom-call(s32[16,6]{1,0:T(8,128)S(1)} %copy.13.refs_0_, bf16[512,512]{1,0:T(8,128)(2,1)S(1)} %get-tuple-element.34.refs_1_, ...), custom_call_target="tpu_custom_call" | custom-call | bytes 1048576 | tf_op jit(solution)/shard_map/pallas_call | solution.py:268
  30.2 0.0 collective-permute-done.9.refs_14_
  30.2 0.3 collective-permute-done.10.refs_15_
  30.5 5.8 %shard_map.124 = (bf16[512,128]{1,0:T(8,128)(2,1)S(1)}, bf16[512,128]{1,0:T(8,128)(2,1)S(1)}, bf16[48,512]{1,0:T(8,128)(2,1)S(1)}, bf16[48,256]{1,0:T(8,128)(2,1)S(1)}) custom-call(s32[16,6]{1,0:T(8,128)S(1)} %copy.13.refs_0_, bf16[512,512]{1,0:T(8,128)(2,1)S(1)} %get-tuple-element.34.refs_1_, bf16[256,512]{1,0:T(8,128)(2,1)S(1)} %collective-permute-done.refs_2_, ...), custom_call_target="tpu_custom_call" | custom-call | flops 4000000000 | bytes 1048576 | tf_op jit(solution)/shard_map/pallas_call | solution.py:268
  36.3 0.0 collective-permute-start.12
  36.4 1.2 %collective-permute-done.12.sibling_ref = bf16[48,512]{1,0:T(8,128)(2,1)S(1)} collective-permute-done((bf16[48,512]{1,0:T(8,128)(2,1)S(1)}, bf16[48,512]{1,0:T(8,128)(2,1)S(1)}, u32[]{:S(2)}, u32[]{:S(2)}) %collective-permute-start.12) | collective-permute-done | bytes 49184 | tf_op jit(solution)/shard_map/ppermute | solution.py:281
  37.6 0.6 %collective-permute-start.13 = (bf16[48,768]{1,0:T(8,128)(2,1)S(1)}, bf16[48,768]{1,0:T(8,128)(2,1)S(1)}, u32[]{:S(2)}, u32[]{:S(2)}) collective-permute-start(bf16[48,768]{1,0:T(8,128)(2,1)S(1)} %shard_map.126), channel_id=1, source_target_pairs={{0,2},{2,0},{1,3},{3,1},{4,6},{6,4},{5,7},{7,5},{8,10},{10,8},{9,1... | collective-permute-start | bytes 221192 | tf_op jit(solution)/shard_map/ppermute | solution.py:281
  38.2 3.8 %collective-permute-done.13 = bf16[48,768]{1,0:T(8,128)(2,1)S(1)} collective-permute-done((bf16[48,768]{1,0:T(8,128)(2,1)S(1)}, bf16[48,768]{1,0:T(8,128)(2,1)S(1)}, u32[]{:S(2)}, u32[]{:S(2)}) %collective-permute-start.13) | collective-permute-done | bytes 73760 | tf_op jit(solution)/shard_map/ppermute | solution.py:281
  42.1 1.7 %collective-permute-start.14 = (bf16[48,768]{1,0:T(8,128)(2,1)S(1)}, bf16[48,768]{1,0:T(8,128)(2,1)S(1)}, u32[]{:S(2)}, u32[]{:S(2)}) collective-permute-start(bf16[48,768]{1,0:T(8,128)(2,1)S(1)} %add_convert_fusion.2), channel_id=1, source_target_pairs={{0,4},{4,0},{8,12},{12,8},{1,5},{5,1},{9,13},{13,9},{2,6},{6,2},{1... | collective-permute-start | bytes 221192 | tf_op jit(solution)/shard_map/ppermute | solution.py:281
  43.8 1.0 %shard_map.125 = (f32[512,256]{1,0:T(8,128)S(1)}, bf16[512,256]{1,0:T(8,128)(2,1)S(1)}) custom-call(s32[1,512]{1,0:T(1,128)S(1)} %get-tuple-element.32.order_ref, bf16[512,256]{1,0:T(8,128)(2,1)S(1)} %get-tuple-element.33.x_ref, bf16[512,128]{1,0:T(8,128)(2,1)S(1)} %get-tuple-element.43.att1_ref, bf16[512,128]{1,0:T(8,128)(2,1)S(1)} %get-tuple-element.48.att2_ref, ...), custom_call_target="tpu_custom_call" | custom-call | flops 1000000000 | bytes 1048576 | tf_op jit(solution)/shard_map/pallas_call | solution.py:268
  44.8 0.1 collective-permute-start.11
  44.9 1.6 %collective-permute-done.14 = bf16[48,768]{1,0:T(8,128)(2,1)S(1)} collective-permute-done((bf16[48,768]{1,0:T(8,128)(2,1)S(1)}, bf16[48,768]{1,0:T(8,128)(2,1)S(1)}, u32[]{:S(2)}, u32[]{:S(2)}) %collective-permute-start.14) | collective-permute-done | bytes 73760 | tf_op jit(solution)/shard_map/ppermute | solution.py:281
  46.5 1.7 %collective-permute-start.15 = (bf16[48,768]{1,0:T(8,128)(2,1)S(1)}, bf16[48,768]{1,0:T(8,128)(2,1)S(1)}, u32[]{:S(2)}, u32[]{:S(2)}) collective-permute-start(bf16[48,768]{1,0:T(8,128)(2,1)S(1)} %add_convert_fusion.1.own_ref), channel_id=1, source_target_pairs={{0,8},{4,12},{8,0},{12,4},{1,9},{5,13},{9,1},{13,5},{2,10},{6,14},... | collective-permute-start | bytes 221192 | tf_op jit(solution)/shard_map/ppermute | solution.py:281
  48.2 0.0 collective-permute-done.11
  48.2 0.8 %fusion = bf16[1,512,256]{2,1,0:T(8,128)(2,1)} fusion(f32[512,256]{1,0:T(8,128)S(1)} %get-tuple-element.51, bf16[512,256]{1,0:T(8,128)(2,1)S(1)} %collective-permute-done.11), kind=kLoop, calls=%fused_computation.1 | loop fusion | flops 393216 | bytes 1048576 | tf_op jit(solution)/shard_map/broadcast_in_dim | solution.py:439
  48.9 2.9 %collective-permute-done.15.recv_ref = bf16[48,768]{1,0:T(8,128)(2,1)S(1)} collective-permute-done((bf16[48,768]{1,0:T(8,128)(2,1)S(1)}, bf16[48,768]{1,0:T(8,128)(2,1)S(1)}, u32[]{:S(2)}, u32[]{:S(2)}) %collective-permute-start.15) | collective-permute-done | bytes 73760 | tf_op jit(solution)/shard_map/ppermute | solution.py:281
  51.8 0.7 %shard_map.127 = (f32[48,512]{1,0:T(8,128)}, f32[48,256]{1,0:T(8,128)}) custom-call(bf16[48,768]{1,0:T(8,128)(2,1)S(1)} %add_convert_fusion.1.own_ref, bf16[48,768]{1,0:T(8,128)(2,1)S(1)} %collective-permute-done.15.recv_ref), custom_call_target="tpu_custom_call" | custom-call | bytes 1048576 | tf_op jit(solution)/shard_map/pallas_call | solution.py:268
  (3 shorter events, 0.1 us)
Async XLA Ops:
  1.7 10.5 %collective-permute-start.2 = (bf16[128,512]{1,0:T(8,128)(2,1)S(1)}, bf16[128,512]{1,0:T(8,128)(2,1)S(1)}, u32[]{:S(2)}, u32[]{:S(2)}) collective-permute-start(bf16[128,512]{1,0:T(8,128)(2,1)S(1)} %get-tuple-element.30.refs_10_), channel_id=1, source_target_pairs={{0,8},{4,12},{8,0},{12,4},{16,28},{20,24},{24,20},{28,16},{1,9},{5... | collective-permute-start | bytes 393224 | tf_op jit(solution)/shard_map/ppermute | solution.py:297
  5.8 6.8 %collective-permute-start.3 = (bf16[128,512]{1,0:T(8,128)(2,1)S(1)}, bf16[128,512]{1,0:T(8,128)(2,1)S(1)}, u32[]{:S(2)}, u32[]{:S(2)}) collective-permute-start(bf16[128,512]{1,0:T(8,128)(2,1)S(1)} %get-tuple-element.30.refs_10_), channel_id=1, source_target_pairs={{0,4},{4,0},{8,12},{12,8},{1,5},{5,1},{9,13},{13,9},{2,6},{6,2},{1... | collective-permute-start | bytes 393224 | tf_op jit(solution)/shard_map/ppermute | solution.py:281
  7.4 16.9 %copy-start = (s32[16,6]{0,1:T(8,128)S(1)}, s32[16,6]{0,1:T(8,128)}, u32[]{:S(2)}) copy-start(s32[16,6]{0,1:T(8,128)} %param.18) | copy-start | bytes 1156
  9.8 8.3 %collective-permute-start = (bf16[256,512]{1,0:T(8,128)(2,1)S(1)}, bf16[256,512]{1,0:T(8,128)(2,1)S(1)}, u32[]{:S(2)}, u32[]{:S(2)}) collective-permute-start(bf16[256,512]{1,0:T(8,128)(2,1)S(1)} %get-tuple-element.35), channel_id=1, source_target_pairs={{0,4},{4,0},{8,12},{12,8},{1,5},{5,1},{9,13},{13,9},{2,6},{6,2},{1... | collective-permute-start | bytes 786440 | tf_op jit(solution)/shard_map/ppermute | solution.py:281
  10.3 7.8 %collective-permute-start.1 = (bf16[256,512]{1,0:T(8,128)(2,1)S(1)}, bf16[256,512]{1,0:T(8,128)(2,1)S(1)}, u32[]{:S(2)}, u32[]{:S(2)}) collective-permute-start(bf16[256,512]{1,0:T(8,128)(2,1)S(1)} %get-tuple-element.35), channel_id=1, source_target_pairs={{0,0},{4,8},{8,4},{12,12},{1,1},{5,9},{9,5},{13,13},{2,2},{6,10},{... | collective-permute-start | bytes 786440 | tf_op jit(solution)/shard_map/ppermute | solution.py:378
  12.6 6.7 %collective-permute-start.4 = (bf16[128,512]{1,0:T(8,128)(2,1)S(1)}, bf16[128,512]{1,0:T(8,128)(2,1)S(1)}, u32[]{:S(2)}, u32[]{:S(2)}) collective-permute-start(bf16[128,512]{1,0:T(8,128)(2,1)S(1)} %collective-permute-done.2.refs_12_), channel_id=1, source_target_pairs={{0,18},{2,16},{16,2},{18,0},{1,19},{3,17},{17,3},{19,1},{4,22},{6,... | collective-permute-start | bytes 393224 | tf_op jit(solution)/shard_map/ppermute | solution.py:305
  16.2 5.6 %collective-permute-start.5 = (bf16[128,512]{1,0:T(8,128)(2,1)S(1)}, bf16[128,512]{1,0:T(8,128)(2,1)S(1)}, u32[]{:S(2)}, u32[]{:S(2)}) collective-permute-start(bf16[128,512]{1,0:T(8,128)(2,1)S(1)} %collective-permute-done.2.refs_12_), channel_id=1, source_target_pairs={{0,16},{16,0},{1,17},{17,1},{2,18},{18,2},{3,19},{19,3},{4,20},{20... | collective-permute-start | bytes 393224 | tf_op jit(solution)/shard_map/ppermute | solution.py:281
  16.2 8.2 %collective-permute-start.8 = (bf16[512,256]{1,0:T(8,128)(2,1)S(1)}, bf16[512,256]{1,0:T(8,128)(2,1)S(1)}, u32[]{:S(2)}, u32[]{:S(2)}) collective-permute-start(bf16[512,256]{1,0:T(8,128)(2,1)S(1)} %get-tuple-element.39.refs_6_), channel_id=1, source_target_pairs={{0,1},{1,0},{2,3},{3,2},{4,5},{5,4},{6,7},{7,6},{8,9},{9,8},{10,11... | collective-permute-start | bytes 786440 | tf_op jit(solution)/shard_map/ppermute | solution.py:281
  21.8 2.6 %collective-permute-start.6 = (bf16[256,512]{1,0:T(8,128)(2,1)S(1)}, bf16[256,512]{1,0:T(8,128)(2,1)S(1)}, u32[]{:S(2)}, u32[]{:S(2)}) collective-permute-start(bf16[256,512]{1,0:T(8,128)(2,1)S(1)} %collective-permute-done.refs_2_), channel_id=1, source_target_pairs={{0,1},{1,0},{2,3},{3,2},{4,5},{5,4},{6,7},{7,6},{8,9},{9,8},{10,11... | collective-permute-start | bytes 786440 | tf_op jit(solution)/shard_map/ppermute | solution.py:281
  21.8 2.6 %collective-permute-start.7 = (bf16[256,512]{1,0:T(8,128)(2,1)S(1)}, bf16[256,512]{1,0:T(8,128)(2,1)S(1)}, u32[]{:S(2)}, u32[]{:S(2)}) collective-permute-start(bf16[256,512]{1,0:T(8,128)(2,1)S(1)} %collective-permute-done.1.refs_4_), channel_id=1, source_target_pairs={{0,1},{1,0},{2,3},{3,2},{4,5},{5,4},{6,7},{7,6},{8,9},{9,8},{10,11... | collective-permute-start | bytes 786440 | tf_op jit(solution)/shard_map/ppermute | solution.py:281
  22.3 7.9 %collective-permute-start.9 = (bf16[128,512]{1,0:T(8,128)(2,1)S(1)}, bf16[128,512]{1,0:T(8,128)(2,1)S(1)}, u32[]{:S(2)}, u32[]{:S(2)}) collective-permute-start(bf16[128,512]{1,0:T(8,128)(2,1)S(1)} %collective-permute-done.3.refs_11_), channel_id=1, source_target_pairs={{0,2},{2,0},{1,3},{3,1},{4,6},{6,4},{5,7},{7,5},{8,10},{10,8},{9,1... | collective-permute-start | bytes 393224 | tf_op jit(solution)/shard_map/ppermute | solution.py:281
  22.8 7.7 %collective-permute-start.10 = (bf16[128,512]{1,0:T(8,128)(2,1)S(1)}, bf16[128,512]{1,0:T(8,128)(2,1)S(1)}, u32[]{:S(2)}, u32[]{:S(2)}) collective-permute-start(bf16[128,512]{1,0:T(8,128)(2,1)S(1)} %collective-permute-done.2.refs_12_), channel_id=1, source_target_pairs={{0,2},{2,0},{1,3},{3,1},{4,6},{6,4},{5,7},{7,5},{8,10},{10,8},{9,1... | collective-permute-start | bytes 393224 | tf_op jit(solution)/shard_map/ppermute | solution.py:281
  36.3 1.2 %collective-permute-start.12 = (bf16[48,512]{1,0:T(8,128)(2,1)S(1)}, bf16[48,512]{1,0:T(8,128)(2,1)S(1)}, u32[]{:S(2)}, u32[]{:S(2)}) collective-permute-start(bf16[48,512]{1,0:T(8,128)(2,1)S(1)} %get-tuple-element.53.down_ref), channel_id=1, source_target_pairs={{0,1},{1,0},{2,3},{3,2},{4,5},{5,4},{6,7},{7,6},{8,9},{9,8},{10,11... | collective-permute-start | bytes 147464 | tf_op jit(solution)/shard_map/ppermute | solution.py:281
  37.6 4.4 %collective-permute-start.13 = (bf16[48,768]{1,0:T(8,128)(2,1)S(1)}, bf16[48,768]{1,0:T(8,128)(2,1)S(1)}, u32[]{:S(2)}, u32[]{:S(2)}) collective-permute-start(bf16[48,768]{1,0:T(8,128)(2,1)S(1)} %shard_map.126), channel_id=1, source_target_pairs={{0,2},{2,0},{1,3},{3,1},{4,6},{6,4},{5,7},{7,5},{8,10},{10,8},{9,1... | collective-permute-start | bytes 221192 | tf_op jit(solution)/shard_map/ppermute | solution.py:281
  42.1 4.4 %collective-permute-start.14 = (bf16[48,768]{1,0:T(8,128)(2,1)S(1)}, bf16[48,768]{1,0:T(8,128)(2,1)S(1)}, u32[]{:S(2)}, u32[]{:S(2)}) collective-permute-start(bf16[48,768]{1,0:T(8,128)(2,1)S(1)} %add_convert_fusion.2), channel_id=1, source_target_pairs={{0,4},{4,0},{8,12},{12,8},{1,5},{5,1},{9,13},{13,9},{2,6},{6,2},{1... | collective-permute-start | bytes 221192 | tf_op jit(solution)/shard_map/ppermute | solution.py:281
  44.8 3.4 %collective-permute-start.11 = (bf16[512,256]{1,0:T(8,128)(2,1)S(1)}, bf16[512,256]{1,0:T(8,128)(2,1)S(1)}, u32[]{:S(2)}, u32[]{:S(2)}) collective-permute-start(bf16[512,256]{1,0:T(8,128)(2,1)S(1)} %get-tuple-element.52), channel_id=1, source_target_pairs={{0,1},{1,0},{2,3},{3,2},{4,5},{5,4},{6,7},{7,6},{8,9},{9,8},{10,11... | collective-permute-start | bytes 786440 | tf_op jit(solution)/shard_map/ppermute | solution.py:281
  46.5 5.3 %collective-permute-start.15 = (bf16[48,768]{1,0:T(8,128)(2,1)S(1)}, bf16[48,768]{1,0:T(8,128)(2,1)S(1)}, u32[]{:S(2)}, u32[]{:S(2)}) collective-permute-start(bf16[48,768]{1,0:T(8,128)(2,1)S(1)} %add_convert_fusion.1.own_ref), channel_id=1, source_target_pairs={{0,8},{4,12},{8,0},{12,4},{1,9},{5,13},{9,1},{13,5},{2,10},{6,14},... | collective-permute-start | bytes 221192 | tf_op jit(solution)/shard_map/ppermute | solution.py:281

commit v7 on v6

--- a/solution.py
+++ b/solution.py
@@ -68,10 +68,10 @@
 
 
 def prep_kernel(*refs):
-    sources, outs, buffers, sems = refs[:5], refs[5:-3], refs[-3:-1], refs[-1]
-    order_ref, down_ref, up_ref, x_own_ref, normed_ref, half_ref, cot_out_ref = outs
+    sources, outs, buffers, sems = refs[:6], refs[6:-3], refs[-3:-1], refs[-1]
+    order_ref, table_ref, down_ref, up_ref, x_own_ref, normed_ref, half_ref, cot_out_ref = outs
     x_ref, cot_ref = buffers
-    copies = load_all(sources, (order_ref, x_ref, cot_ref, down_ref, up_ref), sems)
+    copies = load_all(sources, (order_ref, x_ref, cot_ref, down_ref, up_ref, table_ref), sems)
     rows = x_ref.shape[0]
     copies[0].wait()
     place = scatter_matrix(order_ref, rows)
@@ -90,17 +90,20 @@
 
 
 def head_kernel(split, which, piece_rows, *refs):
-    table_ref, normed_ref, a_own_ref, a_sib_ref, b_own_ref, b_sib_ref = refs[:6]
+    table_vmem, normed_ref, a_own_ref, a_sib_ref, b_own_ref, b_sib_ref = refs[:6]
     cot_own_ref, cot_sib_ref, down_ref, up_ref = refs[6:10]
-    rest, scratch = refs[10:-8], refs[-8:]
+    rest, scratch = refs[10:-11], refs[-11:]
     if which == 0:
         pieces, (att_ref, wo_ref, low_ref, acc_ref, up_out) = rest[:-5], rest[-5:]
     else:
         low_ref, acc_in, up_in = rest[:3]
-        pieces, (att_ref, wo_ref, down_out, up_out) = rest[3:-4], rest[-4:]
+        pieces, (att_ref, wo_ref, keep_ref, send_ref, up_out) = rest[3:-5], rest[-5:]
     w_ref, kv_ref, q_ref, do_ref, dq_ref, t_ref, back_ref = scratch[:7]
+    table_ref, table_sem = scratch[8:10]
     if which:
         acc_ref = scratch[7]
+    table_copy = pltpu.make_async_copy(table_vmem, table_ref, table_sem)
+    table_copy.start()
     rows, width = normed_ref.shape
     blocks, half = rows // BLK, rows // 2
     node, core = lax.axis_index("node"), lax.axis_index("head")
@@ -108,9 +111,13 @@
     first = node * blocks
     inverse_root = 1.0 / math.sqrt(DH)
 
-    for piece, row in zip(pieces, piece_rows(node)):
-        start = row if isinstance(row, int) else pl.multiple_of(row, pieces[0].shape[0])
-        w_ref[pl.ds(start, piece.shape[0]), :] = piece[...]
+    places = piece_rows(node)
+    step = width // len(places)
+    for piece in pieces:
+        for j in range(0, piece.shape[0], step):
+            row, *places = places
+            start = row if isinstance(row, int) else pl.multiple_of(row, step)
+            w_ref[pl.ds(start, step), :] = piece[j : j + step, :]
     wo_ref[...] = w_ref[:width, 3 * DH :]
     w_ref[width:, :] = jnp.zeros((LOW, 4 * DH), BF16)
     for j in range(3):
@@ -151,11 +158,12 @@
     query_up = nt(up_k, q_ref[...]).astype(BF16)
     grad_up = nt(up_v, do_ref[...]).astype(BF16)
 
+    table_copy.wait()
     odd = lax.rem(node, 2)
     left, right = 2 - odd, 1 + odd
     all_starts = []
     for i in range(blocks):
-        named = [table_ref[first + i, e] for e in range(table_ref.shape[1])]
+        named = [table_ref[e, first + i] for e in range(table_ref.shape[0])]
         starts, valid = [], []
         for e, c in enumerate(named):
             rel = c - first
@@ -219,10 +227,17 @@
     halo = jnp.zeros((2 * RANK, width), F32)
     for member, start in segments[1:]:
         halo += nn(acc_ref[RANK:, pl.ds(start, half)].astype(BF16), member[...])
-    down_out[:RANK, :] = total[:RANK].astype(BF16)
-    down_out[RANK:, :] = (total[RANK:] + halo).astype(BF16)
+    sum_ref = scratch[10]
+    sum_ref[:RANK, :] = total[:RANK]
+    sum_ref[RANK:, :] = total[RANK:] + halo
+    keep_ref[...] = sum_ref[:, half_lanes(core, width)].astype(BF16)
+    send_ref[...] = sum_ref[:, half_lanes(1 - core, width)].astype(BF16)
     up_out[:, lanes_at(head)] = up_grad.astype(BF16)
     up_out[:, lanes_at(1 - head)] = up_in[...].astype(BF16)
+
+
+def half_lanes(side, width):
+    return pl.ds(pl.multiple_of(side * (width // 2), width // 2), width // 2)
 
 
 def merge_kernel(down_ref, sibling_ref, up_ref, out_ref):
@@ -231,11 +246,20 @@
     out_ref[:, width:] = up_ref[...]
 
 
-def final_kernel(own_ref, recv_ref, down_ref, up_ref):
+def total_kernel(*refs):
+    terms, (down_ref, up_ref) = [r[...].astype(F32) for r in refs[:-2]], refs[-2:]
+    while len(terms) > 1:
+        terms = [a + b for a, b in zip(terms[::2], terms[1::2])]
     width = down_ref.shape[1]
-    total = own_ref[...].astype(F32) + recv_ref[...].astype(F32)
-    down_ref[...] = total[:, :width]
-    up_ref[...] = total[:, width:]
+    down_ref[...] = terms[0][:, :width]
+    up_ref[...] = terms[0][:, width:]
+
+
+def final_kernel(own_ref, recv_ref, up_ref, out_ref, up_out):
+    core, width = lax.axis_index("head"), out_ref.shape[1]
+    up_out[...] = up_ref[...]
+    out_ref[:, half_lanes(core, width)] = own_ref[...]
+    out_ref[:, half_lanes(1 - core, width)] = recv_ref[...]
 
 
 def out_kernel(order_ref, x_ref, att1_ref, att2_ref, wo1_ref, wo2_ref, base_ref, other_ref):
@@ -254,21 +278,21 @@
 
 HBM = pl.BlockSpec(memory_space=pltpu.HBM)
 VMEM = pl.BlockSpec(memory_space=pltpu.VMEM)
-SMEM = pl.BlockSpec(memory_space=pltpu.SMEM)
 
 
 def shape(dims, dtype=BF16):
     return jax.ShapeDtypeStruct(dims, dtype)
 
 
-def call(kernel, outs, ins, scratch=(), smem=0, hbm=0, flops=0, limit=None):
+def call(kernel, outs, ins, scratch=(), hbm=0, flops=0, limit=None, pin=False):
     if hbm:
         ins = tuple(pltpu.with_memory_space_constraint(x, pltpu.HBM) for x in ins)
+    if hbm or pin:
         outs = tuple(pltpu.VMEM(x.shape, x.dtype) for x in outs)
     return pl.pallas_call(
         kernel,
         out_shape=outs,
-        in_specs=[SMEM] * smem + [HBM] * hbm + [VMEM] * (len(ins) - smem - hbm),
+        in_specs=[HBM] * hbm + [VMEM] * (len(ins) - hbm),
         out_specs=(VMEM,) * len(outs),
         scratch_shapes=list(scratch),
         cost_estimate=pl.CostEstimate(flops=flops, bytes_accessed=1 << 20, transcendentals=0),
@@ -286,6 +310,12 @@
     for i in range(1, size - 1, 2):
         pairs[i], pairs[i + 1] = i + 1, i
     return sorted(pairs.items())
+
+
+def pair_kernel(one_ref, two_ref, out_ref):
+    depth = one_ref.shape[0]
+    out_ref[:depth, :] = one_ref[...]
+    out_ref[depth:, :] = two_ref[...]
 
 
 def gather_weights(first, second, half):
@@ -297,20 +327,17 @@
     far = lax.ppermute(first, ("group", "node"), far_pairs)
     near = swap(first, "node")
     far, near, _ = lax.optimization_barrier((far, near, half))
-    diagonal = [(i, 3 - i) for i in range(4)]
-    theirs = [
-        second,
-        swap(near, "sample"),
-        swap(far, "sample"),
-        lax.ppermute(far, ("group", "sample"), diagonal),
-    ]
+    other_far = swap(far, "group")
+    near_theirs = swap(near, "sample")
+    far_held, _ = lax.optimization_barrier((far, near_theirs))
+    pair = call(pair_kernel, (shape((2 * depth, 4 * DH)),), (far_held, other_far), limit=16)[0]
+    theirs = [second, near_theirs, swap(pair, "sample")]
 
     def piece_rows(node):
         group = lax.axis_index("group")
         return [jnp.bitwise_xor(node, k) * depth for k in (0, 1, 2 + group, 3 - group)]
 
-    ours = [first, near, far, swap(far, "group")]
-    return [ours, theirs], piece_rows, (theirs[3], ours[3])
+    return [[first, near, far, other_far], theirs], piece_rows, other_far
 
 
 def split_weights():
@@ -346,10 +373,11 @@
         limit=16,
     )
     order, _ = lax.optimization_barrier((order, packed[0]))
-    order, down, up, x_own, normed, half, cot_own = call(
+    order, table, down, up, x_own, normed, half, cot_own = call(
         prep_kernel,
         (
             shape((1, rows), jnp.int32),
+            shape(neighbour_key_blocks.shape[::-1], jnp.int32),
             shape((3 * RANK, width)),
             shape((3 * RANK, cols)),
             shape((rows, cols)),
@@ -363,13 +391,14 @@
             cotangent[0],
             adapter_down_weight.transpose(0, 2, 1).reshape(3 * RANK, width),
             adapter_up_weight.reshape(3 * RANK, cols),
+            neighbour_key_blocks.T,
         ),
         [
             pltpu.VMEM((rows, width), BF16),
             pltpu.VMEM((rows, cols), BF16),
-            pltpu.SemaphoreType.DMA((5,)),
+            pltpu.SemaphoreType.DMA((6,)),
         ],
-        hbm=5,
+        hbm=6,
         flops=2 * rows * rows * (width + cols),
         limit=16,
     )
@@ -382,7 +411,7 @@
     b_sib = swap(b_half, "head")
 
     shared = (
-        neighbour_key_blocks,
+        table,
         normed,
         a_own,
         a_sib,
@@ -403,6 +432,9 @@
         pltpu.VMEM((rows, 2 * LOW), BF16),
         pltpu.VMEM((rows // BLK, 2 * RANK, entries * BLK), F32),
         pltpu.VMEM((3 * RANK, 3 * rows), F32),
+        pltpu.SMEM(table.shape, jnp.int32),
+        pltpu.SemaphoreType.DMA,
+        pltpu.VMEM((3 * RANK, width), F32),
     ]
     att1, wo1, low, acc, up1 = call(
         functools.partial(head_kernel, split, 0, piece_rows),
@@ -415,19 +447,23 @@
         ),
         shared + tuple(pieces[0]),
         scratch,
-        smem=1,
         limit=32,
     )
-    att2, wo2, down2, up2 = call(
+    att2, wo2, keep, send, up2 = call(
         functools.partial(head_kernel, split, 1, piece_rows),
-        (shape((rows, DH)), shape((width, DH)), shape((3 * RANK, width)), shape((3 * RANK, cols))),
+        (
+            shape((rows, DH)),
+            shape((width, DH)),
+            shape((3 * RANK, width // 2)),
+            shape((3 * RANK, width // 2)),
+            shape((3 * RANK, cols)),
+        ),
         shared + (low, acc, up1) + tuple(pieces[1]),
         scratch,
-        smem=1,
         limit=32,
         flops=4 * 10**9,
     )
-    down_sib = swap(down2, "head")
+    received = swap(send, "head")
     base, other = call(
         out_kernel,
         (shape((rows, cols), F32), shape((rows, cols))),
@@ -435,17 +471,29 @@
         flops=10**9,
         limit=16,
     )
-    lora = call(merge_kernel, (shape((3 * RANK, width + cols)),), (down2, down_sib, up2), limit=16)[0]
     mesh_out = (base + swap(other, "head").astype(F32)).astype(BF16)[None]
-
+    size = (3 * RANK, width // 2 + cols)
+    lora = call(merge_kernel, (shape(size),), (keep, received, up2), limit=16)[0]
     hops = [("sample", 1 << i) for i in range(lax.axis_size("sample").bit_length() - 1)]
-    hops += [("node", 1 << i) for i in range(lax.axis_size("node").bit_length() - 1)]
-    for axis, step in hops[:-1]:
+    count = lax.axis_size("node")
+    if count != 4:
+        hops += [("node", 1 << i) for i in range(count.bit_length() - 2)]
+    for axis, step in hops:
         lora = (lora.astype(F32) + swap(lora, axis, step).astype(F32)).astype(BF16)
+    steps = (1, 2, 3) if count == 4 else (count // 2,)
+    terms = (lora, *[swap(lora, "node", k) for k in steps])
+    terms, mesh_out = lax.optimization_barrier((terms, mesh_out))
+    down_half, up_total = call(
+        total_kernel,
+        (shape((3 * RANK, width // 2), F32), shape((3 * RANK, cols), F32)),
+        terms,
+        limit=16,
+        pin=True,
+    )
     down_total, up_total = call(
         final_kernel,
         (shape((3 * RANK, width), F32), shape((3 * RANK, cols), F32)),
-        (lora, swap(lora, *hops[-1])),
+        (down_half, swap(down_half, "head"), up_total),
         limit=16,
     )
     down_total = down_total.reshape(3, RANK, width).transpose(0, 2, 1)

time: 52.7 us -> 49.6 us (0.941)
  waiting for transfers between devices: 17 us -> 12.1 us
  starting transfers between devices: 17.1 us -> 19.8 us
  Pallas kernels: 16.8 us -> 16 us
    ppermute x13 -> x15, starting transfers between devices: 8.68 us -> 15 us  [swap(): return lax.ppermute(value, axis, [(i, i ^ step) for i in range(size)])]
    ppermute x13 -> x15, waiting for transfers between devices: 14.6 us -> 10.8 us  [swap(): return lax.ppermute(value, axis, [(i, i ^ step) for i in range(size)])]
    ppermute x1 -> x0, starting transfers between devices: 3.63 us -> none  [gather_weights(): lax.ppermute(far, ('group', 'sample'), diagonal)]
    ppermute x1 -> x0, waiting for transfers between devices: 1.21 us -> none  [gather_weights(): lax.ppermute(far, ('group', 'sample'), diagonal)]
    pallas_call x7 -> x9, Pallas kernels: 16.8 us -> 16 us  [call(): pl.pallas_call(kernel, out_shape=outs, in_specs=[HBM] * hbm + [VMEM] * (l...]
  transfers between devices with their start and end apart: 16 -> 17, of which waited for: 10 -> 9; matrix products, arithmetic and copies ran while one was open for 2% -> 2% of each run, Pallas kernels for 17% -> 18%
where the time goes in v7:
time: 49.6 us; the launch traced here: 49.4 us
  starting transfers between devices  19.8 us (40%)
  Pallas kernels  16 us (32%)
  waiting for transfers between devices  12.1 us (24%)
  other arithmetic  0.78 us (2%)
  between operations  0.75 us (2%)
    pallas_call x9, Pallas kernels, call(): pl.pallas_call(kernel, out_shape=outs, in_specs=[HBM] * hbm + [VMEM] * (l...  16 us
    ppermute x15, starting transfers between devices, swap(): return lax.ppermute(value, axis, [(i, i ^ step) for i in range(size)])  15 us
    ppermute x15, waiting for transfers between devices, swap(): return lax.ppermute(value, axis, [(i, i ^ step) for i in range(size)])  10.8 us
    ppermute x1, starting transfers between devices, gather_weights(): far = lax.ppermute(first, ('group', 'node'), far_pairs)  4.1 us
    ppermute x1, waiting for transfers between devices, gather_weights(): far = lax.ppermute(first, ('group', 'node'), far_pairs)  1.27 us
  transfers between devices with their start and end apart: 17, of which 9 were waited for; matrix products, arithmetic and copies ran while one was open for 2% of the time, Pallas kernels for 18%

profile of v7, /device:TPU:0, one launch (start us, length us, event | category | flops | bytes accessed | tf_op | source)
XLA Modules:
  0.0 49.4 jit_solution(11934988799839721647)
XLA Ops:
  0.6 1.1 %shard_map.121 = (bf16[128,512]{1,0:T(8,128)(2,1)S(1)}, bf16[128,512]{1,0:T(8,128)(2,1)S(1)}) custom-call(bf16[128,256]{1,0:T(8,128)(2,1)} %refs_0_.1, bf16[128,256]{1,0:T(8,128)(2,1)} %refs_1_.1, bf16[128,256]{1,0:T(8,128)(2,1)} %refs_2_.1, bf16[256,128]{1,0:T(8,128)(2,1)} %refs_3_.1), custom_call_target="tpu_custom_call" | custom-call | bytes 1048576 | tf_op jit(solution)/shard_map/pallas_call | solution.py:292
  1.7 4.1 %collective-permute-start.2 = (bf16[128,512]{1,0:T(8,128)(2,1)S(1)}, bf16[128,512]{1,0:T(8,128)(2,1)S(1)}, u32[]{:S(2)}, u32[]{:S(2)}) collective-permute-start(bf16[128,512]{1,0:T(8,128)(2,1)S(1)} %get-tuple-element.40.refs_10_), channel_id=1, source_target_pairs={{0,8},{4,12},{8,0},{12,4},{16,28},{20,24},{24,20},{28,16},{1,9},{5... | collective-permute-start | bytes 393224 | tf_op jit(solution)/shard_map/ppermute | solution.py:327
  5.8 1.6 %collective-permute-start.3 = (bf16[128,512]{1,0:T(8,128)(2,1)S(1)}, bf16[128,512]{1,0:T(8,128)(2,1)S(1)}, u32[]{:S(2)}, u32[]{:S(2)}) collective-permute-start(bf16[128,512]{1,0:T(8,128)(2,1)S(1)} %get-tuple-element.40.refs_10_), channel_id=1, source_target_pairs={{0,4},{4,0},{8,12},{12,8},{1,5},{5,1},{9,13},{13,9},{2,6},{6,2},{1... | collective-permute-start | bytes 393224 | tf_op jit(solution)/shard_map/ppermute | solution.py:305
  7.4 2.4 %shard_map.122 = (s32[1,512]{1,0:T(1,128)S(1)}, s32[6,16]{1,0:T(8,128)S(1)}, bf16[48,512]{1,0:T(8,128)(2,1)S(1)}, bf16[48,256]{1,0:T(8,128)(2,1)S(1)}, bf16[512,...) custom-call(s32[1,512]{1,0:T(1,128)} %bitcast.21, ...), custom_call_target="tpu_custom_call" | custom-call | flops 402653184 | bytes 1048576 | tf_op jit(solution)/shard_map/pallas_call | solution.py:292
  9.8 0.5 %collective-permute-start = (bf16[256,512]{1,0:T(8,128)(2,1)S(1)}, bf16[256,512]{1,0:T(8,128)(2,1)S(1)}, u32[]{:S(2)}, u32[]{:S(2)}) collective-permute-start(bf16[256,512]{1,0:T(8,128)(2,1)S(1)} %get-tuple-element.44), channel_id=1, source_target_pairs={{0,4},{4,0},{8,12},{12,8},{1,5},{5,1},{9,13},{13,9},{2,6},{6,2},{1... | collective-permute-start | bytes 786440 | tf_op jit(solution)/shard_map/ppermute | solution.py:305
  10.3 0.7 %collective-permute-start.1 = (bf16[256,512]{1,0:T(8,128)(2,1)S(1)}, bf16[256,512]{1,0:T(8,128)(2,1)S(1)}, u32[]{:S(2)}, u32[]{:S(2)}) collective-permute-start(bf16[256,512]{1,0:T(8,128)(2,1)S(1)} %get-tuple-element.44), channel_id=1, source_target_pairs={{0,0},{4,8},{8,4},{12,12},{1,1},{5,9},{9,5},{13,13},{2,2},{6,10},{... | collective-permute-start | bytes 786440 | tf_op jit(solution)/shard_map/ppermute | solution.py:407
  10.9 1.3 %collective-permute-done.2.refs_12_.one_ref = bf16[128,512]{1,0:T(8,128)(2,1)S(1)} collective-permute-done((bf16[128,512]{1,0:T(8,128)(2,1)S(1)}, bf16[128,512]{1,0:T(8,128)(2,1)S(1)}, u32[]{:S(2)}, u32[]{:S(2)}) %collective-permute-start.2) | collective-permute-done | bytes 131104 | tf_op jit(solution)/shard_map/ppermute | solution.py:327
  12.2 0.3 collective-permute-done.3.refs_11_
  12.6 2.7 %collective-permute-start.4 = (bf16[128,512]{1,0:T(8,128)(2,1)S(1)}, bf16[128,512]{1,0:T(8,128)(2,1)S(1)}, u32[]{:S(2)}, u32[]{:S(2)}) collective-permute-start(bf16[128,512]{1,0:T(8,128)(2,1)S(1)} %collective-permute-done.2.refs_12_.one_ref), channel_id=1, source_target_pairs={{0,16},{16,0},{1,17},{17,1},{2,18},{18,2},{3,19},{19,3},{4,20},{20... | collective-permute-start | bytes 393224 | tf_op jit(solution)/shard_map/ppermute | solution.py:305
  15.3 1.5 %collective-permute-start.8 = (bf16[128,512]{1,0:T(8,128)(2,1)S(1)}, bf16[128,512]{1,0:T(8,128)(2,1)S(1)}, u32[]{:S(2)}, u32[]{:S(2)}) collective-permute-start(bf16[128,512]{1,0:T(8,128)(2,1)S(1)} %collective-permute-done.3.refs_11_), channel_id=1, source_target_pairs={{0,2},{2,0},{1,3},{3,1},{4,6},{6,4},{5,7},{7,5},{8,10},{10,8},{9,1... | collective-permute-start | bytes 393224 | tf_op jit(solution)/shard_map/ppermute | solution.py:305
  16.8 0.0 collective-permute-start.7
  16.8 1.4 %collective-permute-done.4.refs_13_.two_ref = bf16[128,512]{1,0:T(8,128)(2,1)S(1)} collective-permute-done((bf16[128,512]{1,0:T(8,128)(2,1)S(1)}, bf16[128,512]{1,0:T(8,128)(2,1)S(1)}, u32[]{:S(2)}, u32[]{:S(2)}) %collective-permute-start.4) | collective-permute-done | bytes 131104 | tf_op jit(solution)/shard_map/ppermute | solution.py:305
  18.2 0.0 collective-permute-done.refs_2_
  18.2 0.0 collective-permute-done.1.refs_4_
  18.2 0.0 collective-permute-start.5
  18.2 0.5 %collective-permute-start.6 = (bf16[256,512]{1,0:T(8,128)(2,1)S(1)}, bf16[256,512]{1,0:T(8,128)(2,1)S(1)}, u32[]{:S(2)}, u32[]{:S(2)}) collective-permute-start(bf16[256,512]{1,0:T(8,128)(2,1)S(1)} %collective-permute-done.1.refs_4_), channel_id=1, source_target_pairs={{0,1},{1,0},{2,3},{3,2},{4,5},{5,4},{6,7},{7,6},{8,9},{9,8},{10,11... | collective-permute-start | bytes 786440 | tf_op jit(solution)/shard_map/ppermute | solution.py:305
  18.7 1.5 %collective-permute-done.8.refs_14_ = bf16[128,512]{1,0:T(8,128)(2,1)S(1)} collective-permute-done((bf16[128,512]{1,0:T(8,128)(2,1)S(1)}, bf16[128,512]{1,0:T(8,128)(2,1)S(1)}, u32[]{:S(2)}, u32[]{:S(2)}) %collective-permute-start.8) | collective-permute-done | bytes 131104 | tf_op jit(solution)/shard_map/ppermute | solution.py:305
  20.3 1.6 %collective-permute-start.9 = (bf16[256,512]{1,0:T(8,128)(2,1)S(1)}, bf16[256,512]{1,0:T(8,128)(2,1)S(1)}, u32[]{:S(2)}, u32[]{:S(2)}) collective-permute-start(bf16[256,512]{1,0:T(8,128)(2,1)S(1)} %shard_map.124), channel_id=1, source_target_pairs={{0,2},{2,0},{1,3},{3,1},{4,6},{6,4},{5,7},{7,5},{8,10},{10,8},{9,1... | collective-permute-start | bytes 786440 | tf_op jit(solution)/shard_map/ppermute | solution.py:305
  21.8 0.0 collective-permute-done.7.refs_7_
  21.8 0.0 collective-permute-done.5.refs_3_
  21.8 0.0 collective-permute-done.6.refs_5_
  21.8 5.4 %shard_map.123 = (bf16[512,128]{1,0:T(8,128)(2,1)S(1)}, bf16[512,128]{1,0:T(8,128)(2,1)S(1)}, bf16[1536,128]{1,0:T(8,128)(2,1)S(1)}, f32[48,1536]{1,0:T(8,128)S(1)}, f32[48,128]{1,0:T(8,128)S(1)}) custom-call(s32[6,16]{1,0:T(8,128)S(1)} %get-tuple-element.42.refs_0_, bf16[512,512]{1,0:T(8,128)(2,1)S(1)} %get-tuple-element.43.refs_1_, ...), custom_call_target="tpu_custom_call" | custom-call | bytes 1048576 | tf_op jit(solution)/shard_map/pallas_call | solution.py:292
  27.2 0.0 collective-permute-done.9.refs_15_
  27.2 5.5 %shard_map.125 = (bf16[512,128]{1,0:T(8,128)(2,1)S(1)}, bf16[512,128]{1,0:T(8,128)(2,1)S(1)}, bf16[48,256]{1,0:T(8,128)(2,1)S(1)}, bf16[48,256]{1,0:T(8,128)(2,1)S(1)}, bf16[48,256]{1,0:T(8,128)(2,1)S(1)}) custom-call(s32[6,16]{1,0:T(8,128)S(1)} %get-tuple-element.42.refs_0_, bf16[512,512]{1,0:T(8,128)(2,1)S(1)} %get-tuple-element.43.refs_1_, ...), custom_call_target="tpu_custom_call" | custom-call | flops 4000000000 | bytes 1048576 | tf_op jit(solution)/shard_map/pallas_call | solution.py:292
  32.7 0.1 collective-permute-start.10
  32.8 1.2 %collective-permute-done.10.sibling_ref = bf16[48,256]{1,0:T(8,128)(2,1)S(1)} collective-permute-done((bf16[48,256]{1,0:T(8,128)(2,1)S(1)}, bf16[48,256]{1,0:T(8,128)(2,1)S(1)}, u32[]{:S(2)}, u32[]{:S(2)}) %collective-permute-start.10) | collective-permute-done | bytes 24608 | tf_op jit(solution)/shard_map/ppermute | solution.py:305
  34.0 1.4 %collective-permute-start.11 = (bf16[48,512]{1,0:T(8,128)(2,1)S(1)}, bf16[48,512]{1,0:T(8,128)(2,1)S(1)}, u32[]{:S(2)}, u32[]{:S(2)}) collective-permute-start(bf16[48,512]{1,0:T(8,128)(2,1)S(1)} %shard_map.126), channel_id=1, source_target_pairs={{0,2},{2,0},{1,3},{3,1},{4,6},{6,4},{5,7},{7,5},{8,10},{10,8},{9,1... | collective-permute-start | bytes 147464 | tf_op jit(solution)/shard_map/ppermute | solution.py:305
  35.4 1.0 %shard_map.127 = (f32[512,256]{1,0:T(8,128)S(1)}, bf16[512,256]{1,0:T(8,128)(2,1)S(1)}) custom-call(s32[1,512]{1,0:T(1,128)S(1)} %get-tuple-element.60.order_ref, bf16[512,256]{1,0:T(8,128)(2,1)S(1)} %get-tuple-element.61.x_ref, bf16[512,128]{1,0:T(8,128)(2,1)S(1)} %get-tuple-element.62.att1_ref, bf16[512,128]{1,0:T(8,128)(2,1)S(1)} %get-tuple-element.63.att2_ref, ...), custom_call_target="tpu_custom_call" | custom-call | flops 1000000000 | bytes 1048576 | tf_op jit(solution)/shard_map/pallas_call | solution.py:292
  36.4 0.1 collective-permute-start.15
  36.5 1.6 %collective-permute-done.11 = bf16[48,512]{1,0:T(8,128)(2,1)S(1)} collective-permute-done((bf16[48,512]{1,0:T(8,128)(2,1)S(1)}, bf16[48,512]{1,0:T(8,128)(2,1)S(1)}, u32[]{:S(2)}, u32[]{:S(2)}) %collective-permute-start.11) | collective-permute-done | bytes 49184 | tf_op jit(solution)/shard_map/ppermute | solution.py:305
  38.1 2.6 %collective-permute-start.12 = (bf16[48,512]{1,0:T(8,128)(2,1)S(1)}, bf16[48,512]{1,0:T(8,128)(2,1)S(1)}, u32[]{:S(2)}, u32[]{:S(2)}) collective-permute-start(bf16[48,512]{1,0:T(8,128)(2,1)S(1)} %add_convert_fusion.1.refs_0_), channel_id=1, source_target_pairs={{0,4},{4,0},{8,12},{12,8},{1,5},{5,1},{9,13},{13,9},{2,6},{6,2},{1... | collective-permute-start | bytes 147464 | tf_op jit(solution)/shard_map/ppermute | solution.py:305
  40.7 0.8 %collective-permute-start.13 = (bf16[48,512]{1,0:T(8,128)(2,1)S(1)}, bf16[48,512]{1,0:T(8,128)(2,1)S(1)}, u32[]{:S(2)}, u32[]{:S(2)}) collective-permute-start(bf16[48,512]{1,0:T(8,128)(2,1)S(1)} %add_convert_fusion.1.refs_0_), channel_id=1, source_target_pairs={{0,8},{4,12},{8,0},{12,4},{1,9},{5,13},{9,1},{13,5},{2,10},{6,14},... | collective-permute-start | bytes 147464 | tf_op jit(solution)/shard_map/ppermute | solution.py:305
  41.5 1.6 %collective-permute-start.14 = (bf16[48,512]{1,0:T(8,128)(2,1)S(1)}, bf16[48,512]{1,0:T(8,128)(2,1)S(1)}, u32[]{:S(2)}, u32[]{:S(2)}) collective-permute-start(bf16[48,512]{1,0:T(8,128)(2,1)S(1)} %add_convert_fusion.1.refs_0_), channel_id=1, source_target_pairs={{0,12},{4,8},{8,4},{12,0},{1,13},{5,9},{9,5},{13,1},{2,14},{6,10},... | collective-permute-start | bytes 147464 | tf_op jit(solution)/shard_map/ppermute | solution.py:305
  43.2 0.0 collective-permute-done.15
  43.2 0.8 %fusion = bf16[1,512,256]{2,1,0:T(8,128)(2,1)} fusion(f32[512,256]{1,0:T(8,128)S(1)} %get-tuple-element.66, bf16[512,256]{1,0:T(8,128)(2,1)S(1)} %collective-permute-done.15), kind=kLoop, calls=%fused_computation.1 | loop fusion | flops 393216 | bytes 1048576 | tf_op jit(solution)/shard_map/broadcast_in_dim | solution.py:474
  44.0 0.0 collective-permute-done.12.refs_1_
  44.0 2.0 %collective-permute-done.13.refs_2_ = bf16[48,512]{1,0:T(8,128)(2,1)S(1)} collective-permute-done((bf16[48,512]{1,0:T(8,128)(2,1)S(1)}, bf16[48,512]{1,0:T(8,128)(2,1)S(1)}, u32[]{:S(2)}, u32[]{:S(2)}) %collective-permute-start.13) | collective-permute-done | bytes 49184 | tf_op jit(solution)/shard_map/ppermute | solution.py:305
  46.0 1.5 %collective-permute-done.14.refs_3_ = bf16[48,512]{1,0:T(8,128)(2,1)S(1)} collective-permute-done((bf16[48,512]{1,0:T(8,128)(2,1)S(1)}, bf16[48,512]{1,0:T(8,128)(2,1)S(1)}, u32[]{:S(2)}, u32[]{:S(2)}) %collective-permute-start.14) | collective-permute-done | bytes 49184 | tf_op jit(solution)/shard_map/ppermute | solution.py:305
  47.5 0.1 collective-permute-start.16
  47.5 1.2 %collective-permute-done.16.recv_ref = f32[48,256]{1,0:T(8,128)S(1)} collective-permute-done((f32[48,256]{1,0:T(8,128)S(1)}, f32[48,256]{1,0:T(8,128)S(1)}, u32[]{:S(2)}, u32[]{:S(2)}) %collective-permute-start.16) | collective-permute-done | bytes 49184 | tf_op jit(solution)/shard_map/ppermute | solution.py:305
  48.8 0.7 %shard_map.129 = (f32[48,512]{1,0:T(8,128)}, f32[48,256]{1,0:T(8,128)}) custom-call(f32[48,256]{1,0:T(8,128)S(1)} %get-tuple-element.73.own_ref, f32[48,256]{1,0:T(8,128)S(1)} %collective-permute-done.16.recv_ref, f32[48,256]{1,0:T(8,128)S(1)} %get-tuple-element.74.up_ref), custom_call_target="tpu_custom_call" | custom-call | bytes 1048576 | tf_op jit(solution)/shard_map/pallas_call | solution.py:292
  (4 shorter events, 0.1 us)
Async XLA Ops:
  1.7 10.5 %collective-permute-start.2 = (bf16[128,512]{1,0:T(8,128)(2,1)S(1)}, bf16[128,512]{1,0:T(8,128)(2,1)S(1)}, u32[]{:S(2)}, u32[]{:S(2)}) collective-permute-start(bf16[128,512]{1,0:T(8,128)(2,1)S(1)} %get-tuple-element.40.refs_10_), channel_id=1, source_target_pairs={{0,8},{4,12},{8,0},{12,4},{16,28},{20,24},{24,20},{28,16},{1,9},{5... | collective-permute-start | bytes 393224 | tf_op jit(solution)/shard_map/ppermute | solution.py:327
  5.8 6.8 %collective-permute-start.3 = (bf16[128,512]{1,0:T(8,128)(2,1)S(1)}, bf16[128,512]{1,0:T(8,128)(2,1)S(1)}, u32[]{:S(2)}, u32[]{:S(2)}) collective-permute-start(bf16[128,512]{1,0:T(8,128)(2,1)S(1)} %get-tuple-element.40.refs_10_), channel_id=1, source_target_pairs={{0,4},{4,0},{8,12},{12,8},{1,5},{5,1},{9,13},{13,9},{2,6},{6,2},{1... | collective-permute-start | bytes 393224 | tf_op jit(solution)/shard_map/ppermute | solution.py:305
  9.8 8.5 %collective-permute-start = (bf16[256,512]{1,0:T(8,128)(2,1)S(1)}, bf16[256,512]{1,0:T(8,128)(2,1)S(1)}, u32[]{:S(2)}, u32[]{:S(2)}) collective-permute-start(bf16[256,512]{1,0:T(8,128)(2,1)S(1)} %get-tuple-element.44), channel_id=1, source_target_pairs={{0,4},{4,0},{8,12},{12,8},{1,5},{5,1},{9,13},{13,9},{2,6},{6,2},{1... | collective-permute-start | bytes 786440 | tf_op jit(solution)/shard_map/ppermute | solution.py:305
  10.3 7.9 %collective-permute-start.1 = (bf16[256,512]{1,0:T(8,128)(2,1)S(1)}, bf16[256,512]{1,0:T(8,128)(2,1)S(1)}, u32[]{:S(2)}, u32[]{:S(2)}) collective-permute-start(bf16[256,512]{1,0:T(8,128)(2,1)S(1)} %get-tuple-element.44), channel_id=1, source_target_pairs={{0,0},{4,8},{8,4},{12,12},{1,1},{5,9},{9,5},{13,13},{2,2},{6,10},{... | collective-permute-start | bytes 786440 | tf_op jit(solution)/shard_map/ppermute | solution.py:407
  12.6 5.6 %collective-permute-start.4 = (bf16[128,512]{1,0:T(8,128)(2,1)S(1)}, bf16[128,512]{1,0:T(8,128)(2,1)S(1)}, u32[]{:S(2)}, u32[]{:S(2)}) collective-permute-start(bf16[128,512]{1,0:T(8,128)(2,1)S(1)} %collective-permute-done.2.refs_12_.one_ref), channel_id=1, source_target_pairs={{0,16},{16,0},{1,17},{17,1},{2,18},{18,2},{3,19},{19,3},{4,20},{20... | collective-permute-start | bytes 393224 | tf_op jit(solution)/shard_map/ppermute | solution.py:305
  15.3 5.0 %collective-permute-start.8 = (bf16[128,512]{1,0:T(8,128)(2,1)S(1)}, bf16[128,512]{1,0:T(8,128)(2,1)S(1)}, u32[]{:S(2)}, u32[]{:S(2)}) collective-permute-start(bf16[128,512]{1,0:T(8,128)(2,1)S(1)} %collective-permute-done.3.refs_11_), channel_id=1, source_target_pairs={{0,2},{2,0},{1,3},{3,1},{4,6},{6,4},{5,7},{7,5},{8,10},{10,8},{9,1... | collective-permute-start | bytes 393224 | tf_op jit(solution)/shard_map/ppermute | solution.py:305
  16.8 5.1 %collective-permute-start.7 = (bf16[512,256]{1,0:T(8,128)(2,1)S(1)}, bf16[512,256]{1,0:T(8,128)(2,1)S(1)}, u32[]{:S(2)}, u32[]{:S(2)}) collective-permute-start(bf16[512,256]{1,0:T(8,128)(2,1)S(1)} %get-tuple-element.48.refs_6_), channel_id=1, source_target_pairs={{0,1},{1,0},{2,3},{3,2},{4,5},{5,4},{6,7},{7,6},{8,9},{9,8},{10,11... | collective-permute-start | bytes 786440 | tf_op jit(solution)/shard_map/ppermute | solution.py:305
  18.2 3.6 %collective-permute-start.5 = (bf16[256,512]{1,0:T(8,128)(2,1)S(1)}, bf16[256,512]{1,0:T(8,128)(2,1)S(1)}, u32[]{:S(2)}, u32[]{:S(2)}) collective-permute-start(bf16[256,512]{1,0:T(8,128)(2,1)S(1)} %collective-permute-done.refs_2_), channel_id=1, source_target_pairs={{0,1},{1,0},{2,3},{3,2},{4,5},{5,4},{6,7},{7,6},{8,9},{9,8},{10,11... | collective-permute-start | bytes 786440 | tf_op jit(solution)/shard_map/ppermute | solution.py:305
  18.2 3.6 %collective-permute-start.6 = (bf16[256,512]{1,0:T(8,128)(2,1)S(1)}, bf16[256,512]{1,0:T(8,128)(2,1)S(1)}, u32[]{:S(2)}, u32[]{:S(2)}) collective-permute-start(bf16[256,512]{1,0:T(8,128)(2,1)S(1)} %collective-permute-done.1.refs_4_), channel_id=1, source_target_pairs={{0,1},{1,0},{2,3},{3,2},{4,5},{5,4},{6,7},{7,6},{8,9},{9,8},{10,11... | collective-permute-start | bytes 786440 | tf_op jit(solution)/shard_map/ppermute | solution.py:305
  20.3 6.9 %collective-permute-start.9 = (bf16[256,512]{1,0:T(8,128)(2,1)S(1)}, bf16[256,512]{1,0:T(8,128)(2,1)S(1)}, u32[]{:S(2)}, u32[]{:S(2)}) collective-permute-start(bf16[256,512]{1,0:T(8,128)(2,1)S(1)} %shard_map.124), channel_id=1, source_target_pairs={{0,2},{2,0},{1,3},{3,1},{4,6},{6,4},{5,7},{7,5},{8,10},{10,8},{9,1... | collective-permute-start | bytes 786440 | tf_op jit(solution)/shard_map/ppermute | solution.py:305
  32.7 1.3 %collective-permute-start.10 = (bf16[48,256]{1,0:T(8,128)(2,1)S(1)}, bf16[48,256]{1,0:T(8,128)(2,1)S(1)}, u32[]{:S(2)}, u32[]{:S(2)}) collective-permute-start(bf16[48,256]{1,0:T(8,128)(2,1)S(1)} %get-tuple-element.58), channel_id=1, source_target_pairs={{0,1},{1,0},{2,3},{3,2},{4,5},{5,4},{6,7},{7,6},{8,9},{9,8},{10,11... | collective-permute-start | bytes 73736 | tf_op jit(solution)/shard_map/ppermute | solution.py:305
  34.0 4.2 %collective-permute-start.11 = (bf16[48,512]{1,0:T(8,128)(2,1)S(1)}, bf16[48,512]{1,0:T(8,128)(2,1)S(1)}, u32[]{:S(2)}, u32[]{:S(2)}) collective-permute-start(bf16[48,512]{1,0:T(8,128)(2,1)S(1)} %shard_map.126), channel_id=1, source_target_pairs={{0,2},{2,0},{1,3},{3,1},{4,6},{6,4},{5,7},{7,5},{8,10},{10,8},{9,1... | collective-permute-start | bytes 147464 | tf_op jit(solution)/shard_map/ppermute | solution.py:305
  36.4 6.8 %collective-permute-start.15 = (bf16[512,256]{1,0:T(8,128)(2,1)S(1)}, bf16[512,256]{1,0:T(8,128)(2,1)S(1)}, u32[]{:S(2)}, u32[]{:S(2)}) collective-permute-start(bf16[512,256]{1,0:T(8,128)(2,1)S(1)} %get-tuple-element.67), channel_id=1, source_target_pairs={{0,1},{1,0},{2,3},{3,2},{4,5},{5,4},{6,7},{7,6},{8,9},{9,8},{10,11... | collective-permute-start | bytes 786440 | tf_op jit(solution)/shard_map/ppermute | solution.py:305
  38.1 5.8 %collective-permute-start.12 = (bf16[48,512]{1,0:T(8,128)(2,1)S(1)}, bf16[48,512]{1,0:T(8,128)(2,1)S(1)}, u32[]{:S(2)}, u32[]{:S(2)}) collective-permute-start(bf16[48,512]{1,0:T(8,128)(2,1)S(1)} %add_convert_fusion.1.refs_0_), channel_id=1, source_target_pairs={{0,4},{4,0},{8,12},{12,8},{1,5},{5,1},{9,13},{13,9},{2,6},{6,2},{1... | collective-permute-start | bytes 147464 | tf_op jit(solution)/shard_map/ppermute | solution.py:305
  40.7 5.2 %collective-permute-start.13 = (bf16[48,512]{1,0:T(8,128)(2,1)S(1)}, bf16[48,512]{1,0:T(8,128)(2,1)S(1)}, u32[]{:S(2)}, u32[]{:S(2)}) collective-permute-start(bf16[48,512]{1,0:T(8,128)(2,1)S(1)} %add_convert_fusion.1.refs_0_), channel_id=1, source_target_pairs={{0,8},{4,12},{8,0},{12,4},{1,9},{5,13},{9,1},{13,5},{2,10},{6,14},... | collective-permute-start | bytes 147464 | tf_op jit(solution)/shard_map/ppermute | solution.py:305
  41.5 5.9 %collective-permute-start.14 = (bf16[48,512]{1,0:T(8,128)(2,1)S(1)}, bf16[48,512]{1,0:T(8,128)(2,1)S(1)}, u32[]{:S(2)}, u32[]{:S(2)}) collective-permute-start(bf16[48,512]{1,0:T(8,128)(2,1)S(1)} %add_convert_fusion.1.refs_0_), channel_id=1, source_target_pairs={{0,12},{4,8},{8,4},{12,0},{1,13},{5,9},{9,5},{13,1},{2,14},{6,10},... | collective-permute-start | bytes 147464 | tf_op jit(solution)/shard_map/ppermute | solution.py:305
  47.5 1.3 %collective-permute-start.16 = (f32[48,256]{1,0:T(8,128)S(1)}, f32[48,256]{1,0:T(8,128)S(1)}, u32[]{:S(2)}, u32[]{:S(2)}) collective-permute-start(f32[48,256]{1,0:T(8,128)S(1)} %get-tuple-element.73.own_ref), channel_id=1, source_target_pairs={{0,1},{1,0},{2,3},{3,2},{4,5},{5,4},{6,7},{7,6},{8,9},{9,8},{10,11... | collective-permute-start | bytes 147464 | tf_op jit(solution)/shard_map/ppermute | solution.py:305

commit v8 on v7

--- a/solution.py
+++ b/solution.py
@@ -161,7 +161,7 @@
     table_copy.wait()
     odd = lax.rem(node, 2)
     left, right = 2 - odd, 1 + odd
-    all_starts = []
+    all_starts, all_valid = [], []
     for i in range(blocks):
         named = [table_ref[e, first + i] for e in range(table_ref.shape[0])]
         starts, valid = [], []
@@ -178,34 +178,51 @@
                 fresh = jnp.logical_and(fresh, c != before)
             valid.append(fresh)
         all_starts.append(starts)
-        own = slice(i * BLK, (i + 1) * BLK)
-        low_sel = jnp.concatenate([low_ref[pl.ds(s, BLK), :] for s in starts], axis=0)
-        keys = jnp.concatenate([kv_ref[pl.ds(s, BLK), :DH] for s in starts], axis=0)
-        values = jnp.concatenate([kv_ref[pl.ds(s, BLK), DH:] for s in starts], axis=0)
-        query, grad = q_ref[own, :], do_ref[own, :]
-        scores = nt(query, keys) * inverse_root
-        scores = jnp.concatenate(
+        all_valid.append(valid)
+
+    def chosen(ref, i, lanes=slice(None)):
+        return jnp.concatenate([ref[pl.ds(s, BLK), lanes] for s in all_starts[i]], axis=0)
+
+    def masked(scores, i):
+        return jnp.concatenate(
             [
                 jnp.where(ok, scores[:, e * BLK : (e + 1) * BLK], masked_value)
-                for e, ok in enumerate(valid)
+                for e, ok in enumerate(all_valid[i])
             ],
             axis=1,
         )
-        row_max = jnp.max(scores, axis=-1, keepdims=True)
-        weights = jnp.exp(scores - row_max)
-        prob = weights * (1.0 / jnp.sum(weights, axis=-1, keepdims=True))
-        prob_b = prob.astype(BF16)
-        mixed = nn(prob_b, jnp.concatenate([values, low_sel], axis=1))
-        attended = mixed[:, :DH].astype(BF16)
-        att_ref[own, :] = attended
-        t_ref[own, LOW:] = mixed[:, DH:].astype(BF16)
-        delta = jnp.sum(grad.astype(F32) * attended.astype(F32), axis=-1, keepdims=True)
-        score_grad = (prob * (nt(grad, values) - delta) * inverse_root).astype(BF16)
-        mixed = nn(score_grad, jnp.concatenate([keys, low_sel], axis=1))
-        dq_ref[own, :] = mixed[:, :DH].astype(BF16)
-        t_ref[own, :LOW] = mixed[:, DH:].astype(BF16)
-        back_ref[i, :RANK, :] = nn(query_up[:, own], score_grad)
-        back_ref[i, RANK:, :] = nn(grad_up[:, own], prob_b)
+
+    units = range(blocks)
+    own = [slice(i * BLK, (i + 1) * BLK) for i in units]
+    key_lanes, value_lanes = slice(0, DH), slice(DH, 2 * DH)
+    for base in range(0, blocks, 4):
+        some = range(base, base + 4)
+        scores = [
+            masked(nt(q_ref[own[i], :], chosen(kv_ref, i, key_lanes)) * inverse_root, i) for i in some
+        ]
+        prob_grads = [nt(do_ref[own[i], :], chosen(kv_ref, i, value_lanes)) for i in some]
+        probs, probs_b, score_grads = [], [], []
+        for score in scores:
+            weights = jnp.exp(score - jnp.max(score, axis=-1, keepdims=True))
+            prob = weights * (1.0 / jnp.sum(weights, axis=-1, keepdims=True))
+            probs.append(prob)
+            probs_b.append(prob.astype(BF16))
+        for i, prob, prob_b, prob_grad in zip(some, probs, probs_b, prob_grads):
+            rhs = jnp.concatenate([chosen(kv_ref, i, value_lanes), chosen(low_ref, i)], axis=1)
+            mixed = nn(prob_b, rhs)
+            attended = mixed[:, :DH].astype(BF16)
+            att_ref[own[i], :] = attended
+            t_ref[own[i], LOW:] = mixed[:, DH:].astype(BF16)
+            terms = do_ref[own[i], :].astype(F32) * attended.astype(F32)
+            delta = jnp.sum(terms, axis=-1, keepdims=True)
+            score_grads.append((prob * (prob_grad - delta) * inverse_root).astype(BF16))
+        for i, prob_b, score_grad in zip(some, probs_b, score_grads):
+            rhs = jnp.concatenate([chosen(kv_ref, i, key_lanes), chosen(low_ref, i)], axis=1)
+            mixed = nn(score_grad, rhs)
+            dq_ref[own[i], :] = mixed[:, :DH].astype(BF16)
+            t_ref[own[i], :LOW] = mixed[:, DH:].astype(BF16)
+            back_ref[i, :RANK, :] = nn(query_up[:, own[i]], score_grad)
+            back_ref[i, RANK:, :] = nn(grad_up[:, own[i]], prob_b)
 
     acc_ref[...] = acc_in[...] if which else jnp.zeros_like(acc_ref)
     acc_ref[:RANK, :rows] += nt(up_q, dq_ref[...])

time: 49.6 us -> 48 us (0.968)
  Pallas kernels: 16 us -> 12.8 us
  waiting for transfers between devices: 12.1 us -> 13.4 us
    pallas_call x9, Pallas kernels: 16 us -> 12.8 us  [call(): pl.pallas_call(kernel, out_shape=outs, in_specs=[HBM] * hbm + [VMEM] * (l...]
    ppermute x15, waiting for transfers between devices: 10.8 us -> 12.2 us  [swap(): return lax.ppermute(value, axis, [(i, i ^ step) for i in range(size)])]
  transfers between devices with their start and end apart: 17 -> 17, of which waited for: 9 -> 10; matrix products, arithmetic and copies ran while one was open for 2% -> 2% of each run, Pallas kernels for 18% -> 15%
where the time goes in v8:
time: 48 us; the launch traced here: 47.8 us
  starting transfers between devices  20.1 us (42%)
  waiting for transfers between devices  13.4 us (28%)
  Pallas kernels  12.8 us (27%)
  other arithmetic  0.78 us (2%)
  between operations  0.74 us (2%)
    ppermute x15, starting transfers between devices, swap(): return lax.ppermute(value, axis, [(i, i ^ step) for i in range(size)])  15.3 us
    pallas_call x9, Pallas kernels, call(): pl.pallas_call(kernel, out_shape=outs, in_specs=[HBM] * hbm + [VMEM] * (l...  12.8 us
    ppermute x15, waiting for transfers between devices, swap(): return lax.ppermute(value, axis, [(i, i ^ step) for i in range(size)])  12.2 us
    ppermute x1, starting transfers between devices, gather_weights(): far = lax.ppermute(first, ('group', 'node'), far_pairs)  4.1 us
    ppermute x1, waiting for transfers between devices, gather_weights(): far = lax.ppermute(first, ('group', 'node'), far_pairs)  1.27 us
  transfers between devices with their start and end apart: 17, of which 10 were waited for; matrix products, arithmetic and copies ran while one was open for 2% of the time, Pallas kernels for 15%

profile of v8, /device:TPU:0, one launch (start us, length us, event | category | flops | bytes accessed | tf_op | source)
XLA Modules:
  0.0 47.8 jit_solution(1836479028225077531)
XLA Ops:
  0.6 1.1 %shard_map.121 = (bf16[128,512]{1,0:T(8,128)(2,1)S(1)}, bf16[128,512]{1,0:T(8,128)(2,1)S(1)}) custom-call(bf16[128,256]{1,0:T(8,128)(2,1)} %refs_0_.1, bf16[128,256]{1,0:T(8,128)(2,1)} %refs_1_.1, bf16[128,256]{1,0:T(8,128)(2,1)} %refs_2_.1, bf16[256,128]{1,0:T(8,128)(2,1)} %refs_3_.1), custom_call_target="tpu_custom_call" | custom-call | bytes 1048576 | tf_op jit(solution)/shard_map/pallas_call | solution.py:309
  1.7 4.1 %collective-permute-start.2 = (bf16[128,512]{1,0:T(8,128)(2,1)S(1)}, bf16[128,512]{1,0:T(8,128)(2,1)S(1)}, u32[]{:S(2)}, u32[]{:S(2)}) collective-permute-start(bf16[128,512]{1,0:T(8,128)(2,1)S(1)} %get-tuple-element.40.refs_10_), channel_id=1, source_target_pairs={{0,8},{4,12},{8,0},{12,4},{16,28},{20,24},{24,20},{28,16},{1,9},{5... | collective-permute-start | bytes 393224 | tf_op jit(solution)/shard_map/ppermute | solution.py:344
  5.8 1.6 %collective-permute-start.3 = (bf16[128,512]{1,0:T(8,128)(2,1)S(1)}, bf16[128,512]{1,0:T(8,128)(2,1)S(1)}, u32[]{:S(2)}, u32[]{:S(2)}) collective-permute-start(bf16[128,512]{1,0:T(8,128)(2,1)S(1)} %get-tuple-element.40.refs_10_), channel_id=1, source_target_pairs={{0,4},{4,0},{8,12},{12,8},{1,5},{5,1},{9,13},{13,9},{2,6},{6,2},{1... | collective-permute-start | bytes 393224 | tf_op jit(solution)/shard_map/ppermute | solution.py:322
  7.4 2.4 %shard_map.122 = (s32[1,512]{1,0:T(1,128)S(1)}, s32[6,16]{1,0:T(8,128)S(1)}, bf16[48,512]{1,0:T(8,128)(2,1)S(1)}, bf16[48,256]{1,0:T(8,128)(2,1)S(1)}, bf16[512,...) custom-call(s32[1,512]{1,0:T(1,128)} %bitcast.21, ...), custom_call_target="tpu_custom_call" | custom-call | flops 402653184 | bytes 1048576 | tf_op jit(solution)/shard_map/pallas_call | solution.py:309
  9.8 0.5 %collective-permute-start = (bf16[256,512]{1,0:T(8,128)(2,1)S(1)}, bf16[256,512]{1,0:T(8,128)(2,1)S(1)}, u32[]{:S(2)}, u32[]{:S(2)}) collective-permute-start(bf16[256,512]{1,0:T(8,128)(2,1)S(1)} %get-tuple-element.44), channel_id=1, source_target_pairs={{0,4},{4,0},{8,12},{12,8},{1,5},{5,1},{9,13},{13,9},{2,6},{6,2},{1... | collective-permute-start | bytes 786440 | tf_op jit(solution)/shard_map/ppermute | solution.py:322
  10.3 0.7 %collective-permute-start.1 = (bf16[256,512]{1,0:T(8,128)(2,1)S(1)}, bf16[256,512]{1,0:T(8,128)(2,1)S(1)}, u32[]{:S(2)}, u32[]{:S(2)}) collective-permute-start(bf16[256,512]{1,0:T(8,128)(2,1)S(1)} %get-tuple-element.44), channel_id=1, source_target_pairs={{0,0},{4,8},{8,4},{12,12},{1,1},{5,9},{9,5},{13,13},{2,2},{6,10},{... | collective-permute-start | bytes 786440 | tf_op jit(solution)/shard_map/ppermute | solution.py:424
  10.9 1.3 %collective-permute-done.2.refs_12_.one_ref = bf16[128,512]{1,0:T(8,128)(2,1)S(1)} collective-permute-done((bf16[128,512]{1,0:T(8,128)(2,1)S(1)}, bf16[128,512]{1,0:T(8,128)(2,1)S(1)}, u32[]{:S(2)}, u32[]{:S(2)}) %collective-permute-start.2) | collective-permute-done | bytes 131104 | tf_op jit(solution)/shard_map/ppermute | solution.py:344
  12.2 0.3 collective-permute-done.3.refs_11_
  12.6 2.7 %collective-permute-start.4 = (bf16[128,512]{1,0:T(8,128)(2,1)S(1)}, bf16[128,512]{1,0:T(8,128)(2,1)S(1)}, u32[]{:S(2)}, u32[]{:S(2)}) collective-permute-start(bf16[128,512]{1,0:T(8,128)(2,1)S(1)} %collective-permute-done.2.refs_12_.one_ref), channel_id=1, source_target_pairs={{0,16},{16,0},{1,17},{17,1},{2,18},{18,2},{3,19},{19,3},{4,20},{20... | collective-permute-start | bytes 393224 | tf_op jit(solution)/shard_map/ppermute | solution.py:322
  15.3 1.5 %collective-permute-start.8 = (bf16[128,512]{1,0:T(8,128)(2,1)S(1)}, bf16[128,512]{1,0:T(8,128)(2,1)S(1)}, u32[]{:S(2)}, u32[]{:S(2)}) collective-permute-start(bf16[128,512]{1,0:T(8,128)(2,1)S(1)} %collective-permute-done.3.refs_11_), channel_id=1, source_target_pairs={{0,2},{2,0},{1,3},{3,1},{4,6},{6,4},{5,7},{7,5},{8,10},{10,8},{9,1... | collective-permute-start | bytes 393224 | tf_op jit(solution)/shard_map/ppermute | solution.py:322
  16.8 0.0 collective-permute-start.7
  16.8 1.4 %collective-permute-done.4.refs_13_.two_ref = bf16[128,512]{1,0:T(8,128)(2,1)S(1)} collective-permute-done((bf16[128,512]{1,0:T(8,128)(2,1)S(1)}, bf16[128,512]{1,0:T(8,128)(2,1)S(1)}, u32[]{:S(2)}, u32[]{:S(2)}) %collective-permute-start.4) | collective-permute-done | bytes 131104 | tf_op jit(solution)/shard_map/ppermute | solution.py:322
  18.2 0.0 collective-permute-done.refs_2_
  18.2 0.0 collective-permute-done.1.refs_4_
  18.2 0.0 collective-permute-start.5
  18.2 0.5 %collective-permute-start.6 = (bf16[256,512]{1,0:T(8,128)(2,1)S(1)}, bf16[256,512]{1,0:T(8,128)(2,1)S(1)}, u32[]{:S(2)}, u32[]{:S(2)}) collective-permute-start(bf16[256,512]{1,0:T(8,128)(2,1)S(1)} %collective-permute-done.1.refs_4_), channel_id=1, source_target_pairs={{0,1},{1,0},{2,3},{3,2},{4,5},{5,4},{6,7},{7,6},{8,9},{9,8},{10,11... | collective-permute-start | bytes 786440 | tf_op jit(solution)/shard_map/ppermute | solution.py:322
  18.7 1.5 %collective-permute-done.8.refs_14_ = bf16[128,512]{1,0:T(8,128)(2,1)S(1)} collective-permute-done((bf16[128,512]{1,0:T(8,128)(2,1)S(1)}, bf16[128,512]{1,0:T(8,128)(2,1)S(1)}, u32[]{:S(2)}, u32[]{:S(2)}) %collective-permute-start.8) | collective-permute-done | bytes 131104 | tf_op jit(solution)/shard_map/ppermute | solution.py:322
  20.3 1.6 %collective-permute-start.9 = (bf16[256,512]{1,0:T(8,128)(2,1)S(1)}, bf16[256,512]{1,0:T(8,128)(2,1)S(1)}, u32[]{:S(2)}, u32[]{:S(2)}) collective-permute-start(bf16[256,512]{1,0:T(8,128)(2,1)S(1)} %shard_map.124), channel_id=1, source_target_pairs={{0,2},{2,0},{1,3},{3,1},{4,6},{6,4},{5,7},{7,5},{8,10},{10,8},{9,1... | collective-permute-start | bytes 786440 | tf_op jit(solution)/shard_map/ppermute | solution.py:322
  21.8 0.0 collective-permute-done.7.refs_7_
  21.8 0.0 collective-permute-done.5.refs_3_
  21.8 0.0 collective-permute-done.6.refs_5_
  21.8 3.8 %shard_map.123 = (bf16[512,128]{1,0:T(8,128)(2,1)S(1)}, bf16[512,128]{1,0:T(8,128)(2,1)S(1)}, bf16[1536,128]{1,0:T(8,128)(2,1)S(1)}, f32[48,1536]{1,0:T(8,128)S(1)}, f32[48,128]{1,0:T(8,128)S(1)}) custom-call(s32[6,16]{1,0:T(8,128)S(1)} %get-tuple-element.42.refs_0_, bf16[512,512]{1,0:T(8,128)(2,1)S(1)} %get-tuple-element.43.refs_1_, ...), custom_call_target="tpu_custom_call" | custom-call | bytes 1048576 | tf_op jit(solution)/shard_map/pallas_call | solution.py:309
  25.6 1.5 %collective-permute-done.9.refs_15_ = bf16[256,512]{1,0:T(8,128)(2,1)S(1)} collective-permute-done((bf16[256,512]{1,0:T(8,128)(2,1)S(1)}, bf16[256,512]{1,0:T(8,128)(2,1)S(1)}, u32[]{:S(2)}, u32[]{:S(2)}) %collective-permute-start.9) | collective-permute-done | bytes 262176 | tf_op jit(solution)/shard_map/ppermute | solution.py:322
  27.1 3.8 %shard_map.125 = (bf16[512,128]{1,0:T(8,128)(2,1)S(1)}, bf16[512,128]{1,0:T(8,128)(2,1)S(1)}, bf16[48,256]{1,0:T(8,128)(2,1)S(1)}, bf16[48,256]{1,0:T(8,128)(2,1)S(1)}, bf16[48,256]{1,0:T(8,128)(2,1)S(1)}) custom-call(s32[6,16]{1,0:T(8,128)S(1)} %get-tuple-element.42.refs_0_, bf16[512,512]{1,0:T(8,128)(2,1)S(1)} %get-tuple-element.43.refs_1_, ...), custom_call_target="tpu_custom_call" | custom-call | flops 4000000000 | bytes 1048576 | tf_op jit(solution)/shard_map/pallas_call | solution.py:309
  31.0 0.1 collective-permute-start.10
  31.0 1.2 %collective-permute-done.10.sibling_ref = bf16[48,256]{1,0:T(8,128)(2,1)S(1)} collective-permute-done((bf16[48,256]{1,0:T(8,128)(2,1)S(1)}, bf16[48,256]{1,0:T(8,128)(2,1)S(1)}, u32[]{:S(2)}, u32[]{:S(2)}) %collective-permute-start.10) | collective-permute-done | bytes 24608 | tf_op jit(solution)/shard_map/ppermute | solution.py:322
  32.2 1.6 %collective-permute-start.11 = (bf16[48,512]{1,0:T(8,128)(2,1)S(1)}, bf16[48,512]{1,0:T(8,128)(2,1)S(1)}, u32[]{:S(2)}, u32[]{:S(2)}) collective-permute-start(bf16[48,512]{1,0:T(8,128)(2,1)S(1)} %shard_map.126), channel_id=1, source_target_pairs={{0,2},{2,0},{1,3},{3,1},{4,6},{6,4},{5,7},{7,5},{8,10},{10,8},{9,1... | collective-permute-start | bytes 147464 | tf_op jit(solution)/shard_map/ppermute | solution.py:322
  33.8 1.0 %shard_map.127 = (f32[512,256]{1,0:T(8,128)S(1)}, bf16[512,256]{1,0:T(8,128)(2,1)S(1)}) custom-call(s32[1,512]{1,0:T(1,128)S(1)} %get-tuple-element.60.order_ref, bf16[512,256]{1,0:T(8,128)(2,1)S(1)} %get-tuple-element.61.x_ref, bf16[512,128]{1,0:T(8,128)(2,1)S(1)} %get-tuple-element.62.att1_ref, bf16[512,128]{1,0:T(8,128)(2,1)S(1)} %get-tuple-element.63.att2_ref, ...), custom_call_target="tpu_custom_call" | custom-call | flops 1000000000 | bytes 1048576 | tf_op jit(solution)/shard_map/pallas_call | solution.py:309
  34.8 0.1 collective-permute-start.15
  34.9 1.5 %collective-permute-done.11 = bf16[48,512]{1,0:T(8,128)(2,1)S(1)} collective-permute-done((bf16[48,512]{1,0:T(8,128)(2,1)S(1)}, bf16[48,512]{1,0:T(8,128)(2,1)S(1)}, u32[]{:S(2)}, u32[]{:S(2)}) %collective-permute-start.11) | collective-permute-done | bytes 49184 | tf_op jit(solution)/shard_map/ppermute | solution.py:322
  36.4 2.7 %collective-permute-start.12 = (bf16[48,512]{1,0:T(8,128)(2,1)S(1)}, bf16[48,512]{1,0:T(8,128)(2,1)S(1)}, u32[]{:S(2)}, u32[]{:S(2)}) collective-permute-start(bf16[48,512]{1,0:T(8,128)(2,1)S(1)} %add_convert_fusion.1.refs_0_), channel_id=1, source_target_pairs={{0,4},{4,0},{8,12},{12,8},{1,5},{5,1},{9,13},{13,9},{2,6},{6,2},{1... | collective-permute-start | bytes 147464 | tf_op jit(solution)/shard_map/ppermute | solution.py:322
  39.1 0.8 %collective-permute-start.13 = (bf16[48,512]{1,0:T(8,128)(2,1)S(1)}, bf16[48,512]{1,0:T(8,128)(2,1)S(1)}, u32[]{:S(2)}, u32[]{:S(2)}) collective-permute-start(bf16[48,512]{1,0:T(8,128)(2,1)S(1)} %add_convert_fusion.1.refs_0_), channel_id=1, source_target_pairs={{0,8},{4,12},{8,0},{12,4},{1,9},{5,13},{9,1},{13,5},{2,10},{6,14},... | collective-permute-start | bytes 147464 | tf_op jit(solution)/shard_map/ppermute | solution.py:322
  39.9 1.6 %collective-permute-start.14 = (bf16[48,512]{1,0:T(8,128)(2,1)S(1)}, bf16[48,512]{1,0:T(8,128)(2,1)S(1)}, u32[]{:S(2)}, u32[]{:S(2)}) collective-permute-start(bf16[48,512]{1,0:T(8,128)(2,1)S(1)} %add_convert_fusion.1.refs_0_), channel_id=1, source_target_pairs={{0,12},{4,8},{8,4},{12,0},{1,13},{5,9},{9,5},{13,1},{2,14},{6,10},... | collective-permute-start | bytes 147464 | tf_op jit(solution)/shard_map/ppermute | solution.py:322
  41.6 0.0 collective-permute-done.15
  41.6 0.8 %fusion = bf16[1,512,256]{2,1,0:T(8,128)(2,1)} fusion(f32[512,256]{1,0:T(8,128)S(1)} %get-tuple-element.66, bf16[512,256]{1,0:T(8,128)(2,1)S(1)} %collective-permute-done.15), kind=kLoop, calls=%fused_computation.1 | loop fusion | flops 393216 | bytes 1048576 | tf_op jit(solution)/shard_map/broadcast_in_dim | solution.py:491
  42.4 0.0 collective-permute-done.12.refs_1_
  42.4 2.0 %collective-permute-done.13.refs_2_ = bf16[48,512]{1,0:T(8,128)(2,1)S(1)} collective-permute-done((bf16[48,512]{1,0:T(8,128)(2,1)S(1)}, bf16[48,512]{1,0:T(8,128)(2,1)S(1)}, u32[]{:S(2)}, u32[]{:S(2)}) %collective-permute-start.13) | collective-permute-done | bytes 49184 | tf_op jit(solution)/shard_map/ppermute | solution.py:322
  44.4 1.5 %collective-permute-done.14.refs_3_ = bf16[48,512]{1,0:T(8,128)(2,1)S(1)} collective-permute-done((bf16[48,512]{1,0:T(8,128)(2,1)S(1)}, bf16[48,512]{1,0:T(8,128)(2,1)S(1)}, u32[]{:S(2)}, u32[]{:S(2)}) %collective-permute-start.14) | collective-permute-done | bytes 49184 | tf_op jit(solution)/shard_map/ppermute | solution.py:322
  45.9 0.1 collective-permute-start.16
  45.9 1.2 %collective-permute-done.16.recv_ref = f32[48,256]{1,0:T(8,128)S(1)} collective-permute-done((f32[48,256]{1,0:T(8,128)S(1)}, f32[48,256]{1,0:T(8,128)S(1)}, u32[]{:S(2)}, u32[]{:S(2)}) %collective-permute-start.16) | collective-permute-done | bytes 49184 | tf_op jit(solution)/shard_map/ppermute | solution.py:322
  47.1 0.7 %shard_map.129 = (f32[48,512]{1,0:T(8,128)}, f32[48,256]{1,0:T(8,128)}) custom-call(f32[48,256]{1,0:T(8,128)S(1)} %get-tuple-element.73.own_ref, f32[48,256]{1,0:T(8,128)S(1)} %collective-permute-done.16.recv_ref, f32[48,256]{1,0:T(8,128)S(1)} %get-tuple-element.74.up_ref), custom_call_target="tpu_custom_call" | custom-call | bytes 1048576 | tf_op jit(solution)/shard_map/pallas_call | solution.py:309
  (4 shorter events, 0.1 us)
Async XLA Ops:
  1.7 10.5 %collective-permute-start.2 = (bf16[128,512]{1,0:T(8,128)(2,1)S(1)}, bf16[128,512]{1,0:T(8,128)(2,1)S(1)}, u32[]{:S(2)}, u32[]{:S(2)}) collective-permute-start(bf16[128,512]{1,0:T(8,128)(2,1)S(1)} %get-tuple-element.40.refs_10_), channel_id=1, source_target_pairs={{0,8},{4,12},{8,0},{12,4},{16,28},{20,24},{24,20},{28,16},{1,9},{5... | collective-permute-start | bytes 393224 | tf_op jit(solution)/shard_map/ppermute | solution.py:344
  5.8 6.8 %collective-permute-start.3 = (bf16[128,512]{1,0:T(8,128)(2,1)S(1)}, bf16[128,512]{1,0:T(8,128)(2,1)S(1)}, u32[]{:S(2)}, u32[]{:S(2)}) collective-permute-start(bf16[128,512]{1,0:T(8,128)(2,1)S(1)} %get-tuple-element.40.refs_10_), channel_id=1, source_target_pairs={{0,4},{4,0},{8,12},{12,8},{1,5},{5,1},{9,13},{13,9},{2,6},{6,2},{1... | collective-permute-start | bytes 393224 | tf_op jit(solution)/shard_map/ppermute | solution.py:322
  9.8 8.5 %collective-permute-start = (bf16[256,512]{1,0:T(8,128)(2,1)S(1)}, bf16[256,512]{1,0:T(8,128)(2,1)S(1)}, u32[]{:S(2)}, u32[]{:S(2)}) collective-permute-start(bf16[256,512]{1,0:T(8,128)(2,1)S(1)} %get-tuple-element.44), channel_id=1, source_target_pairs={{0,4},{4,0},{8,12},{12,8},{1,5},{5,1},{9,13},{13,9},{2,6},{6,2},{1... | collective-permute-start | bytes 786440 | tf_op jit(solution)/shard_map/ppermute | solution.py:322
  10.3 7.9 %collective-permute-start.1 = (bf16[256,512]{1,0:T(8,128)(2,1)S(1)}, bf16[256,512]{1,0:T(8,128)(2,1)S(1)}, u32[]{:S(2)}, u32[]{:S(2)}) collective-permute-start(bf16[256,512]{1,0:T(8,128)(2,1)S(1)} %get-tuple-element.44), channel_id=1, source_target_pairs={{0,0},{4,8},{8,4},{12,12},{1,1},{5,9},{9,5},{13,13},{2,2},{6,10},{... | collective-permute-start | bytes 786440 | tf_op jit(solution)/shard_map/ppermute | solution.py:424
  12.6 5.6 %collective-permute-start.4 = (bf16[128,512]{1,0:T(8,128)(2,1)S(1)}, bf16[128,512]{1,0:T(8,128)(2,1)S(1)}, u32[]{:S(2)}, u32[]{:S(2)}) collective-permute-start(bf16[128,512]{1,0:T(8,128)(2,1)S(1)} %collective-permute-done.2.refs_12_.one_ref), channel_id=1, source_target_pairs={{0,16},{16,0},{1,17},{17,1},{2,18},{18,2},{3,19},{19,3},{4,20},{20... | collective-permute-start | bytes 393224 | tf_op jit(solution)/shard_map/ppermute | solution.py:322
  15.3 5.0 %collective-permute-start.8 = (bf16[128,512]{1,0:T(8,128)(2,1)S(1)}, bf16[128,512]{1,0:T(8,128)(2,1)S(1)}, u32[]{:S(2)}, u32[]{:S(2)}) collective-permute-start(bf16[128,512]{1,0:T(8,128)(2,1)S(1)} %collective-permute-done.3.refs_11_), channel_id=1, source_target_pairs={{0,2},{2,0},{1,3},{3,1},{4,6},{6,4},{5,7},{7,5},{8,10},{10,8},{9,1... | collective-permute-start | bytes 393224 | tf_op jit(solution)/shard_map/ppermute | solution.py:322
  16.8 5.1 %collective-permute-start.7 = (bf16[512,256]{1,0:T(8,128)(2,1)S(1)}, bf16[512,256]{1,0:T(8,128)(2,1)S(1)}, u32[]{:S(2)}, u32[]{:S(2)}) collective-permute-start(bf16[512,256]{1,0:T(8,128)(2,1)S(1)} %get-tuple-element.48.refs_6_), channel_id=1, source_target_pairs={{0,1},{1,0},{2,3},{3,2},{4,5},{5,4},{6,7},{7,6},{8,9},{9,8},{10,11... | collective-permute-start | bytes 786440 | tf_op jit(solution)/shard_map/ppermute | solution.py:322
  18.2 3.6 %collective-permute-start.5 = (bf16[256,512]{1,0:T(8,128)(2,1)S(1)}, bf16[256,512]{1,0:T(8,128)(2,1)S(1)}, u32[]{:S(2)}, u32[]{:S(2)}) collective-permute-start(bf16[256,512]{1,0:T(8,128)(2,1)S(1)} %collective-permute-done.refs_2_), channel_id=1, source_target_pairs={{0,1},{1,0},{2,3},{3,2},{4,5},{5,4},{6,7},{7,6},{8,9},{9,8},{10,11... | collective-permute-start | bytes 786440 | tf_op jit(solution)/shard_map/ppermute | solution.py:322
  18.2 3.6 %collective-permute-start.6 = (bf16[256,512]{1,0:T(8,128)(2,1)S(1)}, bf16[256,512]{1,0:T(8,128)(2,1)S(1)}, u32[]{:S(2)}, u32[]{:S(2)}) collective-permute-start(bf16[256,512]{1,0:T(8,128)(2,1)S(1)} %collective-permute-done.1.refs_4_), channel_id=1, source_target_pairs={{0,1},{1,0},{2,3},{3,2},{4,5},{5,4},{6,7},{7,6},{8,9},{9,8},{10,11... | collective-permute-start | bytes 786440 | tf_op jit(solution)/shard_map/ppermute | solution.py:322
  20.3 6.8 %collective-permute-start.9 = (bf16[256,512]{1,0:T(8,128)(2,1)S(1)}, bf16[256,512]{1,0:T(8,128)(2,1)S(1)}, u32[]{:S(2)}, u32[]{:S(2)}) collective-permute-start(bf16[256,512]{1,0:T(8,128)(2,1)S(1)} %shard_map.124), channel_id=1, source_target_pairs={{0,2},{2,0},{1,3},{3,1},{4,6},{6,4},{5,7},{7,5},{8,10},{10,8},{9,1... | collective-permute-start | bytes 786440 | tf_op jit(solution)/shard_map/ppermute | solution.py:322
  31.0 1.3 %collective-permute-start.10 = (bf16[48,256]{1,0:T(8,128)(2,1)S(1)}, bf16[48,256]{1,0:T(8,128)(2,1)S(1)}, u32[]{:S(2)}, u32[]{:S(2)}) collective-permute-start(bf16[48,256]{1,0:T(8,128)(2,1)S(1)} %get-tuple-element.58), channel_id=1, source_target_pairs={{0,1},{1,0},{2,3},{3,2},{4,5},{5,4},{6,7},{7,6},{8,9},{9,8},{10,11... | collective-permute-start | bytes 73736 | tf_op jit(solution)/shard_map/ppermute | solution.py:322
  32.2 4.2 %collective-permute-start.11 = (bf16[48,512]{1,0:T(8,128)(2,1)S(1)}, bf16[48,512]{1,0:T(8,128)(2,1)S(1)}, u32[]{:S(2)}, u32[]{:S(2)}) collective-permute-start(bf16[48,512]{1,0:T(8,128)(2,1)S(1)} %shard_map.126), channel_id=1, source_target_pairs={{0,2},{2,0},{1,3},{3,1},{4,6},{6,4},{5,7},{7,5},{8,10},{10,8},{9,1... | collective-permute-start | bytes 147464 | tf_op jit(solution)/shard_map/ppermute | solution.py:322
  34.8 6.8 %collective-permute-start.15 = (bf16[512,256]{1,0:T(8,128)(2,1)S(1)}, bf16[512,256]{1,0:T(8,128)(2,1)S(1)}, u32[]{:S(2)}, u32[]{:S(2)}) collective-permute-start(bf16[512,256]{1,0:T(8,128)(2,1)S(1)} %get-tuple-element.67), channel_id=1, source_target_pairs={{0,1},{1,0},{2,3},{3,2},{4,5},{5,4},{6,7},{7,6},{8,9},{9,8},{10,11... | collective-permute-start | bytes 786440 | tf_op jit(solution)/shard_map/ppermute | solution.py:322
  36.4 5.9 %collective-permute-start.12 = (bf16[48,512]{1,0:T(8,128)(2,1)S(1)}, bf16[48,512]{1,0:T(8,128)(2,1)S(1)}, u32[]{:S(2)}, u32[]{:S(2)}) collective-permute-start(bf16[48,512]{1,0:T(8,128)(2,1)S(1)} %add_convert_fusion.1.refs_0_), channel_id=1, source_target_pairs={{0,4},{4,0},{8,12},{12,8},{1,5},{5,1},{9,13},{13,9},{2,6},{6,2},{1... | collective-permute-start | bytes 147464 | tf_op jit(solution)/shard_map/ppermute | solution.py:322
  39.1 5.2 %collective-permute-start.13 = (bf16[48,512]{1,0:T(8,128)(2,1)S(1)}, bf16[48,512]{1,0:T(8,128)(2,1)S(1)}, u32[]{:S(2)}, u32[]{:S(2)}) collective-permute-start(bf16[48,512]{1,0:T(8,128)(2,1)S(1)} %add_convert_fusion.1.refs_0_), channel_id=1, source_target_pairs={{0,8},{4,12},{8,0},{12,4},{1,9},{5,13},{9,1},{13,5},{2,10},{6,14},... | collective-permute-start | bytes 147464 | tf_op jit(solution)/shard_map/ppermute | solution.py:322
  39.9 5.9 %collective-permute-start.14 = (bf16[48,512]{1,0:T(8,128)(2,1)S(1)}, bf16[48,512]{1,0:T(8,128)(2,1)S(1)}, u32[]{:S(2)}, u32[]{:S(2)}) collective-permute-start(bf16[48,512]{1,0:T(8,128)(2,1)S(1)} %add_convert_fusion.1.refs_0_), channel_id=1, source_target_pairs={{0,12},{4,8},{8,4},{12,0},{1,13},{5,9},{9,5},{13,1},{2,14},{6,10},... | collective-permute-start | bytes 147464 | tf_op jit(solution)/shard_map/ppermute | solution.py:322
  45.9 1.3 %collective-permute-start.16 = (f32[48,256]{1,0:T(8,128)S(1)}, f32[48,256]{1,0:T(8,128)S(1)}, u32[]{:S(2)}, u32[]{:S(2)}) collective-permute-start(f32[48,256]{1,0:T(8,128)S(1)} %get-tuple-element.73.own_ref), channel_id=1, source_target_pairs={{0,1},{1,0},{2,3},{3,2},{4,5},{5,4},{6,7},{7,6},{8,9},{9,8},{10,11... | collective-permute-start | bytes 147464 | tf_op jit(solution)/shard_map/ppermute | solution.py:322

commit v9 on v8

--- a/solution.py
+++ b/solution.py
@@ -90,9 +90,9 @@
 
 
 def head_kernel(split, which, piece_rows, *refs):
-    table_vmem, normed_ref, a_own_ref, a_sib_ref, b_own_ref, b_sib_ref = refs[:6]
-    cot_own_ref, cot_sib_ref, down_ref, up_ref = refs[6:10]
-    rest, scratch = refs[10:-11], refs[-11:]
+    table_vmem, normed_ref, a_own_ref, a_sib_ref, a_sib2_ref = refs[:5]
+    b_own_ref, b_sib_ref, b_sib2_ref, cot_own_ref, cot_sib_ref, down_ref, up_ref = refs[5:12]
+    rest, scratch = refs[12:-11], refs[-11:]
     if which == 0:
         pieces, (att_ref, wo_ref, low_ref, acc_ref, up_out) = rest[:-5], rest[-5:]
     else:
@@ -127,20 +127,23 @@
         )
 
     segments = [
-        (normed_ref, 0),
-        (a_own_ref, pl.multiple_of(rows + core * half, half)),
-        (a_sib_ref, pl.multiple_of(rows + (1 - core) * half, half)),
-        (b_own_ref, pl.multiple_of(2 * rows + core * half, half)),
-        (b_sib_ref, pl.multiple_of(2 * rows + (1 - core) * half, half)),
+        ((normed_ref,), 0),
+        ((a_own_ref,), pl.multiple_of(rows + core * half, half)),
+        ((a_sib_ref, a_sib2_ref), pl.multiple_of(rows + (1 - core) * half, half)),
+        ((b_own_ref,), pl.multiple_of(2 * rows + core * half, half)),
+        ((b_sib_ref, b_sib2_ref), pl.multiple_of(2 * rows + (1 - core) * half, half)),
     ]
+    def rows_of(members):
+        return jnp.concatenate([m[...] for m in members], axis=0)
+
     if which == 0:
-        for member, start in segments:
-            low = nt(member[...], down_ref[...]).astype(BF16)
+        for members, start in segments:
+            low = nt(rows_of(members), down_ref[...]).astype(BF16)
             blank = jnp.zeros((low.shape[0], LOW - 3 * RANK), BF16)
             low_ref[pl.ds(start, low.shape[0]), :] = jnp.concatenate([low, blank], axis=1)
-    for j, (member, start) in enumerate(segments):
-        span = pl.ds(start, member.shape[0])
-        value = jnp.concatenate([member[...], low_ref[span, :]], axis=1)
+    for j, (members, start) in enumerate(segments):
+        span = pl.ds(start, half if j else rows)
+        value = jnp.concatenate([rows_of(members), low_ref[span, :]], axis=1)
         projected = nn(value, w_ref[:, (DH if j else 0) : 3 * DH]).astype(BF16)
         if j == 0:
             q_ref[...] = projected[:, :DH]
@@ -242,8 +245,8 @@
         return
     total = nn(acc_ref[:, :rows].astype(BF16), normed_ref[...])
     halo = jnp.zeros((2 * RANK, width), F32)
-    for member, start in segments[1:]:
-        halo += nn(acc_ref[RANK:, pl.ds(start, half)].astype(BF16), member[...])
+    for members, start in segments[1:]:
+        halo += nn(acc_ref[RANK:, pl.ds(start, half)].astype(BF16), rows_of(members))
     sum_ref = scratch[10]
     sum_ref[:RANK, :] = total[:RANK]
     sum_ref[RANK:, :] = total[RANK:] + halo
@@ -329,6 +332,12 @@
     return sorted(pairs.items())
 
 
+def split_kernel(a_ref, b_ref, *outs):
+    rows = outs[0].shape[0]
+    for out, (ref, start) in zip(outs, ((a_ref, 0), (a_ref, rows), (b_ref, 0), (b_ref, rows))):
+        out[...] = ref[start : start + rows, :]
+
+
 def pair_kernel(one_ref, two_ref, out_ref):
     depth = one_ref.shape[0]
     out_ref[:depth, :] = one_ref[...]
@@ -345,10 +354,9 @@
     near = swap(first, "node")
     far, near, _ = lax.optimization_barrier((far, near, half))
     other_far = swap(far, "group")
-    near_theirs = swap(near, "sample")
-    far_held, _ = lax.optimization_barrier((far, near_theirs))
-    pair = call(pair_kernel, (shape((2 * depth, 4 * DH)),), (far_held, other_far), limit=16)[0]
-    theirs = [second, near_theirs, swap(pair, "sample")]
+    pair = call(pair_kernel, (shape((2 * depth, 4 * DH)),), (near, far), limit=16)[0]
+    pair = swap(pair, "sample")
+    theirs = [second, pair, swap(other_far, "sample")]
 
     def piece_rows(node):
         group = lax.axis_index("group")
@@ -424,16 +432,18 @@
     b_own = lax.ppermute(half, "node", chain_pairs(lax.axis_size("node")))
     cot_sib = swap(cot_own, "head")
     a_half, b_half, _ = lax.optimization_barrier((a_own, b_own, late))
-    a_sib = swap(a_half, "head")
-    b_sib = swap(b_half, "head")
+    quarters = call(split_kernel, (shape((rows // 4, width)),) * 4, (a_half, b_half), limit=16)
+    a_sib, a_sib2, b_sib, b_sib2 = [swap(q, "head") for q in quarters]
 
     shared = (
         table,
         normed,
         a_own,
         a_sib,
+        a_sib2,
         b_own,
         b_sib,
+        b_sib2,
         cot_own,
         cot_sib,
         down,

time: 48 us -> 47 us (0.979)
  waiting for transfers between devices: 13.4 us -> 12.2 us
    ppermute x15 -> x17, waiting for transfers between devices: 12.2 us -> 11 us  [swap(): return lax.ppermute(value, axis, [(i, i ^ step) for i in range(size)])]
    ppermute x15 -> x17, starting transfers between devices: 15.3 us -> 15.5 us  [swap(): return lax.ppermute(value, axis, [(i, i ^ step) for i in range(size)])]
    pallas_call x9 -> x10, Pallas kernels: 12.8 us -> 12.8 us  [call(): pl.pallas_call(kernel, out_shape=outs, in_specs=[HBM] * hbm + [VMEM] * (l...]
  transfers between devices with their start and end apart: 17 -> 19, of which waited for: 10 -> 10; matrix products, arithmetic and copies ran while one was open for 2% -> 2% of each run, Pallas kernels for 15% -> 15%
where the time goes in v9:
time: 47 us; the launch traced here: 46.8 us
  starting transfers between devices  20.2 us (43%)
  Pallas kernels  12.8 us (27%)
  waiting for transfers between devices  12.2 us (26%)
  other arithmetic  0.78 us (2%)
  between operations  0.76 us (2%)
    ppermute x17, starting transfers between devices, swap(): return lax.ppermute(value, axis, [(i, i ^ step) for i in range(size)])  15.5 us
    pallas_call x10, Pallas kernels, call(): pl.pallas_call(kernel, out_shape=outs, in_specs=[HBM] * hbm + [VMEM] * (l...  12.8 us
    ppermute x17, waiting for transfers between devices, swap(): return lax.ppermute(value, axis, [(i, i ^ step) for i in range(size)])  11 us
    ppermute x1, starting transfers between devices, gather_weights(): far = lax.ppermute(first, ('group', 'node'), far_pairs)  4.1 us
    ppermute x1, waiting for transfers between devices, gather_weights(): far = lax.ppermute(first, ('group', 'node'), far_pairs)  1.27 us
  transfers between devices with their start and end apart: 19, of which 10 were waited for; matrix products, arithmetic and copies ran while one was open for 2% of the time, Pallas kernels for 15%

profile of v9, /device:TPU:0, one launch (start us, length us, event | category | flops | bytes accessed | tf_op | source)
XLA Modules:
  0.0 46.8 jit_solution(18333531675594048667)
XLA Ops:
  0.6 1.1 %shard_map.121 = (bf16[128,512]{1,0:T(8,128)(2,1)S(1)}, bf16[128,512]{1,0:T(8,128)(2,1)S(1)}) custom-call(bf16[128,256]{1,0:T(8,128)(2,1)} %refs_0_.1, bf16[128,256]{1,0:T(8,128)(2,1)} %refs_1_.1, bf16[128,256]{1,0:T(8,128)(2,1)} %refs_2_.1, bf16[256,128]{1,0:T(8,128)(2,1)} %refs_3_.1), custom_call_target="tpu_custom_call" | custom-call | bytes 1048576 | tf_op jit(solution)/shard_map/pallas_call | solution.py:312
  1.7 4.1 %collective-permute-start.2 = (bf16[128,512]{1,0:T(8,128)(2,1)S(1)}, bf16[128,512]{1,0:T(8,128)(2,1)S(1)}, u32[]{:S(2)}, u32[]{:S(2)}) collective-permute-start(bf16[128,512]{1,0:T(8,128)(2,1)S(1)} %get-tuple-element.43.refs_12_), channel_id=1, source_target_pairs={{0,8},{4,12},{8,0},{12,4},{16,28},{20,24},{24,20},{28,16},{1,9},{5... | collective-permute-start | bytes 393224 | tf_op jit(solution)/shard_map/ppermute | solution.py:353
  5.8 1.6 %collective-permute-start.3 = (bf16[128,512]{1,0:T(8,128)(2,1)S(1)}, bf16[128,512]{1,0:T(8,128)(2,1)S(1)}, u32[]{:S(2)}, u32[]{:S(2)}) collective-permute-start(bf16[128,512]{1,0:T(8,128)(2,1)S(1)} %get-tuple-element.43.refs_12_), channel_id=1, source_target_pairs={{0,4},{4,0},{8,12},{12,8},{1,5},{5,1},{9,13},{13,9},{2,6},{6,2},{1... | collective-permute-start | bytes 393224 | tf_op jit(solution)/shard_map/ppermute | solution.py:325
  7.4 2.4 %shard_map.122 = (s32[1,512]{1,0:T(1,128)S(1)}, s32[6,16]{1,0:T(8,128)S(1)}, bf16[48,512]{1,0:T(8,128)(2,1)S(1)}, bf16[48,256]{1,0:T(8,128)(2,1)S(1)}, bf16[512,...) custom-call(s32[1,512]{1,0:T(1,128)} %bitcast.21, ...), custom_call_target="tpu_custom_call" | custom-call | flops 402653184 | bytes 1048576 | tf_op jit(solution)/shard_map/pallas_call | solution.py:312
  9.8 0.5 %collective-permute-start = (bf16[256,512]{1,0:T(8,128)(2,1)S(1)}, bf16[256,512]{1,0:T(8,128)(2,1)S(1)}, u32[]{:S(2)}, u32[]{:S(2)}) collective-permute-start(bf16[256,512]{1,0:T(8,128)(2,1)S(1)} %get-tuple-element.47), channel_id=1, source_target_pairs={{0,4},{4,0},{8,12},{12,8},{1,5},{5,1},{9,13},{13,9},{2,6},{6,2},{1... | collective-permute-start | bytes 786440 | tf_op jit(solution)/shard_map/ppermute | solution.py:325
  10.3 0.7 %collective-permute-start.1 = (bf16[256,512]{1,0:T(8,128)(2,1)S(1)}, bf16[256,512]{1,0:T(8,128)(2,1)S(1)}, u32[]{:S(2)}, u32[]{:S(2)}) collective-permute-start(bf16[256,512]{1,0:T(8,128)(2,1)S(1)} %get-tuple-element.47), channel_id=1, source_target_pairs={{0,0},{4,8},{8,4},{12,12},{1,1},{5,9},{9,5},{13,13},{2,2},{6,10},{... | collective-permute-start | bytes 786440 | tf_op jit(solution)/shard_map/ppermute | solution.py:432
  10.9 1.3 %collective-permute-done.2.refs_14_.two_ref = bf16[128,512]{1,0:T(8,128)(2,1)S(1)} collective-permute-done((bf16[128,512]{1,0:T(8,128)(2,1)S(1)}, bf16[128,512]{1,0:T(8,128)(2,1)S(1)}, u32[]{:S(2)}, u32[]{:S(2)}) %collective-permute-start.2) | collective-permute-done | bytes 131104 | tf_op jit(solution)/shard_map/ppermute | solution.py:353
  12.2 0.3 collective-permute-done.3.refs_13_.one_ref
  12.6 2.7 %collective-permute-start.4 = (bf16[128,512]{1,0:T(8,128)(2,1)S(1)}, bf16[128,512]{1,0:T(8,128)(2,1)S(1)}, u32[]{:S(2)}, u32[]{:S(2)}) collective-permute-start(bf16[128,512]{1,0:T(8,128)(2,1)S(1)} %collective-permute-done.2.refs_14_.two_ref), channel_id=1, source_target_pairs={{0,16},{16,0},{1,17},{17,1},{2,18},{18,2},{3,19},{19,3},{4,20},{20... | collective-permute-start | bytes 393224 | tf_op jit(solution)/shard_map/ppermute | solution.py:325
  15.3 0.0 collective-permute-start.9
  15.3 1.6 %collective-permute-start.10 = (bf16[256,512]{1,0:T(8,128)(2,1)S(1)}, bf16[256,512]{1,0:T(8,128)(2,1)S(1)}, u32[]{:S(2)}, u32[]{:S(2)}) collective-permute-start(bf16[256,512]{1,0:T(8,128)(2,1)S(1)} %shard_map.125), channel_id=1, source_target_pairs={{0,2},{2,0},{1,3},{3,1},{4,6},{6,4},{5,7},{7,5},{8,10},{10,8},{9,1... | collective-permute-start | bytes 786440 | tf_op jit(solution)/shard_map/ppermute | solution.py:325
  16.9 1.4 %collective-permute-done.4.refs_15_ = bf16[128,512]{1,0:T(8,128)(2,1)S(1)} collective-permute-done((bf16[128,512]{1,0:T(8,128)(2,1)S(1)}, bf16[128,512]{1,0:T(8,128)(2,1)S(1)}, u32[]{:S(2)}, u32[]{:S(2)}) %collective-permute-start.4) | collective-permute-done | bytes 131104 | tf_op jit(solution)/shard_map/ppermute | solution.py:325
  18.2 0.0 collective-permute-done.a_ref.refs_2_
  18.2 0.0 collective-permute-done.1.b_ref.refs_5_
  18.3 0.1 collective-permute-start.5
  18.3 0.5 %collective-permute-start.6 = (bf16[128,512]{1,0:T(8,128)(2,1)S(1)}, bf16[128,512]{1,0:T(8,128)(2,1)S(1)}, u32[]{:S(2)}, u32[]{:S(2)}) collective-permute-start(bf16[128,512]{1,0:T(8,128)(2,1)S(1)} %get-tuple-element.52), channel_id=1, source_target_pairs={{0,1},{1,0},{2,3},{3,2},{4,5},{5,4},{6,7},{7,6},{8,9},{9,8},{10,11... | collective-permute-start | bytes 393224 | tf_op jit(solution)/shard_map/ppermute | solution.py:325
  18.8 0.1 collective-permute-start.7
  18.9 0.0 collective-permute-done.9.refs_9_
  18.9 0.4 collective-permute-start.8
  19.4 0.3 collective-permute-done.5.refs_3_
  19.7 1.5 %collective-permute-start.11 = (bf16[128,512]{1,0:T(8,128)(2,1)S(1)}, bf16[128,512]{1,0:T(8,128)(2,1)S(1)}, u32[]{:S(2)}, u32[]{:S(2)}) collective-permute-start(bf16[128,512]{1,0:T(8,128)(2,1)S(1)} %collective-permute-done.4.refs_15_), channel_id=1, source_target_pairs={{0,2},{2,0},{1,3},{3,1},{4,6},{6,4},{5,7},{7,5},{8,10},{10,8},{9,1... | collective-permute-start | bytes 393224 | tf_op jit(solution)/shard_map/ppermute | solution.py:325
  21.2 0.0 collective-permute-done.6.refs_4_
  21.2 0.0 collective-permute-done.7.refs_6_
  21.2 0.0 collective-permute-done.8.refs_7_
  21.2 3.8 %shard_map.124 = (bf16[512,128]{1,0:T(8,128)(2,1)S(1)}, bf16[512,128]{1,0:T(8,128)(2,1)S(1)}, bf16[1536,128]{1,0:T(8,128)(2,1)S(1)}, f32[48,1536]{1,0:T(8,128)S(1)}, f32[48,128]{1,0:T(8,128)S(1)}) custom-call(s32[6,16]{1,0:T(8,128)S(1)} %get-tuple-element.45.refs_0_, bf16[512,512]{1,0:T(8,128)(2,1)S(1)} %get-tuple-element.46.refs_1_, ...), custom_call_target="tpu_custom_call" | custom-call | bytes 1048576 | tf_op jit(solution)/shard_map/pallas_call | solution.py:312
  25.0 0.0 collective-permute-done.10.refs_16_
  25.0 1.9 %collective-permute-done.11.refs_17_ = bf16[128,512]{1,0:T(8,128)(2,1)S(1)} collective-permute-done((bf16[128,512]{1,0:T(8,128)(2,1)S(1)}, bf16[128,512]{1,0:T(8,128)(2,1)S(1)}, u32[]{:S(2)}, u32[]{:S(2)}) %collective-permute-start.11) | collective-permute-done | bytes 131104 | tf_op jit(solution)/shard_map/ppermute | solution.py:325
  26.9 3.8 %shard_map.126 = (bf16[512,128]{1,0:T(8,128)(2,1)S(1)}, bf16[512,128]{1,0:T(8,128)(2,1)S(1)}, bf16[48,256]{1,0:T(8,128)(2,1)S(1)}, bf16[48,256]{1,0:T(8,128)(2,1)S(1)}, bf16[48,256]{1,0:T(8,128)(2,1)S(1)}) custom-call(s32[6,16]{1,0:T(8,128)S(1)} %get-tuple-element.45.refs_0_, bf16[512,512]{1,0:T(8,128)(2,1)S(1)} %get-tuple-element.46.refs_1_, ...), custom_call_target="tpu_custom_call" | custom-call | flops 4000000000 | bytes 1048576 | tf_op jit(solution)/shard_map/pallas_call | solution.py:312
  30.7 0.1 collective-permute-start.12
  30.8 1.2 %collective-permute-done.12.sibling_ref = bf16[48,256]{1,0:T(8,128)(2,1)S(1)} collective-permute-done((bf16[48,256]{1,0:T(8,128)(2,1)S(1)}, bf16[48,256]{1,0:T(8,128)(2,1)S(1)}, u32[]{:S(2)}, u32[]{:S(2)}) %collective-permute-start.12) | collective-permute-done | bytes 24608 | tf_op jit(solution)/shard_map/ppermute | solution.py:325
  32.0 1.6 %collective-permute-start.13 = (bf16[48,512]{1,0:T(8,128)(2,1)S(1)}, bf16[48,512]{1,0:T(8,128)(2,1)S(1)}, u32[]{:S(2)}, u32[]{:S(2)}) collective-permute-start(bf16[48,512]{1,0:T(8,128)(2,1)S(1)} %shard_map.127), channel_id=1, source_target_pairs={{0,2},{2,0},{1,3},{3,1},{4,6},{6,4},{5,7},{7,5},{8,10},{10,8},{9,1... | collective-permute-start | bytes 147464 | tf_op jit(solution)/shard_map/ppermute | solution.py:325
  33.6 1.0 %shard_map.128 = (f32[512,256]{1,0:T(8,128)S(1)}, bf16[512,256]{1,0:T(8,128)(2,1)S(1)}) custom-call(s32[1,512]{1,0:T(1,128)S(1)} %get-tuple-element.66.order_ref, bf16[512,256]{1,0:T(8,128)(2,1)S(1)} %get-tuple-element.67.x_ref, bf16[512,128]{1,0:T(8,128)(2,1)S(1)} %get-tuple-element.68.att1_ref, bf16[512,128]{1,0:T(8,128)(2,1)S(1)} %get-tuple-element.69.att2_ref, ...), custom_call_target="tpu_custom_call" | custom-call | flops 1000000000 | bytes 1048576 | tf_op jit(solution)/shard_map/pallas_call | solution.py:312
  34.6 0.1 collective-permute-start.17
  34.7 1.5 %collective-permute-done.13 = bf16[48,512]{1,0:T(8,128)(2,1)S(1)} collective-permute-done((bf16[48,512]{1,0:T(8,128)(2,1)S(1)}, bf16[48,512]{1,0:T(8,128)(2,1)S(1)}, u32[]{:S(2)}, u32[]{:S(2)}) %collective-permute-start.13) | collective-permute-done | bytes 49184 | tf_op jit(solution)/shard_map/ppermute | solution.py:325
  36.2 2.3 %collective-permute-start.14 = (bf16[48,512]{1,0:T(8,128)(2,1)S(1)}, bf16[48,512]{1,0:T(8,128)(2,1)S(1)}, u32[]{:S(2)}, u32[]{:S(2)}) collective-permute-start(bf16[48,512]{1,0:T(8,128)(2,1)S(1)} %add_convert_fusion.1.refs_0_), channel_id=1, source_target_pairs={{0,4},{4,0},{8,12},{12,8},{1,5},{5,1},{9,13},{13,9},{2,6},{6,2},{1... | collective-permute-start | bytes 147464 | tf_op jit(solution)/shard_map/ppermute | solution.py:325
  38.5 0.4 collective-permute-start.15
  38.9 2.1 %collective-permute-start.16 = (bf16[48,512]{1,0:T(8,128)(2,1)S(1)}, bf16[48,512]{1,0:T(8,128)(2,1)S(1)}, u32[]{:S(2)}, u32[]{:S(2)}) collective-permute-start(bf16[48,512]{1,0:T(8,128)(2,1)S(1)} %add_convert_fusion.1.refs_0_), channel_id=1, source_target_pairs={{0,12},{4,8},{8,4},{12,0},{1,13},{5,9},{9,5},{13,1},{2,14},{6,10},... | collective-permute-start | bytes 147464 | tf_op jit(solution)/shard_map/ppermute | solution.py:325
  40.9 0.0 collective-permute-done.17
  40.9 0.8 %fusion = bf16[1,512,256]{2,1,0:T(8,128)(2,1)} fusion(f32[512,256]{1,0:T(8,128)S(1)} %get-tuple-element.72, bf16[512,256]{1,0:T(8,128)(2,1)S(1)} %collective-permute-done.17), kind=kLoop, calls=%fused_computation.1 | loop fusion | flops 393216 | bytes 1048576 | tf_op jit(solution)/shard_map/broadcast_in_dim | solution.py:501
  41.7 0.0 collective-permute-done.14.refs_1_
  41.7 2.1 %collective-permute-done.15.refs_2_ = bf16[48,512]{1,0:T(8,128)(2,1)S(1)} collective-permute-done((bf16[48,512]{1,0:T(8,128)(2,1)S(1)}, bf16[48,512]{1,0:T(8,128)(2,1)S(1)}, u32[]{:S(2)}, u32[]{:S(2)}) %collective-permute-start.15) | collective-permute-done | bytes 49184 | tf_op jit(solution)/shard_map/ppermute | solution.py:325
  43.8 1.1 %collective-permute-done.16.refs_3_ = bf16[48,512]{1,0:T(8,128)(2,1)S(1)} collective-permute-done((bf16[48,512]{1,0:T(8,128)(2,1)S(1)}, bf16[48,512]{1,0:T(8,128)(2,1)S(1)}, u32[]{:S(2)}, u32[]{:S(2)}) %collective-permute-start.16) | collective-permute-done | bytes 49184 | tf_op jit(solution)/shard_map/ppermute | solution.py:325
  44.9 0.1 collective-permute-start.18
  44.9 1.2 %collective-permute-done.18.recv_ref = f32[48,256]{1,0:T(8,128)S(1)} collective-permute-done((f32[48,256]{1,0:T(8,128)S(1)}, f32[48,256]{1,0:T(8,128)S(1)}, u32[]{:S(2)}, u32[]{:S(2)}) %collective-permute-start.18) | collective-permute-done | bytes 49184 | tf_op jit(solution)/shard_map/ppermute | solution.py:325
  46.2 0.7 %shard_map.130 = (f32[48,512]{1,0:T(8,128)}, f32[48,256]{1,0:T(8,128)}) custom-call(f32[48,256]{1,0:T(8,128)S(1)} %get-tuple-element.79.own_ref, f32[48,256]{1,0:T(8,128)S(1)} %collective-permute-done.18.recv_ref, f32[48,256]{1,0:T(8,128)S(1)} %get-tuple-element.80.up_ref), custom_call_target="tpu_custom_call" | custom-call | bytes 1048576 | tf_op jit(solution)/shard_map/pallas_call | solution.py:312
  (5 shorter events, 0.1 us)
Async XLA Ops:
  1.7 10.5 %collective-permute-start.2 = (bf16[128,512]{1,0:T(8,128)(2,1)S(1)}, bf16[128,512]{1,0:T(8,128)(2,1)S(1)}, u32[]{:S(2)}, u32[]{:S(2)}) collective-permute-start(bf16[128,512]{1,0:T(8,128)(2,1)S(1)} %get-tuple-element.43.refs_12_), channel_id=1, source_target_pairs={{0,8},{4,12},{8,0},{12,4},{16,28},{20,24},{24,20},{28,16},{1,9},{5... | collective-permute-start | bytes 393224 | tf_op jit(solution)/shard_map/ppermute | solution.py:353
  5.8 6.8 %collective-permute-start.3 = (bf16[128,512]{1,0:T(8,128)(2,1)S(1)}, bf16[128,512]{1,0:T(8,128)(2,1)S(1)}, u32[]{:S(2)}, u32[]{:S(2)}) collective-permute-start(bf16[128,512]{1,0:T(8,128)(2,1)S(1)} %get-tuple-element.43.refs_12_), channel_id=1, source_target_pairs={{0,4},{4,0},{8,12},{12,8},{1,5},{5,1},{9,13},{13,9},{2,6},{6,2},{1... | collective-permute-start | bytes 393224 | tf_op jit(solution)/shard_map/ppermute | solution.py:325
  9.8 8.5 %collective-permute-start = (bf16[256,512]{1,0:T(8,128)(2,1)S(1)}, bf16[256,512]{1,0:T(8,128)(2,1)S(1)}, u32[]{:S(2)}, u32[]{:S(2)}) collective-permute-start(bf16[256,512]{1,0:T(8,128)(2,1)S(1)} %get-tuple-element.47), channel_id=1, source_target_pairs={{0,4},{4,0},{8,12},{12,8},{1,5},{5,1},{9,13},{13,9},{2,6},{6,2},{1... | collective-permute-start | bytes 786440 | tf_op jit(solution)/shard_map/ppermute | solution.py:325
  10.3 7.9 %collective-permute-start.1 = (bf16[256,512]{1,0:T(8,128)(2,1)S(1)}, bf16[256,512]{1,0:T(8,128)(2,1)S(1)}, u32[]{:S(2)}, u32[]{:S(2)}) collective-permute-start(bf16[256,512]{1,0:T(8,128)(2,1)S(1)} %get-tuple-element.47), channel_id=1, source_target_pairs={{0,0},{4,8},{8,4},{12,12},{1,1},{5,9},{9,5},{13,13},{2,2},{6,10},{... | collective-permute-start | bytes 786440 | tf_op jit(solution)/shard_map/ppermute | solution.py:432
  12.6 5.6 %collective-permute-start.4 = (bf16[128,512]{1,0:T(8,128)(2,1)S(1)}, bf16[128,512]{1,0:T(8,128)(2,1)S(1)}, u32[]{:S(2)}, u32[]{:S(2)}) collective-permute-start(bf16[128,512]{1,0:T(8,128)(2,1)S(1)} %collective-permute-done.2.refs_14_.two_ref), channel_id=1, source_target_pairs={{0,16},{16,0},{1,17},{17,1},{2,18},{18,2},{3,19},{19,3},{4,20},{20... | collective-permute-start | bytes 393224 | tf_op jit(solution)/shard_map/ppermute | solution.py:325
  15.3 3.6 %collective-permute-start.9 = (bf16[512,256]{1,0:T(8,128)(2,1)S(1)}, bf16[512,256]{1,0:T(8,128)(2,1)S(1)}, u32[]{:S(2)}, u32[]{:S(2)}) collective-permute-start(bf16[512,256]{1,0:T(8,128)(2,1)S(1)} %get-tuple-element.55.refs_8_), channel_id=1, source_target_pairs={{0,1},{1,0},{2,3},{3,2},{4,5},{5,4},{6,7},{7,6},{8,9},{9,8},{10,11... | collective-permute-start | bytes 786440 | tf_op jit(solution)/shard_map/ppermute | solution.py:325
  15.3 9.7 %collective-permute-start.10 = (bf16[256,512]{1,0:T(8,128)(2,1)S(1)}, bf16[256,512]{1,0:T(8,128)(2,1)S(1)}, u32[]{:S(2)}, u32[]{:S(2)}) collective-permute-start(bf16[256,512]{1,0:T(8,128)(2,1)S(1)} %shard_map.125), channel_id=1, source_target_pairs={{0,2},{2,0},{1,3},{3,1},{4,6},{6,4},{5,7},{7,5},{8,10},{10,8},{9,1... | collective-permute-start | bytes 786440 | tf_op jit(solution)/shard_map/ppermute | solution.py:325
  18.3 1.4 %collective-permute-start.5 = (bf16[128,512]{1,0:T(8,128)(2,1)S(1)}, bf16[128,512]{1,0:T(8,128)(2,1)S(1)}, u32[]{:S(2)}, u32[]{:S(2)}) collective-permute-start(bf16[128,512]{1,0:T(8,128)(2,1)S(1)} %get-tuple-element.51), channel_id=1, source_target_pairs={{0,1},{1,0},{2,3},{3,2},{4,5},{5,4},{6,7},{7,6},{8,9},{9,8},{10,11... | collective-permute-start | bytes 393224 | tf_op jit(solution)/shard_map/ppermute | solution.py:325
  18.3 2.8 %collective-permute-start.6 = (bf16[128,512]{1,0:T(8,128)(2,1)S(1)}, bf16[128,512]{1,0:T(8,128)(2,1)S(1)}, u32[]{:S(2)}, u32[]{:S(2)}) collective-permute-start(bf16[128,512]{1,0:T(8,128)(2,1)S(1)} %get-tuple-element.52), channel_id=1, source_target_pairs={{0,1},{1,0},{2,3},{3,2},{4,5},{5,4},{6,7},{7,6},{8,9},{9,8},{10,11... | collective-permute-start | bytes 393224 | tf_op jit(solution)/shard_map/ppermute | solution.py:325
  18.8 2.3 %collective-permute-start.7 = (bf16[128,512]{1,0:T(8,128)(2,1)S(1)}, bf16[128,512]{1,0:T(8,128)(2,1)S(1)}, u32[]{:S(2)}, u32[]{:S(2)}) collective-permute-start(bf16[128,512]{1,0:T(8,128)(2,1)S(1)} %get-tuple-element.53), channel_id=1, source_target_pairs={{0,1},{1,0},{2,3},{3,2},{4,5},{5,4},{6,7},{7,6},{8,9},{9,8},{10,11... | collective-permute-start | bytes 393224 | tf_op jit(solution)/shard_map/ppermute | solution.py:325
  18.9 2.3 %collective-permute-start.8 = (bf16[128,512]{1,0:T(8,128)(2,1)S(1)}, bf16[128,512]{1,0:T(8,128)(2,1)S(1)}, u32[]{:S(2)}, u32[]{:S(2)}) collective-permute-start(bf16[128,512]{1,0:T(8,128)(2,1)S(1)} %get-tuple-element.54), channel_id=1, source_target_pairs={{0,1},{1,0},{2,3},{3,2},{4,5},{5,4},{6,7},{7,6},{8,9},{9,8},{10,11... | collective-permute-start | bytes 393224 | tf_op jit(solution)/shard_map/ppermute | solution.py:325
  19.7 7.2 %collective-permute-start.11 = (bf16[128,512]{1,0:T(8,128)(2,1)S(1)}, bf16[128,512]{1,0:T(8,128)(2,1)S(1)}, u32[]{:S(2)}, u32[]{:S(2)}) collective-permute-start(bf16[128,512]{1,0:T(8,128)(2,1)S(1)} %collective-permute-done.4.refs_15_), channel_id=1, source_target_pairs={{0,2},{2,0},{1,3},{3,1},{4,6},{6,4},{5,7},{7,5},{8,10},{10,8},{9,1... | collective-permute-start | bytes 393224 | tf_op jit(solution)/shard_map/ppermute | solution.py:325
  30.7 1.3 %collective-permute-start.12 = (bf16[48,256]{1,0:T(8,128)(2,1)S(1)}, bf16[48,256]{1,0:T(8,128)(2,1)S(1)}, u32[]{:S(2)}, u32[]{:S(2)}) collective-permute-start(bf16[48,256]{1,0:T(8,128)(2,1)S(1)} %get-tuple-element.64), channel_id=1, source_target_pairs={{0,1},{1,0},{2,3},{3,2},{4,5},{5,4},{6,7},{7,6},{8,9},{9,8},{10,11... | collective-permute-start | bytes 73736 | tf_op jit(solution)/shard_map/ppermute | solution.py:325
  32.0 4.2 %collective-permute-start.13 = (bf16[48,512]{1,0:T(8,128)(2,1)S(1)}, bf16[48,512]{1,0:T(8,128)(2,1)S(1)}, u32[]{:S(2)}, u32[]{:S(2)}) collective-permute-start(bf16[48,512]{1,0:T(8,128)(2,1)S(1)} %shard_map.127), channel_id=1, source_target_pairs={{0,2},{2,0},{1,3},{3,1},{4,6},{6,4},{5,7},{7,5},{8,10},{10,8},{9,1... | collective-permute-start | bytes 147464 | tf_op jit(solution)/shard_map/ppermute | solution.py:325
  34.6 6.4 %collective-permute-start.17 = (bf16[512,256]{1,0:T(8,128)(2,1)S(1)}, bf16[512,256]{1,0:T(8,128)(2,1)S(1)}, u32[]{:S(2)}, u32[]{:S(2)}) collective-permute-start(bf16[512,256]{1,0:T(8,128)(2,1)S(1)} %get-tuple-element.73), channel_id=1, source_target_pairs={{0,1},{1,0},{2,3},{3,2},{4,5},{5,4},{6,7},{7,6},{8,9},{9,8},{10,11... | collective-permute-start | bytes 786440 | tf_op jit(solution)/shard_map/ppermute | solution.py:325
  36.2 5.5 %collective-permute-start.14 = (bf16[48,512]{1,0:T(8,128)(2,1)S(1)}, bf16[48,512]{1,0:T(8,128)(2,1)S(1)}, u32[]{:S(2)}, u32[]{:S(2)}) collective-permute-start(bf16[48,512]{1,0:T(8,128)(2,1)S(1)} %add_convert_fusion.1.refs_0_), channel_id=1, source_target_pairs={{0,4},{4,0},{8,12},{12,8},{1,5},{5,1},{9,13},{13,9},{2,6},{6,2},{1... | collective-permute-start | bytes 147464 | tf_op jit(solution)/shard_map/ppermute | solution.py:325
  38.5 5.3 %collective-permute-start.15 = (bf16[48,512]{1,0:T(8,128)(2,1)S(1)}, bf16[48,512]{1,0:T(8,128)(2,1)S(1)}, u32[]{:S(2)}, u32[]{:S(2)}) collective-permute-start(bf16[48,512]{1,0:T(8,128)(2,1)S(1)} %add_convert_fusion.1.refs_0_), channel_id=1, source_target_pairs={{0,8},{4,12},{8,0},{12,4},{1,9},{5,13},{9,1},{13,5},{2,10},{6,14},... | collective-permute-start | bytes 147464 | tf_op jit(solution)/shard_map/ppermute | solution.py:325
  38.9 6.0 %collective-permute-start.16 = (bf16[48,512]{1,0:T(8,128)(2,1)S(1)}, bf16[48,512]{1,0:T(8,128)(2,1)S(1)}, u32[]{:S(2)}, u32[]{:S(2)}) collective-permute-start(bf16[48,512]{1,0:T(8,128)(2,1)S(1)} %add_convert_fusion.1.refs_0_), channel_id=1, source_target_pairs={{0,12},{4,8},{8,4},{12,0},{1,13},{5,9},{9,5},{13,1},{2,14},{6,10},... | collective-permute-start | bytes 147464 | tf_op jit(solution)/shard_map/ppermute | solution.py:325
  44.9 1.3 %collective-permute-start.18 = (f32[48,256]{1,0:T(8,128)S(1)}, f32[48,256]{1,0:T(8,128)S(1)}, u32[]{:S(2)}, u32[]{:S(2)}) collective-permute-start(f32[48,256]{1,0:T(8,128)S(1)} %get-tuple-element.79.own_ref), channel_id=1, source_target_pairs={{0,1},{1,0},{2,3},{3,2},{4,5},{5,4},{6,7},{7,6},{8,9},{9,8},{10,11... | collective-permute-start | bytes 147464 | tf_op jit(solution)/shard_map/ppermute | solution.py:325

commit v10 on v9

--- a/solution.py
+++ b/solution.py
@@ -507,7 +507,7 @@
         hops += [("node", 1 << i) for i in range(count.bit_length() - 2)]
     for axis, step in hops:
         lora = (lora.astype(F32) + swap(lora, axis, step).astype(F32)).astype(BF16)
-    steps = (1, 2, 3) if count == 4 else (count // 2,)
+    steps = (3, 2, 1) if count == 4 else (count // 2,)
     terms = (lora, *[swap(lora, "node", k) for k in steps])
     terms, mesh_out = lax.optimization_barrier((terms, mesh_out))
     down_half, up_total = call(

time: 47 us -> 46.5 us (0.989)
  transfers between devices with their start and end apart: 19 -> 19, of which waited for: 10 -> 11; matrix products, arithmetic and copies ran while one was open for 2% -> 2% of each run, Pallas kernels for 15% -> 16%
where the time goes in v10:
time: 46.5 us; the launch traced here: 46.3 us
  starting transfers between devices  19.9 us (43%)
  Pallas kernels  12.8 us (28%)
  waiting for transfers between devices  12 us (26%)
  other arithmetic  0.78 us (2%)
  between operations  0.76 us (2%)
    ppermute x17, starting transfers between devices, swap(): return lax.ppermute(value, axis, [(i, i ^ step) for i in range(size)])  15.1 us
    pallas_call x10, Pallas kernels, call(): pl.pallas_call(kernel, out_shape=outs, in_specs=[HBM] * hbm + [VMEM] * (l...  12.8 us
    ppermute x17, waiting for transfers between devices, swap(): return lax.ppermute(value, axis, [(i, i ^ step) for i in range(size)])  10.7 us
    ppermute x1, starting transfers between devices, gather_weights(): far = lax.ppermute(first, ('group', 'node'), far_pairs)  4.1 us
    ppermute x1, waiting for transfers between devices, gather_weights(): far = lax.ppermute(first, ('group', 'node'), far_pairs)  1.27 us
  transfers between devices with their start and end apart: 19, of which 11 were waited for; matrix products, arithmetic and copies ran while one was open for 2% of the time, Pallas kernels for 16%

profile of v10, /device:TPU:0, one launch (start us, length us, event | category | flops | bytes accessed | tf_op | source)
XLA Modules:
  0.0 46.3 jit_solution(12181433450008571191)
XLA Ops:
  0.6 1.1 %shard_map.121 = (bf16[128,512]{1,0:T(8,128)(2,1)S(1)}, bf16[128,512]{1,0:T(8,128)(2,1)S(1)}) custom-call(bf16[128,256]{1,0:T(8,128)(2,1)} %refs_0_.1, bf16[128,256]{1,0:T(8,128)(2,1)} %refs_1_.1, bf16[128,256]{1,0:T(8,128)(2,1)} %refs_2_.1, bf16[256,128]{1,0:T(8,128)(2,1)} %refs_3_.1), custom_call_target="tpu_custom_call" | custom-call | bytes 1048576 | tf_op jit(solution)/shard_map/pallas_call | solution.py:312
  1.7 4.1 %collective-permute-start.2 = (bf16[128,512]{1,0:T(8,128)(2,1)S(1)}, bf16[128,512]{1,0:T(8,128)(2,1)S(1)}, u32[]{:S(2)}, u32[]{:S(2)}) collective-permute-start(bf16[128,512]{1,0:T(8,128)(2,1)S(1)} %get-tuple-element.43.refs_12_), channel_id=1, source_target_pairs={{0,8},{4,12},{8,0},{12,4},{16,28},{20,24},{24,20},{28,16},{1,9},{5... | collective-permute-start | bytes 393224 | tf_op jit(solution)/shard_map/ppermute | solution.py:353
  5.8 1.6 %collective-permute-start.3 = (bf16[128,512]{1,0:T(8,128)(2,1)S(1)}, bf16[128,512]{1,0:T(8,128)(2,1)S(1)}, u32[]{:S(2)}, u32[]{:S(2)}) collective-permute-start(bf16[128,512]{1,0:T(8,128)(2,1)S(1)} %get-tuple-element.43.refs_12_), channel_id=1, source_target_pairs={{0,4},{4,0},{8,12},{12,8},{1,5},{5,1},{9,13},{13,9},{2,6},{6,2},{1... | collective-permute-start | bytes 393224 | tf_op jit(solution)/shard_map/ppermute | solution.py:325
  7.4 2.4 %shard_map.122 = (s32[1,512]{1,0:T(1,128)S(1)}, s32[6,16]{1,0:T(8,128)S(1)}, bf16[48,512]{1,0:T(8,128)(2,1)S(1)}, bf16[48,256]{1,0:T(8,128)(2,1)S(1)}, bf16[512,...) custom-call(s32[1,512]{1,0:T(1,128)} %bitcast.21, ...), custom_call_target="tpu_custom_call" | custom-call | flops 402653184 | bytes 1048576 | tf_op jit(solution)/shard_map/pallas_call | solution.py:312
  9.8 0.5 %collective-permute-start = (bf16[256,512]{1,0:T(8,128)(2,1)S(1)}, bf16[256,512]{1,0:T(8,128)(2,1)S(1)}, u32[]{:S(2)}, u32[]{:S(2)}) collective-permute-start(bf16[256,512]{1,0:T(8,128)(2,1)S(1)} %get-tuple-element.47), channel_id=1, source_target_pairs={{0,4},{4,0},{8,12},{12,8},{1,5},{5,1},{9,13},{13,9},{2,6},{6,2},{1... | collective-permute-start | bytes 786440 | tf_op jit(solution)/shard_map/ppermute | solution.py:325
  10.3 0.7 %collective-permute-start.1 = (bf16[256,512]{1,0:T(8,128)(2,1)S(1)}, bf16[256,512]{1,0:T(8,128)(2,1)S(1)}, u32[]{:S(2)}, u32[]{:S(2)}) collective-permute-start(bf16[256,512]{1,0:T(8,128)(2,1)S(1)} %get-tuple-element.47), channel_id=1, source_target_pairs={{0,0},{4,8},{8,4},{12,12},{1,1},{5,9},{9,5},{13,13},{2,2},{6,10},{... | collective-permute-start | bytes 786440 | tf_op jit(solution)/shard_map/ppermute | solution.py:432
  10.9 1.3 %collective-permute-done.2.refs_14_.two_ref = bf16[128,512]{1,0:T(8,128)(2,1)S(1)} collective-permute-done((bf16[128,512]{1,0:T(8,128)(2,1)S(1)}, bf16[128,512]{1,0:T(8,128)(2,1)S(1)}, u32[]{:S(2)}, u32[]{:S(2)}) %collective-permute-start.2) | collective-permute-done | bytes 131104 | tf_op jit(solution)/shard_map/ppermute | solution.py:353
  12.2 0.3 collective-permute-done.3.refs_13_.one_ref
  12.6 2.7 %collective-permute-start.4 = (bf16[128,512]{1,0:T(8,128)(2,1)S(1)}, bf16[128,512]{1,0:T(8,128)(2,1)S(1)}, u32[]{:S(2)}, u32[]{:S(2)}) collective-permute-start(bf16[128,512]{1,0:T(8,128)(2,1)S(1)} %collective-permute-done.2.refs_14_.two_ref), channel_id=1, source_target_pairs={{0,16},{16,0},{1,17},{17,1},{2,18},{18,2},{3,19},{19,3},{4,20},{20... | collective-permute-start | bytes 393224 | tf_op jit(solution)/shard_map/ppermute | solution.py:325
  15.3 0.0 collective-permute-start.9
  15.3 1.6 %collective-permute-start.10 = (bf16[256,512]{1,0:T(8,128)(2,1)S(1)}, bf16[256,512]{1,0:T(8,128)(2,1)S(1)}, u32[]{:S(2)}, u32[]{:S(2)}) collective-permute-start(bf16[256,512]{1,0:T(8,128)(2,1)S(1)} %shard_map.125), channel_id=1, source_target_pairs={{0,2},{2,0},{1,3},{3,1},{4,6},{6,4},{5,7},{7,5},{8,10},{10,8},{9,1... | collective-permute-start | bytes 786440 | tf_op jit(solution)/shard_map/ppermute | solution.py:325
  16.9 1.4 %collective-permute-done.4.refs_15_ = bf16[128,512]{1,0:T(8,128)(2,1)S(1)} collective-permute-done((bf16[128,512]{1,0:T(8,128)(2,1)S(1)}, bf16[128,512]{1,0:T(8,128)(2,1)S(1)}, u32[]{:S(2)}, u32[]{:S(2)}) %collective-permute-start.4) | collective-permute-done | bytes 131104 | tf_op jit(solution)/shard_map/ppermute | solution.py:325
  18.2 0.0 collective-permute-done.a_ref.refs_2_
  18.2 0.0 collective-permute-done.1.b_ref.refs_5_
  18.3 0.1 collective-permute-start.5
  18.3 0.5 %collective-permute-start.6 = (bf16[128,512]{1,0:T(8,128)(2,1)S(1)}, bf16[128,512]{1,0:T(8,128)(2,1)S(1)}, u32[]{:S(2)}, u32[]{:S(2)}) collective-permute-start(bf16[128,512]{1,0:T(8,128)(2,1)S(1)} %get-tuple-element.52), channel_id=1, source_target_pairs={{0,1},{1,0},{2,3},{3,2},{4,5},{5,4},{6,7},{7,6},{8,9},{9,8},{10,11... | collective-permute-start | bytes 393224 | tf_op jit(solution)/shard_map/ppermute | solution.py:325
  18.8 0.1 collective-permute-start.7
  18.9 0.0 collective-permute-done.9.refs_9_
  18.9 0.4 collective-permute-start.8
  19.4 0.3 collective-permute-done.5.refs_3_
  19.7 1.5 %collective-permute-start.11 = (bf16[128,512]{1,0:T(8,128)(2,1)S(1)}, bf16[128,512]{1,0:T(8,128)(2,1)S(1)}, u32[]{:S(2)}, u32[]{:S(2)}) collective-permute-start(bf16[128,512]{1,0:T(8,128)(2,1)S(1)} %collective-permute-done.4.refs_15_), channel_id=1, source_target_pairs={{0,2},{2,0},{1,3},{3,1},{4,6},{6,4},{5,7},{7,5},{8,10},{10,8},{9,1... | collective-permute-start | bytes 393224 | tf_op jit(solution)/shard_map/ppermute | solution.py:325
  21.2 0.0 collective-permute-done.6.refs_4_
  21.2 0.0 collective-permute-done.7.refs_6_
  21.2 0.0 collective-permute-done.8.refs_7_
  21.2 3.8 %shard_map.124 = (bf16[512,128]{1,0:T(8,128)(2,1)S(1)}, bf16[512,128]{1,0:T(8,128)(2,1)S(1)}, bf16[1536,128]{1,0:T(8,128)(2,1)S(1)}, f32[48,1536]{1,0:T(8,128)S(1)}, f32[48,128]{1,0:T(8,128)S(1)}) custom-call(s32[6,16]{1,0:T(8,128)S(1)} %get-tuple-element.45.refs_0_, bf16[512,512]{1,0:T(8,128)(2,1)S(1)} %get-tuple-element.46.refs_1_, ...), custom_call_target="tpu_custom_call" | custom-call | bytes 1048576 | tf_op jit(solution)/shard_map/pallas_call | solution.py:312
  25.0 0.0 collective-permute-done.10.refs_16_
  25.0 1.9 %collective-permute-done.11.refs_17_ = bf16[128,512]{1,0:T(8,128)(2,1)S(1)} collective-permute-done((bf16[128,512]{1,0:T(8,128)(2,1)S(1)}, bf16[128,512]{1,0:T(8,128)(2,1)S(1)}, u32[]{:S(2)}, u32[]{:S(2)}) %collective-permute-start.11) | collective-permute-done | bytes 131104 | tf_op jit(solution)/shard_map/ppermute | solution.py:325
  26.9 3.8 %shard_map.126 = (bf16[512,128]{1,0:T(8,128)(2,1)S(1)}, bf16[512,128]{1,0:T(8,128)(2,1)S(1)}, bf16[48,256]{1,0:T(8,128)(2,1)S(1)}, bf16[48,256]{1,0:T(8,128)(2,1)S(1)}, bf16[48,256]{1,0:T(8,128)(2,1)S(1)}) custom-call(s32[6,16]{1,0:T(8,128)S(1)} %get-tuple-element.45.refs_0_, bf16[512,512]{1,0:T(8,128)(2,1)S(1)} %get-tuple-element.46.refs_1_, ...), custom_call_target="tpu_custom_call" | custom-call | flops 4000000000 | bytes 1048576 | tf_op jit(solution)/shard_map/pallas_call | solution.py:312
  30.7 0.1 collective-permute-start.12
  30.8 1.2 %collective-permute-done.12.sibling_ref = bf16[48,256]{1,0:T(8,128)(2,1)S(1)} collective-permute-done((bf16[48,256]{1,0:T(8,128)(2,1)S(1)}, bf16[48,256]{1,0:T(8,128)(2,1)S(1)}, u32[]{:S(2)}, u32[]{:S(2)}) %collective-permute-start.12) | collective-permute-done | bytes 24608 | tf_op jit(solution)/shard_map/ppermute | solution.py:325
  32.0 1.6 %collective-permute-start.13 = (bf16[48,512]{1,0:T(8,128)(2,1)S(1)}, bf16[48,512]{1,0:T(8,128)(2,1)S(1)}, u32[]{:S(2)}, u32[]{:S(2)}) collective-permute-start(bf16[48,512]{1,0:T(8,128)(2,1)S(1)} %shard_map.127), channel_id=1, source_target_pairs={{0,2},{2,0},{1,3},{3,1},{4,6},{6,4},{5,7},{7,5},{8,10},{10,8},{9,1... | collective-permute-start | bytes 147464 | tf_op jit(solution)/shard_map/ppermute | solution.py:325
  33.6 1.0 %shard_map.128 = (f32[512,256]{1,0:T(8,128)S(1)}, bf16[512,256]{1,0:T(8,128)(2,1)S(1)}) custom-call(s32[1,512]{1,0:T(1,128)S(1)} %get-tuple-element.66.order_ref, bf16[512,256]{1,0:T(8,128)(2,1)S(1)} %get-tuple-element.67.x_ref, bf16[512,128]{1,0:T(8,128)(2,1)S(1)} %get-tuple-element.68.att1_ref, bf16[512,128]{1,0:T(8,128)(2,1)S(1)} %get-tuple-element.69.att2_ref, ...), custom_call_target="tpu_custom_call" | custom-call | flops 1000000000 | bytes 1048576 | tf_op jit(solution)/shard_map/pallas_call | solution.py:312
  34.6 0.1 collective-permute-start.17
  34.7 1.5 %collective-permute-done.13 = bf16[48,512]{1,0:T(8,128)(2,1)S(1)} collective-permute-done((bf16[48,512]{1,0:T(8,128)(2,1)S(1)}, bf16[48,512]{1,0:T(8,128)(2,1)S(1)}, u32[]{:S(2)}, u32[]{:S(2)}) %collective-permute-start.13) | collective-permute-done | bytes 49184 | tf_op jit(solution)/shard_map/ppermute | solution.py:325
  36.2 2.1 %collective-permute-start.14 = (bf16[48,512]{1,0:T(8,128)(2,1)S(1)}, bf16[48,512]{1,0:T(8,128)(2,1)S(1)}, u32[]{:S(2)}, u32[]{:S(2)}) collective-permute-start(bf16[48,512]{1,0:T(8,128)(2,1)S(1)} %add_convert_fusion.1.refs_0_), channel_id=1, source_target_pairs={{0,12},{4,8},{8,4},{12,0},{1,13},{5,9},{9,5},{13,1},{2,14},{6,10},... | collective-permute-start | bytes 147464 | tf_op jit(solution)/shard_map/ppermute | solution.py:325
  38.3 1.6 %collective-permute-start.15 = (bf16[48,512]{1,0:T(8,128)(2,1)S(1)}, bf16[48,512]{1,0:T(8,128)(2,1)S(1)}, u32[]{:S(2)}, u32[]{:S(2)}) collective-permute-start(bf16[48,512]{1,0:T(8,128)(2,1)S(1)} %add_convert_fusion.1.refs_0_), channel_id=1, source_target_pairs={{0,8},{4,12},{8,0},{12,4},{1,9},{5,13},{9,1},{13,5},{2,10},{6,14},... | collective-permute-start | bytes 147464 | tf_op jit(solution)/shard_map/ppermute | solution.py:325
  40.0 0.7 %collective-permute-start.16 = (bf16[48,512]{1,0:T(8,128)(2,1)S(1)}, bf16[48,512]{1,0:T(8,128)(2,1)S(1)}, u32[]{:S(2)}, u32[]{:S(2)}) collective-permute-start(bf16[48,512]{1,0:T(8,128)(2,1)S(1)} %add_convert_fusion.1.refs_0_), channel_id=1, source_target_pairs={{0,4},{4,0},{8,12},{12,8},{1,5},{5,1},{9,13},{13,9},{2,6},{6,2},{1... | collective-permute-start | bytes 147464 | tf_op jit(solution)/shard_map/ppermute | solution.py:325
  40.6 0.0 collective-permute-done.17
  40.6 0.8 %fusion = bf16[1,512,256]{2,1,0:T(8,128)(2,1)} fusion(f32[512,256]{1,0:T(8,128)S(1)} %get-tuple-element.72, bf16[512,256]{1,0:T(8,128)(2,1)S(1)} %collective-permute-done.17), kind=kLoop, calls=%fused_computation.1 | loop fusion | flops 393216 | bytes 1048576 | tf_op jit(solution)/shard_map/broadcast_in_dim | solution.py:501
  41.4 1.1 %collective-permute-done.14.refs_1_ = bf16[48,512]{1,0:T(8,128)(2,1)S(1)} collective-permute-done((bf16[48,512]{1,0:T(8,128)(2,1)S(1)}, bf16[48,512]{1,0:T(8,128)(2,1)S(1)}, u32[]{:S(2)}, u32[]{:S(2)}) %collective-permute-start.14) | collective-permute-done | bytes 49184 | tf_op jit(solution)/shard_map/ppermute | solution.py:325
  42.5 1.2 %collective-permute-done.15.refs_2_ = bf16[48,512]{1,0:T(8,128)(2,1)S(1)} collective-permute-done((bf16[48,512]{1,0:T(8,128)(2,1)S(1)}, bf16[48,512]{1,0:T(8,128)(2,1)S(1)}, u32[]{:S(2)}, u32[]{:S(2)}) %collective-permute-start.15) | collective-permute-done | bytes 49184 | tf_op jit(solution)/shard_map/ppermute | solution.py:325
  43.8 0.5 %collective-permute-done.16.refs_3_ = bf16[48,512]{1,0:T(8,128)(2,1)S(1)} collective-permute-done((bf16[48,512]{1,0:T(8,128)(2,1)S(1)}, bf16[48,512]{1,0:T(8,128)(2,1)S(1)}, u32[]{:S(2)}, u32[]{:S(2)}) %collective-permute-start.16) | collective-permute-done | bytes 49184 | tf_op jit(solution)/shard_map/ppermute | solution.py:325
  44.3 0.1 collective-permute-start.18
  44.4 1.2 %collective-permute-done.18.recv_ref = f32[48,256]{1,0:T(8,128)S(1)} collective-permute-done((f32[48,256]{1,0:T(8,128)S(1)}, f32[48,256]{1,0:T(8,128)S(1)}, u32[]{:S(2)}, u32[]{:S(2)}) %collective-permute-start.18) | collective-permute-done | bytes 49184 | tf_op jit(solution)/shard_map/ppermute | solution.py:325
  45.6 0.7 %shard_map.130 = (f32[48,512]{1,0:T(8,128)}, f32[48,256]{1,0:T(8,128)}) custom-call(f32[48,256]{1,0:T(8,128)S(1)} %get-tuple-element.79.own_ref, f32[48,256]{1,0:T(8,128)S(1)} %collective-permute-done.18.recv_ref, f32[48,256]{1,0:T(8,128)S(1)} %get-tuple-element.80.up_ref), custom_call_target="tpu_custom_call" | custom-call | bytes 1048576 | tf_op jit(solution)/shard_map/pallas_call | solution.py:312
  (5 shorter events, 0.1 us)
Async XLA Ops:
  1.7 10.5 %collective-permute-start.2 = (bf16[128,512]{1,0:T(8,128)(2,1)S(1)}, bf16[128,512]{1,0:T(8,128)(2,1)S(1)}, u32[]{:S(2)}, u32[]{:S(2)}) collective-permute-start(bf16[128,512]{1,0:T(8,128)(2,1)S(1)} %get-tuple-element.43.refs_12_), channel_id=1, source_target_pairs={{0,8},{4,12},{8,0},{12,4},{16,28},{20,24},{24,20},{28,16},{1,9},{5... | collective-permute-start | bytes 393224 | tf_op jit(solution)/shard_map/ppermute | solution.py:353
  5.8 6.8 %collective-permute-start.3 = (bf16[128,512]{1,0:T(8,128)(2,1)S(1)}, bf16[128,512]{1,0:T(8,128)(2,1)S(1)}, u32[]{:S(2)}, u32[]{:S(2)}) collective-permute-start(bf16[128,512]{1,0:T(8,128)(2,1)S(1)} %get-tuple-element.43.refs_12_), channel_id=1, source_target_pairs={{0,4},{4,0},{8,12},{12,8},{1,5},{5,1},{9,13},{13,9},{2,6},{6,2},{1... | collective-permute-start | bytes 393224 | tf_op jit(solution)/shard_map/ppermute | solution.py:325
  9.8 8.5 %collective-permute-start = (bf16[256,512]{1,0:T(8,128)(2,1)S(1)}, bf16[256,512]{1,0:T(8,128)(2,1)S(1)}, u32[]{:S(2)}, u32[]{:S(2)}) collective-permute-start(bf16[256,512]{1,0:T(8,128)(2,1)S(1)} %get-tuple-element.47), channel_id=1, source_target_pairs={{0,4},{4,0},{8,12},{12,8},{1,5},{5,1},{9,13},{13,9},{2,6},{6,2},{1... | collective-permute-start | bytes 786440 | tf_op jit(solution)/shard_map/ppermute | solution.py:325
  10.3 7.9 %collective-permute-start.1 = (bf16[256,512]{1,0:T(8,128)(2,1)S(1)}, bf16[256,512]{1,0:T(8,128)(2,1)S(1)}, u32[]{:S(2)}, u32[]{:S(2)}) collective-permute-start(bf16[256,512]{1,0:T(8,128)(2,1)S(1)} %get-tuple-element.47), channel_id=1, source_target_pairs={{0,0},{4,8},{8,4},{12,12},{1,1},{5,9},{9,5},{13,13},{2,2},{6,10},{... | collective-permute-start | bytes 786440 | tf_op jit(solution)/shard_map/ppermute | solution.py:432
  12.6 5.6 %collective-permute-start.4 = (bf16[128,512]{1,0:T(8,128)(2,1)S(1)}, bf16[128,512]{1,0:T(8,128)(2,1)S(1)}, u32[]{:S(2)}, u32[]{:S(2)}) collective-permute-start(bf16[128,512]{1,0:T(8,128)(2,1)S(1)} %collective-permute-done.2.refs_14_.two_ref), channel_id=1, source_target_pairs={{0,16},{16,0},{1,17},{17,1},{2,18},{18,2},{3,19},{19,3},{4,20},{20... | collective-permute-start | bytes 393224 | tf_op jit(solution)/shard_map/ppermute | solution.py:325
  15.3 3.6 %collective-permute-start.9 = (bf16[512,256]{1,0:T(8,128)(2,1)S(1)}, bf16[512,256]{1,0:T(8,128)(2,1)S(1)}, u32[]{:S(2)}, u32[]{:S(2)}) collective-permute-start(bf16[512,256]{1,0:T(8,128)(2,1)S(1)} %get-tuple-element.55.refs_8_), channel_id=1, source_target_pairs={{0,1},{1,0},{2,3},{3,2},{4,5},{5,4},{6,7},{7,6},{8,9},{9,8},{10,11... | collective-permute-start | bytes 786440 | tf_op jit(solution)/shard_map/ppermute | solution.py:325
  15.3 9.7 %collective-permute-start.10 = (bf16[256,512]{1,0:T(8,128)(2,1)S(1)}, bf16[256,512]{1,0:T(8,128)(2,1)S(1)}, u32[]{:S(2)}, u32[]{:S(2)}) collective-permute-start(bf16[256,512]{1,0:T(8,128)(2,1)S(1)} %shard_map.125), channel_id=1, source_target_pairs={{0,2},{2,0},{1,3},{3,1},{4,6},{6,4},{5,7},{7,5},{8,10},{10,8},{9,1... | collective-permute-start | bytes 786440 | tf_op jit(solution)/shard_map/ppermute | solution.py:325
  18.3 1.4 %collective-permute-start.5 = (bf16[128,512]{1,0:T(8,128)(2,1)S(1)}, bf16[128,512]{1,0:T(8,128)(2,1)S(1)}, u32[]{:S(2)}, u32[]{:S(2)}) collective-permute-start(bf16[128,512]{1,0:T(8,128)(2,1)S(1)} %get-tuple-element.51), channel_id=1, source_target_pairs={{0,1},{1,0},{2,3},{3,2},{4,5},{5,4},{6,7},{7,6},{8,9},{9,8},{10,11... | collective-permute-start | bytes 393224 | tf_op jit(solution)/shard_map/ppermute | solution.py:325
  18.3 2.8 %collective-permute-start.6 = (bf16[128,512]{1,0:T(8,128)(2,1)S(1)}, bf16[128,512]{1,0:T(8,128)(2,1)S(1)}, u32[]{:S(2)}, u32[]{:S(2)}) collective-permute-start(bf16[128,512]{1,0:T(8,128)(2,1)S(1)} %get-tuple-element.52), channel_id=1, source_target_pairs={{0,1},{1,0},{2,3},{3,2},{4,5},{5,4},{6,7},{7,6},{8,9},{9,8},{10,11... | collective-permute-start | bytes 393224 | tf_op jit(solution)/shard_map/ppermute | solution.py:325
  18.8 2.3 %collective-permute-start.7 = (bf16[128,512]{1,0:T(8,128)(2,1)S(1)}, bf16[128,512]{1,0:T(8,128)(2,1)S(1)}, u32[]{:S(2)}, u32[]{:S(2)}) collective-permute-start(bf16[128,512]{1,0:T(8,128)(2,1)S(1)} %get-tuple-element.53), channel_id=1, source_target_pairs={{0,1},{1,0},{2,3},{3,2},{4,5},{5,4},{6,7},{7,6},{8,9},{9,8},{10,11... | collective-permute-start | bytes 393224 | tf_op jit(solution)/shard_map/ppermute | solution.py:325
  18.9 2.3 %collective-permute-start.8 = (bf16[128,512]{1,0:T(8,128)(2,1)S(1)}, bf16[128,512]{1,0:T(8,128)(2,1)S(1)}, u32[]{:S(2)}, u32[]{:S(2)}) collective-permute-start(bf16[128,512]{1,0:T(8,128)(2,1)S(1)} %get-tuple-element.54), channel_id=1, source_target_pairs={{0,1},{1,0},{2,3},{3,2},{4,5},{5,4},{6,7},{7,6},{8,9},{9,8},{10,11... | collective-permute-start | bytes 393224 | tf_op jit(solution)/shard_map/ppermute | solution.py:325
  19.7 7.2 %collective-permute-start.11 = (bf16[128,512]{1,0:T(8,128)(2,1)S(1)}, bf16[128,512]{1,0:T(8,128)(2,1)S(1)}, u32[]{:S(2)}, u32[]{:S(2)}) collective-permute-start(bf16[128,512]{1,0:T(8,128)(2,1)S(1)} %collective-permute-done.4.refs_15_), channel_id=1, source_target_pairs={{0,2},{2,0},{1,3},{3,1},{4,6},{6,4},{5,7},{7,5},{8,10},{10,8},{9,1... | collective-permute-start | bytes 393224 | tf_op jit(solution)/shard_map/ppermute | solution.py:325
  30.7 1.3 %collective-permute-start.12 = (bf16[48,256]{1,0:T(8,128)(2,1)S(1)}, bf16[48,256]{1,0:T(8,128)(2,1)S(1)}, u32[]{:S(2)}, u32[]{:S(2)}) collective-permute-start(bf16[48,256]{1,0:T(8,128)(2,1)S(1)} %get-tuple-element.64), channel_id=1, source_target_pairs={{0,1},{1,0},{2,3},{3,2},{4,5},{5,4},{6,7},{7,6},{8,9},{9,8},{10,11... | collective-permute-start | bytes 73736 | tf_op jit(solution)/shard_map/ppermute | solution.py:325
  32.0 4.2 %collective-permute-start.13 = (bf16[48,512]{1,0:T(8,128)(2,1)S(1)}, bf16[48,512]{1,0:T(8,128)(2,1)S(1)}, u32[]{:S(2)}, u32[]{:S(2)}) collective-permute-start(bf16[48,512]{1,0:T(8,128)(2,1)S(1)} %shard_map.127), channel_id=1, source_target_pairs={{0,2},{2,0},{1,3},{3,1},{4,6},{6,4},{5,7},{7,5},{8,10},{10,8},{9,1... | collective-permute-start | bytes 147464 | tf_op jit(solution)/shard_map/ppermute | solution.py:325
  34.6 6.1 %collective-permute-start.17 = (bf16[512,256]{1,0:T(8,128)(2,1)S(1)}, bf16[512,256]{1,0:T(8,128)(2,1)S(1)}, u32[]{:S(2)}, u32[]{:S(2)}) collective-permute-start(bf16[512,256]{1,0:T(8,128)(2,1)S(1)} %get-tuple-element.73), channel_id=1, source_target_pairs={{0,1},{1,0},{2,3},{3,2},{4,5},{5,4},{6,7},{7,6},{8,9},{9,8},{10,11... | collective-permute-start | bytes 786440 | tf_op jit(solution)/shard_map/ppermute | solution.py:325
  36.2 6.4 %collective-permute-start.14 = (bf16[48,512]{1,0:T(8,128)(2,1)S(1)}, bf16[48,512]{1,0:T(8,128)(2,1)S(1)}, u32[]{:S(2)}, u32[]{:S(2)}) collective-permute-start(bf16[48,512]{1,0:T(8,128)(2,1)S(1)} %add_convert_fusion.1.refs_0_), channel_id=1, source_target_pairs={{0,12},{4,8},{8,4},{12,0},{1,13},{5,9},{9,5},{13,1},{2,14},{6,10},... | collective-permute-start | bytes 147464 | tf_op jit(solution)/shard_map/ppermute | solution.py:325
  38.3 5.5 %collective-permute-start.15 = (bf16[48,512]{1,0:T(8,128)(2,1)S(1)}, bf16[48,512]{1,0:T(8,128)(2,1)S(1)}, u32[]{:S(2)}, u32[]{:S(2)}) collective-permute-start(bf16[48,512]{1,0:T(8,128)(2,1)S(1)} %add_convert_fusion.1.refs_0_), channel_id=1, source_target_pairs={{0,8},{4,12},{8,0},{12,4},{1,9},{5,13},{9,1},{13,5},{2,10},{6,14},... | collective-permute-start | bytes 147464 | tf_op jit(solution)/shard_map/ppermute | solution.py:325
  40.0 4.3 %collective-permute-start.16 = (bf16[48,512]{1,0:T(8,128)(2,1)S(1)}, bf16[48,512]{1,0:T(8,128)(2,1)S(1)}, u32[]{:S(2)}, u32[]{:S(2)}) collective-permute-start(bf16[48,512]{1,0:T(8,128)(2,1)S(1)} %add_convert_fusion.1.refs_0_), channel_id=1, source_target_pairs={{0,4},{4,0},{8,12},{12,8},{1,5},{5,1},{9,13},{13,9},{2,6},{6,2},{1... | collective-permute-start | bytes 147464 | tf_op jit(solution)/shard_map/ppermute | solution.py:325
  44.3 1.3 %collective-permute-start.18 = (f32[48,256]{1,0:T(8,128)S(1)}, f32[48,256]{1,0:T(8,128)S(1)}, u32[]{:S(2)}, u32[]{:S(2)}) collective-permute-start(f32[48,256]{1,0:T(8,128)S(1)} %get-tuple-element.79.own_ref), channel_id=1, source_target_pairs={{0,1},{1,0},{2,3},{3,2},{4,5},{5,4},{6,7},{7,6},{8,9},{9,8},{10,11... | collective-permute-start | bytes 147464 | tf_op jit(solution)/shard_map/ppermute | solution.py:325

commit v11 on v10

--- a/solution.py
+++ b/solution.py
@@ -350,8 +350,8 @@
         whole = [lax.all_gather(m, "node", axis=0, tiled=True) for m in (first, second)]
         return [whole[:1], whole[1:]], lambda node: [0], whole
     far_pairs = [(g * 4 + n, g * 4 + (n ^ (2 + g))) for g in range(2) for n in range(4)]
+    near = swap(first, "node")
     far = lax.ppermute(first, ("group", "node"), far_pairs)
-    near = swap(first, "node")
     far, near, _ = lax.optimization_barrier((far, near, half))
     other_far = swap(far, "group")
     pair = call(pair_kernel, (shape((2 * depth, 4 * DH)),), (near, far), limit=16)[0]
@@ -507,8 +507,8 @@
         hops += [("node", 1 << i) for i in range(count.bit_length() - 2)]
     for axis, step in hops:
         lora = (lora.astype(F32) + swap(lora, axis, step).astype(F32)).astype(BF16)
-    steps = (3, 2, 1) if count == 4 else (count // 2,)
-    terms = (lora, *[swap(lora, "node", k) for k in steps])
+    steps = (2, 1, 3) if count == 4 else (count // 2,)
+    terms = (lora, *[lax.ppermute(lora, "node", [(i, (i + k) % count) for i in range(count)]) for k in steps])
     terms, mesh_out = lax.optimization_barrier((terms, mesh_out))
     down_half, up_total = call(
         total_kernel,

time: 46.5 us -> 45.8 us (0.985)
  waiting for transfers between devices: 12 us -> 10.9 us
  starting transfers between devices: 19.9 us -> 20.4 us
    ppermute x0 -> x3, starting transfers between devices: none -> 4.91 us  [shards(): lax.ppermute(lora, 'node', [(i, (i + k) % count) for i in range(count)])]
    ppermute x17 -> x14, starting transfers between devices: 15.1 us -> 10.7 us  [swap(): return lax.ppermute(value, axis, [(i, i ^ step) for i in range(size)])]
    ppermute x17 -> x14, waiting for transfers between devices: 10.7 us -> 7.83 us  [swap(): return lax.ppermute(value, axis, [(i, i ^ step) for i in range(size)])]
    ppermute x0 -> x3, waiting for transfers between devices: none -> 1.76 us  [shards(): lax.ppermute(lora, 'node', [(i, (i + k) % count) for i in range(count)])]
  transfers between devices with their start and end apart: 19 -> 19, of which waited for: 11 -> 9; matrix products, arithmetic and copies ran while one was open for 2% -> 2% of each run, Pallas kernels for 16% -> 16%
where the time goes in v11:
time: 45.8 us; the launch traced here: 45.6 us
  starting transfers between devices  20.4 us (45%)
  Pallas kernels  12.8 us (28%)
  waiting for transfers between devices  10.9 us (24%)
  other arithmetic  0.78 us (2%)
  between operations  0.76 us (2%)
    pallas_call x10, Pallas kernels, call(): pl.pallas_call(kernel, out_shape=outs, in_specs=[HBM] * hbm + [VMEM] * (l...  12.8 us
    ppermute x14, starting transfers between devices, swap(): return lax.ppermute(value, axis, [(i, i ^ step) for i in range(size)])  10.7 us
    ppermute x14, waiting for transfers between devices, swap(): return lax.ppermute(value, axis, [(i, i ^ step) for i in range(size)])  7.83 us
    ppermute x3, starting transfers between devices, shards(): lax.ppermute(lora, 'node', [(i, (i + k) % count) for i in range(count)])  4.91 us
    ppermute x1, starting transfers between devices, gather_weights(): far = lax.ppermute(first, ('group', 'node'), far_pairs)  4.1 us
    ppermute x3, waiting for transfers between devices, shards(): lax.ppermute(lora, 'node', [(i, (i + k) % count) for i in range(count)])  1.76 us
    ppermute x1, waiting for transfers between devices, gather_weights(): far = lax.ppermute(first, ('group', 'node'), far_pairs)  1.27 us
  transfers between devices with their start and end apart: 19, of which 9 were waited for; matrix products, arithmetic and copies ran while one was open for 2% of the time, Pallas kernels for 16%

profile of v11, /device:TPU:0, one launch (start us, length us, event | category | flops | bytes accessed | tf_op | source)
XLA Modules:
  0.0 45.6 jit_solution(8260200027795608198)
XLA Ops:
  0.6 1.1 %shard_map.121 = (bf16[128,512]{1,0:T(8,128)(2,1)S(1)}, bf16[128,512]{1,0:T(8,128)(2,1)S(1)}) custom-call(bf16[128,256]{1,0:T(8,128)(2,1)} %refs_0_.1, bf16[128,256]{1,0:T(8,128)(2,1)} %refs_1_.1, bf16[128,256]{1,0:T(8,128)(2,1)} %refs_2_.1, bf16[256,128]{1,0:T(8,128)(2,1)} %refs_3_.1), custom_call_target="tpu_custom_call" | custom-call | bytes 1048576 | tf_op jit(solution)/shard_map/pallas_call | solution.py:312
  1.7 4.1 %collective-permute-start.2 = (bf16[128,512]{1,0:T(8,128)(2,1)S(1)}, bf16[128,512]{1,0:T(8,128)(2,1)S(1)}, u32[]{:S(2)}, u32[]{:S(2)}) collective-permute-start(bf16[128,512]{1,0:T(8,128)(2,1)S(1)} %get-tuple-element.43.refs_12_), channel_id=1, source_target_pairs={{0,8},{4,12},{8,0},{12,4},{16,28},{20,24},{24,20},{28,16},{1,9},{5... | collective-permute-start | bytes 393224 | tf_op jit(solution)/shard_map/ppermute | solution.py:354
  5.8 1.6 %collective-permute-start.3 = (bf16[128,512]{1,0:T(8,128)(2,1)S(1)}, bf16[128,512]{1,0:T(8,128)(2,1)S(1)}, u32[]{:S(2)}, u32[]{:S(2)}) collective-permute-start(bf16[128,512]{1,0:T(8,128)(2,1)S(1)} %get-tuple-element.43.refs_12_), channel_id=1, source_target_pairs={{0,4},{4,0},{8,12},{12,8},{1,5},{5,1},{9,13},{13,9},{2,6},{6,2},{1... | collective-permute-start | bytes 393224 | tf_op jit(solution)/shard_map/ppermute | solution.py:325
  7.4 2.4 %shard_map.122 = (s32[1,512]{1,0:T(1,128)S(1)}, s32[6,16]{1,0:T(8,128)S(1)}, bf16[48,512]{1,0:T(8,128)(2,1)S(1)}, bf16[48,256]{1,0:T(8,128)(2,1)S(1)}, bf16[512,...) custom-call(s32[1,512]{1,0:T(1,128)} %bitcast.21, ...), custom_call_target="tpu_custom_call" | custom-call | flops 402653184 | bytes 1048576 | tf_op jit(solution)/shard_map/pallas_call | solution.py:312
  9.8 0.5 %collective-permute-start = (bf16[256,512]{1,0:T(8,128)(2,1)S(1)}, bf16[256,512]{1,0:T(8,128)(2,1)S(1)}, u32[]{:S(2)}, u32[]{:S(2)}) collective-permute-start(bf16[256,512]{1,0:T(8,128)(2,1)S(1)} %get-tuple-element.47), channel_id=1, source_target_pairs={{0,4},{4,0},{8,12},{12,8},{1,5},{5,1},{9,13},{13,9},{2,6},{6,2},{1... | collective-permute-start | bytes 786440 | tf_op jit(solution)/shard_map/ppermute | solution.py:325
  10.3 0.7 %collective-permute-start.1 = (bf16[256,512]{1,0:T(8,128)(2,1)S(1)}, bf16[256,512]{1,0:T(8,128)(2,1)S(1)}, u32[]{:S(2)}, u32[]{:S(2)}) collective-permute-start(bf16[256,512]{1,0:T(8,128)(2,1)S(1)} %get-tuple-element.47), channel_id=1, source_target_pairs={{0,0},{4,8},{8,4},{12,12},{1,1},{5,9},{9,5},{13,13},{2,2},{6,10},{... | collective-permute-start | bytes 786440 | tf_op jit(solution)/shard_map/ppermute | solution.py:432
  10.9 1.3 %collective-permute-done.2.refs_14_.two_ref = bf16[128,512]{1,0:T(8,128)(2,1)S(1)} collective-permute-done((bf16[128,512]{1,0:T(8,128)(2,1)S(1)}, bf16[128,512]{1,0:T(8,128)(2,1)S(1)}, u32[]{:S(2)}, u32[]{:S(2)}) %collective-permute-start.2) | collective-permute-done | bytes 131104 | tf_op jit(solution)/shard_map/ppermute | solution.py:354
  12.2 0.3 collective-permute-done.3.refs_13_.one_ref
  12.6 2.7 %collective-permute-start.4 = (bf16[128,512]{1,0:T(8,128)(2,1)S(1)}, bf16[128,512]{1,0:T(8,128)(2,1)S(1)}, u32[]{:S(2)}, u32[]{:S(2)}) collective-permute-start(bf16[128,512]{1,0:T(8,128)(2,1)S(1)} %collective-permute-done.2.refs_14_.two_ref), channel_id=1, source_target_pairs={{0,16},{16,0},{1,17},{17,1},{2,18},{18,2},{3,19},{19,3},{4,20},{20... | collective-permute-start | bytes 393224 | tf_op jit(solution)/shard_map/ppermute | solution.py:325
  15.3 0.0 collective-permute-start.9
  15.3 1.6 %collective-permute-start.10 = (bf16[256,512]{1,0:T(8,128)(2,1)S(1)}, bf16[256,512]{1,0:T(8,128)(2,1)S(1)}, u32[]{:S(2)}, u32[]{:S(2)}) collective-permute-start(bf16[256,512]{1,0:T(8,128)(2,1)S(1)} %shard_map.125), channel_id=1, source_target_pairs={{0,2},{2,0},{1,3},{3,1},{4,6},{6,4},{5,7},{7,5},{8,10},{10,8},{9,1... | collective-permute-start | bytes 786440 | tf_op jit(solution)/shard_map/ppermute | solution.py:325
  16.9 1.4 %collective-permute-done.4.refs_15_ = bf16[128,512]{1,0:T(8,128)(2,1)S(1)} collective-permute-done((bf16[128,512]{1,0:T(8,128)(2,1)S(1)}, bf16[128,512]{1,0:T(8,128)(2,1)S(1)}, u32[]{:S(2)}, u32[]{:S(2)}) %collective-permute-start.4) | collective-permute-done | bytes 131104 | tf_op jit(solution)/shard_map/ppermute | solution.py:325
  18.2 0.0 collective-permute-done.a_ref.refs_2_
  18.2 0.0 collective-permute-done.1.b_ref.refs_5_
  18.3 0.1 collective-permute-start.5
  18.3 0.5 %collective-permute-start.6 = (bf16[128,512]{1,0:T(8,128)(2,1)S(1)}, bf16[128,512]{1,0:T(8,128)(2,1)S(1)}, u32[]{:S(2)}, u32[]{:S(2)}) collective-permute-start(bf16[128,512]{1,0:T(8,128)(2,1)S(1)} %get-tuple-element.52), channel_id=1, source_target_pairs={{0,1},{1,0},{2,3},{3,2},{4,5},{5,4},{6,7},{7,6},{8,9},{9,8},{10,11... | collective-permute-start | bytes 393224 | tf_op jit(solution)/shard_map/ppermute | solution.py:325
  18.8 0.1 collective-permute-start.7
  18.9 0.0 collective-permute-done.9.refs_9_
  18.9 0.4 collective-permute-start.8
  19.4 0.3 collective-permute-done.5.refs_3_
  19.7 1.5 %collective-permute-start.11 = (bf16[128,512]{1,0:T(8,128)(2,1)S(1)}, bf16[128,512]{1,0:T(8,128)(2,1)S(1)}, u32[]{:S(2)}, u32[]{:S(2)}) collective-permute-start(bf16[128,512]{1,0:T(8,128)(2,1)S(1)} %collective-permute-done.4.refs_15_), channel_id=1, source_target_pairs={{0,2},{2,0},{1,3},{3,1},{4,6},{6,4},{5,7},{7,5},{8,10},{10,8},{9,1... | collective-permute-start | bytes 393224 | tf_op jit(solution)/shard_map/ppermute | solution.py:325
  21.2 0.0 collective-permute-done.6.refs_4_
  21.2 0.0 collective-permute-done.7.refs_6_
  21.2 0.0 collective-permute-done.8.refs_7_
  21.2 3.8 %shard_map.124 = (bf16[512,128]{1,0:T(8,128)(2,1)S(1)}, bf16[512,128]{1,0:T(8,128)(2,1)S(1)}, bf16[1536,128]{1,0:T(8,128)(2,1)S(1)}, f32[48,1536]{1,0:T(8,128)S(1)}, f32[48,128]{1,0:T(8,128)S(1)}) custom-call(s32[6,16]{1,0:T(8,128)S(1)} %get-tuple-element.45.refs_0_, bf16[512,512]{1,0:T(8,128)(2,1)S(1)} %get-tuple-element.46.refs_1_, ...), custom_call_target="tpu_custom_call" | custom-call | bytes 1048576 | tf_op jit(solution)/shard_map/pallas_call | solution.py:312
  25.0 0.0 collective-permute-done.10.refs_16_
  25.0 1.9 %collective-permute-done.11.refs_17_ = bf16[128,512]{1,0:T(8,128)(2,1)S(1)} collective-permute-done((bf16[128,512]{1,0:T(8,128)(2,1)S(1)}, bf16[128,512]{1,0:T(8,128)(2,1)S(1)}, u32[]{:S(2)}, u32[]{:S(2)}) %collective-permute-start.11) | collective-permute-done | bytes 131104 | tf_op jit(solution)/shard_map/ppermute | solution.py:325
  26.9 3.8 %shard_map.126 = (bf16[512,128]{1,0:T(8,128)(2,1)S(1)}, bf16[512,128]{1,0:T(8,128)(2,1)S(1)}, bf16[48,256]{1,0:T(8,128)(2,1)S(1)}, bf16[48,256]{1,0:T(8,128)(2,1)S(1)}, bf16[48,256]{1,0:T(8,128)(2,1)S(1)}) custom-call(s32[6,16]{1,0:T(8,128)S(1)} %get-tuple-element.45.refs_0_, bf16[512,512]{1,0:T(8,128)(2,1)S(1)} %get-tuple-element.46.refs_1_, ...), custom_call_target="tpu_custom_call" | custom-call | flops 4000000000 | bytes 1048576 | tf_op jit(solution)/shard_map/pallas_call | solution.py:312
  30.7 0.1 collective-permute-start.12
  30.8 1.2 %collective-permute-done.12.sibling_ref = bf16[48,256]{1,0:T(8,128)(2,1)S(1)} collective-permute-done((bf16[48,256]{1,0:T(8,128)(2,1)S(1)}, bf16[48,256]{1,0:T(8,128)(2,1)S(1)}, u32[]{:S(2)}, u32[]{:S(2)}) %collective-permute-start.12) | collective-permute-done | bytes 24608 | tf_op jit(solution)/shard_map/ppermute | solution.py:325
  32.0 1.6 %collective-permute-start.13 = (bf16[48,512]{1,0:T(8,128)(2,1)S(1)}, bf16[48,512]{1,0:T(8,128)(2,1)S(1)}, u32[]{:S(2)}, u32[]{:S(2)}) collective-permute-start(bf16[48,512]{1,0:T(8,128)(2,1)S(1)} %shard_map.127), channel_id=1, source_target_pairs={{0,2},{2,0},{1,3},{3,1},{4,6},{6,4},{5,7},{7,5},{8,10},{10,8},{9,1... | collective-permute-start | bytes 147464 | tf_op jit(solution)/shard_map/ppermute | solution.py:325
  33.6 1.0 %shard_map.128 = (f32[512,256]{1,0:T(8,128)S(1)}, bf16[512,256]{1,0:T(8,128)(2,1)S(1)}) custom-call(s32[1,512]{1,0:T(1,128)S(1)} %get-tuple-element.66.order_ref, bf16[512,256]{1,0:T(8,128)(2,1)S(1)} %get-tuple-element.67.x_ref, bf16[512,128]{1,0:T(8,128)(2,1)S(1)} %get-tuple-element.68.att1_ref, bf16[512,128]{1,0:T(8,128)(2,1)S(1)} %get-tuple-element.69.att2_ref, ...), custom_call_target="tpu_custom_call" | custom-call | flops 1000000000 | bytes 1048576 | tf_op jit(solution)/shard_map/pallas_call | solution.py:312
  34.6 0.1 collective-permute-start.17
  34.7 1.5 %collective-permute-done.13 = bf16[48,512]{1,0:T(8,128)(2,1)S(1)} collective-permute-done((bf16[48,512]{1,0:T(8,128)(2,1)S(1)}, bf16[48,512]{1,0:T(8,128)(2,1)S(1)}, u32[]{:S(2)}, u32[]{:S(2)}) %collective-permute-start.13) | collective-permute-done | bytes 49184 | tf_op jit(solution)/shard_map/ppermute | solution.py:325
  36.2 1.1 %collective-permute-start.14 = (bf16[48,512]{1,0:T(8,128)(2,1)S(1)}, bf16[48,512]{1,0:T(8,128)(2,1)S(1)}, u32[]{:S(2)}, u32[]{:S(2)}) collective-permute-start(bf16[48,512]{1,0:T(8,128)(2,1)S(1)} %add_convert_fusion.1.refs_0_), channel_id=1, source_target_pairs={{0,8},{4,12},{8,0},{12,4},{1,9},{5,13},{9,1},{13,5},{2,10},{6,14},... | collective-permute-start | bytes 147464 | tf_op jit(solution)/shard_map/ppermute | solution.py:511
  37.3 1.6 %collective-permute-start.15 = (bf16[48,512]{1,0:T(8,128)(2,1)S(1)}, bf16[48,512]{1,0:T(8,128)(2,1)S(1)}, u32[]{:S(2)}, u32[]{:S(2)}) collective-permute-start(bf16[48,512]{1,0:T(8,128)(2,1)S(1)} %add_convert_fusion.1.refs_0_), channel_id=1, source_target_pairs={{0,4},{4,8},{8,12},{12,0},{1,5},{5,9},{9,13},{13,1},{2,6},{6,10},{... | collective-permute-start | bytes 147464 | tf_op jit(solution)/shard_map/ppermute | solution.py:511
  38.9 2.2 %collective-permute-start.16 = (bf16[48,512]{1,0:T(8,128)(2,1)S(1)}, bf16[48,512]{1,0:T(8,128)(2,1)S(1)}, u32[]{:S(2)}, u32[]{:S(2)}) collective-permute-start(bf16[48,512]{1,0:T(8,128)(2,1)S(1)} %add_convert_fusion.1.refs_0_), channel_id=1, source_target_pairs={{0,12},{4,0},{8,4},{12,8},{1,13},{5,1},{9,5},{13,9},{2,14},{6,2},{... | collective-permute-start | bytes 147464 | tf_op jit(solution)/shard_map/ppermute | solution.py:511
  41.1 0.0 collective-permute-done.17
  41.1 0.8 %fusion = bf16[1,512,256]{2,1,0:T(8,128)(2,1)} fusion(f32[512,256]{1,0:T(8,128)S(1)} %get-tuple-element.72, bf16[512,256]{1,0:T(8,128)(2,1)S(1)} %collective-permute-done.17), kind=kLoop, calls=%fused_computation.1 | loop fusion | flops 393216 | bytes 1048576 | tf_op jit(solution)/shard_map/broadcast_in_dim | solution.py:501
  41.9 1.8 %collective-permute-done.14.refs_1_ = bf16[48,512]{1,0:T(8,128)(2,1)S(1)} collective-permute-done((bf16[48,512]{1,0:T(8,128)(2,1)S(1)}, bf16[48,512]{1,0:T(8,128)(2,1)S(1)}, u32[]{:S(2)}, u32[]{:S(2)}) %collective-permute-start.14) | collective-permute-done | bytes 49184 | tf_op jit(solution)/shard_map/ppermute | solution.py:511
  43.6 0.0 collective-permute-done.15.refs_2_
  43.6 0.0 collective-permute-done.16.refs_3_
  43.7 0.1 collective-permute-start.18
  43.7 1.2 %collective-permute-done.18.recv_ref = f32[48,256]{1,0:T(8,128)S(1)} collective-permute-done((f32[48,256]{1,0:T(8,128)S(1)}, f32[48,256]{1,0:T(8,128)S(1)}, u32[]{:S(2)}, u32[]{:S(2)}) %collective-permute-start.18) | collective-permute-done | bytes 49184 | tf_op jit(solution)/shard_map/ppermute | solution.py:325
  44.9 0.7 %shard_map.130 = (f32[48,512]{1,0:T(8,128)}, f32[48,256]{1,0:T(8,128)}) custom-call(f32[48,256]{1,0:T(8,128)S(1)} %get-tuple-element.79.own_ref, f32[48,256]{1,0:T(8,128)S(1)} %collective-permute-done.18.recv_ref, f32[48,256]{1,0:T(8,128)S(1)} %get-tuple-element.80.up_ref), custom_call_target="tpu_custom_call" | custom-call | bytes 1048576 | tf_op jit(solution)/shard_map/pallas_call | solution.py:312
  (5 shorter events, 0.1 us)
Async XLA Ops:
  1.7 10.5 %collective-permute-start.2 = (bf16[128,512]{1,0:T(8,128)(2,1)S(1)}, bf16[128,512]{1,0:T(8,128)(2,1)S(1)}, u32[]{:S(2)}, u32[]{:S(2)}) collective-permute-start(bf16[128,512]{1,0:T(8,128)(2,1)S(1)} %get-tuple-element.43.refs_12_), channel_id=1, source_target_pairs={{0,8},{4,12},{8,0},{12,4},{16,28},{20,24},{24,20},{28,16},{1,9},{5... | collective-permute-start | bytes 393224 | tf_op jit(solution)/shard_map/ppermute | solution.py:354
  5.8 6.8 %collective-permute-start.3 = (bf16[128,512]{1,0:T(8,128)(2,1)S(1)}, bf16[128,512]{1,0:T(8,128)(2,1)S(1)}, u32[]{:S(2)}, u32[]{:S(2)}) collective-permute-start(bf16[128,512]{1,0:T(8,128)(2,1)S(1)} %get-tuple-element.43.refs_12_), channel_id=1, source_target_pairs={{0,4},{4,0},{8,12},{12,8},{1,5},{5,1},{9,13},{13,9},{2,6},{6,2},{1... | collective-permute-start | bytes 393224 | tf_op jit(solution)/shard_map/ppermute | solution.py:325
  9.8 8.5 %collective-permute-start = (bf16[256,512]{1,0:T(8,128)(2,1)S(1)}, bf16[256,512]{1,0:T(8,128)(2,1)S(1)}, u32[]{:S(2)}, u32[]{:S(2)}) collective-permute-start(bf16[256,512]{1,0:T(8,128)(2,1)S(1)} %get-tuple-element.47), channel_id=1, source_target_pairs={{0,4},{4,0},{8,12},{12,8},{1,5},{5,1},{9,13},{13,9},{2,6},{6,2},{1... | collective-permute-start | bytes 786440 | tf_op jit(solution)/shard_map/ppermute | solution.py:325
  10.3 7.9 %collective-permute-start.1 = (bf16[256,512]{1,0:T(8,128)(2,1)S(1)}, bf16[256,512]{1,0:T(8,128)(2,1)S(1)}, u32[]{:S(2)}, u32[]{:S(2)}) collective-permute-start(bf16[256,512]{1,0:T(8,128)(2,1)S(1)} %get-tuple-element.47), channel_id=1, source_target_pairs={{0,0},{4,8},{8,4},{12,12},{1,1},{5,9},{9,5},{13,13},{2,2},{6,10},{... | collective-permute-start | bytes 786440 | tf_op jit(solution)/shard_map/ppermute | solution.py:432
  12.6 5.6 %collective-permute-start.4 = (bf16[128,512]{1,0:T(8,128)(2,1)S(1)}, bf16[128,512]{1,0:T(8,128)(2,1)S(1)}, u32[]{:S(2)}, u32[]{:S(2)}) collective-permute-start(bf16[128,512]{1,0:T(8,128)(2,1)S(1)} %collective-permute-done.2.refs_14_.two_ref), channel_id=1, source_target_pairs={{0,16},{16,0},{1,17},{17,1},{2,18},{18,2},{3,19},{19,3},{4,20},{20... | collective-permute-start | bytes 393224 | tf_op jit(solution)/shard_map/ppermute | solution.py:325
  15.3 3.6 %collective-permute-start.9 = (bf16[512,256]{1,0:T(8,128)(2,1)S(1)}, bf16[512,256]{1,0:T(8,128)(2,1)S(1)}, u32[]{:S(2)}, u32[]{:S(2)}) collective-permute-start(bf16[512,256]{1,0:T(8,128)(2,1)S(1)} %get-tuple-element.55.refs_8_), channel_id=1, source_target_pairs={{0,1},{1,0},{2,3},{3,2},{4,5},{5,4},{6,7},{7,6},{8,9},{9,8},{10,11... | collective-permute-start | bytes 786440 | tf_op jit(solution)/shard_map/ppermute | solution.py:325
  15.3 9.7 %collective-permute-start.10 = (bf16[256,512]{1,0:T(8,128)(2,1)S(1)}, bf16[256,512]{1,0:T(8,128)(2,1)S(1)}, u32[]{:S(2)}, u32[]{:S(2)}) collective-permute-start(bf16[256,512]{1,0:T(8,128)(2,1)S(1)} %shard_map.125), channel_id=1, source_target_pairs={{0,2},{2,0},{1,3},{3,1},{4,6},{6,4},{5,7},{7,5},{8,10},{10,8},{9,1... | collective-permute-start | bytes 786440 | tf_op jit(solution)/shard_map/ppermute | solution.py:325
  18.3 1.4 %collective-permute-start.5 = (bf16[128,512]{1,0:T(8,128)(2,1)S(1)}, bf16[128,512]{1,0:T(8,128)(2,1)S(1)}, u32[]{:S(2)}, u32[]{:S(2)}) collective-permute-start(bf16[128,512]{1,0:T(8,128)(2,1)S(1)} %get-tuple-element.51), channel_id=1, source_target_pairs={{0,1},{1,0},{2,3},{3,2},{4,5},{5,4},{6,7},{7,6},{8,9},{9,8},{10,11... | collective-permute-start | bytes 393224 | tf_op jit(solution)/shard_map/ppermute | solution.py:325
  18.3 2.8 %collective-permute-start.6 = (bf16[128,512]{1,0:T(8,128)(2,1)S(1)}, bf16[128,512]{1,0:T(8,128)(2,1)S(1)}, u32[]{:S(2)}, u32[]{:S(2)}) collective-permute-start(bf16[128,512]{1,0:T(8,128)(2,1)S(1)} %get-tuple-element.52), channel_id=1, source_target_pairs={{0,1},{1,0},{2,3},{3,2},{4,5},{5,4},{6,7},{7,6},{8,9},{9,8},{10,11... | collective-permute-start | bytes 393224 | tf_op jit(solution)/shard_map/ppermute | solution.py:325
  18.8 2.3 %collective-permute-start.7 = (bf16[128,512]{1,0:T(8,128)(2,1)S(1)}, bf16[128,512]{1,0:T(8,128)(2,1)S(1)}, u32[]{:S(2)}, u32[]{:S(2)}) collective-permute-start(bf16[128,512]{1,0:T(8,128)(2,1)S(1)} %get-tuple-element.53), channel_id=1, source_target_pairs={{0,1},{1,0},{2,3},{3,2},{4,5},{5,4},{6,7},{7,6},{8,9},{9,8},{10,11... | collective-permute-start | bytes 393224 | tf_op jit(solution)/shard_map/ppermute | solution.py:325
  18.9 2.3 %collective-permute-start.8 = (bf16[128,512]{1,0:T(8,128)(2,1)S(1)}, bf16[128,512]{1,0:T(8,128)(2,1)S(1)}, u32[]{:S(2)}, u32[]{:S(2)}) collective-permute-start(bf16[128,512]{1,0:T(8,128)(2,1)S(1)} %get-tuple-element.54), channel_id=1, source_target_pairs={{0,1},{1,0},{2,3},{3,2},{4,5},{5,4},{6,7},{7,6},{8,9},{9,8},{10,11... | collective-permute-start | bytes 393224 | tf_op jit(solution)/shard_map/ppermute | solution.py:325
  19.7 7.2 %collective-permute-start.11 = (bf16[128,512]{1,0:T(8,128)(2,1)S(1)}, bf16[128,512]{1,0:T(8,128)(2,1)S(1)}, u32[]{:S(2)}, u32[]{:S(2)}) collective-permute-start(bf16[128,512]{1,0:T(8,128)(2,1)S(1)} %collective-permute-done.4.refs_15_), channel_id=1, source_target_pairs={{0,2},{2,0},{1,3},{3,1},{4,6},{6,4},{5,7},{7,5},{8,10},{10,8},{9,1... | collective-permute-start | bytes 393224 | tf_op jit(solution)/shard_map/ppermute | solution.py:325
  30.7 1.3 %collective-permute-start.12 = (bf16[48,256]{1,0:T(8,128)(2,1)S(1)}, bf16[48,256]{1,0:T(8,128)(2,1)S(1)}, u32[]{:S(2)}, u32[]{:S(2)}) collective-permute-start(bf16[48,256]{1,0:T(8,128)(2,1)S(1)} %get-tuple-element.64), channel_id=1, source_target_pairs={{0,1},{1,0},{2,3},{3,2},{4,5},{5,4},{6,7},{7,6},{8,9},{9,8},{10,11... | collective-permute-start | bytes 73736 | tf_op jit(solution)/shard_map/ppermute | solution.py:325
  32.0 4.2 %collective-permute-start.13 = (bf16[48,512]{1,0:T(8,128)(2,1)S(1)}, bf16[48,512]{1,0:T(8,128)(2,1)S(1)}, u32[]{:S(2)}, u32[]{:S(2)}) collective-permute-start(bf16[48,512]{1,0:T(8,128)(2,1)S(1)} %shard_map.127), channel_id=1, source_target_pairs={{0,2},{2,0},{1,3},{3,1},{4,6},{6,4},{5,7},{7,5},{8,10},{10,8},{9,1... | collective-permute-start | bytes 147464 | tf_op jit(solution)/shard_map/ppermute | solution.py:325
  34.6 6.5 %collective-permute-start.17 = (bf16[512,256]{1,0:T(8,128)(2,1)S(1)}, bf16[512,256]{1,0:T(8,128)(2,1)S(1)}, u32[]{:S(2)}, u32[]{:S(2)}) collective-permute-start(bf16[512,256]{1,0:T(8,128)(2,1)S(1)} %get-tuple-element.73), channel_id=1, source_target_pairs={{0,1},{1,0},{2,3},{3,2},{4,5},{5,4},{6,7},{7,6},{8,9},{9,8},{10,11... | collective-permute-start | bytes 786440 | tf_op jit(solution)/shard_map/ppermute | solution.py:325
  36.2 7.4 %collective-permute-start.14 = (bf16[48,512]{1,0:T(8,128)(2,1)S(1)}, bf16[48,512]{1,0:T(8,128)(2,1)S(1)}, u32[]{:S(2)}, u32[]{:S(2)}) collective-permute-start(bf16[48,512]{1,0:T(8,128)(2,1)S(1)} %add_convert_fusion.1.refs_0_), channel_id=1, source_target_pairs={{0,8},{4,12},{8,0},{12,4},{1,9},{5,13},{9,1},{13,5},{2,10},{6,14},... | collective-permute-start | bytes 147464 | tf_op jit(solution)/shard_map/ppermute | solution.py:511
  37.3 6.4 %collective-permute-start.15 = (bf16[48,512]{1,0:T(8,128)(2,1)S(1)}, bf16[48,512]{1,0:T(8,128)(2,1)S(1)}, u32[]{:S(2)}, u32[]{:S(2)}) collective-permute-start(bf16[48,512]{1,0:T(8,128)(2,1)S(1)} %add_convert_fusion.1.refs_0_), channel_id=1, source_target_pairs={{0,4},{4,8},{8,12},{12,0},{1,5},{5,9},{9,13},{13,1},{2,6},{6,10},{... | collective-permute-start | bytes 147464 | tf_op jit(solution)/shard_map/ppermute | solution.py:511
  38.9 4.7 %collective-permute-start.16 = (bf16[48,512]{1,0:T(8,128)(2,1)S(1)}, bf16[48,512]{1,0:T(8,128)(2,1)S(1)}, u32[]{:S(2)}, u32[]{:S(2)}) collective-permute-start(bf16[48,512]{1,0:T(8,128)(2,1)S(1)} %add_convert_fusion.1.refs_0_), channel_id=1, source_target_pairs={{0,12},{4,0},{8,4},{12,8},{1,13},{5,1},{9,5},{13,9},{2,14},{6,2},{... | collective-permute-start | bytes 147464 | tf_op jit(solution)/shard_map/ppermute | solution.py:511
  43.7 1.3 %collective-permute-start.18 = (f32[48,256]{1,0:T(8,128)S(1)}, f32[48,256]{1,0:T(8,128)S(1)}, u32[]{:S(2)}, u32[]{:S(2)}) collective-permute-start(f32[48,256]{1,0:T(8,128)S(1)} %get-tuple-element.79.own_ref), channel_id=1, source_target_pairs={{0,1},{1,0},{2,3},{3,2},{4,5},{5,4},{6,7},{7,6},{8,9},{9,8},{10,11... | collective-permute-start | bytes 147464 | tf_op jit(solution)/shard_map/ppermute | solution.py:325

commit v12 on v11

--- a/solution.py
+++ b/solution.py
@@ -92,7 +92,7 @@
 def head_kernel(split, which, piece_rows, *refs):
     table_vmem, normed_ref, a_own_ref, a_sib_ref, a_sib2_ref = refs[:5]
     b_own_ref, b_sib_ref, b_sib2_ref, cot_own_ref, cot_sib_ref, down_ref, up_ref = refs[5:12]
-    rest, scratch = refs[12:-11], refs[-11:]
+    rest, scratch = refs[12:-12], refs[-12:]
     if which == 0:
         pieces, (att_ref, wo_ref, low_ref, acc_ref, up_out) = rest[:-5], rest[-5:]
     else:
@@ -100,6 +100,7 @@
         pieces, (att_ref, wo_ref, keep_ref, send_ref, up_out) = rest[3:-5], rest[-5:]
     w_ref, kv_ref, q_ref, do_ref, dq_ref, t_ref, back_ref = scratch[:7]
     table_ref, table_sem = scratch[8:10]
+    more_ref = scratch[11]
     if which:
         acc_ref = scratch[7]
     table_copy = pltpu.make_async_copy(table_vmem, table_ref, table_sem)
@@ -229,9 +230,12 @@
 
     acc_ref[...] = acc_in[...] if which else jnp.zeros_like(acc_ref)
     acc_ref[:RANK, :rows] += nt(up_q, dq_ref[...])
-    for i, starts in enumerate(all_starts):
-        for e, s in enumerate(starts):
-            acc_ref[RANK:, pl.ds(s, BLK)] += back_ref[i, :, e * BLK : (e + 1) * BLK]
+    half_acc = [acc_ref.at[RANK:, :], more_ref]
+    more_ref[...] = jnp.zeros_like(more_ref)
+    for e in range(len(all_starts[0])):
+        for i, starts in enumerate(all_starts):
+            half_acc[i % 2][:, pl.ds(starts[e], BLK)] += back_ref[i, :, e * BLK : (e + 1) * BLK]
+    acc_ref[RANK:, :] += more_ref[...]
     up_grad = adapter_scale * jnp.concatenate(
         [
             tn(low_ref[:rows, :], dq_ref[...])[0:RANK],
@@ -349,7 +353,7 @@
     if not split_weights():
         whole = [lax.all_gather(m, "node", axis=0, tiled=True) for m in (first, second)]
         return [whole[:1], whole[1:]], lambda node: [0], whole
-    far_pairs = [(g * 4 + n, g * 4 + (n ^ (2 + g))) for g in range(2) for n in range(4)]
+    far_pairs = [(g * 4 + n, g * 4 + (n ^ (3 - g))) for g in range(2) for n in range(4)]
     near = swap(first, "node")
     far = lax.ppermute(first, ("group", "node"), far_pairs)
     far, near, _ = lax.optimization_barrier((far, near, half))
@@ -360,7 +364,7 @@
 
     def piece_rows(node):
         group = lax.axis_index("group")
-        return [jnp.bitwise_xor(node, k) * depth for k in (0, 1, 2 + group, 3 - group)]
+        return [jnp.bitwise_xor(node, k) * depth for k in (0, 1, 3 - group, 2 + group)]
 
     return [[first, near, far, other_far], theirs], piece_rows, other_far
 
@@ -462,6 +466,7 @@
         pltpu.SMEM(table.shape, jnp.int32),
         pltpu.SemaphoreType.DMA,
         pltpu.VMEM((3 * RANK, width), F32),
+        pltpu.VMEM((2 * RANK, 3 * rows), F32),
     ]
     att1, wo1, low, acc, up1 = call(
         functools.partial(head_kernel, split, 0, piece_rows),
@@ -507,7 +512,7 @@
         hops += [("node", 1 << i) for i in range(count.bit_length() - 2)]
     for axis, step in hops:
         lora = (lora.astype(F32) + swap(lora, axis, step).astype(F32)).astype(BF16)
-    steps = (2, 1, 3) if count == 4 else (count // 2,)
+    steps = (1, 2, 3) if count == 4 else (count // 2,)
     terms = (lora, *[lax.ppermute(lora, "node", [(i, (i + k) % count) for i in range(count)]) for k in steps])
     terms, mesh_out = lax.optimization_barrier((terms, mesh_out))
     down_half, up_total = call(

time: 45.8 us -> 45.2 us (0.987)
  starting transfers between devices: 20.4 us -> 19.8 us
    ppermute x14, starting transfers between devices: 10.7 us -> 8.47 us  [swap(): return lax.ppermute(value, axis, [(i, i ^ step) for i in range(size)])]
    ppermute x14, waiting for transfers between devices: 7.83 us -> 9.34 us  [swap(): return lax.ppermute(value, axis, [(i, i ^ step) for i in range(size)])]
    ppermute x1, waiting for transfers between devices: 1.27 us -> 0.01 us  [gather_weights(): far = lax.ppermute(first, ('group', 'node'), far_pairs)]
    ppermute x1, starting transfers between devices: 4.1 us -> 5.11 us  [gather_weights(): far = lax.ppermute(first, ('group', 'node'), far_pairs)]
    ppermute x3, starting transfers between devices: 4.91 us -> 5.56 us  [shards(): lax.ppermute(lora, 'node', [(i, (i + k) % count) for i in range(count)])]
where the time goes in v12:
time: 45.2 us; the launch traced here: 45 us
  starting transfers between devices  19.8 us (44%)
  Pallas kernels  12.7 us (28%)
  waiting for transfers between devices  10.9 us (24%)
  other arithmetic  0.78 us (2%)
  between operations  0.76 us (2%)
    pallas_call x10, Pallas kernels, call(): pl.pallas_call(kernel, out_shape=outs, in_specs=[HBM] * hbm + [VMEM] * (l...  12.7 us
    ppermute x14, waiting for transfers between devices, swap(): return lax.ppermute(value, axis, [(i, i ^ step) for i in range(size)])  9.34 us
    ppermute x14, starting transfers between devices, swap(): return lax.ppermute(value, axis, [(i, i ^ step) for i in range(size)])  8.47 us
    ppermute x3, starting transfers between devices, shards(): lax.ppermute(lora, 'node', [(i, (i + k) % count) for i in range(count)])  5.56 us
    ppermute x1, starting transfers between devices, gather_weights(): far = lax.ppermute(first, ('group', 'node'), far_pairs)  5.11 us
    ppermute x3, waiting for transfers between devices, shards(): lax.ppermute(lora, 'node', [(i, (i + k) % count) for i in range(count)])  1.55 us
  transfers between devices with their start and end apart: 19, of which 9 were waited for; matrix products, arithmetic and copies ran while one was open for 2% of the time, Pallas kernels for 16%

profile of v12, /device:TPU:0, one launch (start us, length us, event | category | flops | bytes accessed | tf_op | source)
XLA Modules:
  0.0 45.0 jit_solution(409443497796208849)
XLA Ops:
  0.6 1.1 %shard_map.121 = (bf16[128,512]{1,0:T(8,128)(2,1)S(1)}, bf16[128,512]{1,0:T(8,128)(2,1)S(1)}) custom-call(bf16[128,256]{1,0:T(8,128)(2,1)} %refs_0_.1, bf16[128,256]{1,0:T(8,128)(2,1)} %refs_1_.1, bf16[128,256]{1,0:T(8,128)(2,1)} %refs_2_.1, bf16[256,128]{1,0:T(8,128)(2,1)} %refs_3_.1), custom_call_target="tpu_custom_call" | custom-call | bytes 1048576 | tf_op jit(solution)/shard_map/pallas_call | solution.py:316
  1.7 5.1 %collective-permute-start.2 = (bf16[128,512]{1,0:T(8,128)(2,1)S(1)}, bf16[128,512]{1,0:T(8,128)(2,1)S(1)}, u32[]{:S(2)}, u32[]{:S(2)}) collective-permute-start(bf16[128,512]{1,0:T(8,128)(2,1)S(1)} %get-tuple-element.43.refs_12_), channel_id=1, source_target_pairs={{0,12},{4,8},{8,4},{12,0},{16,24},{20,28},{24,16},{28,20},{1,13},{... | collective-permute-start | bytes 393224 | tf_op jit(solution)/shard_map/ppermute | solution.py:358
  6.8 0.0 collective-permute-start.3
  6.8 2.4 %shard_map.122 = (s32[1,512]{1,0:T(1,128)S(1)}, s32[6,16]{1,0:T(8,128)S(1)}, bf16[48,512]{1,0:T(8,128)(2,1)S(1)}, bf16[48,256]{1,0:T(8,128)(2,1)S(1)}, bf16[512,...) custom-call(s32[1,512]{1,0:T(1,128)} %bitcast.21, ...), custom_call_target="tpu_custom_call" | custom-call | flops 402653184 | bytes 1048576 | tf_op jit(solution)/shard_map/pallas_call | solution.py:316
  9.2 2.1 %collective-permute-start = (bf16[256,512]{1,0:T(8,128)(2,1)S(1)}, bf16[256,512]{1,0:T(8,128)(2,1)S(1)}, u32[]{:S(2)}, u32[]{:S(2)}) collective-permute-start(bf16[256,512]{1,0:T(8,128)(2,1)S(1)} %get-tuple-element.47), channel_id=1, source_target_pairs={{0,4},{4,0},{8,12},{12,8},{1,5},{5,1},{9,13},{13,9},{2,6},{6,2},{1... | collective-permute-start | bytes 786440 | tf_op jit(solution)/shard_map/ppermute | solution.py:329
  11.3 0.7 %collective-permute-start.1 = (bf16[256,512]{1,0:T(8,128)(2,1)S(1)}, bf16[256,512]{1,0:T(8,128)(2,1)S(1)}, u32[]{:S(2)}, u32[]{:S(2)}) collective-permute-start(bf16[256,512]{1,0:T(8,128)(2,1)S(1)} %get-tuple-element.47), channel_id=1, source_target_pairs={{0,0},{4,8},{8,4},{12,12},{1,1},{5,9},{9,5},{13,13},{2,2},{6,10},{... | collective-permute-start | bytes 786440 | tf_op jit(solution)/shard_map/ppermute | solution.py:436
  12.0 0.0 collective-permute-done.2.refs_14_.two_ref
  12.0 1.7 %collective-permute-done.3.refs_13_.one_ref = bf16[128,512]{1,0:T(8,128)(2,1)S(1)} collective-permute-done((bf16[128,512]{1,0:T(8,128)(2,1)S(1)}, bf16[128,512]{1,0:T(8,128)(2,1)S(1)}, u32[]{:S(2)}, u32[]{:S(2)}) %collective-permute-start.3) | collective-permute-done | bytes 131104 | tf_op jit(solution)/shard_map/ppermute | solution.py:329
  13.7 0.5 %collective-permute-start.4 = (bf16[128,512]{1,0:T(8,128)(2,1)S(1)}, bf16[128,512]{1,0:T(8,128)(2,1)S(1)}, u32[]{:S(2)}, u32[]{:S(2)}) collective-permute-start(bf16[128,512]{1,0:T(8,128)(2,1)S(1)} %collective-permute-done.2.refs_14_.two_ref), channel_id=1, source_target_pairs={{0,16},{16,0},{1,17},{17,1},{2,18},{18,2},{3,19},{19,3},{4,20},{20... | collective-permute-start | bytes 393224 | tf_op jit(solution)/shard_map/ppermute | solution.py:329
  14.1 0.0 collective-permute-start.9
  14.2 1.6 %collective-permute-start.10 = (bf16[256,512]{1,0:T(8,128)(2,1)S(1)}, bf16[256,512]{1,0:T(8,128)(2,1)S(1)}, u32[]{:S(2)}, u32[]{:S(2)}) collective-permute-start(bf16[256,512]{1,0:T(8,128)(2,1)S(1)} %shard_map.125), channel_id=1, source_target_pairs={{0,2},{2,0},{1,3},{3,1},{4,6},{6,4},{5,7},{7,5},{8,10},{10,8},{9,1... | collective-permute-start | bytes 786440 | tf_op jit(solution)/shard_map/ppermute | solution.py:329
  15.7 2.9 %collective-permute-done.4.refs_15_ = bf16[128,512]{1,0:T(8,128)(2,1)S(1)} collective-permute-done((bf16[128,512]{1,0:T(8,128)(2,1)S(1)}, bf16[128,512]{1,0:T(8,128)(2,1)S(1)}, u32[]{:S(2)}, u32[]{:S(2)}) %collective-permute-start.4) | collective-permute-done | bytes 131104 | tf_op jit(solution)/shard_map/ppermute | solution.py:329
  18.6 0.2 collective-permute-done.a_ref.refs_2_
  18.8 0.0 collective-permute-done.1.b_ref.refs_5_
  18.9 0.1 collective-permute-start.5
  19.0 0.5 %collective-permute-start.6 = (bf16[128,512]{1,0:T(8,128)(2,1)S(1)}, bf16[128,512]{1,0:T(8,128)(2,1)S(1)}, u32[]{:S(2)}, u32[]{:S(2)}) collective-permute-start(bf16[128,512]{1,0:T(8,128)(2,1)S(1)} %get-tuple-element.52), channel_id=1, source_target_pairs={{0,1},{1,0},{2,3},{3,2},{4,5},{5,4},{6,7},{7,6},{8,9},{9,8},{10,11... | collective-permute-start | bytes 393224 | tf_op jit(solution)/shard_map/ppermute | solution.py:329
  19.5 0.1 collective-permute-start.7
  19.5 0.0 collective-permute-done.9.refs_9_
  19.5 0.4 collective-permute-start.8
  20.0 0.3 collective-permute-done.5.refs_3_
  20.3 1.5 %collective-permute-start.11 = (bf16[128,512]{1,0:T(8,128)(2,1)S(1)}, bf16[128,512]{1,0:T(8,128)(2,1)S(1)}, u32[]{:S(2)}, u32[]{:S(2)}) collective-permute-start(bf16[128,512]{1,0:T(8,128)(2,1)S(1)} %collective-permute-done.4.refs_15_), channel_id=1, source_target_pairs={{0,2},{2,0},{1,3},{3,1},{4,6},{6,4},{5,7},{7,5},{8,10},{10,8},{9,1... | collective-permute-start | bytes 393224 | tf_op jit(solution)/shard_map/ppermute | solution.py:329
  21.8 0.0 collective-permute-done.6.refs_4_
  21.8 0.0 collective-permute-done.7.refs_6_
  21.8 0.0 collective-permute-done.8.refs_7_
  21.8 3.7 %shard_map.124 = (bf16[512,128]{1,0:T(8,128)(2,1)S(1)}, bf16[512,128]{1,0:T(8,128)(2,1)S(1)}, bf16[1536,128]{1,0:T(8,128)(2,1)S(1)}, f32[48,1536]{1,0:T(8,128)S(1)}, f32[48,128]{1,0:T(8,128)S(1)}) custom-call(s32[6,16]{1,0:T(8,128)S(1)} %get-tuple-element.45.refs_0_, bf16[512,512]{1,0:T(8,128)(2,1)S(1)} %get-tuple-element.46.refs_1_, ...), custom_call_target="tpu_custom_call" | custom-call | bytes 1048576 | tf_op jit(solution)/shard_map/pallas_call | solution.py:316
  25.6 0.0 collective-permute-done.10.refs_16_
  25.6 0.3 collective-permute-done.11.refs_17_
  25.9 3.8 %shard_map.126 = (bf16[512,128]{1,0:T(8,128)(2,1)S(1)}, bf16[512,128]{1,0:T(8,128)(2,1)S(1)}, bf16[48,256]{1,0:T(8,128)(2,1)S(1)}, bf16[48,256]{1,0:T(8,128)(2,1)S(1)}, bf16[48,256]{1,0:T(8,128)(2,1)S(1)}) custom-call(s32[6,16]{1,0:T(8,128)S(1)} %get-tuple-element.45.refs_0_, bf16[512,512]{1,0:T(8,128)(2,1)S(1)} %get-tuple-element.46.refs_1_, ...), custom_call_target="tpu_custom_call" | custom-call | flops 4000000000 | bytes 1048576 | tf_op jit(solution)/shard_map/pallas_call | solution.py:316
  29.7 0.1 collective-permute-start.12
  29.7 1.2 %collective-permute-done.12.sibling_ref = bf16[48,256]{1,0:T(8,128)(2,1)S(1)} collective-permute-done((bf16[48,256]{1,0:T(8,128)(2,1)S(1)}, bf16[48,256]{1,0:T(8,128)(2,1)S(1)}, u32[]{:S(2)}, u32[]{:S(2)}) %collective-permute-start.12) | collective-permute-done | bytes 24608 | tf_op jit(solution)/shard_map/ppermute | solution.py:329
  30.9 1.6 %collective-permute-start.13 = (bf16[48,512]{1,0:T(8,128)(2,1)S(1)}, bf16[48,512]{1,0:T(8,128)(2,1)S(1)}, u32[]{:S(2)}, u32[]{:S(2)}) collective-permute-start(bf16[48,512]{1,0:T(8,128)(2,1)S(1)} %shard_map.127), channel_id=1, source_target_pairs={{0,2},{2,0},{1,3},{3,1},{4,6},{6,4},{5,7},{7,5},{8,10},{10,8},{9,1... | collective-permute-start | bytes 147464 | tf_op jit(solution)/shard_map/ppermute | solution.py:329
  32.5 1.0 %shard_map.128 = (f32[512,256]{1,0:T(8,128)S(1)}, bf16[512,256]{1,0:T(8,128)(2,1)S(1)}) custom-call(s32[1,512]{1,0:T(1,128)S(1)} %get-tuple-element.66.order_ref, bf16[512,256]{1,0:T(8,128)(2,1)S(1)} %get-tuple-element.67.x_ref, bf16[512,128]{1,0:T(8,128)(2,1)S(1)} %get-tuple-element.68.att1_ref, bf16[512,128]{1,0:T(8,128)(2,1)S(1)} %get-tuple-element.69.att2_ref, ...), custom_call_target="tpu_custom_call" | custom-call | flops 1000000000 | bytes 1048576 | tf_op jit(solution)/shard_map/pallas_call | solution.py:316
  33.5 0.1 collective-permute-start.17
  33.6 1.5 %collective-permute-done.13 = bf16[48,512]{1,0:T(8,128)(2,1)S(1)} collective-permute-done((bf16[48,512]{1,0:T(8,128)(2,1)S(1)}, bf16[48,512]{1,0:T(8,128)(2,1)S(1)}, u32[]{:S(2)}, u32[]{:S(2)}) %collective-permute-start.13) | collective-permute-done | bytes 49184 | tf_op jit(solution)/shard_map/ppermute | solution.py:329
  35.1 2.3 %collective-permute-start.14 = (bf16[48,512]{1,0:T(8,128)(2,1)S(1)}, bf16[48,512]{1,0:T(8,128)(2,1)S(1)}, u32[]{:S(2)}, u32[]{:S(2)}) collective-permute-start(bf16[48,512]{1,0:T(8,128)(2,1)S(1)} %add_convert_fusion.1.refs_0_), channel_id=1, source_target_pairs={{0,4},{4,8},{8,12},{12,0},{1,5},{5,9},{9,13},{13,1},{2,6},{6,10},{... | collective-permute-start | bytes 147464 | tf_op jit(solution)/shard_map/ppermute | solution.py:516
  37.5 1.3 %collective-permute-start.15 = (bf16[48,512]{1,0:T(8,128)(2,1)S(1)}, bf16[48,512]{1,0:T(8,128)(2,1)S(1)}, u32[]{:S(2)}, u32[]{:S(2)}) collective-permute-start(bf16[48,512]{1,0:T(8,128)(2,1)S(1)} %add_convert_fusion.1.refs_0_), channel_id=1, source_target_pairs={{0,8},{4,12},{8,0},{12,4},{1,9},{5,13},{9,1},{13,5},{2,10},{6,14},... | collective-permute-start | bytes 147464 | tf_op jit(solution)/shard_map/ppermute | solution.py:516
  38.8 1.9 %collective-permute-start.16 = (bf16[48,512]{1,0:T(8,128)(2,1)S(1)}, bf16[48,512]{1,0:T(8,128)(2,1)S(1)}, u32[]{:S(2)}, u32[]{:S(2)}) collective-permute-start(bf16[48,512]{1,0:T(8,128)(2,1)S(1)} %add_convert_fusion.1.refs_0_), channel_id=1, source_target_pairs={{0,12},{4,0},{8,4},{12,8},{1,13},{5,1},{9,5},{13,9},{2,14},{6,2},{... | collective-permute-start | bytes 147464 | tf_op jit(solution)/shard_map/ppermute | solution.py:516
  40.7 0.0 collective-permute-done.17
  40.7 0.8 %fusion = bf16[1,512,256]{2,1,0:T(8,128)(2,1)} fusion(f32[512,256]{1,0:T(8,128)S(1)} %get-tuple-element.72, bf16[512,256]{1,0:T(8,128)(2,1)S(1)} %collective-permute-done.17), kind=kLoop, calls=%fused_computation.1 | loop fusion | flops 393216 | bytes 1048576 | tf_op jit(solution)/shard_map/broadcast_in_dim | solution.py:506
  41.4 0.0 collective-permute-done.14.refs_1_
  41.5 1.5 %collective-permute-done.15.refs_2_ = bf16[48,512]{1,0:T(8,128)(2,1)S(1)} collective-permute-done((bf16[48,512]{1,0:T(8,128)(2,1)S(1)}, bf16[48,512]{1,0:T(8,128)(2,1)S(1)}, u32[]{:S(2)}, u32[]{:S(2)}) %collective-permute-start.15) | collective-permute-done | bytes 49184 | tf_op jit(solution)/shard_map/ppermute | solution.py:516
  43.0 0.0 collective-permute-done.16.refs_3_
  43.0 0.1 collective-permute-start.18
  43.1 1.2 %collective-permute-done.18.recv_ref = f32[48,256]{1,0:T(8,128)S(1)} collective-permute-done((f32[48,256]{1,0:T(8,128)S(1)}, f32[48,256]{1,0:T(8,128)S(1)}, u32[]{:S(2)}, u32[]{:S(2)}) %collective-permute-start.18) | collective-permute-done | bytes 49184 | tf_op jit(solution)/shard_map/ppermute | solution.py:329
  44.3 0.7 %shard_map.130 = (f32[48,512]{1,0:T(8,128)}, f32[48,256]{1,0:T(8,128)}) custom-call(f32[48,256]{1,0:T(8,128)S(1)} %get-tuple-element.79.own_ref, f32[48,256]{1,0:T(8,128)S(1)} %collective-permute-done.18.recv_ref, f32[48,256]{1,0:T(8,128)S(1)} %get-tuple-element.80.up_ref), custom_call_target="tpu_custom_call" | custom-call | bytes 1048576 | tf_op jit(solution)/shard_map/pallas_call | solution.py:316
  (5 shorter events, 0.1 us)
Async XLA Ops:
  1.7 10.3 %collective-permute-start.2 = (bf16[128,512]{1,0:T(8,128)(2,1)S(1)}, bf16[128,512]{1,0:T(8,128)(2,1)S(1)}, u32[]{:S(2)}, u32[]{:S(2)}) collective-permute-start(bf16[128,512]{1,0:T(8,128)(2,1)S(1)} %get-tuple-element.43.refs_12_), channel_id=1, source_target_pairs={{0,12},{4,8},{8,4},{12,0},{16,24},{20,28},{24,16},{28,20},{1,13},{... | collective-permute-start | bytes 393224 | tf_op jit(solution)/shard_map/ppermute | solution.py:358
  6.8 6.8 %collective-permute-start.3 = (bf16[128,512]{1,0:T(8,128)(2,1)S(1)}, bf16[128,512]{1,0:T(8,128)(2,1)S(1)}, u32[]{:S(2)}, u32[]{:S(2)}) collective-permute-start(bf16[128,512]{1,0:T(8,128)(2,1)S(1)} %get-tuple-element.43.refs_12_), channel_id=1, source_target_pairs={{0,4},{4,0},{8,12},{12,8},{1,5},{5,1},{9,13},{13,9},{2,6},{6,2},{1... | collective-permute-start | bytes 393224 | tf_op jit(solution)/shard_map/ppermute | solution.py:329
  9.2 9.7 %collective-permute-start = (bf16[256,512]{1,0:T(8,128)(2,1)S(1)}, bf16[256,512]{1,0:T(8,128)(2,1)S(1)}, u32[]{:S(2)}, u32[]{:S(2)}) collective-permute-start(bf16[256,512]{1,0:T(8,128)(2,1)S(1)} %get-tuple-element.47), channel_id=1, source_target_pairs={{0,4},{4,0},{8,12},{12,8},{1,5},{5,1},{9,13},{13,9},{2,6},{6,2},{1... | collective-permute-start | bytes 786440 | tf_op jit(solution)/shard_map/ppermute | solution.py:329
  11.3 7.6 %collective-permute-start.1 = (bf16[256,512]{1,0:T(8,128)(2,1)S(1)}, bf16[256,512]{1,0:T(8,128)(2,1)S(1)}, u32[]{:S(2)}, u32[]{:S(2)}) collective-permute-start(bf16[256,512]{1,0:T(8,128)(2,1)S(1)} %get-tuple-element.47), channel_id=1, source_target_pairs={{0,0},{4,8},{8,4},{12,12},{1,1},{5,9},{9,5},{13,13},{2,2},{6,10},{... | collective-permute-start | bytes 786440 | tf_op jit(solution)/shard_map/ppermute | solution.py:436
  13.7 5.0 %collective-permute-start.4 = (bf16[128,512]{1,0:T(8,128)(2,1)S(1)}, bf16[128,512]{1,0:T(8,128)(2,1)S(1)}, u32[]{:S(2)}, u32[]{:S(2)}) collective-permute-start(bf16[128,512]{1,0:T(8,128)(2,1)S(1)} %collective-permute-done.2.refs_14_.two_ref), channel_id=1, source_target_pairs={{0,16},{16,0},{1,17},{17,1},{2,18},{18,2},{3,19},{19,3},{4,20},{20... | collective-permute-start | bytes 393224 | tf_op jit(solution)/shard_map/ppermute | solution.py:329
  14.1 5.4 %collective-permute-start.9 = (bf16[512,256]{1,0:T(8,128)(2,1)S(1)}, bf16[512,256]{1,0:T(8,128)(2,1)S(1)}, u32[]{:S(2)}, u32[]{:S(2)}) collective-permute-start(bf16[512,256]{1,0:T(8,128)(2,1)S(1)} %get-tuple-element.55.refs_8_), channel_id=1, source_target_pairs={{0,1},{1,0},{2,3},{3,2},{4,5},{5,4},{6,7},{7,6},{8,9},{9,8},{10,11... | collective-permute-start | bytes 786440 | tf_op jit(solution)/shard_map/ppermute | solution.py:329
  14.2 11.4 %collective-permute-start.10 = (bf16[256,512]{1,0:T(8,128)(2,1)S(1)}, bf16[256,512]{1,0:T(8,128)(2,1)S(1)}, u32[]{:S(2)}, u32[]{:S(2)}) collective-permute-start(bf16[256,512]{1,0:T(8,128)(2,1)S(1)} %shard_map.125), channel_id=1, source_target_pairs={{0,2},{2,0},{1,3},{3,1},{4,6},{6,4},{5,7},{7,5},{8,10},{10,8},{9,1... | collective-permute-start | bytes 786440 | tf_op jit(solution)/shard_map/ppermute | solution.py:329
  18.9 1.4 %collective-permute-start.5 = (bf16[128,512]{1,0:T(8,128)(2,1)S(1)}, bf16[128,512]{1,0:T(8,128)(2,1)S(1)}, u32[]{:S(2)}, u32[]{:S(2)}) collective-permute-start(bf16[128,512]{1,0:T(8,128)(2,1)S(1)} %get-tuple-element.51), channel_id=1, source_target_pairs={{0,1},{1,0},{2,3},{3,2},{4,5},{5,4},{6,7},{7,6},{8,9},{9,8},{10,11... | collective-permute-start | bytes 393224 | tf_op jit(solution)/shard_map/ppermute | solution.py:329
  19.0 2.8 %collective-permute-start.6 = (bf16[128,512]{1,0:T(8,128)(2,1)S(1)}, bf16[128,512]{1,0:T(8,128)(2,1)S(1)}, u32[]{:S(2)}, u32[]{:S(2)}) collective-permute-start(bf16[128,512]{1,0:T(8,128)(2,1)S(1)} %get-tuple-element.52), channel_id=1, source_target_pairs={{0,1},{1,0},{2,3},{3,2},{4,5},{5,4},{6,7},{7,6},{8,9},{9,8},{10,11... | collective-permute-start | bytes 393224 | tf_op jit(solution)/shard_map/ppermute | solution.py:329
  19.5 2.3 %collective-permute-start.7 = (bf16[128,512]{1,0:T(8,128)(2,1)S(1)}, bf16[128,512]{1,0:T(8,128)(2,1)S(1)}, u32[]{:S(2)}, u32[]{:S(2)}) collective-permute-start(bf16[128,512]{1,0:T(8,128)(2,1)S(1)} %get-tuple-element.53), channel_id=1, source_target_pairs={{0,1},{1,0},{2,3},{3,2},{4,5},{5,4},{6,7},{7,6},{8,9},{9,8},{10,11... | collective-permute-start | bytes 393224 | tf_op jit(solution)/shard_map/ppermute | solution.py:329
  19.5 2.3 %collective-permute-start.8 = (bf16[128,512]{1,0:T(8,128)(2,1)S(1)}, bf16[128,512]{1,0:T(8,128)(2,1)S(1)}, u32[]{:S(2)}, u32[]{:S(2)}) collective-permute-start(bf16[128,512]{1,0:T(8,128)(2,1)S(1)} %get-tuple-element.54), channel_id=1, source_target_pairs={{0,1},{1,0},{2,3},{3,2},{4,5},{5,4},{6,7},{7,6},{8,9},{9,8},{10,11... | collective-permute-start | bytes 393224 | tf_op jit(solution)/shard_map/ppermute | solution.py:329
  20.3 5.6 %collective-permute-start.11 = (bf16[128,512]{1,0:T(8,128)(2,1)S(1)}, bf16[128,512]{1,0:T(8,128)(2,1)S(1)}, u32[]{:S(2)}, u32[]{:S(2)}) collective-permute-start(bf16[128,512]{1,0:T(8,128)(2,1)S(1)} %collective-permute-done.4.refs_15_), channel_id=1, source_target_pairs={{0,2},{2,0},{1,3},{3,1},{4,6},{6,4},{5,7},{7,5},{8,10},{10,8},{9,1... | collective-permute-start | bytes 393224 | tf_op jit(solution)/shard_map/ppermute | solution.py:329
  29.7 1.3 %collective-permute-start.12 = (bf16[48,256]{1,0:T(8,128)(2,1)S(1)}, bf16[48,256]{1,0:T(8,128)(2,1)S(1)}, u32[]{:S(2)}, u32[]{:S(2)}) collective-permute-start(bf16[48,256]{1,0:T(8,128)(2,1)S(1)} %get-tuple-element.64), channel_id=1, source_target_pairs={{0,1},{1,0},{2,3},{3,2},{4,5},{5,4},{6,7},{7,6},{8,9},{9,8},{10,11... | collective-permute-start | bytes 73736 | tf_op jit(solution)/shard_map/ppermute | solution.py:329
  30.9 4.2 %collective-permute-start.13 = (bf16[48,512]{1,0:T(8,128)(2,1)S(1)}, bf16[48,512]{1,0:T(8,128)(2,1)S(1)}, u32[]{:S(2)}, u32[]{:S(2)}) collective-permute-start(bf16[48,512]{1,0:T(8,128)(2,1)S(1)} %shard_map.127), channel_id=1, source_target_pairs={{0,2},{2,0},{1,3},{3,1},{4,6},{6,4},{5,7},{7,5},{8,10},{10,8},{9,1... | collective-permute-start | bytes 147464 | tf_op jit(solution)/shard_map/ppermute | solution.py:329
  33.5 7.2 %collective-permute-start.17 = (bf16[512,256]{1,0:T(8,128)(2,1)S(1)}, bf16[512,256]{1,0:T(8,128)(2,1)S(1)}, u32[]{:S(2)}, u32[]{:S(2)}) collective-permute-start(bf16[512,256]{1,0:T(8,128)(2,1)S(1)} %get-tuple-element.73), channel_id=1, source_target_pairs={{0,1},{1,0},{2,3},{3,2},{4,5},{5,4},{6,7},{7,6},{8,9},{9,8},{10,11... | collective-permute-start | bytes 786440 | tf_op jit(solution)/shard_map/ppermute | solution.py:329
  35.1 6.3 %collective-permute-start.14 = (bf16[48,512]{1,0:T(8,128)(2,1)S(1)}, bf16[48,512]{1,0:T(8,128)(2,1)S(1)}, u32[]{:S(2)}, u32[]{:S(2)}) collective-permute-start(bf16[48,512]{1,0:T(8,128)(2,1)S(1)} %add_convert_fusion.1.refs_0_), channel_id=1, source_target_pairs={{0,4},{4,8},{8,12},{12,0},{1,5},{5,9},{9,13},{13,1},{2,6},{6,10},{... | collective-permute-start | bytes 147464 | tf_op jit(solution)/shard_map/ppermute | solution.py:516
  37.5 5.5 %collective-permute-start.15 = (bf16[48,512]{1,0:T(8,128)(2,1)S(1)}, bf16[48,512]{1,0:T(8,128)(2,1)S(1)}, u32[]{:S(2)}, u32[]{:S(2)}) collective-permute-start(bf16[48,512]{1,0:T(8,128)(2,1)S(1)} %add_convert_fusion.1.refs_0_), channel_id=1, source_target_pairs={{0,8},{4,12},{8,0},{12,4},{1,9},{5,13},{9,1},{13,5},{2,10},{6,14},... | collective-permute-start | bytes 147464 | tf_op jit(solution)/shard_map/ppermute | solution.py:516
  38.8 4.2 %collective-permute-start.16 = (bf16[48,512]{1,0:T(8,128)(2,1)S(1)}, bf16[48,512]{1,0:T(8,128)(2,1)S(1)}, u32[]{:S(2)}, u32[]{:S(2)}) collective-permute-start(bf16[48,512]{1,0:T(8,128)(2,1)S(1)} %add_convert_fusion.1.refs_0_), channel_id=1, source_target_pairs={{0,12},{4,0},{8,4},{12,8},{1,13},{5,1},{9,5},{13,9},{2,14},{6,2},{... | collective-permute-start | bytes 147464 | tf_op jit(solution)/shard_map/ppermute | solution.py:516
  43.0 1.3 %collective-permute-start.18 = (f32[48,256]{1,0:T(8,128)S(1)}, f32[48,256]{1,0:T(8,128)S(1)}, u32[]{:S(2)}, u32[]{:S(2)}) collective-permute-start(f32[48,256]{1,0:T(8,128)S(1)} %get-tuple-element.79.own_ref), channel_id=1, source_target_pairs={{0,1},{1,0},{2,3},{3,2},{4,5},{5,4},{6,7},{7,6},{8,9},{9,8},{10,11... | collective-permute-start | bytes 147464 | tf_op jit(solution)/shard_map/ppermute | solution.py:329

commit v13 on v12

--- a/solution.py
+++ b/solution.py
@@ -273,7 +273,7 @@
 def total_kernel(*refs):
     terms, (down_ref, up_ref) = [r[...].astype(F32) for r in refs[:-2]], refs[-2:]
     while len(terms) > 1:
-        terms = [a + b for a, b in zip(terms[::2], terms[1::2])]
+        terms = [a + b for a, b in zip(terms, terms[len(terms) // 2 :])]
     width = down_ref.shape[1]
     down_ref[...] = terms[0][:, :width]
     up_ref[...] = terms[0][:, width:]

time: 45.2 us -> 45.2 us (level)
  no operation moved by 1% of the time
where the time goes in v13:
time: 45.2 us; the launch traced here: 45 us
  starting transfers between devices  19.8 us (44%)
  Pallas kernels  12.7 us (28%)
  waiting for transfers between devices  10.9 us (24%)
  other arithmetic  0.78 us (2%)
  between operations  0.76 us (2%)
    pallas_call x10, Pallas kernels, call(): pl.pallas_call(kernel, out_shape=outs, in_specs=[HBM] * hbm + [VMEM] * (l...  12.7 us
    ppermute x14, waiting for transfers between devices, swap(): return lax.ppermute(value, axis, [(i, i ^ step) for i in range(size)])  9.34 us
    ppermute x14, starting transfers between devices, swap(): return lax.ppermute(value, axis, [(i, i ^ step) for i in range(size)])  8.47 us
    ppermute x3, starting transfers between devices, shards(): lax.ppermute(lora, 'node', [(i, (i + k) % count) for i in range(count)])  5.56 us
    ppermute x1, starting transfers between devices, gather_weights(): far = lax.ppermute(first, ('group', 'node'), far_pairs)  5.11 us
    ppermute x3, waiting for transfers between devices, shards(): lax.ppermute(lora, 'node', [(i, (i + k) % count) for i in range(count)])  1.56 us
  transfers between devices with their start and end apart: 19, of which 9 were waited for; matrix products, arithmetic and copies ran while one was open for 2% of the time, Pallas kernels for 16%

profile of v13, /device:TPU:0, one launch (start us, length us, event | category | flops | bytes accessed | tf_op | source)
XLA Modules:
  0.0 45.0 jit_solution(10026697474022141283)
XLA Ops:
  0.6 1.1 %shard_map.121 = (bf16[128,512]{1,0:T(8,128)(2,1)S(1)}, bf16[128,512]{1,0:T(8,128)(2,1)S(1)}) custom-call(bf16[128,256]{1,0:T(8,128)(2,1)} %refs_0_.1, bf16[128,256]{1,0:T(8,128)(2,1)} %refs_1_.1, bf16[128,256]{1,0:T(8,128)(2,1)} %refs_2_.1, bf16[256,128]{1,0:T(8,128)(2,1)} %refs_3_.1), custom_call_target="tpu_custom_call" | custom-call | bytes 1048576 | tf_op jit(solution)/shard_map/pallas_call | solution.py:316
  1.7 5.1 %collective-permute-start.2 = (bf16[128,512]{1,0:T(8,128)(2,1)S(1)}, bf16[128,512]{1,0:T(8,128)(2,1)S(1)}, u32[]{:S(2)}, u32[]{:S(2)}) collective-permute-start(bf16[128,512]{1,0:T(8,128)(2,1)S(1)} %get-tuple-element.43.refs_12_), channel_id=1, source_target_pairs={{0,12},{4,8},{8,4},{12,0},{16,24},{20,28},{24,16},{28,20},{1,13},{... | collective-permute-start | bytes 393224 | tf_op jit(solution)/shard_map/ppermute | solution.py:358
  6.8 0.0 collective-permute-start.3
  6.8 2.4 %shard_map.122 = (s32[1,512]{1,0:T(1,128)S(1)}, s32[6,16]{1,0:T(8,128)S(1)}, bf16[48,512]{1,0:T(8,128)(2,1)S(1)}, bf16[48,256]{1,0:T(8,128)(2,1)S(1)}, bf16[512,...) custom-call(s32[1,512]{1,0:T(1,128)} %bitcast.21, ...), custom_call_target="tpu_custom_call" | custom-call | flops 402653184 | bytes 1048576 | tf_op jit(solution)/shard_map/pallas_call | solution.py:316
  9.2 2.1 %collective-permute-start = (bf16[256,512]{1,0:T(8,128)(2,1)S(1)}, bf16[256,512]{1,0:T(8,128)(2,1)S(1)}, u32[]{:S(2)}, u32[]{:S(2)}) collective-permute-start(bf16[256,512]{1,0:T(8,128)(2,1)S(1)} %get-tuple-element.47), channel_id=1, source_target_pairs={{0,4},{4,0},{8,12},{12,8},{1,5},{5,1},{9,13},{13,9},{2,6},{6,2},{1... | collective-permute-start | bytes 786440 | tf_op jit(solution)/shard_map/ppermute | solution.py:329
  11.3 0.7 %collective-permute-start.1 = (bf16[256,512]{1,0:T(8,128)(2,1)S(1)}, bf16[256,512]{1,0:T(8,128)(2,1)S(1)}, u32[]{:S(2)}, u32[]{:S(2)}) collective-permute-start(bf16[256,512]{1,0:T(8,128)(2,1)S(1)} %get-tuple-element.47), channel_id=1, source_target_pairs={{0,0},{4,8},{8,4},{12,12},{1,1},{5,9},{9,5},{13,13},{2,2},{6,10},{... | collective-permute-start | bytes 786440 | tf_op jit(solution)/shard_map/ppermute | solution.py:436
  12.0 0.0 collective-permute-done.2.refs_14_.two_ref
  12.0 1.7 %collective-permute-done.3.refs_13_.one_ref = bf16[128,512]{1,0:T(8,128)(2,1)S(1)} collective-permute-done((bf16[128,512]{1,0:T(8,128)(2,1)S(1)}, bf16[128,512]{1,0:T(8,128)(2,1)S(1)}, u32[]{:S(2)}, u32[]{:S(2)}) %collective-permute-start.3) | collective-permute-done | bytes 131104 | tf_op jit(solution)/shard_map/ppermute | solution.py:329
  13.7 0.5 %collective-permute-start.4 = (bf16[128,512]{1,0:T(8,128)(2,1)S(1)}, bf16[128,512]{1,0:T(8,128)(2,1)S(1)}, u32[]{:S(2)}, u32[]{:S(2)}) collective-permute-start(bf16[128,512]{1,0:T(8,128)(2,1)S(1)} %collective-permute-done.2.refs_14_.two_ref), channel_id=1, source_target_pairs={{0,16},{16,0},{1,17},{17,1},{2,18},{18,2},{3,19},{19,3},{4,20},{20... | collective-permute-start | bytes 393224 | tf_op jit(solution)/shard_map/ppermute | solution.py:329
  14.1 0.0 collective-permute-start.9
  14.2 1.6 %collective-permute-start.10 = (bf16[256,512]{1,0:T(8,128)(2,1)S(1)}, bf16[256,512]{1,0:T(8,128)(2,1)S(1)}, u32[]{:S(2)}, u32[]{:S(2)}) collective-permute-start(bf16[256,512]{1,0:T(8,128)(2,1)S(1)} %shard_map.125), channel_id=1, source_target_pairs={{0,2},{2,0},{1,3},{3,1},{4,6},{6,4},{5,7},{7,5},{8,10},{10,8},{9,1... | collective-permute-start | bytes 786440 | tf_op jit(solution)/shard_map/ppermute | solution.py:329
  15.7 2.9 %collective-permute-done.4.refs_15_ = bf16[128,512]{1,0:T(8,128)(2,1)S(1)} collective-permute-done((bf16[128,512]{1,0:T(8,128)(2,1)S(1)}, bf16[128,512]{1,0:T(8,128)(2,1)S(1)}, u32[]{:S(2)}, u32[]{:S(2)}) %collective-permute-start.4) | collective-permute-done | bytes 131104 | tf_op jit(solution)/shard_map/ppermute | solution.py:329
  18.6 0.2 collective-permute-done.a_ref.refs_2_
  18.8 0.0 collective-permute-done.1.b_ref.refs_5_
  18.9 0.1 collective-permute-start.5
  19.0 0.5 %collective-permute-start.6 = (bf16[128,512]{1,0:T(8,128)(2,1)S(1)}, bf16[128,512]{1,0:T(8,128)(2,1)S(1)}, u32[]{:S(2)}, u32[]{:S(2)}) collective-permute-start(bf16[128,512]{1,0:T(8,128)(2,1)S(1)} %get-tuple-element.52), channel_id=1, source_target_pairs={{0,1},{1,0},{2,3},{3,2},{4,5},{5,4},{6,7},{7,6},{8,9},{9,8},{10,11... | collective-permute-start | bytes 393224 | tf_op jit(solution)/shard_map/ppermute | solution.py:329
  19.5 0.1 collective-permute-start.7
  19.5 0.0 collective-permute-done.9.refs_9_
  19.5 0.4 collective-permute-start.8
  20.0 0.3 collective-permute-done.5.refs_3_
  20.3 1.5 %collective-permute-start.11 = (bf16[128,512]{1,0:T(8,128)(2,1)S(1)}, bf16[128,512]{1,0:T(8,128)(2,1)S(1)}, u32[]{:S(2)}, u32[]{:S(2)}) collective-permute-start(bf16[128,512]{1,0:T(8,128)(2,1)S(1)} %collective-permute-done.4.refs_15_), channel_id=1, source_target_pairs={{0,2},{2,0},{1,3},{3,1},{4,6},{6,4},{5,7},{7,5},{8,10},{10,8},{9,1... | collective-permute-start | bytes 393224 | tf_op jit(solution)/shard_map/ppermute | solution.py:329
  21.8 0.0 collective-permute-done.6.refs_4_
  21.8 0.0 collective-permute-done.7.refs_6_
  21.8 0.0 collective-permute-done.8.refs_7_
  21.8 3.7 %shard_map.124 = (bf16[512,128]{1,0:T(8,128)(2,1)S(1)}, bf16[512,128]{1,0:T(8,128)(2,1)S(1)}, bf16[1536,128]{1,0:T(8,128)(2,1)S(1)}, f32[48,1536]{1,0:T(8,128)S(1)}, f32[48,128]{1,0:T(8,128)S(1)}) custom-call(s32[6,16]{1,0:T(8,128)S(1)} %get-tuple-element.45.refs_0_, bf16[512,512]{1,0:T(8,128)(2,1)S(1)} %get-tuple-element.46.refs_1_, ...), custom_call_target="tpu_custom_call" | custom-call | bytes 1048576 | tf_op jit(solution)/shard_map/pallas_call | solution.py:316
  25.6 0.0 collective-permute-done.10.refs_16_
  25.6 0.3 collective-permute-done.11.refs_17_
  25.9 3.8 %shard_map.126 = (bf16[512,128]{1,0:T(8,128)(2,1)S(1)}, bf16[512,128]{1,0:T(8,128)(2,1)S(1)}, bf16[48,256]{1,0:T(8,128)(2,1)S(1)}, bf16[48,256]{1,0:T(8,128)(2,1)S(1)}, bf16[48,256]{1,0:T(8,128)(2,1)S(1)}) custom-call(s32[6,16]{1,0:T(8,128)S(1)} %get-tuple-element.45.refs_0_, bf16[512,512]{1,0:T(8,128)(2,1)S(1)} %get-tuple-element.46.refs_1_, ...), custom_call_target="tpu_custom_call" | custom-call | flops 4000000000 | bytes 1048576 | tf_op jit(solution)/shard_map/pallas_call | solution.py:316
  29.7 0.1 collective-permute-start.12
  29.7 1.2 %collective-permute-done.12.sibling_ref = bf16[48,256]{1,0:T(8,128)(2,1)S(1)} collective-permute-done((bf16[48,256]{1,0:T(8,128)(2,1)S(1)}, bf16[48,256]{1,0:T(8,128)(2,1)S(1)}, u32[]{:S(2)}, u32[]{:S(2)}) %collective-permute-start.12) | collective-permute-done | bytes 24608 | tf_op jit(solution)/shard_map/ppermute | solution.py:329
  30.9 1.6 %collective-permute-start.13 = (bf16[48,512]{1,0:T(8,128)(2,1)S(1)}, bf16[48,512]{1,0:T(8,128)(2,1)S(1)}, u32[]{:S(2)}, u32[]{:S(2)}) collective-permute-start(bf16[48,512]{1,0:T(8,128)(2,1)S(1)} %shard_map.127), channel_id=1, source_target_pairs={{0,2},{2,0},{1,3},{3,1},{4,6},{6,4},{5,7},{7,5},{8,10},{10,8},{9,1... | collective-permute-start | bytes 147464 | tf_op jit(solution)/shard_map/ppermute | solution.py:329
  32.5 1.0 %shard_map.128 = (f32[512,256]{1,0:T(8,128)S(1)}, bf16[512,256]{1,0:T(8,128)(2,1)S(1)}) custom-call(s32[1,512]{1,0:T(1,128)S(1)} %get-tuple-element.66.order_ref, bf16[512,256]{1,0:T(8,128)(2,1)S(1)} %get-tuple-element.67.x_ref, bf16[512,128]{1,0:T(8,128)(2,1)S(1)} %get-tuple-element.68.att1_ref, bf16[512,128]{1,0:T(8,128)(2,1)S(1)} %get-tuple-element.69.att2_ref, ...), custom_call_target="tpu_custom_call" | custom-call | flops 1000000000 | bytes 1048576 | tf_op jit(solution)/shard_map/pallas_call | solution.py:316
  33.5 0.1 collective-permute-start.17
  33.6 1.5 %collective-permute-done.13 = bf16[48,512]{1,0:T(8,128)(2,1)S(1)} collective-permute-done((bf16[48,512]{1,0:T(8,128)(2,1)S(1)}, bf16[48,512]{1,0:T(8,128)(2,1)S(1)}, u32[]{:S(2)}, u32[]{:S(2)}) %collective-permute-start.13) | collective-permute-done | bytes 49184 | tf_op jit(solution)/shard_map/ppermute | solution.py:329
  35.1 2.3 %collective-permute-start.14 = (bf16[48,512]{1,0:T(8,128)(2,1)S(1)}, bf16[48,512]{1,0:T(8,128)(2,1)S(1)}, u32[]{:S(2)}, u32[]{:S(2)}) collective-permute-start(bf16[48,512]{1,0:T(8,128)(2,1)S(1)} %add_convert_fusion.1.refs_0_), channel_id=1, source_target_pairs={{0,4},{4,8},{8,12},{12,0},{1,5},{5,9},{9,13},{13,1},{2,6},{6,10},{... | collective-permute-start | bytes 147464 | tf_op jit(solution)/shard_map/ppermute | solution.py:516
  37.5 1.3 %collective-permute-start.15 = (bf16[48,512]{1,0:T(8,128)(2,1)S(1)}, bf16[48,512]{1,0:T(8,128)(2,1)S(1)}, u32[]{:S(2)}, u32[]{:S(2)}) collective-permute-start(bf16[48,512]{1,0:T(8,128)(2,1)S(1)} %add_convert_fusion.1.refs_0_), channel_id=1, source_target_pairs={{0,8},{4,12},{8,0},{12,4},{1,9},{5,13},{9,1},{13,5},{2,10},{6,14},... | collective-permute-start | bytes 147464 | tf_op jit(solution)/shard_map/ppermute | solution.py:516
  38.8 1.9 %collective-permute-start.16 = (bf16[48,512]{1,0:T(8,128)(2,1)S(1)}, bf16[48,512]{1,0:T(8,128)(2,1)S(1)}, u32[]{:S(2)}, u32[]{:S(2)}) collective-permute-start(bf16[48,512]{1,0:T(8,128)(2,1)S(1)} %add_convert_fusion.1.refs_0_), channel_id=1, source_target_pairs={{0,12},{4,0},{8,4},{12,8},{1,13},{5,1},{9,5},{13,9},{2,14},{6,2},{... | collective-permute-start | bytes 147464 | tf_op jit(solution)/shard_map/ppermute | solution.py:516
  40.7 0.0 collective-permute-done.17
  40.7 0.8 %fusion = bf16[1,512,256]{2,1,0:T(8,128)(2,1)} fusion(f32[512,256]{1,0:T(8,128)S(1)} %get-tuple-element.72, bf16[512,256]{1,0:T(8,128)(2,1)S(1)} %collective-permute-done.17), kind=kLoop, calls=%fused_computation.1 | loop fusion | flops 393216 | bytes 1048576 | tf_op jit(solution)/shard_map/broadcast_in_dim | solution.py:506
  41.4 0.0 collective-permute-done.14.refs_1_
  41.4 1.6 %collective-permute-done.15.refs_2_ = bf16[48,512]{1,0:T(8,128)(2,1)S(1)} collective-permute-done((bf16[48,512]{1,0:T(8,128)(2,1)S(1)}, bf16[48,512]{1,0:T(8,128)(2,1)S(1)}, u32[]{:S(2)}, u32[]{:S(2)}) %collective-permute-start.15) | collective-permute-done | bytes 49184 | tf_op jit(solution)/shard_map/ppermute | solution.py:516
  43.0 0.0 collective-permute-done.16.refs_3_
  43.0 0.1 collective-permute-start.18
  43.1 1.2 %collective-permute-done.18.recv_ref = f32[48,256]{1,0:T(8,128)S(1)} collective-permute-done((f32[48,256]{1,0:T(8,128)S(1)}, f32[48,256]{1,0:T(8,128)S(1)}, u32[]{:S(2)}, u32[]{:S(2)}) %collective-permute-start.18) | collective-permute-done | bytes 49184 | tf_op jit(solution)/shard_map/ppermute | solution.py:329
  44.3 0.7 %shard_map.130 = (f32[48,512]{1,0:T(8,128)}, f32[48,256]{1,0:T(8,128)}) custom-call(f32[48,256]{1,0:T(8,128)S(1)} %get-tuple-element.79.own_ref, f32[48,256]{1,0:T(8,128)S(1)} %collective-permute-done.18.recv_ref, f32[48,256]{1,0:T(8,128)S(1)} %get-tuple-element.80.up_ref), custom_call_target="tpu_custom_call" | custom-call | bytes 1048576 | tf_op jit(solution)/shard_map/pallas_call | solution.py:316
  (5 shorter events, 0.1 us)
Async XLA Ops:
  1.7 10.3 %collective-permute-start.2 = (bf16[128,512]{1,0:T(8,128)(2,1)S(1)}, bf16[128,512]{1,0:T(8,128)(2,1)S(1)}, u32[]{:S(2)}, u32[]{:S(2)}) collective-permute-start(bf16[128,512]{1,0:T(8,128)(2,1)S(1)} %get-tuple-element.43.refs_12_), channel_id=1, source_target_pairs={{0,12},{4,8},{8,4},{12,0},{16,24},{20,28},{24,16},{28,20},{1,13},{... | collective-permute-start | bytes 393224 | tf_op jit(solution)/shard_map/ppermute | solution.py:358
  6.8 6.8 %collective-permute-start.3 = (bf16[128,512]{1,0:T(8,128)(2,1)S(1)}, bf16[128,512]{1,0:T(8,128)(2,1)S(1)}, u32[]{:S(2)}, u32[]{:S(2)}) collective-permute-start(bf16[128,512]{1,0:T(8,128)(2,1)S(1)} %get-tuple-element.43.refs_12_), channel_id=1, source_target_pairs={{0,4},{4,0},{8,12},{12,8},{1,5},{5,1},{9,13},{13,9},{2,6},{6,2},{1... | collective-permute-start | bytes 393224 | tf_op jit(solution)/shard_map/ppermute | solution.py:329
  9.2 9.7 %collective-permute-start = (bf16[256,512]{1,0:T(8,128)(2,1)S(1)}, bf16[256,512]{1,0:T(8,128)(2,1)S(1)}, u32[]{:S(2)}, u32[]{:S(2)}) collective-permute-start(bf16[256,512]{1,0:T(8,128)(2,1)S(1)} %get-tuple-element.47), channel_id=1, source_target_pairs={{0,4},{4,0},{8,12},{12,8},{1,5},{5,1},{9,13},{13,9},{2,6},{6,2},{1... | collective-permute-start | bytes 786440 | tf_op jit(solution)/shard_map/ppermute | solution.py:329
  11.3 7.6 %collective-permute-start.1 = (bf16[256,512]{1,0:T(8,128)(2,1)S(1)}, bf16[256,512]{1,0:T(8,128)(2,1)S(1)}, u32[]{:S(2)}, u32[]{:S(2)}) collective-permute-start(bf16[256,512]{1,0:T(8,128)(2,1)S(1)} %get-tuple-element.47), channel_id=1, source_target_pairs={{0,0},{4,8},{8,4},{12,12},{1,1},{5,9},{9,5},{13,13},{2,2},{6,10},{... | collective-permute-start | bytes 786440 | tf_op jit(solution)/shard_map/ppermute | solution.py:436
  13.7 5.0 %collective-permute-start.4 = (bf16[128,512]{1,0:T(8,128)(2,1)S(1)}, bf16[128,512]{1,0:T(8,128)(2,1)S(1)}, u32[]{:S(2)}, u32[]{:S(2)}) collective-permute-start(bf16[128,512]{1,0:T(8,128)(2,1)S(1)} %collective-permute-done.2.refs_14_.two_ref), channel_id=1, source_target_pairs={{0,16},{16,0},{1,17},{17,1},{2,18},{18,2},{3,19},{19,3},{4,20},{20... | collective-permute-start | bytes 393224 | tf_op jit(solution)/shard_map/ppermute | solution.py:329
  14.1 5.4 %collective-permute-start.9 = (bf16[512,256]{1,0:T(8,128)(2,1)S(1)}, bf16[512,256]{1,0:T(8,128)(2,1)S(1)}, u32[]{:S(2)}, u32[]{:S(2)}) collective-permute-start(bf16[512,256]{1,0:T(8,128)(2,1)S(1)} %get-tuple-element.55.refs_8_), channel_id=1, source_target_pairs={{0,1},{1,0},{2,3},{3,2},{4,5},{5,4},{6,7},{7,6},{8,9},{9,8},{10,11... | collective-permute-start | bytes 786440 | tf_op jit(solution)/shard_map/ppermute | solution.py:329
  14.2 11.4 %collective-permute-start.10 = (bf16[256,512]{1,0:T(8,128)(2,1)S(1)}, bf16[256,512]{1,0:T(8,128)(2,1)S(1)}, u32[]{:S(2)}, u32[]{:S(2)}) collective-permute-start(bf16[256,512]{1,0:T(8,128)(2,1)S(1)} %shard_map.125), channel_id=1, source_target_pairs={{0,2},{2,0},{1,3},{3,1},{4,6},{6,4},{5,7},{7,5},{8,10},{10,8},{9,1... | collective-permute-start | bytes 786440 | tf_op jit(solution)/shard_map/ppermute | solution.py:329
  18.9 1.4 %collective-permute-start.5 = (bf16[128,512]{1,0:T(8,128)(2,1)S(1)}, bf16[128,512]{1,0:T(8,128)(2,1)S(1)}, u32[]{:S(2)}, u32[]{:S(2)}) collective-permute-start(bf16[128,512]{1,0:T(8,128)(2,1)S(1)} %get-tuple-element.51), channel_id=1, source_target_pairs={{0,1},{1,0},{2,3},{3,2},{4,5},{5,4},{6,7},{7,6},{8,9},{9,8},{10,11... | collective-permute-start | bytes 393224 | tf_op jit(solution)/shard_map/ppermute | solution.py:329
  19.0 2.8 %collective-permute-start.6 = (bf16[128,512]{1,0:T(8,128)(2,1)S(1)}, bf16[128,512]{1,0:T(8,128)(2,1)S(1)}, u32[]{:S(2)}, u32[]{:S(2)}) collective-permute-start(bf16[128,512]{1,0:T(8,128)(2,1)S(1)} %get-tuple-element.52), channel_id=1, source_target_pairs={{0,1},{1,0},{2,3},{3,2},{4,5},{5,4},{6,7},{7,6},{8,9},{9,8},{10,11... | collective-permute-start | bytes 393224 | tf_op jit(solution)/shard_map/ppermute | solution.py:329
  19.5 2.3 %collective-permute-start.7 = (bf16[128,512]{1,0:T(8,128)(2,1)S(1)}, bf16[128,512]{1,0:T(8,128)(2,1)S(1)}, u32[]{:S(2)}, u32[]{:S(2)}) collective-permute-start(bf16[128,512]{1,0:T(8,128)(2,1)S(1)} %get-tuple-element.53), channel_id=1, source_target_pairs={{0,1},{1,0},{2,3},{3,2},{4,5},{5,4},{6,7},{7,6},{8,9},{9,8},{10,11... | collective-permute-start | bytes 393224 | tf_op jit(solution)/shard_map/ppermute | solution.py:329
  19.5 2.3 %collective-permute-start.8 = (bf16[128,512]{1,0:T(8,128)(2,1)S(1)}, bf16[128,512]{1,0:T(8,128)(2,1)S(1)}, u32[]{:S(2)}, u32[]{:S(2)}) collective-permute-start(bf16[128,512]{1,0:T(8,128)(2,1)S(1)} %get-tuple-element.54), channel_id=1, source_target_pairs={{0,1},{1,0},{2,3},{3,2},{4,5},{5,4},{6,7},{7,6},{8,9},{9,8},{10,11... | collective-permute-start | bytes 393224 | tf_op jit(solution)/shard_map/ppermute | solution.py:329
  20.3 5.6 %collective-permute-start.11 = (bf16[128,512]{1,0:T(8,128)(2,1)S(1)}, bf16[128,512]{1,0:T(8,128)(2,1)S(1)}, u32[]{:S(2)}, u32[]{:S(2)}) collective-permute-start(bf16[128,512]{1,0:T(8,128)(2,1)S(1)} %collective-permute-done.4.refs_15_), channel_id=1, source_target_pairs={{0,2},{2,0},{1,3},{3,1},{4,6},{6,4},{5,7},{7,5},{8,10},{10,8},{9,1... | collective-permute-start | bytes 393224 | tf_op jit(solution)/shard_map/ppermute | solution.py:329
  29.7 1.3 %collective-permute-start.12 = (bf16[48,256]{1,0:T(8,128)(2,1)S(1)}, bf16[48,256]{1,0:T(8,128)(2,1)S(1)}, u32[]{:S(2)}, u32[]{:S(2)}) collective-permute-start(bf16[48,256]{1,0:T(8,128)(2,1)S(1)} %get-tuple-element.64), channel_id=1, source_target_pairs={{0,1},{1,0},{2,3},{3,2},{4,5},{5,4},{6,7},{7,6},{8,9},{9,8},{10,11... | collective-permute-start | bytes 73736 | tf_op jit(solution)/shard_map/ppermute | solution.py:329
  30.9 4.2 %collective-permute-start.13 = (bf16[48,512]{1,0:T(8,128)(2,1)S(1)}, bf16[48,512]{1,0:T(8,128)(2,1)S(1)}, u32[]{:S(2)}, u32[]{:S(2)}) collective-permute-start(bf16[48,512]{1,0:T(8,128)(2,1)S(1)} %shard_map.127), channel_id=1, source_target_pairs={{0,2},{2,0},{1,3},{3,1},{4,6},{6,4},{5,7},{7,5},{8,10},{10,8},{9,1... | collective-permute-start | bytes 147464 | tf_op jit(solution)/shard_map/ppermute | solution.py:329
  33.5 7.2 %collective-permute-start.17 = (bf16[512,256]{1,0:T(8,128)(2,1)S(1)}, bf16[512,256]{1,0:T(8,128)(2,1)S(1)}, u32[]{:S(2)}, u32[]{:S(2)}) collective-permute-start(bf16[512,256]{1,0:T(8,128)(2,1)S(1)} %get-tuple-element.73), channel_id=1, source_target_pairs={{0,1},{1,0},{2,3},{3,2},{4,5},{5,4},{6,7},{7,6},{8,9},{9,8},{10,11... | collective-permute-start | bytes 786440 | tf_op jit(solution)/shard_map/ppermute | solution.py:329
  35.1 6.3 %collective-permute-start.14 = (bf16[48,512]{1,0:T(8,128)(2,1)S(1)}, bf16[48,512]{1,0:T(8,128)(2,1)S(1)}, u32[]{:S(2)}, u32[]{:S(2)}) collective-permute-start(bf16[48,512]{1,0:T(8,128)(2,1)S(1)} %add_convert_fusion.1.refs_0_), channel_id=1, source_target_pairs={{0,4},{4,8},{8,12},{12,0},{1,5},{5,9},{9,13},{13,1},{2,6},{6,10},{... | collective-permute-start | bytes 147464 | tf_op jit(solution)/shard_map/ppermute | solution.py:516
  37.5 5.5 %collective-permute-start.15 = (bf16[48,512]{1,0:T(8,128)(2,1)S(1)}, bf16[48,512]{1,0:T(8,128)(2,1)S(1)}, u32[]{:S(2)}, u32[]{:S(2)}) collective-permute-start(bf16[48,512]{1,0:T(8,128)(2,1)S(1)} %add_convert_fusion.1.refs_0_), channel_id=1, source_target_pairs={{0,8},{4,12},{8,0},{12,4},{1,9},{5,13},{9,1},{13,5},{2,10},{6,14},... | collective-permute-start | bytes 147464 | tf_op jit(solution)/shard_map/ppermute | solution.py:516
  38.8 4.2 %collective-permute-start.16 = (bf16[48,512]{1,0:T(8,128)(2,1)S(1)}, bf16[48,512]{1,0:T(8,128)(2,1)S(1)}, u32[]{:S(2)}, u32[]{:S(2)}) collective-permute-start(bf16[48,512]{1,0:T(8,128)(2,1)S(1)} %add_convert_fusion.1.refs_0_), channel_id=1, source_target_pairs={{0,12},{4,0},{8,4},{12,8},{1,13},{5,1},{9,5},{13,9},{2,14},{6,2},{... | collective-permute-start | bytes 147464 | tf_op jit(solution)/shard_map/ppermute | solution.py:516
  43.0 1.3 %collective-permute-start.18 = (f32[48,256]{1,0:T(8,128)S(1)}, f32[48,256]{1,0:T(8,128)S(1)}, u32[]{:S(2)}, u32[]{:S(2)}) collective-permute-start(f32[48,256]{1,0:T(8,128)S(1)} %get-tuple-element.79.own_ref), channel_id=1, source_target_pairs={{0,1},{1,0},{2,3},{3,2},{4,5},{5,4},{6,7},{7,6},{8,9},{9,8},{10,11... | collective-permute-start | bytes 147464 | tf_op jit(solution)/shard_map/ppermute | solution.py:329

commit v14 on v13

--- a/solution.py
+++ b/solution.py
@@ -57,14 +57,21 @@
 
 
 def pack_kernel(split, *refs):
-    sources, outs, buffers, sems = refs[:4], refs[4:6], refs[6:-1], refs[-1]
-    for copy in load_all(sources, buffers, sems):
-        copy.wait()
+    sources, outs, out_weight, sems = refs[:4], refs[4:6], refs[6], refs[7]
+    last = pltpu.make_async_copy(sources[3], out_weight, sems.at[6])
+    last.start()
+    copies = []
     for which, out in enumerate(outs):
         lanes = lanes_at(head_at(split, which))
-        for j, member in enumerate(buffers[:3]):
-            out[:, j * DH : (j + 1) * DH] = member[:, lanes]
-        out[:, 3 * DH :] = buffers[3][lanes, :].T
+        for j, member in enumerate(sources[:3]):
+            target = out.at[:, pl.ds(j * DH, DH)]
+            copies.append(pltpu.make_async_copy(member.at[:, lanes], target, sems.at[which * 3 + j]))
+            copies[-1].start()
+    last.wait()
+    for which, out in enumerate(outs):
+        out[:, 3 * DH :] = out_weight[lanes_at(head_at(split, which)), :].T
+    for copy in copies:
+        copy.wait()
 
 
 def prep_kernel(*refs):
@@ -396,8 +403,7 @@
         functools.partial(pack_kernel, split),
         (shape((depth, 4 * DH)),) * 2,
         (query_weight, key_weight, value_weight, output_weight),
-        [pltpu.VMEM((depth, cols), BF16)] * 3
-        + [pltpu.VMEM((cols, depth), BF16), pltpu.SemaphoreType.DMA((4,))],
+        [pltpu.VMEM((cols, depth), BF16), pltpu.SemaphoreType.DMA((7,))],
         hbm=4,
         limit=16,
     )

time: 45.2 us -> 45.1 us (level)
  no operation moved by 1% of the time
where the time goes in v14:
time: 45.1 us; the launch traced here: 44.9 us
  starting transfers between devices  19.8 us (44%)
  Pallas kernels  12.7 us (28%)
  waiting for transfers between devices  10.9 us (24%)
  other arithmetic  0.78 us (2%)
  between operations  0.76 us (2%)
    pallas_call x10, Pallas kernels, call(): pl.pallas_call(kernel, out_shape=outs, in_specs=[HBM] * hbm + [VMEM] * (l...  12.7 us
    ppermute x14, waiting for transfers between devices, swap(): return lax.ppermute(value, axis, [(i, i ^ step) for i in range(size)])  9.34 us
    ppermute x14, starting transfers between devices, swap(): return lax.ppermute(value, axis, [(i, i ^ step) for i in range(size)])  8.47 us
    ppermute x3, starting transfers between devices, shards(): lax.ppermute(lora, 'node', [(i, (i + k) % count) for i in range(count)])  5.56 us
    ppermute x1, starting transfers between devices, gather_weights(): far = lax.ppermute(first, ('group', 'node'), far_pairs)  5.11 us
    ppermute x3, waiting for transfers between devices, shards(): lax.ppermute(lora, 'node', [(i, (i + k) % count) for i in range(count)])  1.55 us
  transfers between devices with their start and end apart: 19, of which 9 were waited for; matrix products, arithmetic and copies ran while one was open for 2% of the time, Pallas kernels for 16%

profile of v14, /device:TPU:0, one launch (start us, length us, event | category | flops | bytes accessed | tf_op | source)
XLA Modules:
  0.0 44.9 jit_solution(2322036852125068023)
XLA Ops:
  0.6 1.0 %shard_map.121 = (bf16[128,512]{1,0:T(8,128)(2,1)S(1)}, bf16[128,512]{1,0:T(8,128)(2,1)S(1)}) custom-call(bf16[128,256]{1,0:T(8,128)(2,1)} %refs_0_.1, bf16[128,256]{1,0:T(8,128)(2,1)} %refs_1_.1, bf16[128,256]{1,0:T(8,128)(2,1)} %refs_2_.1, bf16[256,128]{1,0:T(8,128)(2,1)} %refs_3_.1), custom_call_target="tpu_custom_call" | custom-call | bytes 1048576 | tf_op jit(solution)/shard_map/pallas_call | solution.py:323
  1.6 5.1 %collective-permute-start.2 = (bf16[128,512]{1,0:T(8,128)(2,1)S(1)}, bf16[128,512]{1,0:T(8,128)(2,1)S(1)}, u32[]{:S(2)}, u32[]{:S(2)}) collective-permute-start(bf16[128,512]{1,0:T(8,128)(2,1)S(1)} %get-tuple-element.43.refs_12_), channel_id=1, source_target_pairs={{0,12},{4,8},{8,4},{12,0},{16,24},{20,28},{24,16},{28,20},{1,13},{... | collective-permute-start | bytes 393224 | tf_op jit(solution)/shard_map/ppermute | solution.py:365
  6.7 0.0 collective-permute-start.3
  6.7 2.4 %shard_map.122 = (s32[1,512]{1,0:T(1,128)S(1)}, s32[6,16]{1,0:T(8,128)S(1)}, bf16[48,512]{1,0:T(8,128)(2,1)S(1)}, bf16[48,256]{1,0:T(8,128)(2,1)S(1)}, bf16[512,...) custom-call(s32[1,512]{1,0:T(1,128)} %bitcast.21, ...), custom_call_target="tpu_custom_call" | custom-call | flops 402653184 | bytes 1048576 | tf_op jit(solution)/shard_map/pallas_call | solution.py:323
  9.1 2.1 %collective-permute-start = (bf16[256,512]{1,0:T(8,128)(2,1)S(1)}, bf16[256,512]{1,0:T(8,128)(2,1)S(1)}, u32[]{:S(2)}, u32[]{:S(2)}) collective-permute-start(bf16[256,512]{1,0:T(8,128)(2,1)S(1)} %get-tuple-element.47), channel_id=1, source_target_pairs={{0,4},{4,0},{8,12},{12,8},{1,5},{5,1},{9,13},{13,9},{2,6},{6,2},{1... | collective-permute-start | bytes 786440 | tf_op jit(solution)/shard_map/ppermute | solution.py:336
  11.2 0.7 %collective-permute-start.1 = (bf16[256,512]{1,0:T(8,128)(2,1)S(1)}, bf16[256,512]{1,0:T(8,128)(2,1)S(1)}, u32[]{:S(2)}, u32[]{:S(2)}) collective-permute-start(bf16[256,512]{1,0:T(8,128)(2,1)S(1)} %get-tuple-element.47), channel_id=1, source_target_pairs={{0,0},{4,8},{8,4},{12,12},{1,1},{5,9},{9,5},{13,13},{2,2},{6,10},{... | collective-permute-start | bytes 786440 | tf_op jit(solution)/shard_map/ppermute | solution.py:442
  11.9 0.0 collective-permute-done.2.refs_14_.two_ref
  11.9 1.7 %collective-permute-done.3.refs_13_.one_ref = bf16[128,512]{1,0:T(8,128)(2,1)S(1)} collective-permute-done((bf16[128,512]{1,0:T(8,128)(2,1)S(1)}, bf16[128,512]{1,0:T(8,128)(2,1)S(1)}, u32[]{:S(2)}, u32[]{:S(2)}) %collective-permute-start.3) | collective-permute-done | bytes 131104 | tf_op jit(solution)/shard_map/ppermute | solution.py:336
  13.6 0.5 %collective-permute-start.4 = (bf16[128,512]{1,0:T(8,128)(2,1)S(1)}, bf16[128,512]{1,0:T(8,128)(2,1)S(1)}, u32[]{:S(2)}, u32[]{:S(2)}) collective-permute-start(bf16[128,512]{1,0:T(8,128)(2,1)S(1)} %collective-permute-done.2.refs_14_.two_ref), channel_id=1, source_target_pairs={{0,16},{16,0},{1,17},{17,1},{2,18},{18,2},{3,19},{19,3},{4,20},{20... | collective-permute-start | bytes 393224 | tf_op jit(solution)/shard_map/ppermute | solution.py:336
  14.1 0.0 collective-permute-start.9
  14.1 1.6 %collective-permute-start.10 = (bf16[256,512]{1,0:T(8,128)(2,1)S(1)}, bf16[256,512]{1,0:T(8,128)(2,1)S(1)}, u32[]{:S(2)}, u32[]{:S(2)}) collective-permute-start(bf16[256,512]{1,0:T(8,128)(2,1)S(1)} %shard_map.125), channel_id=1, source_target_pairs={{0,2},{2,0},{1,3},{3,1},{4,6},{6,4},{5,7},{7,5},{8,10},{10,8},{9,1... | collective-permute-start | bytes 786440 | tf_op jit(solution)/shard_map/ppermute | solution.py:336
  15.6 2.9 %collective-permute-done.4.refs_15_ = bf16[128,512]{1,0:T(8,128)(2,1)S(1)} collective-permute-done((bf16[128,512]{1,0:T(8,128)(2,1)S(1)}, bf16[128,512]{1,0:T(8,128)(2,1)S(1)}, u32[]{:S(2)}, u32[]{:S(2)}) %collective-permute-start.4) | collective-permute-done | bytes 131104 | tf_op jit(solution)/shard_map/ppermute | solution.py:336
  18.5 0.2 collective-permute-done.a_ref.refs_2_
  18.8 0.0 collective-permute-done.1.b_ref.refs_5_
  18.8 0.1 collective-permute-start.5
  18.9 0.5 %collective-permute-start.6 = (bf16[128,512]{1,0:T(8,128)(2,1)S(1)}, bf16[128,512]{1,0:T(8,128)(2,1)S(1)}, u32[]{:S(2)}, u32[]{:S(2)}) collective-permute-start(bf16[128,512]{1,0:T(8,128)(2,1)S(1)} %get-tuple-element.52), channel_id=1, source_target_pairs={{0,1},{1,0},{2,3},{3,2},{4,5},{5,4},{6,7},{7,6},{8,9},{9,8},{10,11... | collective-permute-start | bytes 393224 | tf_op jit(solution)/shard_map/ppermute | solution.py:336
  19.4 0.1 collective-permute-start.7
  19.5 0.0 collective-permute-done.9.refs_9_
  19.5 0.4 collective-permute-start.8
  19.9 0.3 collective-permute-done.5.refs_3_
  20.2 1.5 %collective-permute-start.11 = (bf16[128,512]{1,0:T(8,128)(2,1)S(1)}, bf16[128,512]{1,0:T(8,128)(2,1)S(1)}, u32[]{:S(2)}, u32[]{:S(2)}) collective-permute-start(bf16[128,512]{1,0:T(8,128)(2,1)S(1)} %collective-permute-done.4.refs_15_), channel_id=1, source_target_pairs={{0,2},{2,0},{1,3},{3,1},{4,6},{6,4},{5,7},{7,5},{8,10},{10,8},{9,1... | collective-permute-start | bytes 393224 | tf_op jit(solution)/shard_map/ppermute | solution.py:336
  21.7 0.0 collective-permute-done.6.refs_4_
  21.7 0.0 collective-permute-done.7.refs_6_
  21.7 0.0 collective-permute-done.8.refs_7_
  21.7 3.7 %shard_map.124 = (bf16[512,128]{1,0:T(8,128)(2,1)S(1)}, bf16[512,128]{1,0:T(8,128)(2,1)S(1)}, bf16[1536,128]{1,0:T(8,128)(2,1)S(1)}, f32[48,1536]{1,0:T(8,128)S(1)}, f32[48,128]{1,0:T(8,128)S(1)}) custom-call(s32[6,16]{1,0:T(8,128)S(1)} %get-tuple-element.45.refs_0_, bf16[512,512]{1,0:T(8,128)(2,1)S(1)} %get-tuple-element.46.refs_1_, ...), custom_call_target="tpu_custom_call" | custom-call | bytes 1048576 | tf_op jit(solution)/shard_map/pallas_call | solution.py:323
  25.5 0.0 collective-permute-done.10.refs_16_
  25.5 0.3 collective-permute-done.11.refs_17_
  25.8 3.8 %shard_map.126 = (bf16[512,128]{1,0:T(8,128)(2,1)S(1)}, bf16[512,128]{1,0:T(8,128)(2,1)S(1)}, bf16[48,256]{1,0:T(8,128)(2,1)S(1)}, bf16[48,256]{1,0:T(8,128)(2,1)S(1)}, bf16[48,256]{1,0:T(8,128)(2,1)S(1)}) custom-call(s32[6,16]{1,0:T(8,128)S(1)} %get-tuple-element.45.refs_0_, bf16[512,512]{1,0:T(8,128)(2,1)S(1)} %get-tuple-element.46.refs_1_, ...), custom_call_target="tpu_custom_call" | custom-call | flops 4000000000 | bytes 1048576 | tf_op jit(solution)/shard_map/pallas_call | solution.py:323
  29.6 0.1 collective-permute-start.12
  29.7 1.2 %collective-permute-done.12.sibling_ref = bf16[48,256]{1,0:T(8,128)(2,1)S(1)} collective-permute-done((bf16[48,256]{1,0:T(8,128)(2,1)S(1)}, bf16[48,256]{1,0:T(8,128)(2,1)S(1)}, u32[]{:S(2)}, u32[]{:S(2)}) %collective-permute-start.12) | collective-permute-done | bytes 24608 | tf_op jit(solution)/shard_map/ppermute | solution.py:336
  30.9 1.6 %collective-permute-start.13 = (bf16[48,512]{1,0:T(8,128)(2,1)S(1)}, bf16[48,512]{1,0:T(8,128)(2,1)S(1)}, u32[]{:S(2)}, u32[]{:S(2)}) collective-permute-start(bf16[48,512]{1,0:T(8,128)(2,1)S(1)} %shard_map.127), channel_id=1, source_target_pairs={{0,2},{2,0},{1,3},{3,1},{4,6},{6,4},{5,7},{7,5},{8,10},{10,8},{9,1... | collective-permute-start | bytes 147464 | tf_op jit(solution)/shard_map/ppermute | solution.py:336
  32.4 1.0 %shard_map.128 = (f32[512,256]{1,0:T(8,128)S(1)}, bf16[512,256]{1,0:T(8,128)(2,1)S(1)}) custom-call(s32[1,512]{1,0:T(1,128)S(1)} %get-tuple-element.66.order_ref, bf16[512,256]{1,0:T(8,128)(2,1)S(1)} %get-tuple-element.67.x_ref, bf16[512,128]{1,0:T(8,128)(2,1)S(1)} %get-tuple-element.68.att1_ref, bf16[512,128]{1,0:T(8,128)(2,1)S(1)} %get-tuple-element.69.att2_ref, ...), custom_call_target="tpu_custom_call" | custom-call | flops 1000000000 | bytes 1048576 | tf_op jit(solution)/shard_map/pallas_call | solution.py:323
  33.4 0.1 collective-permute-start.17
  33.5 1.5 %collective-permute-done.13 = bf16[48,512]{1,0:T(8,128)(2,1)S(1)} collective-permute-done((bf16[48,512]{1,0:T(8,128)(2,1)S(1)}, bf16[48,512]{1,0:T(8,128)(2,1)S(1)}, u32[]{:S(2)}, u32[]{:S(2)}) %collective-permute-start.13) | collective-permute-done | bytes 49184 | tf_op jit(solution)/shard_map/ppermute | solution.py:336
  35.0 2.3 %collective-permute-start.14 = (bf16[48,512]{1,0:T(8,128)(2,1)S(1)}, bf16[48,512]{1,0:T(8,128)(2,1)S(1)}, u32[]{:S(2)}, u32[]{:S(2)}) collective-permute-start(bf16[48,512]{1,0:T(8,128)(2,1)S(1)} %add_convert_fusion.1.refs_0_), channel_id=1, source_target_pairs={{0,4},{4,8},{8,12},{12,0},{1,5},{5,9},{9,13},{13,1},{2,6},{6,10},{... | collective-permute-start | bytes 147464 | tf_op jit(solution)/shard_map/ppermute | solution.py:522
  37.4 1.3 %collective-permute-start.15 = (bf16[48,512]{1,0:T(8,128)(2,1)S(1)}, bf16[48,512]{1,0:T(8,128)(2,1)S(1)}, u32[]{:S(2)}, u32[]{:S(2)}) collective-permute-start(bf16[48,512]{1,0:T(8,128)(2,1)S(1)} %add_convert_fusion.1.refs_0_), channel_id=1, source_target_pairs={{0,8},{4,12},{8,0},{12,4},{1,9},{5,13},{9,1},{13,5},{2,10},{6,14},... | collective-permute-start | bytes 147464 | tf_op jit(solution)/shard_map/ppermute | solution.py:522
  38.7 1.9 %collective-permute-start.16 = (bf16[48,512]{1,0:T(8,128)(2,1)S(1)}, bf16[48,512]{1,0:T(8,128)(2,1)S(1)}, u32[]{:S(2)}, u32[]{:S(2)}) collective-permute-start(bf16[48,512]{1,0:T(8,128)(2,1)S(1)} %add_convert_fusion.1.refs_0_), channel_id=1, source_target_pairs={{0,12},{4,0},{8,4},{12,8},{1,13},{5,1},{9,5},{13,9},{2,14},{6,2},{... | collective-permute-start | bytes 147464 | tf_op jit(solution)/shard_map/ppermute | solution.py:522
  40.6 0.0 collective-permute-done.17
  40.6 0.8 %fusion = bf16[1,512,256]{2,1,0:T(8,128)(2,1)} fusion(f32[512,256]{1,0:T(8,128)S(1)} %get-tuple-element.72, bf16[512,256]{1,0:T(8,128)(2,1)S(1)} %collective-permute-done.17), kind=kLoop, calls=%fused_computation.1 | loop fusion | flops 393216 | bytes 1048576 | tf_op jit(solution)/shard_map/broadcast_in_dim | solution.py:512
  41.4 0.0 collective-permute-done.14.refs_1_
  41.4 1.5 %collective-permute-done.15.refs_2_ = bf16[48,512]{1,0:T(8,128)(2,1)S(1)} collective-permute-done((bf16[48,512]{1,0:T(8,128)(2,1)S(1)}, bf16[48,512]{1,0:T(8,128)(2,1)S(1)}, u32[]{:S(2)}, u32[]{:S(2)}) %collective-permute-start.15) | collective-permute-done | bytes 49184 | tf_op jit(solution)/shard_map/ppermute | solution.py:522
  42.9 0.0 collective-permute-done.16.refs_3_
  43.0 0.1 collective-permute-start.18
  43.0 1.2 %collective-permute-done.18.recv_ref = f32[48,256]{1,0:T(8,128)S(1)} collective-permute-done((f32[48,256]{1,0:T(8,128)S(1)}, f32[48,256]{1,0:T(8,128)S(1)}, u32[]{:S(2)}, u32[]{:S(2)}) %collective-permute-start.18) | collective-permute-done | bytes 49184 | tf_op jit(solution)/shard_map/ppermute | solution.py:336
  44.2 0.7 %shard_map.130 = (f32[48,512]{1,0:T(8,128)}, f32[48,256]{1,0:T(8,128)}) custom-call(f32[48,256]{1,0:T(8,128)S(1)} %get-tuple-element.79.own_ref, f32[48,256]{1,0:T(8,128)S(1)} %collective-permute-done.18.recv_ref, f32[48,256]{1,0:T(8,128)S(1)} %get-tuple-element.80.up_ref), custom_call_target="tpu_custom_call" | custom-call | bytes 1048576 | tf_op jit(solution)/shard_map/pallas_call | solution.py:323
  (5 shorter events, 0.1 us)
Async XLA Ops:
  1.6 10.3 %collective-permute-start.2 = (bf16[128,512]{1,0:T(8,128)(2,1)S(1)}, bf16[128,512]{1,0:T(8,128)(2,1)S(1)}, u32[]{:S(2)}, u32[]{:S(2)}) collective-permute-start(bf16[128,512]{1,0:T(8,128)(2,1)S(1)} %get-tuple-element.43.refs_12_), channel_id=1, source_target_pairs={{0,12},{4,8},{8,4},{12,0},{16,24},{20,28},{24,16},{28,20},{1,13},{... | collective-permute-start | bytes 393224 | tf_op jit(solution)/shard_map/ppermute | solution.py:365
  6.7 6.8 %collective-permute-start.3 = (bf16[128,512]{1,0:T(8,128)(2,1)S(1)}, bf16[128,512]{1,0:T(8,128)(2,1)S(1)}, u32[]{:S(2)}, u32[]{:S(2)}) collective-permute-start(bf16[128,512]{1,0:T(8,128)(2,1)S(1)} %get-tuple-element.43.refs_12_), channel_id=1, source_target_pairs={{0,4},{4,0},{8,12},{12,8},{1,5},{5,1},{9,13},{13,9},{2,6},{6,2},{1... | collective-permute-start | bytes 393224 | tf_op jit(solution)/shard_map/ppermute | solution.py:336
  9.1 9.7 %collective-permute-start = (bf16[256,512]{1,0:T(8,128)(2,1)S(1)}, bf16[256,512]{1,0:T(8,128)(2,1)S(1)}, u32[]{:S(2)}, u32[]{:S(2)}) collective-permute-start(bf16[256,512]{1,0:T(8,128)(2,1)S(1)} %get-tuple-element.47), channel_id=1, source_target_pairs={{0,4},{4,0},{8,12},{12,8},{1,5},{5,1},{9,13},{13,9},{2,6},{6,2},{1... | collective-permute-start | bytes 786440 | tf_op jit(solution)/shard_map/ppermute | solution.py:336
  11.2 7.6 %collective-permute-start.1 = (bf16[256,512]{1,0:T(8,128)(2,1)S(1)}, bf16[256,512]{1,0:T(8,128)(2,1)S(1)}, u32[]{:S(2)}, u32[]{:S(2)}) collective-permute-start(bf16[256,512]{1,0:T(8,128)(2,1)S(1)} %get-tuple-element.47), channel_id=1, source_target_pairs={{0,0},{4,8},{8,4},{12,12},{1,1},{5,9},{9,5},{13,13},{2,2},{6,10},{... | collective-permute-start | bytes 786440 | tf_op jit(solution)/shard_map/ppermute | solution.py:442
  13.6 5.0 %collective-permute-start.4 = (bf16[128,512]{1,0:T(8,128)(2,1)S(1)}, bf16[128,512]{1,0:T(8,128)(2,1)S(1)}, u32[]{:S(2)}, u32[]{:S(2)}) collective-permute-start(bf16[128,512]{1,0:T(8,128)(2,1)S(1)} %collective-permute-done.2.refs_14_.two_ref), channel_id=1, source_target_pairs={{0,16},{16,0},{1,17},{17,1},{2,18},{18,2},{3,19},{19,3},{4,20},{20... | collective-permute-start | bytes 393224 | tf_op jit(solution)/shard_map/ppermute | solution.py:336
  14.1 5.4 %collective-permute-start.9 = (bf16[512,256]{1,0:T(8,128)(2,1)S(1)}, bf16[512,256]{1,0:T(8,128)(2,1)S(1)}, u32[]{:S(2)}, u32[]{:S(2)}) collective-permute-start(bf16[512,256]{1,0:T(8,128)(2,1)S(1)} %get-tuple-element.55.refs_8_), channel_id=1, source_target_pairs={{0,1},{1,0},{2,3},{3,2},{4,5},{5,4},{6,7},{7,6},{8,9},{9,8},{10,11... | collective-permute-start | bytes 786440 | tf_op jit(solution)/shard_map/ppermute | solution.py:336
  14.1 11.4 %collective-permute-start.10 = (bf16[256,512]{1,0:T(8,128)(2,1)S(1)}, bf16[256,512]{1,0:T(8,128)(2,1)S(1)}, u32[]{:S(2)}, u32[]{:S(2)}) collective-permute-start(bf16[256,512]{1,0:T(8,128)(2,1)S(1)} %shard_map.125), channel_id=1, source_target_pairs={{0,2},{2,0},{1,3},{3,1},{4,6},{6,4},{5,7},{7,5},{8,10},{10,8},{9,1... | collective-permute-start | bytes 786440 | tf_op jit(solution)/shard_map/ppermute | solution.py:336
  18.8 1.4 %collective-permute-start.5 = (bf16[128,512]{1,0:T(8,128)(2,1)S(1)}, bf16[128,512]{1,0:T(8,128)(2,1)S(1)}, u32[]{:S(2)}, u32[]{:S(2)}) collective-permute-start(bf16[128,512]{1,0:T(8,128)(2,1)S(1)} %get-tuple-element.51), channel_id=1, source_target_pairs={{0,1},{1,0},{2,3},{3,2},{4,5},{5,4},{6,7},{7,6},{8,9},{9,8},{10,11... | collective-permute-start | bytes 393224 | tf_op jit(solution)/shard_map/ppermute | solution.py:336
  18.9 2.8 %collective-permute-start.6 = (bf16[128,512]{1,0:T(8,128)(2,1)S(1)}, bf16[128,512]{1,0:T(8,128)(2,1)S(1)}, u32[]{:S(2)}, u32[]{:S(2)}) collective-permute-start(bf16[128,512]{1,0:T(8,128)(2,1)S(1)} %get-tuple-element.52), channel_id=1, source_target_pairs={{0,1},{1,0},{2,3},{3,2},{4,5},{5,4},{6,7},{7,6},{8,9},{9,8},{10,11... | collective-permute-start | bytes 393224 | tf_op jit(solution)/shard_map/ppermute | solution.py:336
  19.4 2.3 %collective-permute-start.7 = (bf16[128,512]{1,0:T(8,128)(2,1)S(1)}, bf16[128,512]{1,0:T(8,128)(2,1)S(1)}, u32[]{:S(2)}, u32[]{:S(2)}) collective-permute-start(bf16[128,512]{1,0:T(8,128)(2,1)S(1)} %get-tuple-element.53), channel_id=1, source_target_pairs={{0,1},{1,0},{2,3},{3,2},{4,5},{5,4},{6,7},{7,6},{8,9},{9,8},{10,11... | collective-permute-start | bytes 393224 | tf_op jit(solution)/shard_map/ppermute | solution.py:336
  19.5 2.3 %collective-permute-start.8 = (bf16[128,512]{1,0:T(8,128)(2,1)S(1)}, bf16[128,512]{1,0:T(8,128)(2,1)S(1)}, u32[]{:S(2)}, u32[]{:S(2)}) collective-permute-start(bf16[128,512]{1,0:T(8,128)(2,1)S(1)} %get-tuple-element.54), channel_id=1, source_target_pairs={{0,1},{1,0},{2,3},{3,2},{4,5},{5,4},{6,7},{7,6},{8,9},{9,8},{10,11... | collective-permute-start | bytes 393224 | tf_op jit(solution)/shard_map/ppermute | solution.py:336
  20.2 5.6 %collective-permute-start.11 = (bf16[128,512]{1,0:T(8,128)(2,1)S(1)}, bf16[128,512]{1,0:T(8,128)(2,1)S(1)}, u32[]{:S(2)}, u32[]{:S(2)}) collective-permute-start(bf16[128,512]{1,0:T(8,128)(2,1)S(1)} %collective-permute-done.4.refs_15_), channel_id=1, source_target_pairs={{0,2},{2,0},{1,3},{3,1},{4,6},{6,4},{5,7},{7,5},{8,10},{10,8},{9,1... | collective-permute-start | bytes 393224 | tf_op jit(solution)/shard_map/ppermute | solution.py:336
  29.6 1.3 %collective-permute-start.12 = (bf16[48,256]{1,0:T(8,128)(2,1)S(1)}, bf16[48,256]{1,0:T(8,128)(2,1)S(1)}, u32[]{:S(2)}, u32[]{:S(2)}) collective-permute-start(bf16[48,256]{1,0:T(8,128)(2,1)S(1)} %get-tuple-element.64), channel_id=1, source_target_pairs={{0,1},{1,0},{2,3},{3,2},{4,5},{5,4},{6,7},{7,6},{8,9},{9,8},{10,11... | collective-permute-start | bytes 73736 | tf_op jit(solution)/shard_map/ppermute | solution.py:336
  30.9 4.2 %collective-permute-start.13 = (bf16[48,512]{1,0:T(8,128)(2,1)S(1)}, bf16[48,512]{1,0:T(8,128)(2,1)S(1)}, u32[]{:S(2)}, u32[]{:S(2)}) collective-permute-start(bf16[48,512]{1,0:T(8,128)(2,1)S(1)} %shard_map.127), channel_id=1, source_target_pairs={{0,2},{2,0},{1,3},{3,1},{4,6},{6,4},{5,7},{7,5},{8,10},{10,8},{9,1... | collective-permute-start | bytes 147464 | tf_op jit(solution)/shard_map/ppermute | solution.py:336
  33.4 7.2 %collective-permute-start.17 = (bf16[512,256]{1,0:T(8,128)(2,1)S(1)}, bf16[512,256]{1,0:T(8,128)(2,1)S(1)}, u32[]{:S(2)}, u32[]{:S(2)}) collective-permute-start(bf16[512,256]{1,0:T(8,128)(2,1)S(1)} %get-tuple-element.73), channel_id=1, source_target_pairs={{0,1},{1,0},{2,3},{3,2},{4,5},{5,4},{6,7},{7,6},{8,9},{9,8},{10,11... | collective-permute-start | bytes 786440 | tf_op jit(solution)/shard_map/ppermute | solution.py:336
  35.0 6.3 %collective-permute-start.14 = (bf16[48,512]{1,0:T(8,128)(2,1)S(1)}, bf16[48,512]{1,0:T(8,128)(2,1)S(1)}, u32[]{:S(2)}, u32[]{:S(2)}) collective-permute-start(bf16[48,512]{1,0:T(8,128)(2,1)S(1)} %add_convert_fusion.1.refs_0_), channel_id=1, source_target_pairs={{0,4},{4,8},{8,12},{12,0},{1,5},{5,9},{9,13},{13,1},{2,6},{6,10},{... | collective-permute-start | bytes 147464 | tf_op jit(solution)/shard_map/ppermute | solution.py:522
  37.4 5.5 %collective-permute-start.15 = (bf16[48,512]{1,0:T(8,128)(2,1)S(1)}, bf16[48,512]{1,0:T(8,128)(2,1)S(1)}, u32[]{:S(2)}, u32[]{:S(2)}) collective-permute-start(bf16[48,512]{1,0:T(8,128)(2,1)S(1)} %add_convert_fusion.1.refs_0_), channel_id=1, source_target_pairs={{0,8},{4,12},{8,0},{12,4},{1,9},{5,13},{9,1},{13,5},{2,10},{6,14},... | collective-permute-start | bytes 147464 | tf_op jit(solution)/shard_map/ppermute | solution.py:522
  38.7 4.2 %collective-permute-start.16 = (bf16[48,512]{1,0:T(8,128)(2,1)S(1)}, bf16[48,512]{1,0:T(8,128)(2,1)S(1)}, u32[]{:S(2)}, u32[]{:S(2)}) collective-permute-start(bf16[48,512]{1,0:T(8,128)(2,1)S(1)} %add_convert_fusion.1.refs_0_), channel_id=1, source_target_pairs={{0,12},{4,0},{8,4},{12,8},{1,13},{5,1},{9,5},{13,9},{2,14},{6,2},{... | collective-permute-start | bytes 147464 | tf_op jit(solution)/shard_map/ppermute | solution.py:522
  43.0 1.3 %collective-permute-start.18 = (f32[48,256]{1,0:T(8,128)S(1)}, f32[48,256]{1,0:T(8,128)S(1)}, u32[]{:S(2)}, u32[]{:S(2)}) collective-permute-start(f32[48,256]{1,0:T(8,128)S(1)} %get-tuple-element.79.own_ref), channel_id=1, source_target_pairs={{0,1},{1,0},{2,3},{3,2},{4,5},{5,4},{6,7},{7,6},{8,9},{9,8},{10,11... | collective-permute-start | bytes 147464 | tf_op jit(solution)/shard_map/ppermute | solution.py:336
